TPU v7x, 32 devices: a whole 2x2x4 slice. The times are simulated.
32 devices in a mesh: seq: 4 (over y, x), fsdp: 8 (over z, core).
Axes of the slice: x: 2, y: 2, z: 4, core: 2. Of those that a mesh axis runs over, the one named last changes fastest.
Arguments:
- tokens: bfloat16 [16, 1024, 2048], P('fsdp', 'seq'), may hold values from -6 to 6
- cotangent: bfloat16 [16, 1024, 2048], P('fsdp', 'seq'), may hold values from -6 to 6
- w_qkv: bfloat16 [2048, 6144], P('fsdp'), may hold values from -0.125 to 0.125
- qv_bias: float32 [2, 2048], replicated, may hold values from -3 to 3
- w_out: bfloat16 [2048, 2048], P('fsdp'), may hold values from -0.375 to 0.375
- out_bias: float32 [2048], replicated, may hold values from -3 to 3
- ln1_gain: float32 [2048], replicated, may hold values from 0.25 to 1.75
- ln1_shift: float32 [2048], replicated, may hold values from -2 to 2
- ln2_gain: float32 [2048], replicated, may hold values from 0.25 to 1.75
- ln2_shift: float32 [2048], replicated, may hold values from -2 to 2
- w_up: bfloat16 [2048, 8192], P('fsdp'), may hold values from -0.125 to 0.125
- up_bias: float32 [8192], replicated, may hold values from -3 to 3
- w_down: bfloat16 [8192, 2048], P(None, 'fsdp'), may hold values from -0.0625 to 0.0625
- down_bias: float32 [2048], replicated, may hold values from -3 to 3
Outputs:
- result: bfloat16 [16, 1024, 2048], P('fsdp', 'seq')
- grad_tokens: bfloat16 [16, 1024, 2048], P('fsdp', 'seq')
- grad_w_qkv: float32 [2048, 6144], P(('seq', 'fsdp'))
- grad_qv_bias: float32 [2, 2048], replicated
- grad_w_out: float32 [2048, 2048], P(('seq', 'fsdp'))
- grad_out_bias: float32 [2048], replicated
- grad_ln1_gain: float32 [2048], replicated
- grad_ln1_shift: float32 [2048], replicated
- grad_ln2_gain: float32 [2048], replicated
- grad_ln2_shift: float32 [2048], replicated
- grad_w_up: float32 [2048, 8192], P(('seq', 'fsdp'))
- grad_up_bias: float32 [8192], replicated
- grad_w_down: float32 [8192, 2048], P(None, ('seq', 'fsdp'))
- grad_down_bias: float32 [2048], replicated
All inputs are finite; a program needn't handle non-finite values.
Results may differ from a plain program's by a relative error of at most 0.012.
Values may be sent and summed in bfloat16 or wider, within the bound.
A program may use at most 768 MiB of HBM per device.

v0:
```python
from functools import partial

import jax
import jax.numpy as jnp
from jax import lax
from jax.sharding import PartitionSpec as P

HEADS = 32
HEAD_DIM = 64
BLOCK = 256


def layer_norm(token_rows, gain_vec, shift_vec):
    average = jnp.mean(token_rows, axis=-1, keepdims=True)
    centred = token_rows - average
    spread = jnp.mean(centred * centred, axis=-1, keepdims=True)
    return centred * lax.rsqrt(spread + 1e-05) * gain_vec + shift_vec


def exact_gelu(values):
    return jax.nn.gelu(values, approximate=False)


def contract_last(left_side, right_side):
    return lax.dot_general(
        left_side, right_side, (((1,), (1,)), ((), ())), preferred_element_type=jnp.float32
    )


def outer_part(left_side, right_side):
    return lax.dot_general(
        left_side, right_side, (((0,), (0,)), ((), ())), preferred_element_type=jnp.float32
    )


def fetch_weights(w_qkv, w_out, w_up, w_down):
    gathered = (
        lax.all_gather(w_qkv, "fsdp", axis=0, tiled=True),
        lax.all_gather(w_out, "fsdp", axis=0, tiled=True),
        lax.all_gather(w_up, "fsdp", axis=0, tiled=True),
    )
    down_full = lax.all_gather(w_down, "fsdp", axis=1, tiled=True)
    return (gathered[0], gathered[1], gathered[2], down_full)


def head_scores(query_rows, key_rows, slopes):
    length = query_rows.shape[0]
    heads_here = slopes.shape[0]
    query_heads = query_rows.reshape(length, heads_here, HEAD_DIM)
    key_heads = key_rows.reshape(length, heads_here, HEAD_DIM)
    scores = jnp.einsum(
        "qhd,khd->hqk", query_heads, key_heads, preferred_element_type=jnp.float32
    ) * HEAD_DIM ** (-0.5)
    position = jnp.arange(length, dtype=jnp.int32)
    distance = jnp.abs(position[:, None] - position[None, :]).astype(jnp.float32)
    allowed = position[None, :] // BLOCK <= position[:, None] // BLOCK
    scores = scores - slopes[:, None, None] * distance[None]
    return jnp.where(allowed[None], scores, -1e30)


def attend_forward(slopes, pieces):
    query_rows, key_rows, value_rows = pieces
    length = query_rows.shape[0]
    heads_here = slopes.shape[0]
    scores = head_scores(query_rows, key_rows, slopes)
    highest = jnp.max(scores, axis=-1, keepdims=True)
    weights = jnp.exp(scores - highest)
    totals = jnp.sum(weights, axis=-1, keepdims=True)
    probs = (weights / totals).astype(jnp.bfloat16)
    value_heads = value_rows.reshape(length, heads_here, HEAD_DIM)
    mixed = jnp.einsum("hqk,khd->qhd", probs, value_heads, preferred_element_type=jnp.float32)
    return (mixed.reshape(length, -1).astype(jnp.bfloat16), (highest + jnp.log(totals))[..., 0])


def attend_backward(slopes, pieces):
    query_rows, key_rows, value_rows, upstream, log_totals = pieces
    length = query_rows.shape[0]
    heads_here = slopes.shape[0]
    scale = HEAD_DIM ** (-0.5)
    scores = head_scores(query_rows, key_rows, slopes)
    probs = jnp.exp(scores - log_totals[..., None])
    query_heads = query_rows.reshape(length, heads_here, HEAD_DIM)
    key_heads = key_rows.reshape(length, heads_here, HEAD_DIM)
    value_heads = value_rows.reshape(length, heads_here, HEAD_DIM)
    upstream_heads = upstream.reshape(length, heads_here, HEAD_DIM)
    value_grad = jnp.einsum(
        "hqk,qhd->khd",
        probs.astype(jnp.bfloat16),
        upstream_heads,
        preferred_element_type=jnp.float32,
    )
    prob_grad = jnp.einsum(
        "qhd,khd->hqk", upstream_heads, value_heads, preferred_element_type=jnp.float32
    )
    inner = jnp.sum(probs * prob_grad, axis=-1, keepdims=True)
    score_grad = (probs * (prob_grad - inner)).astype(jnp.bfloat16)
    query_grad = (
        jnp.einsum("hqk,khd->qhd", score_grad, key_heads, preferred_element_type=jnp.float32)
        * scale
    )
    key_grad = (
        jnp.einsum("hqk,qhd->khd", score_grad, query_heads, preferred_element_type=jnp.float32)
        * scale
    )
    stacked = jnp.stack(
        [
            query_grad.reshape(length, -1),
            key_grad.reshape(length, -1),
            value_grad.reshape(length, -1),
        ],
        axis=1,
    )
    return stacked.astype(jnp.bfloat16)


def local(
    tokens,
    cotangent,
    w_qkv,
    qv_bias,
    w_out,
    out_bias,
    ln1_gain,
    ln1_shift,
    ln2_gain,
    ln2_shift,
    w_up,
    up_bias,
    w_down,
    down_bias,
):
    seq_count, local_len, model_width = tokens.shape
    groups = lax.axis_size("seq")
    heads_here = HEADS // groups
    slab = heads_here * HEAD_DIM
    head_index = lax.axis_index("seq") * heads_here + jnp.arange(1, heads_here + 1, dtype=jnp.int32)
    slopes = 2.0 ** (-8.0 * head_index.astype(jnp.float32) / HEADS)
    full_qkv, full_out, full_up, full_down = fetch_weights(w_qkv, w_out, w_up, w_down)
    token_rows = tokens.reshape(-1, model_width).astype(jnp.float32)
    normed_wide, first_back = jax.vjp(layer_norm, token_rows, ln1_gain, ln1_shift)
    normed = normed_wide.astype(jnp.bfloat16)
    bias_row = jnp.concatenate([qv_bias[0], jnp.zeros_like(qv_bias[0]), qv_bias[1]])
    projected = (jnp.dot(normed, full_qkv, preferred_element_type=jnp.float32) + bias_row).astype(
        jnp.bfloat16
    )
    packed = projected.reshape(seq_count, local_len, 3, groups, slab)
    by_heads = lax.all_to_all(packed, "seq", split_axis=3, concat_axis=1, tiled=True)
    queries = by_heads[:, :, 0, 0]
    key_rows = by_heads[:, :, 1, 0]
    value_rows = by_heads[:, :, 2, 0]
    mixed, log_totals = lax.map(partial(attend_forward, slopes), (queries, key_rows, value_rows))
    back_rows = lax.all_to_all(mixed[:, :, None], "seq", split_axis=1, concat_axis=2, tiled=True)
    mixed_rows = back_rows.reshape(-1, model_width)
    branch = jnp.dot(mixed_rows, full_out, preferred_element_type=jnp.float32) + out_bias
    middle = token_rows + branch
    second_wide, second_back = jax.vjp(layer_norm, middle, ln2_gain, ln2_shift)
    second = second_wide.astype(jnp.bfloat16)
    hidden = jnp.dot(second, full_up, preferred_element_type=jnp.float32) + up_bias
    active_wide, gelu_back = jax.vjp(exact_gelu, hidden)
    active = active_wide.astype(jnp.bfloat16)
    outcome = middle + (jnp.dot(active, full_down, preferred_element_type=jnp.float32) + down_bias)
    result = outcome.astype(jnp.bfloat16).reshape(tokens.shape)
    back_qkv, back_out, back_up, back_down = fetch_weights(w_qkv, w_out, w_up, w_down)
    upstream = cotangent.reshape(-1, model_width)
    upstream_wide = upstream.astype(jnp.float32)
    active_grad = contract_last(upstream, back_down)
    hidden_grad = gelu_back(active_grad)[0].astype(jnp.bfloat16)
    second_grad = contract_last(hidden_grad, back_up)
    middle_part, ln2_gain_grad, ln2_shift_grad = second_back(second_grad)
    middle_grad = upstream_wide + middle_part
    branch_grad = middle_grad.astype(jnp.bfloat16)
    mixed_grad = contract_last(branch_grad, back_out).astype(jnp.bfloat16)
    grad_heads = lax.all_to_all(
        mixed_grad.reshape(seq_count, local_len, groups, slab),
        "seq",
        split_axis=2,
        concat_axis=1,
        tiled=True,
    )
    attention_grads = lax.map(
        partial(attend_backward, slopes),
        (queries, key_rows, value_rows, grad_heads[:, :, 0], log_totals),
    )
    qkv_back = lax.all_to_all(
        attention_grads[:, :, :, None], "seq", split_axis=1, concat_axis=3, tiled=True
    )
    qkv_grad = qkv_back.reshape(-1, 3 * model_width)
    hidden_width = full_up.shape[1]
    summed = lax.psum_scatter(
        jnp.concatenate(
            [
                outer_part(normed, qkv_grad),
                outer_part(mixed_rows, branch_grad),
                jnp.concatenate(
                    [outer_part(second, hidden_grad), outer_part(upstream, active)], axis=1
                ),
            ],
            axis=1,
        ),
        ("seq", "fsdp"),
        scatter_dimension=0,
        tiled=True,
    )
    grad_w_qkv = summed[:, : 3 * model_width]
    grad_w_out = summed[:, 3 * model_width : 4 * model_width]
    grad_w_up = summed[:, 4 * model_width : 4 * model_width + hidden_width]
    grad_w_down = summed[:, 4 * model_width + hidden_width :].T
    normed_grad = contract_last(qkv_grad, back_qkv)
    input_part, ln1_gain_grad, ln1_shift_grad = first_back(normed_grad)
    grad_tokens = (middle_grad + input_part).astype(jnp.bfloat16).reshape(tokens.shape)
    bias_sums = jnp.sum(qkv_grad.astype(jnp.float32), axis=0)
    qv_grad = jnp.stack([bias_sums[:model_width], bias_sums[2 * model_width :]])
    small = lax.psum(
        (
            qv_grad,
            jnp.sum(branch_grad.astype(jnp.float32), axis=0),
            ln1_gain_grad,
            ln1_shift_grad,
            ln2_gain_grad,
            ln2_shift_grad,
            jnp.sum(hidden_grad.astype(jnp.float32), axis=0),
            jnp.sum(upstream_wide, axis=0),
        ),
        ("seq", "fsdp"),
    )
    return (
        result,
        grad_tokens,
        grad_w_qkv,
        small[0],
        grad_w_out,
        small[1],
        small[2],
        small[3],
        small[4],
        small[5],
        grad_w_up,
        small[6],
        grad_w_down,
        small[7],
    )


def solution(mesh):
    return jax.shard_map(
        local,
        mesh=mesh,
        in_specs=(
            P("fsdp", "seq", None),
            P("fsdp", "seq", None),
            P("fsdp", None),
            P(),
            P("fsdp", None),
            P(),
            P(),
            P(),
            P(),
            P(),
            P("fsdp", None),
            P(),
            P(None, "fsdp"),
            P(),
        ),
        out_specs=(
            P("fsdp", "seq", None),
            P("fsdp", "seq", None),
            P(("seq", "fsdp"), None),
            P(),
            P(("seq", "fsdp"), None),
            P(),
            P(),
            P(),
            P(),
            P(),
            P(("seq", "fsdp"), None),
            P(),
            P(None, ("seq", "fsdp")),
            P(),
        ),
        check_vma=False,
    )
```

profile of v0, /device:TPU:0, one launch (start us, length us, event | category | flops | bytes accessed | tf_op | source)
XLA Modules:
  0.0 3308.8 jit_solution(11476624993976321076)
XLA Ops:
  14.5 217.8 %all-gather.5.cloned.1.call-done = bf16[2048,6144]{1,0:T(8,128)(2,1)} async-done(((bf16[256,6144]{1,0:T(8,128)(2,1)}), bf16[2048,6144]{1,0:T(8,128)(2,1)}) %all-gather.5.cloned.1.call-update) | async-done | bytes 25165840 | tf_op jit(solution)/shard_map/all_gather | solution.py:38
  232.3 20.2 add_convert_fusion.1
  278.1 70.5 %all-to-all-done = bf16[2,256,3,4,512]{4,1,2,0,3:T(8,128)(2,1)} async-done(((bf16[2,256,3,4,512]{4,1,2,0,3:T(8,128)(2,1)}), bf16[2,256,3,4,512]{4,1,2,0,3:T(8,128)(2,1)}, u32[]{:S(2)}, u32[]{:S(2)}) %all-to-all-start) | async-done | bytes 6291488 | tf_op jit(solution)/shard_map/all_to_all | solution.py:147
  364.0 126.5 %while.30 = (s32[]{:T(128)}, bf16[2,1024,512]{1,2,0:T(8,128)(2,1)}, f32[2,8,1024]{2,1,0:T(8,128)S(1)}, bf16[2,1024,512]{1,2,0:T(8,128)(2,1)}, bf16[2,1024,512]{1...) while((s32[]{:T(128)}, bf16[2,1024,512]{1,2,0:T(8,128)(2,1)}, ...), condition=%wide.region_5.6_spmd.clone, body=%wide.region_2.5_spmd.clone.sunk | while | flops 2303197184 | bytes 151265552 | solution.py:151
  433.7 19.7 fusion.114
  505.5 20.8 all-to-all-done.1
  542.6 60.4 %all-gather.9.cloned.1.call-done = bf16[2048,8192]{1,0:T(8,128)(2,1)} async-done(((bf16[256,8192]{1,0:T(8,128)(2,1)}), bf16[2048,8192]{1,0:T(8,128)(2,1)}) %all-gather.9.cloned.1.call-update) | async-done | bytes 33554448 | tf_op jit(solution)/shard_map/all_gather | solution.py:40
  602.9 28.8 fusion.49
  631.7 261.4 %all-gather.11.cloned.1.call-done = bf16[8192,2048]{1,0:T(8,128)(2,1)} async-done(((bf16[8192,256]{1,0:T(8,128)(2,1)}), bf16[8192,2048]{1,0:T(8,128)(2,1)}) %all-gather.11.cloned.1.call-update) | async-done | bytes 33554448 | tf_op jit(solution)/shard_map/all_gather | solution.py:42
  893.1 61.8 %convert_reduce_fusion = (f32[8192]{0:T(1024)}, bf16[512,8192]{1,0:T(8,128)(2,1)}, f32[512,8192]{1,0:T(8,128)}) fusion(f32[512,8192]{1,0:T(8,128)} %fusion.49, f32[8192]{0:T(1024)S(1)} %copy-done.41, bf16[512,2048]{1,0:T(8,128)(2,1)S(1)} %bitcast.209, bf16[8192,2048]{1,0:T(8,128)(2,1)} %all-gather.11.cloned.1.call-done), kind=kOutput, calls=%fused_computation.54 | convolution fusion | flops 17494433792 | bytes 77660160 | tf_op jit(solution)/shard_map/dot_general | solution.py:25
  954.9 26.5 multiply_reduce_fusion.1
  1021.7 29.1 convolution_bitcast_fusion
  1066.5 226.7 %while.31 = (s32[]{:T(128)}, bf16[2,1024,3,512]{1,3,2,0:T(8,128)(2,1)}, bf16[2,1024,512]{1,2,0:T(8,128)(2,1)}, bf16[2,1024,512]{1,2,0:T(8,128)(2,1)}, f32[2,8,10...) while((s32[]{:T(128)}, ...), condition=%wide.region_12.13_spmd.clone, body=%wide.region_10.12_spmd.clone.sunk | while | flops 5477236736 | bytes 306356512 | solution.py:180
  1086.3 26.4 multiply_reduce_fusion.5
  1112.6 27.8 multiply_convert_fusion.7
  1199.3 26.4 multiply_reduce_fusion.5
  1225.6 27.8 multiply_convert_fusion.7
  1315.1 32.0 fusion.48
  1347.0 38.5 %all-to-all-done.3 = bf16[2,1024,3,1,512]{4,0,3,2,1:T(2,128)(2,1)} async-done(((bf16[2,1024,3,1,512]{4,0,3,2,1:T(2,128)(2,1)}), bf16[2,1024,3,1,512]{4,0,3,2,1:T(2,128)(2,1)}, u32[]{:S(2)}, u32[]{:S(2)}) %all-to-all-start.3) | async-done | bytes 6291488 | tf_op jit(solution)/shard_map/all_to_all | solution.py:184
  1408.7 22.6 fusion.57
  1431.2 130.5 %pad_maximum_fusion = f32[2048,24576]{1,0:T(8,128)} fusion(f32[2048,8192]{1,0:T(8,128)} %convolution_bitcast_fusion, f32[2048,8192]{1,0:T(8,128)} %fusion.48, f32[2048,2048]{1,0:T(8,128)} %fusion.58, f32[2048,6144]{1,0:T(8,128)} %fusion.57), kind=kLoop, calls=%fused_computation.50 | loop fusion | flops 150994944 | bytes 402653184 | tf_op jit(solution)/shard_map/concatenate | solution.py:190
  1564.3 30.5 add_convert_fusion.3
  1629.3 1531.5 %reduce-scatter.2.cloned.1.call-done = f32[64,24576]{1,0:T(8,128)} async-done(((f32[2048,24576]{1,0:T(8,128)}), f32[64,24576]{1,0:T(8,128)}) %reduce-scatter.2.cloned.1.call-update) | async-done | bytes 6291472 | tf_op jit(solution)/shard_map/reduce_scatter | solution.py:189
  3170.0 121.1 %all-reduce.3.cloned.1.call-done = (f32[2,2048]{1,0:T(2,128)}, f32[2048]{0:T(1024)}, f32[2048]{0:T(1024)}, f32[2048]{0:T(1024)}, f32[2048]{0:T(1024)}, /*index=5*/f32[2048]{0:T(1024)}, f32[8192]{0:T(1024)}, f32[2048]{0:T(1024)}) async-done(((f32[2,2048]{1,0:T(2,128)}, f32[2048]{0:T(1024)}, f32[2048]{0:T(1024)}, f32[2048]{0:T(1024)}, f32[2048]{0:T(1024)}, /*index=5*/f32[2048]{0:T(1024)}, f32[8192]{0:T(1024)}, ...) | async-done | bytes 98320 | tf_op jit(solution)/shard_map/psum | solution.py:213
  (254 shorter events, 460.6 us)
Async XLA Ops:
  7.2 225.1 %all-gather.5.cloned.1.call-start = ((), (), s32[]{:S(2)}) async-start(), calls=%async_computation.5 | async-start | bytes 28311552 | tf_op jit(solution)/shard_map/all_gather | solution.py:38
  7.9 523.7 %all-gather.7.cloned.1.call-start = ((), (), s32[]{:S(2)}) async-start(), calls=%async_computation.6 | async-start | bytes 9437184 | tf_op jit(solution)/shard_map/all_gather | solution.py:39
  8.7 594.2 %all-gather.9.cloned.1.call-start = ((), (), s32[]{:S(2)}) async-start(), calls=%async_computation.7 | async-start | bytes 37748736 | tf_op jit(solution)/shard_map/all_gather | solution.py:40
  9.4 883.6 %all-gather.11.cloned.1.call-start = ((), (), s32[]{:S(2)}) async-start(), calls=%async_computation.8 | async-start | bytes 37748736 | tf_op jit(solution)/shard_map/all_gather | solution.py:42
  272.7 75.9 %all-to-all-start = ((bf16[2,256,3,4,512]{4,1,2,0,3:T(8,128)(2,1)}), bf16[2,256,3,4,512]{4,1,2,0,3:T(8,128)(2,1)}, u32[]{:S(2)}, u32[]{:S(2)}) async-start(bf16[2,256,3,4,512]{4,1,2,0,3:T(8,128)(2,1)} %copy.83), calls=%async_computation | async-start | bytes 12582912 | tf_op jit(solution)/shard_map/all_to_all | solution.py:147
  433.7 19.7 copy-start
  497.2 29.2 all-to-all-start.1
  501.7 30.0 copy-start.52
  531.7 71.3 %copy-start.25 = (f32[2048]{0:T(1024)S(1)}, f32[2048]{0:T(1024)}, u32[]{:S(2)}) copy-start(f32[2048]{0:T(1024)} %param.26) | copy-start | bytes 24580
  531.7 71.3 %copy-start.28 = (f32[2048]{0:T(1024)S(1)}, f32[2048]{0:T(1024)}, u32[]{:S(2)}) copy-start(f32[2048]{0:T(1024)} %param.27) | copy-start | bytes 24580
  539.5 92.2 %copy-start.19 = (f32[512]{0:T(512)}, f32[512]{0:T(512)S(1)}, u32[]{:S(2)}) copy-start(f32[512]{0:T(512)S(1)} %broadcast_multiply_fusion) | copy-start | bytes 6148
  542.6 89.2 %copy-start.22 = (f32[512]{0:T(512)}, f32[512]{0:T(512)S(1)}, u32[]{:S(2)}) copy-start(f32[512]{0:T(512)S(1)} %fusion.43) | copy-start | bytes 6148
  542.6 350.5 %copy-start.13 = (bf16[2,256,2048]{2,1,0:T(8,128)(2,1)S(1)}, bf16[2,256,2048]{2,1,0:T(8,128)(2,1)}, u32[]{:S(2)}) copy-start(bf16[2,256,2048]{2,1,0:T(8,128)(2,1)} %param.19) | copy-start | bytes 6291460
  542.6 350.5 %copy-start.41 = (f32[8192]{0:T(1024)S(1)}, f32[8192]{0:T(1024)}, u32[]{:S(2)}) copy-start(f32[8192]{0:T(1024)} %param.29) | copy-start | bytes 98308
  893.1 61.8 %copy-start.12 = (f32[512,2048]{1,0:T(8,128)S(1)}, f32[512,2048]{1,0:T(8,128)}, u32[]{:S(2)}) copy-start(f32[512,2048]{1,0:T(8,128)} %copy-done.11) | copy-start | bytes 12582916
  893.1 61.8 %copy-start.20 = (f32[512]{0:T(512)S(1)}, f32[512]{0:T(512)}, u32[]{:S(2)}) copy-start(f32[512]{0:T(512)} %copy-done.19) | copy-start | bytes 6148
  893.1 61.8 %copy-start.23 = (f32[512]{0:T(512)S(1)}, f32[512]{0:T(512)}, u32[]{:S(2)}) copy-start(f32[512]{0:T(512)} %copy-done.22) | copy-start | bytes 6148
  893.1 61.8 %copy-start.26 = (f32[2048]{0:T(1024)S(1)}, f32[2048]{0:T(1024)}, u32[]{:S(2)}) copy-start(f32[2048]{0:T(1024)} %param.26) | copy-start | bytes 24580
  954.9 26.5 copy-start.43
  1017.3 46.2 %all-to-all-start.2 = ((bf16[2,256,4,512]{3,1,0,2:T(8,128)(2,1)}), bf16[2,256,4,512]{3,1,0,2:T(8,128)(2,1)}, u32[]{:S(2)}, u32[]{:S(2)}) async-start(bf16[2,256,4,512]{3,1,0,2:T(8,128)(2,1)} %copy.90), calls=%async_computation.2 | async-start | bytes 4194304 | tf_op jit(solution)/shard_map/all_to_all | solution.py:173
  1309.6 76.0 %all-to-all-start.3 = ((bf16[2,1024,3,1,512]{4,0,3,2,1:T(2,128)(2,1)}), bf16[2,1024,3,1,512]{4,0,3,2,1:T(2,128)(2,1)}, u32[]{:S(2)}, u32[]{:S(2)}) async-start(bf16[2,1024,3,1,512]{4,0,3,2,1:T(2,128)(2,1)} %bitcast.206), calls=%async_computation.3 | async-start | bytes 12582912 | tf_op jit(solution)/shard_map/all_to_all | solution.py:184
  1315.0 1845.9 %reduce-scatter.2.cloned.1.call-start = ((), (), s32[]{:S(2)}) async-start(), calls=%async_computation.9 | async-start | bytes 207618048 | tf_op jit(solution)/shard_map/reduce_scatter | solution.py:189
  1561.8 1729.4 %all-reduce.3.cloned.1.call-start = ((), (), s32[]{:S(2)}) async-start(), calls=%async_computation.10 | async-start | bytes 196608 | tf_op jit(solution)/shard_map/psum | solution.py:213
  1564.3 39.1 %copy-start.15 = (bf16[512,6144]{1,0:T(8,128)(2,1)S(1)}, bf16[512,6144]{1,0:T(8,128)(2,1)}, u32[]{:S(2)}) copy-start(bf16[512,6144]{1,0:T(8,128)(2,1)} %reshape.580) | copy-start | bytes 18874372
  (47 other events, 377.7 us)
Sparse Core Ops, SparseCore 0:
  9.7 222.5 all-gather.4
  233.9 80.2 all-gather.6
  315.8 287.1 all-gather.8
  604.4 288.6 all-gather.10
  1561.9 1598.9 reduce-scatter.1
  3168.3 122.8 all-reduce.2
where the time goes:
time: 3320 us; the launch traced here: 3310 us
  waiting for transfers between devices  2320 us (70%)
  matrix products  526 us (16%)
  other arithmetic  272 us (8%)
  local copies, waits for them, and re-layouts  150 us (5%)
    reduce_scatter x1, waiting for transfers between devices, local(): lax.psum_scatter(jnp.concatenate([outer_part(normed, qkv_grad), outer_par...  1530 us
    all_gather x1, waiting for transfers between devices, fetch_weights(): down_full = lax.all_gather(w_down, 'fsdp', axis=1, tiled=True)  261 us
    all_gather x1, waiting for transfers between devices, fetch_weights(): lax.all_gather(w_qkv, 'fsdp', axis=0, tiled=True)  218 us
    concatenate x1, other arithmetic, local(): jnp.concatenate([outer_part(normed, qkv_grad), outer_part(mixed_rows, bra...  130 us
    psum x1, waiting for transfers between devices, local(): lax.psum((qv_grad, jnp.sum(branch_grad.astype(jnp.float32), axis=0), ln1_...  121 us
    dot_general x4, matrix products, contract_last(): lax.dot_general(left_side, right_side, (((1,), (1,)), ((), ())), preferre...  113 us
    dot_general x4, matrix products, outer_part(): lax.dot_general(left_side, right_side, (((0,), (0,)), ((), ())), preferre...  96.2 us
    dot_general x4, matrix products, head_scores(): jnp.einsum('qhd,khd->hqk', query_heads, key_heads, preferred_element_type...  92.1 us
  transfers between devices with their start and end apart: 10, of which 8 were waited for; matrix products, arithmetic and copies ran while one was open for 12% of the time, Pallas kernels for 0%

commit v1 on v0

v1 whole, which is shorter than its diff:
```python
from functools import partial

import jax
import jax.numpy as jnp
from jax import lax
from jax.experimental import pallas as pl
from jax.experimental.pallas import tpu as pltpu
from jax.sharding import PartitionSpec as P

HEADS = 32
HEAD_DIM = 64
BLOCK = 256
PAIR = 2 * HEAD_DIM


def layer_norm(token_rows, gain_vec, shift_vec):
    average = jnp.mean(token_rows, axis=-1, keepdims=True)
    centred = token_rows - average
    spread = jnp.mean(centred * centred, axis=-1, keepdims=True)
    return centred * lax.rsqrt(spread + 1e-05) * gain_vec + shift_vec


def exact_gelu(values):
    return jax.nn.gelu(values, approximate=False)


def contract(left_side, right_side):
    return lax.dot_general(
        left_side, right_side, (((1,), (0,)), ((), ())), preferred_element_type=jnp.float32
    )


def contract_last(left_side, right_side):
    return lax.dot_general(
        left_side, right_side, (((1,), (1,)), ((), ())), preferred_element_type=jnp.float32
    )


def contract_first(left_side, right_side):
    return lax.dot_general(
        left_side, right_side, (((0,), (0,)), ((), ())), preferred_element_type=jnp.float32
    )


def attend_forward_kernel(mask_ref, slope_ref, qkv_ref, mixed_ref, lse_ref, *, blocks):
    pair = pl.program_id(0)
    mask = mask_ref[0]
    lane = lax.broadcasted_iota(jnp.int32, (BLOCK, PAIR), 1)
    row = lax.broadcasted_iota(jnp.int32, (BLOCK, BLOCK), 0)
    column = lax.broadcasted_iota(jnp.int32, (BLOCK, BLOCK), 1)
    gap = (row - column).astype(jnp.float32)

    def rows(block):
        return pl.ds(pl.multiple_of((block ^ mask) * BLOCK, BLOCK), BLOCK)

    for i in range(blocks):
        q_pair = qkv_ref[rows(i), 0:PAIR]
        outs, lses = [], []
        for head in range(2):
            slope = slope_ref[pair * 2 + head]
            mine = (lane >= head * HEAD_DIM) & (lane < (head + 1) * HEAD_DIM)
            q = jnp.where(mine, q_pair, jnp.zeros_like(q_pair)) * jnp.bfloat16(HEAD_DIM**-0.5)
            parts, highest = [], None
            for j in range(i + 1):
                scores = contract_last(q, qkv_ref[rows(j), PAIR : 2 * PAIR])
                distance = jnp.abs(gap) if i == j else gap + float(BLOCK * (i - j))
                scores = scores - slope * distance
                parts.append(scores)
                top = jnp.max(scores, axis=-1, keepdims=True)
                highest = top if highest is None else jnp.maximum(highest, top)
            total, out = None, None
            for j in range(i + 1):
                weights = jnp.exp(parts[j] - highest)
                part = jnp.sum(weights, axis=-1, keepdims=True)
                mixed = contract(weights.astype(jnp.bfloat16), qkv_ref[rows(j), 2 * PAIR : 3 * PAIR])
                total = part if total is None else total + part
                out = mixed if out is None else out + mixed
            outs.append(out / total)
            lses.append(highest + jnp.log(total))
        first = lane < HEAD_DIM
        mixed_ref[rows(i), :] = jnp.where(first, outs[0], outs[1]).astype(mixed_ref.dtype)
        lse_ref[rows(i), :] = jnp.where(first, lses[0], lses[1])


def attend_backward_kernel(
    mask_ref, slope_ref, qkv_ref, lse_ref, mixed_ref, grad_ref, out_ref, dq_ref, dk_ref, dv_ref, *, blocks
):
    pair = pl.program_id(0)
    mask = mask_ref[0]
    lane = lax.broadcasted_iota(jnp.int32, (BLOCK, PAIR), 1)
    key = lax.broadcasted_iota(jnp.int32, (BLOCK, BLOCK), 0)
    query = lax.broadcasted_iota(jnp.int32, (BLOCK, BLOCK), 1)
    gap = (query - key).astype(jnp.float32)

    def rows(block):
        return pl.ds(pl.multiple_of((block ^ mask) * BLOCK, BLOCK), BLOCK)

    for i in range(blocks):
        q_pair = qkv_ref[rows(i), 0:PAIR]
        up_pair = grad_ref[rows(i), :]
        inner_all = (up_pair.astype(jnp.float32) * mixed_ref[rows(i), :].astype(jnp.float32)).T
        lse_all = lse_ref[rows(i), :].T
        dq = None
        for head in range(2):
            slope = slope_ref[pair * 2 + head]
            mine = (lane >= head * HEAD_DIM) & (lane < (head + 1) * HEAD_DIM)
            zero = jnp.zeros_like(q_pair)
            q = jnp.where(mine, q_pair, zero) * jnp.bfloat16(HEAD_DIM**-0.5)
            up = jnp.where(mine, up_pair, zero)
            inner = jnp.sum(inner_all[head * HEAD_DIM : (head + 1) * HEAD_DIM], axis=0, keepdims=True)
            lse = lse_all[head * HEAD_DIM : head * HEAD_DIM + 1]
            for j in range(i + 1):
                k_pair = qkv_ref[rows(j), PAIR : 2 * PAIR]
                distance = jnp.abs(gap) if i == j else gap + float(BLOCK * (i - j))
                probs = jnp.exp(contract_last(k_pair, q) - slope * distance - lse)
                prob_grad = contract_last(qkv_ref[rows(j), 2 * PAIR : 3 * PAIR], up)
                score_grad = (probs * (prob_grad - inner)).astype(jnp.bfloat16)
                dv = contract(probs.astype(jnp.bfloat16), up)
                dk = contract(score_grad, q)
                part = contract_first(score_grad, jnp.where(mine, k_pair, zero))
                dq = part if dq is None else dq + part
                if i == j and head == 0:
                    dv_ref[j] = dv
                    dk_ref[j] = dk
                else:
                    dv_ref[j] += dv
                    dk_ref[j] += dk
        dq_ref[i] = dq
    for i in range(blocks):
        out_ref[rows(i), 0:PAIR] = (dq_ref[i] * HEAD_DIM**-0.5).astype(out_ref.dtype)
        out_ref[rows(i), PAIR : 2 * PAIR] = dk_ref[i].astype(out_ref.dtype)
        out_ref[rows(i), 2 * PAIR : 3 * PAIR] = dv_ref[i].astype(out_ref.dtype)


def attend_forward(mask, slopes, qkv):
    length, width = qkv.shape
    pairs, blocks = width // (3 * PAIR), length // BLOCK
    scored = pairs * blocks * (blocks + 1) * BLOCK * BLOCK
    return pl.pallas_call(
        partial(attend_forward_kernel, blocks=blocks),
        grid_spec=pltpu.PrefetchScalarGridSpec(
            num_scalar_prefetch=2,
            grid=(pairs,),
            in_specs=[pl.BlockSpec((length, 3 * PAIR), lambda p, *_: (0, p))],
            out_specs=[pl.BlockSpec((length, PAIR), lambda p, *_: (0, p))] * 2,
        ),
        out_shape=[
            jax.ShapeDtypeStruct((length, pairs * PAIR), jnp.bfloat16),
            jax.ShapeDtypeStruct((length, pairs * PAIR), jnp.float32),
        ],
        compiler_params=pltpu.CompilerParams(vmem_limit_bytes=40 * 2**20),
        cost_estimate=pl.CostEstimate(
            flops=scored * 2 * 512, bytes_accessed=length * pairs * PAIR * 12, transcendentals=scored
        ),
        name="attend_forward",
    )(mask, slopes, qkv)


def attend_backward(mask, slopes, qkv, lse, mixed, grad):
    length, width = qkv.shape
    pairs, blocks = width // (3 * PAIR), length // BLOCK
    scored = pairs * blocks * (blocks + 1) * BLOCK * BLOCK
    narrow = pl.BlockSpec((length, PAIR), lambda p, *_: (0, p))
    wide = pl.BlockSpec((length, 3 * PAIR), lambda p, *_: (0, p))
    return pl.pallas_call(
        partial(attend_backward_kernel, blocks=blocks),
        grid_spec=pltpu.PrefetchScalarGridSpec(
            num_scalar_prefetch=2,
            grid=(pairs,),
            in_specs=[wide, narrow, narrow, narrow],
            out_specs=wide,
            scratch_shapes=[pltpu.VMEM((blocks, BLOCK, PAIR), jnp.float32)] * 3,
        ),
        out_shape=jax.ShapeDtypeStruct((length, width), jnp.bfloat16),
        compiler_params=pltpu.CompilerParams(vmem_limit_bytes=40 * 2**20),
        cost_estimate=pl.CostEstimate(
            flops=scored * 2 * 1280, bytes_accessed=length * pairs * PAIR * 20, transcendentals=scored
        ),
        name="attend_backward",
    )(mask, slopes, qkv, lse, mixed, grad)


def swap(values, bit):
    return lax.ppermute(values, "seq", [(i, i ^ bit) for i in range(4)])


def by_index(parts, me):
    odd, upper = (me & 1) == 1, (me & 2) == 2
    a, b, c, d = parts
    a, b, c, d = (
        jnp.where(odd, b, a),
        jnp.where(odd, a, b),
        jnp.where(odd, d, c),
        jnp.where(odd, c, d),
    )
    return [jnp.where(upper, c, a), jnp.where(upper, d, b), jnp.where(upper, a, c), jnp.where(upper, b, d)]


def gather_rows(rows):
    if lax.axis_size("seq") != 4:
        return lax.all_gather(rows, "seq", axis=0, tiled=True)
    half = rows.shape[0] // 2
    first, second = swap(rows, 1), swap(rows, 2)
    return jnp.concatenate([rows, first, second, swap(second[:half], 1), swap(first[half:], 2)], axis=0)


def scatter_rows(slots):
    groups = lax.axis_size("seq")
    if groups != 4:
        return lax.psum_scatter(slots, "seq", scatter_dimension=0, tiled=True).astype(jnp.float32)
    rows = slots.shape[0] // groups
    half = rows // 2
    own, first, second, far = (slots[j * rows : (j + 1) * rows].astype(jnp.float32) for j in range(4))
    low_far = far.astype(slots.dtype)
    top, bottom = swap(low_far[:half], 1), swap(low_far[half:], 2)
    first = jnp.concatenate([first[:half], first[half:] + bottom.astype(jnp.float32)], axis=0)
    second = jnp.concatenate([second[:half] + top.astype(jnp.float32), second[half:]], axis=0)
    from_first, from_second = swap(first.astype(slots.dtype), 1), swap(second.astype(slots.dtype), 2)
    return own + from_first.astype(jnp.float32) + from_second.astype(jnp.float32)


def heads_to_rows(slots, me):
    groups = lax.axis_size("seq")
    rows = slots.shape[0] // groups
    parts = slots.reshape(groups, rows, slots.shape[1])
    if groups != 4:
        swapped = lax.all_to_all(parts, "seq", split_axis=0, concat_axis=0, tiled=True)
        return jnp.swapaxes(swapped, 0, 1).reshape(rows, -1)
    return jnp.concatenate(by_index([parts[0]] + [swap(parts[j], j) for j in (1, 2, 3)], me), axis=1)


def rows_to_heads(rows, me):
    groups = lax.axis_size("seq")
    slab = rows.shape[1] // groups
    parts = [rows[:, j * slab : (j + 1) * slab] for j in range(groups)]
    if groups != 4:
        swapped = lax.all_to_all(jnp.stack(parts), "seq", split_axis=0, concat_axis=0, tiled=True)
        return swapped.reshape(-1, slab)
    parts = by_index(parts, me)
    return jnp.concatenate([parts[0]] + [swap(parts[j], j) for j in (1, 2, 3)], axis=0)


def scatter_slab(partial_sums, me):
    groups, shards = lax.axis_size("seq"), lax.axis_size("fsdp")
    width = partial_sums.shape[1]
    parts = partial_sums.astype(jnp.bfloat16).reshape(groups, shards, -1, width)
    parts = jnp.swapaxes(parts, 0, 1).reshape(-1, width)
    summed = lax.psum_scatter(parts, "fsdp", scatter_dimension=0, tiled=True).reshape(groups, -1, width)
    slabs = lax.all_to_all(summed, "seq", split_axis=0, concat_axis=0, tiled=True)
    return jnp.swapaxes(slabs, 0, 1).astype(jnp.float32)


def local(
    tokens,
    cotangent,
    w_qkv,
    qv_bias,
    w_out,
    out_bias,
    ln1_gain,
    ln1_shift,
    ln2_gain,
    ln2_shift,
    w_up,
    up_bias,
    w_down,
    down_bias,
):
    seq_count, local_len, model_width = tokens.shape
    groups = lax.axis_size("seq")
    me = lax.axis_index("seq")
    heads_here = HEADS // groups
    slab = heads_here * HEAD_DIM
    pairs = slab // PAIR
    hidden_width = w_up.shape[1]
    hidden_slab = hidden_width // groups
    shard = w_qkv.shape[0]
    sequences = range(seq_count)
    mask = jnp.reshape(me if groups == 4 else jnp.zeros_like(me), (1,)).astype(jnp.int32)
    head_index = me * heads_here + jnp.arange(1, heads_here + 1, dtype=jnp.int32)
    slopes = 2.0 ** (-8.0 * head_index.astype(jnp.float32) / HEADS)

    def head_columns(values):
        split = values.reshape(-1, 3, groups, pairs, PAIR)
        mine = lax.dynamic_index_in_dim(split, me, axis=2, keepdims=False)
        return jnp.swapaxes(mine, 1, 2).reshape(values.shape[0], -1)

    qkv_slab = lax.all_gather(head_columns(w_qkv), "fsdp", axis=0, tiled=True)
    full_out = lax.all_gather(w_out, "fsdp", axis=0, tiled=True)
    up_slab = lax.all_gather(
        lax.dynamic_slice_in_dim(w_up, me * hidden_slab, hidden_slab, axis=1), "fsdp", axis=0, tiled=True
    )
    down_slab = lax.all_gather(
        lax.dynamic_slice_in_dim(w_down, me * hidden_slab, hidden_slab, axis=0), "fsdp", axis=1, tiled=True
    )
    qkv_bias = head_columns(
        jnp.concatenate([qv_bias[0], jnp.zeros_like(qv_bias[0]), qv_bias[1]])[None]
    )
    up_bias_slab = lax.dynamic_slice_in_dim(up_bias, me * hidden_slab, hidden_slab, axis=0)

    x = [tokens[b].astype(jnp.float32) for b in sequences]
    dz = [cotangent[b].astype(jnp.float32) for b in sequences]
    first_norm = [jax.vjp(layer_norm, x[b], ln1_gain, ln1_shift) for b in sequences]
    normed = [gather_rows(first_norm[b][0].astype(jnp.bfloat16)) for b in sequences]
    qkv = [(contract(normed[b], qkv_slab) + qkv_bias).astype(jnp.bfloat16) for b in sequences]
    attended = [attend_forward(mask, slopes, qkv[b]) for b in sequences]
    mixed_rows = [heads_to_rows(attended[b][0], me) for b in sequences]
    middle = [x[b] + (contract(mixed_rows[b], full_out) + out_bias) for b in sequences]
    second_norm = [jax.vjp(layer_norm, middle[b], ln2_gain, ln2_shift) for b in sequences]
    second = [gather_rows(second_norm[b][0].astype(jnp.bfloat16)) for b in sequences]
    upstream = [gather_rows(cotangent[b]) for b in sequences]
    hidden = [contract(second[b], up_slab) + up_bias_slab for b in sequences]
    gelu = [jax.vjp(exact_gelu, hidden[b]) for b in sequences]
    active = [gelu[b][0].astype(jnp.bfloat16) for b in sequences]
    hidden_grad = [
        gelu[b][1](contract_last(upstream[b], down_slab))[0].astype(jnp.bfloat16) for b in sequences
    ]
    second_grad = [
        scatter_rows(contract_last(hidden_grad[b], up_slab).astype(jnp.bfloat16)) for b in sequences
    ]
    outcome = [scatter_rows(contract(active[b], down_slab).astype(jnp.bfloat16)) for b in sequences]
    result = jnp.stack([(middle[b] + (outcome[b] + down_bias)).astype(jnp.bfloat16) for b in sequences])

    second_back = [second_norm[b][1](second_grad[b]) for b in sequences]
    middle_grad = [dz[b] + second_back[b][0] for b in sequences]
    branch_grad = [middle_grad[b].astype(jnp.bfloat16) for b in sequences]
    mixed_grad = [
        rows_to_heads(contract_last(branch_grad[b], full_out).astype(jnp.bfloat16), me) for b in sequences
    ]
    qkv_grad = [
        attend_backward(mask, slopes, qkv[b], attended[b][1], attended[b][0], mixed_grad[b]) for b in sequences
    ]
    normed_grad = [
        scatter_rows(contract_last(qkv_grad[b], qkv_slab).astype(jnp.bfloat16)) for b in sequences
    ]
    first_back = [first_norm[b][1](normed_grad[b]) for b in sequences]
    grad_tokens = jnp.stack([(middle_grad[b] + first_back[b][0]).astype(jnp.bfloat16) for b in sequences])

    def outer(left_parts, right_parts):
        return contract_first(jnp.concatenate(left_parts, axis=0), jnp.concatenate(right_parts, axis=0))

    grad_w_up = scatter_slab(outer(second, hidden_grad), me).reshape(-1, hidden_width)
    grad_w_down = scatter_slab(outer(upstream, active), me).reshape(-1, hidden_width).T
    grad_w_out = lax.psum_scatter(
        outer(mixed_rows, branch_grad).astype(jnp.bfloat16), ("seq", "fsdp"), scatter_dimension=0, tiled=True
    ).astype(jnp.float32)
    grad_w_qkv = scatter_slab(outer(normed, qkv_grad), me).reshape(-1, groups, pairs, 3, PAIR)
    grad_w_qkv = jnp.transpose(grad_w_qkv, (0, 3, 1, 2, 4)).reshape(-1, 3 * model_width)

    def column_sum(parts):
        return sum(jnp.sum(part.astype(jnp.float32), axis=0) for part in parts)

    hidden_sum = lax.dynamic_update_slice_in_dim(
        jnp.zeros((hidden_width,), jnp.float32), column_sum(hidden_grad), me * hidden_slab, axis=0
    )
    qkv_sum = jnp.transpose(column_sum(qkv_grad).reshape(pairs, 3, PAIR), (1, 0, 2)).reshape(3, slab)
    qv_sum = lax.dynamic_update_slice_in_dim(
        jnp.zeros((2, model_width), jnp.float32), qkv_sum[0::2], me * slab, axis=1
    )
    early = lax.psum(
        (
            column_sum(branch_grad),
            sum(part[1] for part in second_back),
            sum(part[2] for part in second_back),
            hidden_sum,
            column_sum(dz),
        ),
        ("seq", "fsdp"),
    )
    late = lax.psum(
        (qv_sum, sum(part[1] for part in first_back), sum(part[2] for part in first_back)), ("seq", "fsdp")
    )
    return (
        result,
        grad_tokens,
        grad_w_qkv,
        late[0],
        grad_w_out,
        early[0],
        late[1],
        late[2],
        early[1],
        early[2],
        grad_w_up,
        early[3],
        grad_w_down,
        early[4],
    )


def solution(mesh):
    return jax.shard_map(
        local,
        mesh=mesh,
        in_specs=(
            P("fsdp", "seq", None),
            P("fsdp", "seq", None),
            P("fsdp", None),
            P(),
            P("fsdp", None),
            P(),
            P(),
            P(),
            P(),
            P(),
            P("fsdp", None),
            P(),
            P(None, "fsdp"),
            P(),
        ),
        out_specs=(
            P("fsdp", "seq", None),
            P("fsdp", "seq", None),
            P(("seq", "fsdp"), None),
            P(),
            P(("seq", "fsdp"), None),
            P(),
            P(),
            P(),
            P(),
            P(),
            P(("seq", "fsdp"), None),
            P(),
            P(None, ("seq", "fsdp")),
            P(),
        ),
        check_vma=False,
    )
```

time: 3320 us -> 1450 us (0.44)
  waiting for transfers between devices: 2320 us -> 808 us
  matrix products: 526 us -> 273 us
  other arithmetic: 272 us -> 75 us
  Pallas kernels: 0 us -> 81.8 us
  starting transfers between devices: 19.8 us -> 84.6 us
  local copies, waits for them, and re-layouts: 150 us -> 106 us
    reduce_scatter x1 -> x4, waiting for transfers between devices: 1530 us -> 225 us  [the longest x1 129 us: local(): lax.psum_scatter(outer(mixed_rows, branch_grad).astype(jnp.bfloat16), ('s...]
    all_gather x4, waiting for transfers between devices: 540 us -> 131 us  [the longest x1 68.4 us: local(): lax.all_gather(lax.dynamic_slice_in_dim(w_down, me * hidden_slab, hidden_...]
    ppermute x0 -> x60, waiting for transfers between devices: none -> 315 us  [swap(): return lax.ppermute(values, 'seq', [(i, i ^ bit) for i in range(4)])]
    dot_general x22 -> x12, matrix products: 412 us -> 153 us  [the longest x8 77.5 us: contract(): lax.dot_general(left_side, right_side, (((1,), (0,)), ((), ())), preferre...]
    concatenate x2 -> x15, other arithmetic: 131 us -> 4.26 us  [the longest x6 2.69 us: scatter_rows(): jnp.concatenate([second[:half] + top.astype(jnp.float32), second[half:]],...]
    all_to_all x4 -> x3, waiting for transfers between devices: 130 us -> 7.62 us  [scatter_slab(): lax.all_to_all(summed, 'seq', split_axis=0, concat_axis=0, tiled=True)]
    pallas_call x0 -> x4, Pallas kernels: none -> 81.8 us  [the longest x2 52.7 us: attend_backward(): pl.pallas_call(partial(attend_backward_kernel, blocks=blocks), grid_spec=...]
    ppermute x0 -> x60, starting transfers between devices: none -> 71.8 us  [swap(): return lax.ppermute(values, 'seq', [(i, i ^ bit) for i in range(4)])]
  transfers between devices with their start and end apart: 10 -> 72, of which waited for: 8 -> 51; matrix products, arithmetic and copies ran while one was open for 12% -> 18% of each run, Pallas kernels for 0% -> 2%
where the time goes in v1:
time: 1450 us; the launch traced here: 1440 us
  waiting for transfers between devices  808 us (56%)
  matrix products  273 us (19%)
  local copies, waits for them, and re-layouts  106 us (7%)
  starting transfers between devices  84.6 us (6%)
  Pallas kernels  81.8 us (6%)
  other arithmetic  75 us (5%)
  between operations  16 us (1%)
    ppermute x60, waiting for transfers between devices, swap(): return lax.ppermute(values, 'seq', [(i, i ^ bit) for i in range(4)])  315 us
    reduce_scatter x1, waiting for transfers between devices, local(): lax.psum_scatter(outer(mixed_rows, branch_grad).astype(jnp.bfloat16), ('s...  129 us
    psum x1, waiting for transfers between devices, local(): lax.psum((qv_sum, sum((part[1] for part in first_back)), sum((part[2] for...  128 us
    dot_general x8, matrix products, contract_last(): lax.dot_general(left_side, right_side, (((1,), (1,)), ((), ())), preferre...  120 us
    reduce_scatter x3, waiting for transfers between devices, scatter_slab(): lax.psum_scatter(parts, 'fsdp', scatter_dimension=0, tiled=True)  95.8 us
    dot_general x8, matrix products, contract(): lax.dot_general(left_side, right_side, (((1,), (0,)), ((), ())), preferre...  77.5 us
    dot_general x4, matrix products, contract_first(): lax.dot_general(left_side, right_side, (((0,), (0,)), ((), ())), preferre...  75.2 us
    ppermute x60, starting transfers between devices, swap(): return lax.ppermute(values, 'seq', [(i, i ^ bit) for i in range(4)])  71.8 us
  transfers between devices with their start and end apart: 72, of which 51 were waited for; matrix products, arithmetic and copies ran while one was open for 18% of the time, Pallas kernels for 2%

profile of v1, /device:TPU:0, one launch (start us, length us, event | category | flops | bytes accessed | tf_op | source)
XLA Modules:
  0.0 1443.4 jit_solution(17640618845208363483)
XLA Ops:
  55.3 19.7 %collective-permute-done.1 = bf16[256,2048]{1,0:T(8,128)(2,1)S(1)} collective-permute-done((bf16[256,2048]{1,0:T(8,128)(2,1)}, bf16[256,2048]{1,0:T(8,128)(2,1)S(1)}, u32[]{:S(2)}, u32[]{:S(2)}) %collective-permute-start.1) | collective-permute-done | bytes 1048608 | tf_op jit(solution)/shard_map/ppermute | solution.py:184
  137.1 29.7 %all-gather.7.cloned.1.call-done = bf16[2048,2048]{1,0:T(8,128)(2,1)} async-done(((bf16[256,2048]{1,0:T(8,128)(2,1)}), bf16[2048,2048]{1,0:T(8,128)(2,1)}) %all-gather.7.cloned.1.call-update) | async-done | bytes 8388624 | tf_op jit(solution)/shard_map/all_gather | solution.py:289
  184.3 16.1 %collective-permute-done.8 = bf16[256,2048]{1,0:T(8,128)(2,1)S(1)} collective-permute-done((bf16[256,2048]{1,0:T(8,128)(2,1)S(1)}, bf16[256,2048]{1,0:T(8,128)(2,1)S(1)}, u32[]{:S(2)}, u32[]{:S(2)}) %collective-permute-start.8) | collective-permute-done | bytes 1048608 | tf_op jit(solution)/shard_map/ppermute | solution.py:184
  216.4 33.2 %all-gather.9.cloned.1.call-done = bf16[2048,2048]{1,0:T(8,128)(2,1)} async-done(((bf16[256,2048]{1,0:T(8,128)(2,1)}), bf16[2048,2048]{1,0:T(8,128)(2,1)}) %all-gather.9.cloned.1.call-update) | async-done | bytes 8388624 | tf_op jit(solution)/shard_map/all_gather | solution.py:290
  264.3 68.4 %all-gather.11.cloned.1.call-done = bf16[2048,2048]{1,0:T(8,128)(2,1)} async-done(((bf16[2048,256]{1,0:T(8,128)(2,1)}), bf16[2048,2048]{1,0:T(8,128)(2,1)}) %all-gather.11.cloned.1.call-update) | async-done | bytes 8388624 | tf_op jit(solution)/shard_map/all_gather | solution.py:293
  332.7 34.3 %convert_reduce_fusion.1 = (f32[2048]{0:T(1024)}, bf16[1024,2048]{1,0:T(8,128)(2,1)}, f32[1024,2048]{1,0:T(8,128)}) fusion(f32[1024,2048]{1,0:T(8,128)} %fusion.128, f32[2048]{0:T(1024)S(1)} %dynamic_slice.20, bf16[1024,2048]{1,0:T(8,128)(2,1)} %constant_dynamic-update-slice_fusion.20, bf16[2048,2048]{1,0:T(8,128)(2,1)} %all-gather.11.cloned.1.call-done), kind=kOutput, calls=%fused_computation.13 | convolution fusion | flops 8747218944 | bytes 33570816 | tf_op jit(solution)/shard_map/dot_general | solution.py:34
  422.8 19.7 %collective-permute-done.37 = bf16[256,2048]{1,0:T(8,128)(2,1)S(1)} collective-permute-done((bf16[256,2048]{1,0:T(8,128)(2,1)S(1)}, bf16[256,2048]{1,0:T(8,128)(2,1)S(1)}, u32[]{:S(2)}, u32[]{:S(2)}) %collective-permute-start.37) | collective-permute-done | bytes 1048608 | tf_op jit(solution)/shard_map/ppermute | solution.py:184
  444.3 19.6 %collective-permute-done.14 = bf16[256,2048]{1,0:T(8,128)(2,1)S(1)} collective-permute-done((bf16[256,2048]{1,0:T(8,128)(2,1)S(1)}, bf16[256,2048]{1,0:T(8,128)(2,1)S(1)}, u32[]{:S(2)}, u32[]{:S(2)}) %collective-permute-start.14) | collective-permute-done | bytes 1048608 | tf_op jit(solution)/shard_map/ppermute | solution.py:184
  484.2 26.2 %attend_backward.2 = bf16[1024,1536]{1,0:T(8,128)(2,1)S(1)} custom-call(s32[1]{0:T(128)} %bitcast.1.mask_ref, f32[8]{0:T(128)S(1)} %multiply_power_fusion.slope_ref, bf16[1024,1536]{1,0:T(8,128)(2,1)S(1)} %copy-done.13, f32[1024,512]{1,0:T(8,128)S(1)} %get-tuple-element.20.lse_ref, bf16[1024,512]{1,0:T(8,128)(2,1)S(1)} %copy-done.7, ...), custom_call_target="tpu_custom_call" | custom-call | flops 13421772800 | bytes 10485760 | tf_op jit(solution)/shard_map/attend_backward/pallas_call | solution.py:165
  532.6 20.1 %collective-permute-done.44 = bf16[256,2048]{1,0:T(8,128)(2,1)S(1)} collective-permute-done((bf16[256,2048]{1,0:T(8,128)(2,1)S(1)}, bf16[256,2048]{1,0:T(8,128)(2,1)S(1)}, u32[]{:S(2)}, u32[]{:S(2)}) %collective-permute-start.44) | collective-permute-done | bytes 1048608 | tf_op jit(solution)/shard_map/ppermute | solution.py:184
  560.6 22.0 %collective-permute-done.16 = bf16[256,2048]{1,0:T(8,128)(2,1)S(1)} collective-permute-done((bf16[256,2048]{1,0:T(8,128)(2,1)S(1)}, bf16[256,2048]{1,0:T(8,128)(2,1)S(1)}, u32[]{:S(2)}, u32[]{:S(2)}) %collective-permute-start.16) | collective-permute-done | bytes 1048608 | tf_op jit(solution)/shard_map/ppermute | solution.py:184
  588.2 24.1 %collective-permute-done.17 = bf16[128,2048]{1,0:T(8,128)(2,1)S(1)} collective-permute-done((bf16[128,2048]{1,0:T(8,128)(2,1)S(1)}, bf16[128,2048]{1,0:T(8,128)(2,1)S(1)}, u32[]{:S(2)}, u32[]{:S(2)}) %collective-permute-start.17) | collective-permute-done | bytes 524320 | tf_op jit(solution)/shard_map/ppermute | solution.py:184
  666.4 16.0 %collective-permute-done.23 = bf16[256,2048]{1,0:T(8,128)(2,1)S(1)} collective-permute-done((bf16[256,2048]{1,0:T(8,128)(2,1)S(1)}, bf16[256,2048]{1,0:T(8,128)(2,1)S(1)}, u32[]{:S(2)}, u32[]{:S(2)}) %collective-permute-start.23) | collective-permute-done | bytes 1048608 | tf_op jit(solution)/shard_map/ppermute | solution.py:184
  705.2 33.8 %convert_reduce_fusion = (f32[2048]{0:T(1024)}, bf16[1024,2048]{1,0:T(8,128)(2,1)}, f32[1024,2048]{1,0:T(8,128)}) fusion(f32[1024,2048]{1,0:T(8,128)S(1)} %fusion.129, f32[2048]{0:T(1024)S(1)} %dynamic_slice.20, bf16[1024,2048]{1,0:T(8,128)(2,1)S(1)} %get-tuple-element.163, bf16[2048,2048]{1,0:T(8,128)(2,1)} %all-gather.11.cloned.1.call-done), kind=kOutput, calls=%fused_computation.12 | convolution fusion | flops 8747218944 | bytes 33570816 | tf_op jit(solution)/shard_map/dot_general | solution.py:34
  794.1 19.0 %collective-permute-done.52 = bf16[256,2048]{1,0:T(8,128)(2,1)S(1)} collective-permute-done((bf16[256,2048]{1,0:T(8,128)(2,1)S(1)}, bf16[256,2048]{1,0:T(8,128)(2,1)S(1)}, u32[]{:S(2)}, u32[]{:S(2)}) %collective-permute-start.52) | collective-permute-done | bytes 1048608 | tf_op jit(solution)/shard_map/ppermute | solution.py:184
  814.3 15.0 %collective-permute-done.29 = bf16[256,2048]{1,0:T(8,128)(2,1)S(1)} collective-permute-done((bf16[256,2048]{1,0:T(8,128)(2,1)S(1)}, bf16[256,2048]{1,0:T(8,128)(2,1)S(1)}, u32[]{:S(2)}, u32[]{:S(2)}) %collective-permute-start.29) | collective-permute-done | bytes 1048608 | tf_op jit(solution)/shard_map/ppermute | solution.py:184
  850.3 26.5 %attend_backward.3 = bf16[1024,1536]{1,0:T(8,128)(2,1)S(1)} custom-call(s32[1]{0:T(128)} %bitcast.1.mask_ref, f32[8]{0:T(128)S(1)} %copy-done.9, bf16[1024,1536]{1,0:T(8,128)(2,1)S(1)} %copy-done.11, f32[1024,512]{1,0:T(8,128)S(1)} %get-tuple-element.21.lse_ref, bf16[1024,512]{1,0:T(8,128)(2,1)S(1)} %copy-done.5, ...), custom_call_target="tpu_custom_call" | custom-call | flops 13421772800 | bytes 10485760 | tf_op jit(solution)/shard_map/attend_backward/pallas_call | solution.py:165
  876.8 16.6 %convolution_convert_fusion.1 = bf16[2048,1536]{1,0:T(8,128)(2,1)S(1)} fusion(bf16[2048,2048]{1,0:T(8,128)(2,1)} %get-tuple-element.170, bf16[1024,1536]{1,0:T(8,128)(2,1)S(1)} %attend_backward.3, bf16[1024,1536]{1,0:T(8,128)(2,1)S(1)} %copy-done.1), kind=kOutput, calls=%fused_computation.47 | convolution fusion | flops 12900630528 | bytes 20971520 | tf_op jit(solution)/shard_map/dot_general | solution.py:40
  896.7 24.6 %fusion.20 = bf16[2048,2048]{1,0:T(8,128)(2,1)} fusion(bf16[2048,2048]{1,0:T(8,128)(2,1)} %get-tuple-element.162, bf16[1024,2048]{1,0:T(8,128)(2,1)} %copy-done.30, bf16[1024,2048]{1,0:T(8,128)(2,1)} %multiply_convert_fusion.1), kind=kOutput, calls=%fused_computation.44 | convolution fusion | flops 17200840704 | bytes 25165824 | tf_op jit(solution)/shard_map/dot_general | solution.py:40
  929.9 23.9 %fusion.23 = bf16[2048,2048]{1,0:T(8,128)(2,1)} fusion(bf16[2048,2048]{1,0:T(8,128)(2,1)} %get-tuple-element.166, bf16[1024,2048]{1,0:T(8,128)(2,1)} %get-tuple-element.52, bf16[1024,2048]{1,0:T(8,128)(2,1)} %get-tuple-element.55), kind=kOutput, calls=%fused_computation.45 | convolution fusion | flops 17200840704 | bytes 25165824 | tf_op jit(solution)/shard_map/dot_general | solution.py:40
  1036.5 17.6 %reduce-scatter.11.cloned.1.call-done = bf16[256,2048]{1,0:T(8,128)(2,1)} async-done(((bf16[2048,2048]{1,0:T(8,128)(2,1)}), bf16[256,2048]{1,0:T(8,128)(2,1)}) %reduce-scatter.11.cloned.1.call-update) | async-done | bytes 1048592 | tf_op jit(solution)/shard_map/reduce_scatter | solution.py:248
  1066.2 78.2 %reduce-scatter.9.cloned.1.call-done = bf16[256,2048]{1,0:T(8,128)(2,1)} async-done(((bf16[2048,2048]{1,0:T(8,128)(2,1)}), bf16[256,2048]{1,0:T(8,128)(2,1)}) %reduce-scatter.9.cloned.1.call-update) | async-done | bytes 1048592 | tf_op jit(solution)/shard_map/reduce_scatter | solution.py:248
  1167.7 128.8 %reduce-scatter.7.cloned.1.call-done = bf16[64,2048]{1,0:T(8,128)(2,1)} async-done(((bf16[2048,2048]{1,0:T(8,128)(2,1)}), bf16[64,2048]{1,0:T(8,128)(2,1)}) %reduce-scatter.7.cloned.1.call-update) | async-done | bytes 262160 | tf_op jit(solution)/shard_map/reduce_scatter | solution.py:344
  1298.2 127.9 %all-reduce.3.cloned.1.call-done = (f32[2,2048]{1,0:T(2,128)}, f32[2048]{0:T(1024)}, f32[2048]{0:T(1024)}, f32[2048]{0:T(1024)}, f32[2048]{0:T(1024)}, /*index=5*/f32[2048]{0:T(1024)}, f32[8192]{0:T(1024)}, f32[2048]{0:T(1024)}) async-done(((f32[2,2048]{1,0:T(2,128)}, f32[2048]{0:T(1024)}, f32[2048]{0:T(1024)}, f32[2048]{0:T(1024)}, f32[2048]{0:T(1024)}, /*index=5*/f32[2048]{0:T(1024)}, f32[8192]{0:T(1024)}, ...) | async-done | bytes 98320 | tf_op jit(solution)/shard_map/psum | solution.py:370
  (547 shorter events, 566.2 us)
Async XLA Ops:
  7.2 90.0 %all-gather.5.cloned.1.call-start = ((), (), s32[]{:S(2)}) async-start(), calls=%async_computation.7 | async-start | bytes 7077888 | tf_op jit(solution)/shard_map/all_gather | solution.py:288
  16.9 149.9 %all-gather.7.cloned.1.call-start = ((), (), s32[]{:S(2)}) async-start(), calls=%async_computation.8 | async-start | bytes 9437184 | tf_op jit(solution)/shard_map/all_gather | solution.py:289
  17.6 232.0 %all-gather.9.cloned.1.call-start = ((), (), s32[]{:S(2)}) async-start(), calls=%async_computation.9 | async-start | bytes 9437184 | tf_op jit(solution)/shard_map/all_gather | solution.py:290
  20.0 312.7 %all-gather.11.cloned.1.call-start = ((), (), s32[]{:S(2)}) async-start(), calls=%async_computation.10 | async-start | bytes 9437184 | tf_op jit(solution)/shard_map/all_gather | solution.py:293
  30.3 994.0 %reduce-scatter.5.cloned.1.call-start = ((), (), s32[]{:S(2)}) async-start(), calls=%async_computation.11 | async-start | bytes 7077888 | tf_op jit(solution)/shard_map/reduce_scatter | solution.py:248
  34.1 40.9 %collective-permute-start.1 = (bf16[256,2048]{1,0:T(8,128)(2,1)}, bf16[256,2048]{1,0:T(8,128)(2,1)S(1)}, u32[]{:S(2)}, u32[]{:S(2)}) collective-permute-start(bf16[256,2048]{1,0:T(8,128)(2,1)} %get-tuple-element.64), channel_id=1, source_target_pairs={{0,16},{8,24},{16,0},{24,8},{1,17},{9,25},{17,1},{25,9},{2,18},{10... | collective-permute-start | bytes 3145736 | tf_op jit(solution)/shard_map/ppermute | solution.py:184
  34.5 40.7 %collective-permute-start = (bf16[256,2048]{1,0:T(8,128)(2,1)}, bf16[256,2048]{1,0:T(8,128)(2,1)S(1)}, u32[]{:S(2)}, u32[]{:S(2)}) collective-permute-start(bf16[256,2048]{1,0:T(8,128)(2,1)} %get-tuple-element.64), channel_id=1, source_target_pairs={{0,8},{8,0},{16,24},{24,16},{1,9},{9,1},{17,25},{25,17},{2,10},{10... | collective-permute-start | bytes 3145736 | tf_op jit(solution)/shard_map/ppermute | solution.py:184
  50.5 35.8 %collective-permute-start.33 = (bf16[128,2048]{1,0:T(8,128)(2,1)S(1)}, bf16[128,2048]{1,0:T(8,128)(2,1)S(1)}, u32[]{:S(2)}, u32[]{:S(2)}) collective-permute-start(bf16[128,2048]{1,0:T(8,128)(2,1)S(1)} %slice.455), channel_id=1, source_target_pairs={{0,16},{8,24},{16,0},{24,8},{1,17},{9,25},{17,1},{25,9},{2,18},{10... | collective-permute-start | bytes 1572872 | tf_op jit(solution)/shard_map/ppermute | solution.py:184
  53.7 30.4 %collective-permute-start.32 = (bf16[128,2048]{1,0:T(8,128)(2,1)S(1)}, bf16[128,2048]{1,0:T(8,128)(2,1)S(1)}, u32[]{:S(2)}, u32[]{:S(2)}) collective-permute-start(bf16[128,2048]{1,0:T(8,128)(2,1)S(1)} %slice.454), channel_id=1, source_target_pairs={{0,8},{8,0},{16,24},{24,16},{1,9},{9,1},{17,25},{25,17},{2,10},{10... | collective-permute-start | bytes 1572872 | tf_op jit(solution)/shard_map/ppermute | solution.py:184
  407.0 35.5 %collective-permute-start.37 = (bf16[256,2048]{1,0:T(8,128)(2,1)S(1)}, bf16[256,2048]{1,0:T(8,128)(2,1)S(1)}, u32[]{:S(2)}, u32[]{:S(2)}) collective-permute-start(bf16[256,2048]{1,0:T(8,128)(2,1)S(1)} %pad_maximum_fusion.7), channel_id=1, source_target_pairs={{0,16},{8,24},{16,0},{24,8},{1,17},{9,25},{17,1},{25,9},{2,18},{10... | collective-permute-start | bytes 3145736 | tf_op jit(solution)/shard_map/ppermute | solution.py:184
  407.9 34.6 %collective-permute-start.35 = (bf16[256,2048]{1,0:T(8,128)(2,1)S(1)}, bf16[256,2048]{1,0:T(8,128)(2,1)S(1)}, u32[]{:S(2)}, u32[]{:S(2)}) collective-permute-start(bf16[256,2048]{1,0:T(8,128)(2,1)S(1)} %pad_maximum_fusion.6), channel_id=1, source_target_pairs={{0,8},{8,0},{16,24},{24,16},{1,9},{9,1},{17,25},{25,17},{2,10},{10... | collective-permute-start | bytes 3145736 | tf_op jit(solution)/shard_map/ppermute | solution.py:184
  420.6 43.3 %collective-permute-start.14 = (bf16[256,2048]{1,0:T(8,128)(2,1)S(1)}, bf16[256,2048]{1,0:T(8,128)(2,1)S(1)}, u32[]{:S(2)}, u32[]{:S(2)}) collective-permute-start(bf16[256,2048]{1,0:T(8,128)(2,1)S(1)} %pad_maximum_fusion.3), channel_id=1, source_target_pairs={{0,16},{8,24},{16,0},{24,8},{1,17},{9,25},{17,1},{25,9},{2,18},{10... | collective-permute-start | bytes 3145736 | tf_op jit(solution)/shard_map/ppermute | solution.py:184
  422.0 41.8 %collective-permute-start.12 = (bf16[256,2048]{1,0:T(8,128)(2,1)S(1)}, bf16[256,2048]{1,0:T(8,128)(2,1)S(1)}, u32[]{:S(2)}, u32[]{:S(2)}) collective-permute-start(bf16[256,2048]{1,0:T(8,128)(2,1)S(1)} %pad_maximum_fusion.2), channel_id=1, source_target_pairs={{0,8},{8,0},{16,24},{24,16},{1,9},{9,1},{17,25},{25,17},{2,10},{10... | collective-permute-start | bytes 3145736 | tf_op jit(solution)/shard_map/ppermute | solution.py:184
  559.6 82.3 %collective-permute-start.45 = (bf16[256,2048]{1,0:T(8,128)(2,1)S(1)}, bf16[256,2048]{1,0:T(8,128)(2,1)S(1)}, u32[]{:S(2)}, u32[]{:S(2)}) collective-permute-start(bf16[256,2048]{1,0:T(8,128)(2,1)S(1)} %copy-done.43), channel_id=1, source_target_pairs={{0,8},{8,0},{16,24},{24,16},{1,9},{9,1},{17,25},{25,17},{2,10},{10... | collective-permute-start | bytes 3145736 | tf_op jit(solution)/shard_map/ppermute | solution.py:184
  560.2 82.2 %collective-permute-start.46 = (bf16[256,2048]{1,0:T(8,128)(2,1)S(1)}, bf16[256,2048]{1,0:T(8,128)(2,1)S(1)}, u32[]{:S(2)}, u32[]{:S(2)}) collective-permute-start(bf16[256,2048]{1,0:T(8,128)(2,1)S(1)} %copy-done.43), channel_id=1, source_target_pairs={{0,16},{8,24},{16,0},{24,8},{1,17},{9,25},{17,1},{25,9},{2,18},{10... | collective-permute-start | bytes 3145736 | tf_op jit(solution)/shard_map/ppermute | solution.py:184
  777.7 35.4 %collective-permute-start.52 = (bf16[256,2048]{1,0:T(8,128)(2,1)S(1)}, bf16[256,2048]{1,0:T(8,128)(2,1)S(1)}, u32[]{:S(2)}, u32[]{:S(2)}) collective-permute-start(bf16[256,2048]{1,0:T(8,128)(2,1)S(1)} %pad_maximum_fusion.12), channel_id=1, source_target_pairs={{0,16},{8,24},{16,0},{24,8},{1,17},{9,25},{17,1},{25,9},{2,18},{10... | collective-permute-start | bytes 3145736 | tf_op jit(solution)/shard_map/ppermute | solution.py:184
  778.5 34.6 %collective-permute-start.50 = (bf16[256,2048]{1,0:T(8,128)(2,1)S(1)}, bf16[256,2048]{1,0:T(8,128)(2,1)S(1)}, u32[]{:S(2)}, u32[]{:S(2)}) collective-permute-start(bf16[256,2048]{1,0:T(8,128)(2,1)S(1)} %pad_maximum_fusion.11), channel_id=1, source_target_pairs={{0,8},{8,0},{16,24},{24,16},{1,9},{9,1},{17,25},{25,17},{2,10},{10... | collective-permute-start | bytes 3145736 | tf_op jit(solution)/shard_map/ppermute | solution.py:184
  791.2 38.1 %collective-permute-start.29 = (bf16[256,2048]{1,0:T(8,128)(2,1)S(1)}, bf16[256,2048]{1,0:T(8,128)(2,1)S(1)}, u32[]{:S(2)}, u32[]{:S(2)}) collective-permute-start(bf16[256,2048]{1,0:T(8,128)(2,1)S(1)} %pad_maximum_fusion.5), channel_id=1, source_target_pairs={{0,16},{8,24},{16,0},{24,8},{1,17},{9,25},{17,1},{25,9},{2,18},{10... | collective-permute-start | bytes 3145736 | tf_op jit(solution)/shard_map/ppermute | solution.py:184
  792.8 36.5 %collective-permute-start.27 = (bf16[256,2048]{1,0:T(8,128)(2,1)S(1)}, bf16[256,2048]{1,0:T(8,128)(2,1)S(1)}, u32[]{:S(2)}, u32[]{:S(2)}) collective-permute-start(bf16[256,2048]{1,0:T(8,128)(2,1)S(1)} %pad_maximum_fusion.4), channel_id=1, source_target_pairs={{0,8},{8,0},{16,24},{24,16},{1,9},{9,1},{17,25},{25,17},{2,10},{10... | collective-permute-start | bytes 3145736 | tf_op jit(solution)/shard_map/ppermute | solution.py:184
  896.7 157.4 %reduce-scatter.11.cloned.1.call-start = ((), (), s32[]{:S(2)}) async-start(), calls=%async_computation.14 | async-start | bytes 9437184 | tf_op jit(solution)/shard_map/reduce_scatter | solution.py:248
  929.9 214.5 %reduce-scatter.9.cloned.1.call-start = ((), (), s32[]{:S(2)}) async-start(), calls=%async_computation.13 | async-start | bytes 9437184 | tf_op jit(solution)/shard_map/reduce_scatter | solution.py:248
  962.2 334.3 %reduce-scatter.7.cloned.1.call-start = ((), (), s32[]{:S(2)}) async-start(), calls=%async_computation.12 | async-start | bytes 8650752 | tf_op jit(solution)/shard_map/reduce_scatter | solution.py:344
  1054.1 90.3 %all-to-all-start.2 = ((bf16[4,64,2048]{2,1,0:T(8,128)(2,1)}), bf16[4,64,2048]{2,1,0:T(8,128)(2,1)S(1)}, u32[]{:S(2)}, u32[]{:S(2)}) async-start(bf16[4,64,2048]{2,1,0:T(8,128)(2,1)} %bitcast.188), calls=%async_computation.6 | async-start | bytes 2097152 | tf_op jit(solution)/shard_map/all_to_all | solution.py:249
  1057.7 368.4 %all-reduce.3.cloned.1.call-start = ((), (), s32[]{:S(2)}) async-start(), calls=%async_computation.15 | async-start | bytes 196608 | tf_op jit(solution)/shard_map/psum | solution.py:370
  (162 other events, 3361.8 us)
Sparse Core Ops, SparseCore 0:
  17.0 67.8 all-gather.4
  86.5 80.2 all-gather.6
  169.0 80.5 all-gather.8
  251.6 81.0 all-gather.10
  896.8 67.0 reduce-scatter.4
  966.1 87.9 reduce-scatter.10
  1056.4 87.9 reduce-scatter.8
  1146.7 149.7 reduce-scatter.6
  1304.0 122.0 all-reduce.2

commit v2 on v1

v2 whole, which is shorter than its diff:
```python
from functools import partial

import jax
import jax.numpy as jnp
from jax import lax
from jax.experimental import pallas as pl
from jax.experimental.pallas import tpu as pltpu
from jax.sharding import PartitionSpec as P

HEADS = 32
HEAD_DIM = 64
BLOCK = 256
PAIR = 2 * HEAD_DIM


def layer_norm(token_rows, gain_vec, shift_vec):
    average = jnp.mean(token_rows, axis=-1, keepdims=True)
    centred = token_rows - average
    spread = jnp.mean(centred * centred, axis=-1, keepdims=True)
    return centred * lax.rsqrt(spread + 1e-05) * gain_vec + shift_vec


def exact_gelu(values):
    return jax.nn.gelu(values, approximate=False)


def contract(left_side, right_side):
    return lax.dot_general(
        left_side, right_side, (((1,), (0,)), ((), ())), preferred_element_type=jnp.float32
    )


def contract_last(left_side, right_side):
    return lax.dot_general(
        left_side, right_side, (((1,), (1,)), ((), ())), preferred_element_type=jnp.float32
    )


def contract_first(left_side, right_side):
    return lax.dot_general(
        left_side, right_side, (((0,), (0,)), ((), ())), preferred_element_type=jnp.float32
    )


def row_pieces(mask, sequence, block, seqs, local):
    per = BLOCK // local
    return [
        pl.ds(pl.multiple_of((((block * per + r) ^ mask) * seqs + sequence) * local, local), local)
        for r in range(per)
    ]


def load_rows(ref, pieces, columns):
    parts = [ref[piece, columns] for piece in pieces]
    return parts[0] if len(parts) == 1 else jnp.concatenate(parts, axis=0)


def store_rows(ref, pieces, columns, values):
    local = values.shape[0] // len(pieces)
    for r, piece in enumerate(pieces):
        ref[piece, columns] = values[r * local : (r + 1) * local]


Q_COLUMNS, K_COLUMNS, V_COLUMNS = (slice(t * PAIR, (t + 1) * PAIR) for t in range(3))


def attend_forward_kernel(mask_ref, slope_ref, qkv_ref, mixed_ref, lse_ref, *, blocks, seqs, local):
    pair, sequence = pl.program_id(0), pl.program_id(1)
    mask = mask_ref[0]
    lane = lax.broadcasted_iota(jnp.int32, (BLOCK, PAIR), 1)
    row = lax.broadcasted_iota(jnp.int32, (BLOCK, BLOCK), 0)
    column = lax.broadcasted_iota(jnp.int32, (BLOCK, BLOCK), 1)
    gap = (row - column).astype(jnp.float32)
    pieces = [row_pieces(mask, sequence, block, seqs, local) for block in range(blocks)]

    for i in range(blocks):
        q_pair = load_rows(qkv_ref, pieces[i], Q_COLUMNS)
        outs, lses = [], []
        for head in range(2):
            slope = slope_ref[pair * 2 + head]
            mine = (lane >= head * HEAD_DIM) & (lane < (head + 1) * HEAD_DIM)
            q = jnp.where(mine, q_pair, jnp.zeros_like(q_pair)) * jnp.bfloat16(HEAD_DIM**-0.5)
            parts, highest = [], None
            for j in range(i + 1):
                scores = contract_last(q, load_rows(qkv_ref, pieces[j], K_COLUMNS))
                distance = jnp.abs(gap) if i == j else gap + float(BLOCK * (i - j))
                scores = scores - slope * distance
                parts.append(scores)
                top = jnp.max(scores, axis=-1, keepdims=True)
                highest = top if highest is None else jnp.maximum(highest, top)
            total, out = None, None
            for j in range(i + 1):
                weights = jnp.exp(parts[j] - highest)
                part = jnp.sum(weights, axis=-1, keepdims=True)
                mixed = contract(weights.astype(jnp.bfloat16), load_rows(qkv_ref, pieces[j], V_COLUMNS))
                total = part if total is None else total + part
                out = mixed if out is None else out + mixed
            outs.append(out / total)
            lses.append(highest + jnp.log(total))
        first = lane < HEAD_DIM
        everything = slice(0, PAIR)
        store_rows(
            mixed_ref, pieces[i], everything, jnp.where(first, outs[0], outs[1]).astype(mixed_ref.dtype)
        )
        store_rows(lse_ref, pieces[i], everything, jnp.where(first, lses[0], lses[1]))


def attend_backward_kernel(
    mask_ref, slope_ref, qkv_ref, lse_ref, mixed_ref, grad_ref, *rest, blocks, seqs, local, start
):
    out_ref, dq_ref, dk_ref, dv_ref = rest[-4:]
    pair, sequence = pl.program_id(0) + start, pl.program_id(1)
    mask = mask_ref[0]
    lane = lax.broadcasted_iota(jnp.int32, (BLOCK, PAIR), 1)
    key = lax.broadcasted_iota(jnp.int32, (BLOCK, BLOCK), 0)
    query = lax.broadcasted_iota(jnp.int32, (BLOCK, BLOCK), 1)
    gap = (query - key).astype(jnp.float32)
    pieces = [row_pieces(mask, sequence, block, seqs, local) for block in range(blocks)]
    everything = slice(0, PAIR)

    for i in range(blocks):
        q_pair = load_rows(qkv_ref, pieces[i], Q_COLUMNS)
        up_pair = load_rows(grad_ref, pieces[i], everything)
        mixed_pair = load_rows(mixed_ref, pieces[i], everything)
        inner_all = (up_pair.astype(jnp.float32) * mixed_pair.astype(jnp.float32)).T
        lse_all = load_rows(lse_ref, pieces[i], everything).T
        dq = None
        for head in range(2):
            slope = slope_ref[pair * 2 + head]
            mine = (lane >= head * HEAD_DIM) & (lane < (head + 1) * HEAD_DIM)
            zero = jnp.zeros_like(q_pair)
            q = jnp.where(mine, q_pair, zero) * jnp.bfloat16(HEAD_DIM**-0.5)
            up = jnp.where(mine, up_pair, zero)
            inner = jnp.sum(inner_all[head * HEAD_DIM : (head + 1) * HEAD_DIM], axis=0, keepdims=True)
            lse = lse_all[head * HEAD_DIM : head * HEAD_DIM + 1]
            for j in range(i + 1):
                k_pair = load_rows(qkv_ref, pieces[j], K_COLUMNS)
                distance = jnp.abs(gap) if i == j else gap + float(BLOCK * (i - j))
                probs = jnp.exp(contract_last(k_pair, q) - slope * distance - lse)
                prob_grad = contract_last(load_rows(qkv_ref, pieces[j], V_COLUMNS), up)
                score_grad = (probs * (prob_grad - inner)).astype(jnp.bfloat16)
                dv = contract(probs.astype(jnp.bfloat16), up)
                dk = contract(score_grad, q)
                part = contract_first(score_grad, jnp.where(mine, k_pair, zero))
                dq = part if dq is None else dq + part
                if i == j and head == 0:
                    dv_ref[j] = dv
                    dk_ref[j] = dk
                else:
                    dv_ref[j] += dv
                    dk_ref[j] += dk
        dq_ref[i] = dq
    for i in range(blocks):
        store_rows(out_ref, pieces[i], Q_COLUMNS, (dq_ref[i] * HEAD_DIM**-0.5).astype(out_ref.dtype))
        store_rows(out_ref, pieces[i], K_COLUMNS, dk_ref[i].astype(out_ref.dtype))
        store_rows(out_ref, pieces[i], V_COLUMNS, dv_ref[i].astype(out_ref.dtype))


def attend_forward(mask, slopes, qkv, seqs, local):
    rows, width = qkv.shape
    pairs, blocks = width // (3 * PAIR), rows // seqs // BLOCK
    scored = pairs * seqs * blocks * (blocks + 1) * BLOCK * BLOCK
    return pl.pallas_call(
        partial(attend_forward_kernel, blocks=blocks, seqs=seqs, local=local),
        grid_spec=pltpu.PrefetchScalarGridSpec(
            num_scalar_prefetch=2,
            grid=(pairs, seqs),
            in_specs=[pl.BlockSpec((rows, 3 * PAIR), lambda p, *_: (0, p))],
            out_specs=[pl.BlockSpec((rows, PAIR), lambda p, *_: (0, p))] * 2,
        ),
        out_shape=[
            jax.ShapeDtypeStruct((rows, pairs * PAIR), jnp.bfloat16),
            jax.ShapeDtypeStruct((rows, pairs * PAIR), jnp.float32),
        ],
        compiler_params=pltpu.CompilerParams(vmem_limit_bytes=40 * 2**20),
        cost_estimate=pl.CostEstimate(
            flops=scored * 2 * 512, bytes_accessed=rows * pairs * PAIR * 12, transcendentals=scored
        ),
        name="attend_forward",
    )(mask, slopes, qkv)


def attend_backward(mask, slopes, qkv, lse, mixed, grad, seqs, local, start, stop, begun=None):
    rows, width = qkv.shape
    blocks = rows // seqs // BLOCK
    scored = (stop - start) * seqs * blocks * (blocks + 1) * BLOCK * BLOCK
    narrow = pl.BlockSpec((rows, PAIR), lambda p, *_: (0, p + start))
    wide = pl.BlockSpec((rows, 3 * PAIR), lambda p, *_: (0, p + start))
    earlier = [] if begun is None else [begun]
    return pl.pallas_call(
        partial(attend_backward_kernel, blocks=blocks, seqs=seqs, local=local, start=start),
        grid_spec=pltpu.PrefetchScalarGridSpec(
            num_scalar_prefetch=2,
            grid=(stop - start, seqs),
            in_specs=[wide, narrow, narrow, narrow] + [pl.BlockSpec(memory_space=pl.ANY)] * len(earlier),
            out_specs=wide,
            scratch_shapes=[pltpu.VMEM((blocks, BLOCK, PAIR), jnp.float32)] * 3,
        ),
        out_shape=jax.ShapeDtypeStruct((rows, width), jnp.bfloat16),
        input_output_aliases={6: 0} if earlier else {},
        compiler_params=pltpu.CompilerParams(vmem_limit_bytes=40 * 2**20),
        cost_estimate=pl.CostEstimate(
            flops=scored * 2 * 1280,
            bytes_accessed=rows * (stop - start) * PAIR * 20,
            transcendentals=scored,
        ),
        name="attend_backward",
    )(mask, slopes, qkv, lse, mixed, grad, *earlier)


def swap(values, bit):
    return lax.ppermute(values, "seq", [(i, i ^ bit) for i in range(4)])


def by_index(parts, me):
    if len(parts) != 4:
        return parts
    odd, upper = (me & 1) == 1, (me & 2) == 2
    a, b, c, d = parts
    a, b, c, d = (
        jnp.where(odd, b, a),
        jnp.where(odd, a, b),
        jnp.where(odd, d, c),
        jnp.where(odd, c, d),
    )
    return [jnp.where(upper, c, a), jnp.where(upper, d, b), jnp.where(upper, a, c), jnp.where(upper, b, d)]


def gather(rows):
    if lax.axis_size("seq") != 4:
        return [lax.all_gather(rows, "seq", axis=0, tiled=True)]
    half = rows.shape[0] // 2
    first, second = swap(rows, 1), swap(rows, 2)
    return [rows, first, second, swap(second[:half], 1), swap(first[half:], 2)]


def near(slots):
    far, first, second, own = slots
    half = far.shape[0] // 2
    top, bottom = swap(far[:half], 1), swap(far[half:], 2)
    wide = jnp.float32
    low_first = (first[half:].astype(wide) + bottom.astype(wide)).astype(first.dtype)
    low_second = (second[:half].astype(wide) + top.astype(wide)).astype(first.dtype)
    first = jnp.concatenate([first[:half], low_first], axis=0)
    second = jnp.concatenate([low_second, second[half:]], axis=0)
    return first, second, own


def close(first, second, own):
    wide = jnp.float32
    return own.astype(wide) + swap(first, 1).astype(wide) + swap(second, 2).astype(wide)


def exchange(slots):
    if lax.axis_size("seq") != 4:
        return list(lax.all_to_all(jnp.stack(slots), "seq", split_axis=0, concat_axis=0, tiled=True))
    return [slots[0]] + [swap(slots[j], j) for j in (1, 2, 3)]


def total(values):
    for axis in ("fsdp", "seq"):
        count, bit = lax.axis_size(axis), 1
        while bit < count:
            other = [(i, i ^ bit) for i in range(count)]
            values = values + lax.ppermute(values, axis, other)
            bit *= 2
    return values


def scatter_slab(partial_sums, me):
    groups, shards = lax.axis_size("seq"), lax.axis_size("fsdp")
    width = partial_sums.shape[1]
    parts = jnp.swapaxes(partial_sums.reshape(groups, shards, -1, width), 0, 1).reshape(-1, width)
    summed = lax.psum_scatter(parts, "fsdp", scatter_dimension=0, tiled=True).reshape(groups, -1, width)
    slabs = exchange(by_index([summed[j] for j in range(groups)], me))
    return jnp.stack(by_index(slabs, me), axis=1).astype(jnp.float32)


def gate(values, *before):
    return lax.optimization_barrier((values, *before))[0]


class Order:
    def __init__(self):
        self.pending = []

    def after(self, *values):
        self.pending += values

    def __call__(self, operation, first, *others):
        if self.pending:
            first = gate(first, *self.pending)
        made = operation(first, *others)
        self.pending = [jax.tree.leaves(made)[0]]
        return made


def local(
    tokens,
    cotangent,
    w_qkv,
    qv_bias,
    w_out,
    out_bias,
    ln1_gain,
    ln1_shift,
    ln2_gain,
    ln2_shift,
    w_up,
    up_bias,
    w_down,
    down_bias,
):
    seq_count, local_len, model_width = tokens.shape
    groups, shards = lax.axis_size("seq"), lax.axis_size("fsdp")
    me = lax.axis_index("seq")
    square = groups == 4
    heads_here = HEADS // groups
    slab = heads_here * HEAD_DIM
    pairs = slab // PAIR
    hidden_width = w_up.shape[1]
    hidden_slab = hidden_width // groups
    rows_here = seq_count * local_len
    low, wide = jnp.bfloat16, jnp.float32
    mask = jnp.reshape(me if square else jnp.zeros_like(me), (1,)).astype(jnp.int32)
    head_index = me * heads_here + jnp.arange(1, heads_here + 1, dtype=jnp.int32)
    slopes = 2.0 ** (-8.0 * head_index.astype(wide) / HEADS)

    def head_columns(values):
        split = values.reshape(-1, 3, groups, pairs, PAIR)
        mine = lax.dynamic_index_in_dim(split, me, axis=2, keepdims=False)
        return jnp.swapaxes(mine, 1, 2).reshape(values.shape[0], -1)

    def own_slab(values, axis):
        width = values.shape[axis] // groups
        return lax.dynamic_slice_in_dim(values, me * width, width, axis=axis)

    qkv_slab = lax.all_gather(head_columns(w_qkv), "fsdp", axis=0, tiled=True)
    out_columns = lax.all_gather(gate(own_slab(w_out, 1), qkv_slab), "fsdp", axis=0, tiled=True)
    up_slab = lax.all_gather(own_slab(w_up, 1), "fsdp", axis=0, tiled=True)
    down_slab = lax.all_gather(own_slab(w_down, 0), "fsdp", axis=1, tiled=True)
    qkv_bias = head_columns(jnp.concatenate([qv_bias[0], jnp.zeros_like(qv_bias[0]), qv_bias[1]])[None])
    up_bias_slab = own_slab(up_bias, 0)

    def whole(parts):
        return parts[0] if len(parts) == 1 else jnp.concatenate(parts, axis=0)

    def by_slots(product, rows, order):
        if not square:
            return order(product, rows)
        cut = [rows[j * rows_here : (j + 1) * rows_here] for j in range(4)]
        return [order(product, cut[j]) for j in (3, 1, 2, 0)]

    def sum_over_seq(slots):
        if not square:
            return lax.psum_scatter(slots, "seq", scatter_dimension=0, tiled=True).astype(wide)
        return close(*slots)

    order = Order()
    x = tokens.reshape(rows_here, model_width).astype(wide)
    dz_low = cotangent.reshape(rows_here, model_width)
    dz = dz_low.astype(wide)
    first_norm, first_back = jax.vjp(layer_norm, x, ln1_gain, ln1_shift)
    normed = whole(gather(first_norm.astype(low)))
    qkv = order(lambda rows: (contract(rows, qkv_slab) + qkv_bias).astype(low), normed)
    out_parts = gather(out_columns) if square else None
    attended, log_totals = order(lambda rows: attend_forward(mask, slopes, rows, seq_count, local_len), qkv)
    mixed_slots = exchange([attended[j * rows_here : (j + 1) * rows_here] for j in range(groups)])
    mixed_rows = jnp.concatenate(by_index(mixed_slots, me), axis=1)
    mixed_slots = jnp.concatenate(mixed_slots, axis=1)
    if square:
        out_parts = by_index(out_parts[:3] + [whole(out_parts[3:])], me)
        full_out = jnp.concatenate(out_parts, axis=1)
    else:
        full_out = lax.all_gather(out_columns, "seq", axis=1, tiled=True)
    middle = x + (order(lambda rows: contract(rows, full_out), mixed_rows) + out_bias)
    second_norm, second_back = jax.vjp(layer_norm, middle, ln2_gain, ln2_shift)
    second = whole(gather(second_norm.astype(low)))
    upstream = whole(gather(gate(dz_low, second)))
    hidden = order(lambda rows: contract(rows, up_slab) + up_bias_slab, second)

    def bend(values):
        made, back = jax.vjp(exact_gelu, values)
        return made.astype(low), back(jnp.ones_like(values))[0]

    active, slope = order(bend, hidden)
    order.after(upstream)
    down_sum = order(lambda left: contract_first(left, active).astype(low), upstream)
    hidden_grad = order(lambda rows: (contract_last(rows, down_slab) * slope).astype(low), upstream)
    second_parts = by_slots(lambda rows: contract_last(rows, up_slab).astype(low), hidden_grad, order)
    if square:
        second_parts = near(second_parts)
        order.after(*second_parts)
    up_sum = order(lambda left: contract_first(left, hidden_grad).astype(low), second)
    outcome = by_slots(lambda rows: contract(rows, down_slab).astype(low), active, order)
    second_grad = sum_over_seq(second_parts)
    middle_part, ln2_gain_grad, ln2_shift_grad = second_back(second_grad)
    middle_grad = dz + middle_part
    branch_grad = middle_grad.astype(low)
    mixed_grad = order(lambda rows: contract_last(rows, full_out).astype(low), branch_grad)
    mixed_grad = whole(
        exchange(by_index([mixed_grad[:, j * slab : (j + 1) * slab] for j in range(groups)], me))
    )
    out_sum = order(lambda left: contract_first(left, branch_grad).astype(low), mixed_slots)
    if square:
        outcome = near([gate(outcome[0], mixed_grad)] + outcome[1:])
    order.after(mixed_grad)
    attention = (mask, slopes, qkv, log_totals, attended)
    begun = order(lambda rows: attend_backward(*attention, rows, seq_count, local_len, 0, pairs // 2), mixed_grad)
    if square:
        order.after(*outcome)
    qkv_grad = order(
        lambda rows: attend_backward(*attention, rows, seq_count, local_len, pairs // 2, pairs, begun), mixed_grad
    )
    normed_parts = by_slots(lambda rows: contract_last(rows, qkv_slab).astype(low), qkv_grad, order)
    outcome = sum_over_seq(outcome)
    if square:
        normed_parts = near(normed_parts)
        order.after(*normed_parts)
    qkv_sum = order(lambda left: contract_first(left, qkv_grad).astype(low), normed)
    normed_grad = sum_over_seq(normed_parts)
    result = (middle + (outcome + down_bias)).astype(low).reshape(tokens.shape)
    input_part, ln1_gain_grad, ln1_shift_grad = first_back(normed_grad)
    grad_tokens = (middle_grad + input_part).astype(low).reshape(tokens.shape)

    grad_w_down = scatter_slab(down_sum, me).reshape(-1, hidden_width).T
    grad_w_up = scatter_slab(up_sum, me).reshape(-1, hidden_width)
    if square:
        out_slots = [out_sum[j * slab : (j + 1) * slab] for j in (3, 1, 2, 0)]
        out_sum = close(*near([gate(out_slots[0], normed_grad)] + out_slots[1:])).astype(low)
    else:
        out_sum = lax.psum_scatter(out_sum, "seq", scatter_dimension=0, tiled=True)
    grad_w_out = lax.psum_scatter(out_sum, "fsdp", scatter_dimension=0, tiled=True).astype(wide)
    grad_w_qkv = scatter_slab(qkv_sum, me).reshape(-1, groups, pairs, 3, PAIR)
    grad_w_qkv = jnp.transpose(grad_w_qkv, (0, 3, 1, 2, 4)).reshape(-1, 3 * model_width)

    def column_sum(values):
        return jnp.sum(values.astype(wide), axis=0)

    hidden_sum = lax.dynamic_update_slice_in_dim(
        jnp.zeros((hidden_width,), wide), column_sum(hidden_grad), me * hidden_slab, axis=0
    )
    head_sum = jnp.transpose(column_sum(qkv_grad).reshape(pairs, 3, PAIR), (1, 0, 2)).reshape(3, slab)
    qv_sum = lax.dynamic_update_slice_in_dim(
        jnp.zeros((2, model_width), wide), head_sum[0::2], me * slab, axis=1
    )
    early = [column_sum(branch_grad), ln2_gain_grad, ln2_shift_grad, hidden_sum, column_sum(dz)]
    early = total(jnp.concatenate(early).reshape(-1, PAIR)).reshape(-1)
    late = [qv_sum.reshape(-1), ln1_gain_grad, ln1_shift_grad]
    late = total(jnp.concatenate(late).reshape(-1, PAIR)).reshape(-1)

    def cut(values, at, count):
        return values[at * model_width : (at + count) * model_width]

    ratio = hidden_width // model_width
    return (
        result,
        grad_tokens,
        grad_w_qkv,
        cut(late, 0, 2).reshape(2, model_width),
        grad_w_out,
        cut(early, 0, 1),
        cut(late, 2, 1),
        cut(late, 3, 1),
        cut(early, 1, 1),
        cut(early, 2, 1),
        grad_w_up,
        cut(early, 3, ratio),
        grad_w_down,
        cut(early, 3 + ratio, 1),
    )


def solution(mesh):
    return jax.shard_map(
        local,
        mesh=mesh,
        in_specs=(
            P("fsdp", "seq", None),
            P("fsdp", "seq", None),
            P("fsdp", None),
            P(),
            P("fsdp", None),
            P(),
            P(),
            P(),
            P(),
            P(),
            P("fsdp", None),
            P(),
            P(None, "fsdp"),
            P(),
        ),
        out_specs=(
            P("fsdp", "seq", None),
            P("fsdp", "seq", None),
            P(("seq", "fsdp"), None),
            P(),
            P(("seq", "fsdp"), None),
            P(),
            P(),
            P(),
            P(),
            P(),
            P(("seq", "fsdp"), None),
            P(),
            P(None, ("seq", "fsdp")),
            P(),
        ),
        check_vma=False,
    )
```

time: 1450 us -> 1170 us (0.81)
  waiting for transfers between devices: 808 us -> 535 us
  matrix products: 273 us -> 235 us
  other arithmetic: 75 us -> 112 us
  starting transfers between devices: 84.6 us -> 58.3 us
    all_gather x3, waiting for transfers between devices: 131 us -> 0.01 us  [the longest x1 0.01 us: local(): lax.all_gather(gate(own_slab(w_out, 1), qkv_slab), 'fsdp', axis=0, tiled=...]
    reduce_scatter x1, waiting for transfers between devices: 129 us -> 0.01 us  [local(): lax.psum_scatter(out_sum, 'fsdp', scatter_dimension=0, tiled=True)]
    psum x1 -> x0, waiting for transfers between devices: 128 us -> none  [local(): lax.psum((qv_sum, sum((part[1] for part in first_back)), sum((part[2] for...]
    all_gather x1, waiting for transfers between devices: 0.01 us -> 67.2 us  [local(): qkv_slab = lax.all_gather(head_columns(w_qkv), 'fsdp', axis=0, tiled=True)]
    ppermute x60 -> x47, waiting for transfers between devices: 315 us -> 378 us  [swap(): return lax.ppermute(values, 'seq', [(i, i ^ bit) for i in range(4)])]
    convert_element_type x3 -> x12, other arithmetic: 20.2 us -> 57.2 us  [the longest x1 36.8 us: bend(): return (made.astype(low), back(jnp.ones_like(values))[0])]
    reduce_scatter x3, waiting for transfers between devices: 95.8 us -> 65.6 us  [scatter_slab(): lax.psum_scatter(parts, 'fsdp', scatter_dimension=0, tiled=True)]
    dot_general x8 -> x10, matrix products: 120 us -> 92.2 us  [contract_last(): lax.dot_general(left_side, right_side, (((1,), (1,)), ((), ())), preferre...]
  transfers between devices with their start and end apart: 72 -> 65, of which waited for: 51 -> 37; matrix products, arithmetic and copies ran while one was open for 18% -> 33% of each run, Pallas kernels for 2% -> 7%
where the time goes in v2:
time: 1170 us; the launch traced here: 1160 us
  waiting for transfers between devices  535 us (46%)
  matrix products  235 us (20%)
  local copies, waits for them, and re-layouts  116 us (10%)
  other arithmetic  112 us (10%)
  Pallas kernels  84.3 us (7%)
  starting transfers between devices  58.3 us (5%)
  between operations  15.8 us (1%)
    ppermute x47, waiting for transfers between devices, swap(): return lax.ppermute(values, 'seq', [(i, i ^ bit) for i in range(4)])  378 us
    dot_general x10, matrix products, contract_last(): lax.dot_general(left_side, right_side, (((1,), (1,)), ((), ())), preferre...  92.2 us
    dot_general x7, matrix products, contract(): lax.dot_general(left_side, right_side, (((1,), (0,)), ((), ())), preferre...  78.3 us
    all_gather x1, waiting for transfers between devices, local(): qkv_slab = lax.all_gather(head_columns(w_qkv), 'fsdp', axis=0, tiled=True)  67.2 us
    reduce_scatter x3, waiting for transfers between devices, scatter_slab(): lax.psum_scatter(parts, 'fsdp', scatter_dimension=0, tiled=True)  65.6 us
    dot_general x4, matrix products, contract_first(): lax.dot_general(left_side, right_side, (((0,), (0,)), ((), ())), preferre...  64.6 us
    pallas_call x2, Pallas kernels, attend_backward(): pl.pallas_call(partial(attend_backward_kernel, blocks=blocks, seqs=seqs,...  55.7 us
    ppermute x47, starting transfers between devices, swap(): return lax.ppermute(values, 'seq', [(i, i ^ bit) for i in range(4)])  53.1 us
  transfers between devices with their start and end apart: 65, of which 37 were waited for; matrix products, arithmetic and copies ran while one was open for 33% of the time, Pallas kernels for 7%

profile of v2, /device:TPU:0, one launch (start us, length us, event | category | flops | bytes accessed | tf_op | source)
XLA Modules:
  0.0 1156.6 jit_solution(13488077652018048889)
XLA Ops:
  20.1 67.2 %all-gather.5.cloned.1.call-done = bf16[2048,1536]{0,1:T(8,128)(2,1)} async-done(((bf16[256,1536]{0,1:T(8,128)(2,1)}), bf16[2048,1536]{0,1:T(8,128)(2,1)}) %all-gather.5.cloned.1.call-update) | async-done | bytes 6291472 | tf_op jit(solution)/shard_map/all_gather | solution.py:338
  97.6 42.4 %collective-permute-done.1 = bf16[512,2048]{1,0:T(8,128)(2,1)S(1)} collective-permute-done((bf16[512,2048]{1,0:T(8,128)(2,1)}, bf16[512,2048]{1,0:T(8,128)(2,1)S(1)}, u32[]{:S(2)}, u32[]{:S(2)}) %collective-permute-start.1) | collective-permute-done | bytes 2097184 | tf_op jit(solution)/shard_map/ppermute | solution.py:212
  151.1 14.9 %collective-permute-done.2 = bf16[256,2048]{1,0:T(8,128)(2,1)} collective-permute-done((bf16[256,2048]{1,0:T(8,128)(2,1)}, bf16[256,2048]{1,0:T(8,128)(2,1)}, u32[]{:S(2)}, u32[]{:S(2)}) %collective-permute-start.2) | collective-permute-done | bytes 1048608 | tf_op jit(solution)/shard_map/ppermute | solution.py:212
  173.8 17.4 %add_convert_fusion.qkv_ref = bf16[2048,1536]{1,0:T(8,128)(2,1)S(1)} fusion(bf16[2048,2048]{1,0:T(8,128)(2,1)} %constant_dynamic-update-slice_fusion, bf16[2048,1536]{0,1:T(8,128)(2,1)} %all-gather.5.cloned.1.call-done, f32[1536]{0:T(1024)S(1)} %add.204), kind=kOutput, calls=%fused_computation.19 | convolution fusion | flops 12891193344 | bytes 20977664 | tf_op jit(solution)/shard_map/dot_general | solution.py:28
  191.2 28.6 %attend_forward.1 = (bf16[2048,512]{1,0:T(8,128)(2,1)S(1)}, f32[2048,512]{1,0:T(8,128)S(1)}) custom-call(s32[1]{0:T(128)} %bitcast.1.mask_ref, f32[8]{0:T(128)S(1)} %multiply_power_fusion.slope_ref, bf16[2048,1536]{1,0:T(8,128)(2,1)S(1)} %add_convert_fusion.qkv_ref), custom_call_target="tpu_custom_call" | custom-call | flops 10737418240 | bytes 12582912 | tf_op jit(solution)/shard_map/attend_forward/pallas_call | solution.py:163
  254.3 14.6 %collective-permute-done.8 = bf16[1024,512]{1,0:T(8,128)(2,1)} collective-permute-done((bf16[1024,512]{1,0:T(8,128)(2,1)}, bf16[1024,512]{1,0:T(8,128)(2,1)}, u32[]{:S(2)}, u32[]{:S(2)}) %collective-permute-start.8) | collective-permute-done | bytes 1048608 | tf_op jit(solution)/shard_map/ppermute | solution.py:212
  291.1 44.3 %collective-permute-done.12 = bf16[512,2048]{1,0:T(8,128)(2,1)S(1)} collective-permute-done((bf16[512,2048]{1,0:T(8,128)(2,1)S(1)}, bf16[512,2048]{1,0:T(8,128)(2,1)S(1)}, u32[]{:S(2)}, u32[]{:S(2)}) %collective-permute-start.12) | collective-permute-done | bytes 2097184 | tf_op jit(solution)/shard_map/ppermute | solution.py:212
  368.6 21.5 %convolution_add_fusion = f32[2048,2048]{1,0:T(8,128)S(1)} fusion(bf16[2048,2048]{1,0:T(8,128)(2,1)} %constant_dynamic-update-slice_fusion.7, bf16[2048,2048]{1,0:T(8,128)(2,1)} %all-gather.9.cloned.1.call-done, f32[2048]{0:T(1024)S(1)} %dynamic-slice-done), kind=kOutput, calls=%fused_computation.20 | convolution fusion | flops 17184063488 | bytes 33562624 | tf_op jit(solution)/shard_map/dot_general | solution.py:28
  390.1 23.1 %collective-permute-done.16 = bf16[512,2048]{1,0:T(8,128)(2,1)} collective-permute-done((bf16[512,2048]{1,0:T(8,128)(2,1)}, bf16[512,2048]{1,0:T(8,128)(2,1)}, u32[]{:S(2)}, u32[]{:S(2)}) %collective-permute-start.16) | collective-permute-done | bytes 2097184 | tf_op jit(solution)/shard_map/ppermute | solution.py:212
  415.1 36.8 %multiply_convert_fusion.1 = (bf16[2048,2048]{1,0:T(8,128)(2,1)S(1)}, f32[2048,2048]{1,0:T(8,128)}) fusion(f32[2048,2048]{1,0:T(8,128)S(1)} %convolution_add_fusion), kind=kLoop, calls=%fused_computation.4 | loop fusion | flops 272629760 | bytes 41943040 | tf_op jit(solution)/shard_map/convert_element_type | solution.py:384
  460.4 14.8 %collective-permute-done.18 = bf16[256,2048]{1,0:T(8,128)(2,1)S(1)} collective-permute-done((bf16[256,2048]{1,0:T(8,128)(2,1)S(1)}, bf16[256,2048]{1,0:T(8,128)(2,1)S(1)}, u32[]{:S(2)}, u32[]{:S(2)}) %collective-permute-start.18) | collective-permute-done | bytes 1048608 | tf_op jit(solution)/shard_map/ppermute | solution.py:212
  478.7 20.7 %convolution_convert_fusion.2 = bf16[2048,2048]{1,0:T(8,128)(2,1)} fusion(bf16[2048,2048]{1,0:T(8,128)(2,1)S(1)} %constant_dynamic-update-slice_fusion.12, bf16[2048,2048]{1,0:T(8,128)(2,1)S(1)} %get-tuple-element.93), kind=kOutput, calls=%fused_computation.24 | convolution fusion | flops 17184063488 | bytes 25165824 | tf_op jit(solution)/shard_map/dot_general | solution.py:40
  499.4 31.8 %convert_reduce_fusion = (f32[2048]{0:T(1024)}, bf16[2048,2048]{1,0:T(8,128)(2,1)S(1)}) fusion(f32[2048,2048]{1,0:T(8,128)} %get-tuple-element.94, f32[2048,2048]{1,0:T(8,128)} %copy-done.13, bf16[2048,2048]{1,0:T(8,128)(2,1)} %copy-done.39, bf16[2048,2048]{1,0:T(8,128)(2,1)} %all-gather.11.cloned.1.call-done), kind=kOutput, calls=%fused_computation.2 | convolution fusion | flops 17238587392 | bytes 58728448 | tf_op jit(solution)/shard_map/dot_general | solution.py:34
  590.3 27.1 %collective-permute-done.21 = bf16[512,2048]{1,0:T(8,128)(2,1)} collective-permute-done((bf16[512,2048]{1,0:T(8,128)(2,1)}, bf16[512,2048]{1,0:T(8,128)(2,1)}, u32[]{:S(2)}, u32[]{:S(2)}) %collective-permute-start.21) | collective-permute-done | bytes 2097184 | tf_op jit(solution)/shard_map/ppermute | solution.py:212
  618.7 13.8 %multiply_reduce_fusion = (f32[2048]{0:T(1024)}, f32[512]{0:T(512)S(1)}, f32[2048]{0:T(1024)}, bf16[512,2048]{1,0:T(8,128)(2,1)}) fusion(f32[512,2048]{1,0:T(8,128)} %copy-done.8, f32[512]{0:T(512)S(1)} %copy-done.62, f32[512]{0:T(512)S(1)} %copy-done.53, bf16[512,2048]{1,0:T(8,128)(2,1)} %collective-permute-done.22, ...), kind=kOutput, calls=%fused_computation.44 | convolution fusion | flops 4309642752 | bytes 21002240 | tf_op jit(solution)/shard_map/dot_general | solution.py:34
  632.5 21.9 %convolution_convert_fusion.1 = bf16[2048,2048]{1,0:T(8,128)(2,1)} fusion(bf16[2048,2048]{1,0:T(8,128)(2,1)} %constant_dynamic-update-slice_fusion.7, bf16[2048,2048]{1,0:T(8,128)(2,1)S(1)} %bitcast.167), kind=kOutput, calls=%fused_computation.23 | convolution fusion | flops 17184063488 | bytes 25165824 | tf_op jit(solution)/shard_map/dot_general | solution.py:40
  728.0 28.0 %attend_backward.2.rest_0_ = bf16[2048,1536]{1,0:T(8,128)(2,1)} custom-call(s32[1]{0:T(128)} %bitcast.1.mask_ref, f32[8]{0:T(128)S(1)} %multiply_power_fusion.slope_ref, bf16[2048,1536]{1,0:T(8,128)(2,1)} %copy-done.2, f32[2048,512]{1,0:T(8,128)S(1)} %copy-done.4, bf16[2048,512]{1,0:T(8,128)(2,1)S(1)} %get-tuple-element.44.mixed_ref, ...), custom_call_target="tpu_custom_call" | custom-call | flops 13421772800 | bytes 10485760 | tf_op jit(solution)/shard_map/attend_backward/pallas_call | solution.py:190
  761.5 27.7 %attend_backward.3 = bf16[2048,1536]{1,0:T(8,128)(2,1)} custom-call(s32[1]{0:T(128)} %bitcast.1.mask_ref, f32[8]{0:T(128)S(1)} %multiply_power_fusion.slope_ref, bf16[2048,1536]{1,0:T(8,128)(2,1)} %copy-done.2, f32[2048,512]{1,0:T(8,128)S(1)} %copy-done.4, bf16[2048,512]{1,0:T(8,128)(2,1)S(1)} %get-tuple-element.44.mixed_ref, ...), custom_call_target="tpu_custom_call", output_to_operand_aliasing={{}: (6, {})} | custom-call | flops 13421772800 | bytes 10485760 | tf_op jit(solution)/shard_map/attend_backward/pallas_call | solution.py:190
  836.1 31.4 %collective-permute-done.31 = bf16[512,2048]{1,0:T(8,128)(2,1)S(1)} collective-permute-done((bf16[512,2048]{1,0:T(8,128)(2,1)S(1)}, bf16[512,2048]{1,0:T(8,128)(2,1)S(1)}, u32[]{:S(2)}, u32[]{:S(2)}) %collective-permute-start.31) | collective-permute-done | bytes 2097184 | tf_op jit(solution)/shard_map/ppermute | solution.py:212
  873.4 14.4 %collective-permute-done.42 = bf16[256,2048]{1,0:T(8,128)(2,1)S(1)} collective-permute-done((bf16[256,2048]{1,0:T(8,128)(2,1)S(1)}, bf16[256,2048]{1,0:T(8,128)(2,1)S(1)}, u32[]{:S(2)}, u32[]{:S(2)}) %collective-permute-start.42) | collective-permute-done | bytes 1048608 | tf_op jit(solution)/shard_map/ppermute | solution.py:212
  898.8 34.3 %collective-permute-done.43 = bf16[512,2048]{1,0:T(8,128)(2,1)S(1)} collective-permute-done((bf16[512,2048]{1,0:T(8,128)(2,1)S(1)}, bf16[512,2048]{1,0:T(8,128)(2,1)S(1)}, u32[]{:S(2)}, u32[]{:S(2)}) %collective-permute-start.43) | collective-permute-done | bytes 2097184 | tf_op jit(solution)/shard_map/ppermute | solution.py:212
  935.8 17.3 %convolution_convert_fusion.3 = bf16[2048,1536]{1,0:T(8,128)(2,1)S(1)} fusion(bf16[2048,2048]{1,0:T(8,128)(2,1)} %constant_dynamic-update-slice_fusion, bf16[2048,1536]{1,0:T(8,128)(2,1)} %attend_backward.3), kind=kOutput, calls=%fused_computation.25 | convolution fusion | flops 12888047616 | bytes 20971520 | tf_op jit(solution)/shard_map/dot_general | solution.py:40
  1004.5 27.7 %collective-permute-done.27 = bf16[512,2048]{1,0:T(8,128)(2,1)} collective-permute-done((bf16[512,2048]{1,0:T(8,128)(2,1)}, bf16[512,2048]{1,0:T(8,128)(2,1)}, u32[]{:S(2)}, u32[]{:S(2)}) %collective-permute-start.27) | collective-permute-done | bytes 2097184 | tf_op jit(solution)/shard_map/ppermute | solution.py:212
  1066.2 65.6 %reduce-scatter.9.cloned.1.call-done = bf16[256,2048]{1,0:T(8,128)(2,1)} async-done(((bf16[2048,2048]{1,0:T(8,128)(2,1)}), bf16[256,2048]{1,0:T(8,128)(2,1)}) %reduce-scatter.9.cloned.1.call-update) | async-done | bytes 1048592 | tf_op jit(solution)/shard_map/reduce_scatter | solution.py:274
  (460 shorter events, 453.5 us)
Async XLA Ops:
  7.2 80.1 %all-gather.5.cloned.1.call-start = ((), (), s32[]{:S(2)}) async-start(), calls=%async_computation.4 | async-start | bytes 7077888 | tf_op jit(solution)/shard_map/all_gather | solution.py:338
  19.3 152.5 %all-gather.7.cloned.1.call-start = ((), (), s32[]{:S(2)}) async-start(), calls=%async_computation.5 | async-start | bytes 2359296 | tf_op jit(solution)/shard_map/all_gather | solution.py:339
  87.4 281.2 %all-gather.9.cloned.1.call-start = ((), (), s32[]{:S(2)}) async-start(), calls=%async_computation.6 | async-start | bytes 9437184 | tf_op jit(solution)/shard_map/all_gather | solution.py:340
  92.0 48.0 %collective-permute-start.1 = (bf16[512,2048]{1,0:T(8,128)(2,1)}, bf16[512,2048]{1,0:T(8,128)(2,1)S(1)}, u32[]{:S(2)}, u32[]{:S(2)}) collective-permute-start(bf16[512,2048]{1,0:T(8,128)(2,1)} %get-tuple-element.171), channel_id=1, source_target_pairs={{0,16},{8,24},{16,0},{24,8},{1,17},{9,25},{17,1},{25,9},{2,18},{10... | collective-permute-start | bytes 6291464 | tf_op jit(solution)/shard_map/ppermute | solution.py:212
  93.4 49.1 %collective-permute-start = (bf16[512,2048]{1,0:T(8,128)(2,1)}, bf16[512,2048]{1,0:T(8,128)(2,1)}, u32[]{:S(2)}, u32[]{:S(2)}) collective-permute-start(bf16[512,2048]{1,0:T(8,128)(2,1)} %get-tuple-element.171), channel_id=1, source_target_pairs={{0,8},{8,0},{16,24},{24,16},{1,9},{9,1},{17,25},{25,17},{2,10},{10... | collective-permute-start | bytes 6291464 | tf_op jit(solution)/shard_map/ppermute | solution.py:212
  97.3 402.0 %all-gather.11.cloned.1.call-start = ((), (), s32[]{:S(2)}) async-start(), calls=%async_computation.7 | async-start | bytes 9437184 | tf_op jit(solution)/shard_map/all_gather | solution.py:341
  171.8 54.8 %collective-permute-start.7 = (bf16[2048,512]{1,0:T(8,128)(2,1)}, bf16[2048,512]{1,0:T(8,128)(2,1)S(1)}, u32[]{:S(2)}, u32[]{:S(2)}) collective-permute-start(bf16[2048,512]{1,0:T(8,128)(2,1)} %all-gather.7.cloned.1.call-done), channel_id=1, source_target_pairs={{0,16},{8,24},{16,0},{24,8},{1,17},{9,25},{17,1},{25,9},{2,18},{10... | collective-permute-start | bytes 6291464 | tf_op jit(solution)/shard_map/ppermute | solution.py:212
  173.2 57.1 %collective-permute-start.9 = (bf16[2048,512]{1,0:T(8,128)(2,1)}, bf16[2048,512]{1,0:T(8,128)(2,1)S(1)}, u32[]{:S(2)}, u32[]{:S(2)}) collective-permute-start(bf16[2048,512]{1,0:T(8,128)(2,1)} %all-gather.7.cloned.1.call-done), channel_id=1, source_target_pairs={{0,8},{8,0},{16,24},{24,16},{1,9},{9,1},{17,25},{25,17},{2,10},{10... | collective-permute-start | bytes 6291464 | tf_op jit(solution)/shard_map/ppermute | solution.py:212
  288.3 47.1 %collective-permute-start.12 = (bf16[512,2048]{1,0:T(8,128)(2,1)S(1)}, bf16[512,2048]{1,0:T(8,128)(2,1)S(1)}, u32[]{:S(2)}, u32[]{:S(2)}) collective-permute-start(bf16[512,2048]{1,0:T(8,128)(2,1)S(1)} %get-tuple-element.96), channel_id=1, source_target_pairs={{0,16},{8,24},{16,0},{24,8},{1,17},{9,25},{17,1},{25,9},{2,18},{10... | collective-permute-start | bytes 6291464 | tf_op jit(solution)/shard_map/ppermute | solution.py:212
  289.8 48.4 %collective-permute-start.11 = (bf16[512,2048]{1,0:T(8,128)(2,1)S(1)}, bf16[512,2048]{1,0:T(8,128)(2,1)S(1)}, u32[]{:S(2)}, u32[]{:S(2)}) collective-permute-start(bf16[512,2048]{1,0:T(8,128)(2,1)S(1)} %get-tuple-element.96), channel_id=1, source_target_pairs={{0,8},{8,0},{16,24},{24,16},{1,9},{9,1},{17,25},{25,17},{2,10},{10... | collective-permute-start | bytes 6291464 | tf_op jit(solution)/shard_map/ppermute | solution.py:212
  344.4 698.8 %reduce-scatter.11.cloned.1.call-start = ((), (), s32[]{:S(2)}) async-start(), calls=%async_computation.11 | async-start | bytes 9437184 | tf_op jit(solution)/shard_map/reduce_scatter | solution.py:274
  366.5 85.4 %collective-permute-start.15 = (bf16[512,2048]{1,0:T(8,128)(2,1)}, bf16[512,2048]{1,0:T(8,128)(2,1)}, u32[]{:S(2)}, u32[]{:S(2)}) collective-permute-start(bf16[512,2048]{1,0:T(8,128)(2,1)} %bitcast.10), channel_id=1, source_target_pairs={{0,8},{8,0},{16,24},{24,16},{1,9},{9,1},{17,25},{25,17},{2,10},{10... | collective-permute-start | bytes 6291464 | tf_op jit(solution)/shard_map/ppermute | solution.py:212
  368.3 45.0 %collective-permute-start.16 = (bf16[512,2048]{1,0:T(8,128)(2,1)}, bf16[512,2048]{1,0:T(8,128)(2,1)}, u32[]{:S(2)}, u32[]{:S(2)}) collective-permute-start(bf16[512,2048]{1,0:T(8,128)(2,1)} %bitcast.10), channel_id=1, source_target_pairs={{0,16},{8,24},{16,0},{24,8},{1,17},{9,25},{17,1},{25,9},{2,18},{10... | collective-permute-start | bytes 6291464 | tf_op jit(solution)/shard_map/ppermute | solution.py:212
  414.7 45.7 %collective-permute-start.17 = (bf16[256,2048]{1,0:T(8,128)(2,1)S(1)}, bf16[256,2048]{1,0:T(8,128)(2,1)S(1)}, u32[]{:S(2)}, u32[]{:S(2)}) collective-permute-start(bf16[256,2048]{1,0:T(8,128)(2,1)S(1)} %slice.365), channel_id=1, source_target_pairs={{0,8},{8,0},{16,24},{24,16},{1,9},{9,1},{17,25},{25,17},{2,10},{10... | collective-permute-start | bytes 3145736 | tf_op jit(solution)/shard_map/ppermute | solution.py:212
  574.2 43.2 %collective-permute-start.21 = (bf16[512,2048]{1,0:T(8,128)(2,1)}, bf16[512,2048]{1,0:T(8,128)(2,1)}, u32[]{:S(2)}, u32[]{:S(2)}) collective-permute-start(bf16[512,2048]{1,0:T(8,128)(2,1)} %pad_maximum_fusion.2), channel_id=1, source_target_pairs={{0,8},{8,0},{16,24},{24,16},{1,9},{9,1},{17,25},{25,17},{2,10},{10... | collective-permute-start | bytes 6291464 | tf_op jit(solution)/shard_map/ppermute | solution.py:212
  590.2 465.8 %reduce-scatter.7.cloned.1.call-start = ((), (), s32[]{:S(2)}) async-start(), calls=%async_computation.9 | async-start | bytes 2359296 | tf_op jit(solution)/shard_map/reduce_scatter | solution.py:433
  817.0 50.6 %collective-permute-start.31 = (bf16[512,2048]{1,0:T(8,128)(2,1)S(1)}, bf16[512,2048]{1,0:T(8,128)(2,1)S(1)}, u32[]{:S(2)}, u32[]{:S(2)}) collective-permute-start(bf16[512,2048]{1,0:T(8,128)(2,1)S(1)} %pad_maximum_fusion.8), channel_id=1, source_target_pairs={{0,8},{8,0},{16,24},{24,16},{1,9},{9,1},{17,25},{25,17},{2,10},{10... | collective-permute-start | bytes 6291464 | tf_op jit(solution)/shard_map/ppermute | solution.py:212
  935.7 125.5 %reduce-scatter.5.cloned.1.call-start = ((), (), s32[]{:S(2)}) async-start(), calls=%async_computation.8 | async-start | bytes 7077888 | tf_op jit(solution)/shard_map/reduce_scatter | solution.py:274
  956.5 175.3 %reduce-scatter.9.cloned.1.call-start = ((), (), s32[]{:S(2)}) async-start(), calls=%async_computation.10 | async-start | bytes 9437184 | tf_op jit(solution)/shard_map/reduce_scatter | solution.py:274
  987.6 44.6 %collective-permute-start.27 = (bf16[512,2048]{1,0:T(8,128)(2,1)}, bf16[512,2048]{1,0:T(8,128)(2,1)}, u32[]{:S(2)}, u32[]{:S(2)}) collective-permute-start(bf16[512,2048]{1,0:T(8,128)(2,1)} %pad_maximum_fusion.5), channel_id=1, source_target_pairs={{0,8},{8,0},{16,24},{24,16},{1,9},{9,1},{17,25},{25,17},{2,10},{10... | collective-permute-start | bytes 6291464 | tf_op jit(solution)/shard_map/ppermute | solution.py:212
  989.8 43.8 %collective-permute-start.29 = (bf16[512,2048]{1,0:T(8,128)(2,1)}, bf16[512,2048]{1,0:T(8,128)(2,1)}, u32[]{:S(2)}, u32[]{:S(2)}) collective-permute-start(bf16[512,2048]{1,0:T(8,128)(2,1)} %pad_maximum_fusion.6), channel_id=1, source_target_pairs={{0,16},{8,24},{16,0},{24,8},{1,17},{9,25},{17,1},{25,9},{2,18},{10... | collective-permute-start | bytes 6291464 | tf_op jit(solution)/shard_map/ppermute | solution.py:212
  1062.6 74.2 %collective-permute-start.34 = (bf16[64,1536]{1,0:T(8,128)(2,1)S(1)}, bf16[64,1536]{1,0:T(8,128)(2,1)S(1)}, u32[]{:S(2)}, u32[]{:S(2)}) collective-permute-start(bf16[64,1536]{1,0:T(8,128)(2,1)S(1)} %get-tuple-element.159), channel_id=1, source_target_pairs={{0,24},{8,16},{16,8},{24,0},{1,25},{9,17},{17,9},{25,1},{2,26},{10... | collective-permute-start | bytes 589832 | tf_op jit(solution)/shard_map/ppermute | solution.py:212
  1064.8 72.6 %collective-permute-start.35 = (bf16[64,1536]{1,0:T(8,128)(2,1)S(1)}, bf16[64,1536]{1,0:T(8,128)(2,1)S(1)}, u32[]{:S(2)}, u32[]{:S(2)}) collective-permute-start(bf16[64,1536]{1,0:T(8,128)(2,1)S(1)} %get-tuple-element.86), channel_id=1, source_target_pairs={{0,16},{8,24},{16,0},{24,8},{1,17},{9,25},{17,1},{25,9},{2,18},{10... | collective-permute-start | bytes 589832 | tf_op jit(solution)/shard_map/ppermute | solution.py:212
  1065.2 72.2 %collective-permute-start.36 = (bf16[64,1536]{1,0:T(8,128)(2,1)S(1)}, bf16[64,1536]{1,0:T(8,128)(2,1)S(1)}, u32[]{:S(2)}, u32[]{:S(2)}) collective-permute-start(bf16[64,1536]{1,0:T(8,128)(2,1)S(1)} %get-tuple-element.158), channel_id=1, source_target_pairs={{0,8},{8,0},{16,24},{24,16},{1,9},{9,1},{17,25},{25,17},{2,10},{10... | collective-permute-start | bytes 589832 | tf_op jit(solution)/shard_map/ppermute | solution.py:212
  (126 other events, 2341.7 us)
Sparse Core Ops, SparseCore 0:
  19.4 67.8 all-gather.4
  89.5 27.2 all-gather.6
  118.4 81.5 all-gather.8
  344.5 79.8 all-gather.10
  590.4 86.8 reduce-scatter.10
  935.9 33.3 reduce-scatter.6
  971.5 69.8 reduce-scatter.4
  1043.7 87.9 reduce-scatter.8

commit v3 on v2

--- a/solution.py
+++ b/solution.py
@@ -226,56 +226,12 @@
     return [jnp.where(upper, c, a), jnp.where(upper, d, b), jnp.where(upper, a, c), jnp.where(upper, b, d)]
 
 
-def gather(rows):
-    if lax.axis_size("seq") != 4:
-        return [lax.all_gather(rows, "seq", axis=0, tiled=True)]
-    half = rows.shape[0] // 2
-    first, second = swap(rows, 1), swap(rows, 2)
-    return [rows, first, second, swap(second[:half], 1), swap(first[half:], 2)]
-
-
-def near(slots):
-    far, first, second, own = slots
-    half = far.shape[0] // 2
-    top, bottom = swap(far[:half], 1), swap(far[half:], 2)
-    wide = jnp.float32
-    low_first = (first[half:].astype(wide) + bottom.astype(wide)).astype(first.dtype)
-    low_second = (second[:half].astype(wide) + top.astype(wide)).astype(first.dtype)
-    first = jnp.concatenate([first[:half], low_first], axis=0)
-    second = jnp.concatenate([low_second, second[half:]], axis=0)
-    return first, second, own
-
-
-def close(first, second, own):
-    wide = jnp.float32
-    return own.astype(wide) + swap(first, 1).astype(wide) + swap(second, 2).astype(wide)
-
-
 def exchange(slots):
     if lax.axis_size("seq") != 4:
         return list(lax.all_to_all(jnp.stack(slots), "seq", split_axis=0, concat_axis=0, tiled=True))
     return [slots[0]] + [swap(slots[j], j) for j in (1, 2, 3)]
 
 
-def total(values):
-    for axis in ("fsdp", "seq"):
-        count, bit = lax.axis_size(axis), 1
-        while bit < count:
-            other = [(i, i ^ bit) for i in range(count)]
-            values = values + lax.ppermute(values, axis, other)
-            bit *= 2
-    return values
-
-
-def scatter_slab(partial_sums, me):
-    groups, shards = lax.axis_size("seq"), lax.axis_size("fsdp")
-    width = partial_sums.shape[1]
-    parts = jnp.swapaxes(partial_sums.reshape(groups, shards, -1, width), 0, 1).reshape(-1, width)
-    summed = lax.psum_scatter(parts, "fsdp", scatter_dimension=0, tiled=True).reshape(groups, -1, width)
-    slabs = exchange(by_index([summed[j] for j in range(groups)], me))
-    return jnp.stack(by_index(slabs, me), axis=1).astype(jnp.float32)
-
-
 def gate(values, *before):
     return lax.optimization_barrier((values, *before))[0]
 
@@ -287,12 +243,91 @@
     def after(self, *values):
         self.pending += values
 
-    def __call__(self, operation, first, *others):
+    def __call__(self, operation, *operands):
         if self.pending:
-            first = gate(first, *self.pending)
-        made = operation(first, *others)
+            count = len(operands)
+            operands = lax.optimization_barrier((*operands, *self.pending))[:count]
+        made = operation(*operands)
         self.pending = [jax.tree.leaves(made)[0]]
         return made
+
+    def gather(self, rows):
+        if lax.axis_size("seq") != 4:
+            return lax.all_gather(rows, "seq", axis=0, tiled=True), None
+        return rows, (swap(rows, 1), swap(rows, 2))
+
+    def pass_on(self, begun):
+        rows, came = begun
+        if came is None:
+            return rows
+        half = rows.shape[0] // 2
+        top, bottom = self(lambda first, second: (second[:half], first[half:]), *came)
+        return [rows, *came, swap(top, 1), swap(bottom, 2)]
+
+    def scatter(self, product, rows, axis=0):
+        if lax.axis_size("seq") != 4:
+            return lax.psum_scatter(self(product, rows), "seq", scatter_dimension=0, tiled=True), None
+        count = rows.shape[axis] // 4
+        cut = [lax.slice_in_dim(rows, j * count, (j + 1) * count, axis=axis) for j in range(4)]
+        far = self(product, cut[3])
+        half = far.shape[0] // 2
+        top, bottom = swap(far[:half], 1), swap(far[half:], 2)
+        return cut, (self(product, cut[1]), self(product, cut[2]), top, bottom)
+
+    def add_far(self, begun, product):
+        cut, parts = begun
+        if parts is None:
+            return begun
+        half = parts[0].shape[0] // 2
+        wide = jnp.float32
+
+        def add(first, second, top, bottom):
+            first_low = (first[half:].astype(wide) + bottom.astype(wide)).astype(first.dtype)
+            second_low = (second[:half].astype(wide) + top.astype(wide)).astype(first.dtype)
+            return (
+                jnp.concatenate([first[:half], first_low], axis=0),
+                jnp.concatenate([second_low, second[half:]], axis=0),
+            )
+
+        first, second = self(add, *parts)
+        came = swap(first, 1), swap(second, 2)
+        return self(product, cut[0]), came
+
+
+class Total:
+    def __init__(self, values):
+        self.values = values
+        self.steps = [
+            (axis, 1 << bit) for axis in ("fsdp", "seq") for bit in range(lax.axis_size(axis).bit_length() - 1)
+        ]
+        self.send()
+
+    def send(self):
+        self.came = None
+        if self.steps:
+            axis, bit = self.steps.pop(0)
+            other = [(i, i ^ bit) for i in range(lax.axis_size(axis))]
+            self.came = lax.ppermute(self.values, axis, other)
+
+    def step(self, order=None):
+        if self.came is not None:
+            add = lambda own, other: own + other
+            self.values = (order or (lambda operation, *operands: operation(*operands)))(add, self.values, self.came)
+            self.send()
+
+    def done(self):
+        while self.came is not None:
+            self.step()
+        return self.values.reshape(-1)
+
+
+def summed(own, came):
+    wide = jnp.float32
+    return own.astype(wide) if came is None else own.astype(wide) + came[0].astype(wide) + came[1].astype(wide)
+
+
+def whole(parts):
+    return jnp.concatenate(parts, axis=0) if isinstance(parts, list) else parts
 
 
 def local(
@@ -335,48 +370,45 @@
         width = values.shape[axis] // groups
         return lax.dynamic_slice_in_dim(values, me * width, width, axis=axis)
 
+    order = Order()
+    x_low = tokens.reshape(rows_here, model_width)
+    x = x_low.astype(wide)
+    dz_low = cotangent.reshape(rows_here, model_width)
+    dz = dz_low.astype(wide)
     qkv_slab = lax.all_gather(head_columns(w_qkv), "fsdp", axis=0, tiled=True)
-    out_columns = lax.all_gather(gate(own_slab(w_out, 1), qkv_slab), "fsdp", axis=0, tiled=True)
+    qkv_bias = head_columns(jnp.concatenate([qv_bias[0], jnp.zeros_like(qv_bias[0]), qv_bias[1]])[None])
+    up_bias_slab = own_slab(up_bias, 0)
+
+    first_norm, first_back = jax.vjp(layer_norm, x, ln1_gain, ln1_shift)
+    normed = order.gather(order(lambda values: values.astype(low), first_norm))
+    normed = order.pass_on(normed)
+    full_out = lax.all_gather(gate(w_out, *normed[1:3]), "fsdp", axis=0, tiled=True)
     up_slab = lax.all_gather(own_slab(w_up, 1), "fsdp", axis=0, tiled=True)
     down_slab = lax.all_gather(own_slab(w_down, 0), "fsdp", axis=1, tiled=True)
-    qkv_bias = head_columns(jnp.concatenate([qv_bias[0], jnp.zeros_like(qv_bias[0]), qv_bias[1]])[None])
-    up_bias_slab = own_slab(up_bias, 0)
-
-    def whole(parts):
-        return parts[0] if len(parts) == 1 else jnp.concatenate(parts, axis=0)
-
-    def by_slots(product, rows, order):
-        if not square:
-            return order(product, rows)
-        cut = [rows[j * rows_here : (j + 1) * rows_here] for j in range(4)]
-        return [order(product, cut[j]) for j in (3, 1, 2, 0)]
-
-    def sum_over_seq(slots):
-        if not square:
-            return lax.psum_scatter(slots, "seq", scatter_dimension=0, tiled=True).astype(wide)
-        return close(*slots)
-
-    order = Order()
-    x = tokens.reshape(rows_here, model_width).astype(wide)
-    dz_low = cotangent.reshape(rows_here, model_width)
-    dz = dz_low.astype(wide)
-    first_norm, first_back = jax.vjp(layer_norm, x, ln1_gain, ln1_shift)
-    normed = whole(gather(first_norm.astype(low)))
+    normed = whole(normed)
+    upstream = order.gather(gate(dz_low, normed))
     qkv = order(lambda rows: (contract(rows, qkv_slab) + qkv_bias).astype(low), normed)
-    out_parts = gather(out_columns) if square else None
     attended, log_totals = order(lambda rows: attend_forward(mask, slopes, rows, seq_count, local_len), qkv)
     mixed_slots = exchange([attended[j * rows_here : (j + 1) * rows_here] for j in range(groups)])
+    upstream = order.pass_on(upstream)
     mixed_rows = jnp.concatenate(by_index(mixed_slots, me), axis=1)
     mixed_slots = jnp.concatenate(mixed_slots, axis=1)
-    if square:
-        out_parts = by_index(out_parts[:3] + [whole(out_parts[3:])], me)
-        full_out = jnp.concatenate(out_parts, axis=1)
-    else:
-        full_out = lax.all_gather(out_columns, "seq", axis=1, tiled=True)
-    middle = x + (order(lambda rows: contract(rows, full_out), mixed_rows) + out_bias)
+
+    def pair_swap(values):
+        return lax.ppermute(values, "fsdp", [(i, i ^ 1) for i in range(shards)])
+
+    parity = lax.axis_index("fsdp") & 1
+    out_rows = model_width // (groups * shards)
+    halves = mixed_slots.reshape(rows_here, -1, 2, out_rows)
+    mine, theirs = (
+        lax.dynamic_index_in_dim(halves, index, axis=2, keepdims=False).reshape(rows_here, -1)
+        for index in (parity, 1 - parity)
+    )
+    mixed_half = jnp.concatenate([mine, pair_swap(theirs)], axis=0)
+    middle = order(lambda rows: x + (contract(rows, full_out) + out_bias), mixed_rows)
     second_norm, second_back = jax.vjp(layer_norm, middle, ln2_gain, ln2_shift)
-    second = whole(gather(second_norm.astype(low)))
-    upstream = whole(gather(gate(dz_low, second)))
+    second = order.gather(order(lambda values: values.astype(low), second_norm))
+    second = whole(order.pass_on(second))
     hidden = order(lambda rows: contract(rows, up_slab) + up_bias_slab, second)
 
     def bend(values):
@@ -384,70 +416,115 @@
         return made.astype(low), back(jnp.ones_like(values))[0]
 
     active, slope = order(bend, hidden)
-    order.after(upstream)
-    down_sum = order(lambda left: contract_first(left, active).astype(low), upstream)
+    upstream = whole(upstream)
+
+    def slab_sum(left, right):
+        made = order(lambda rows: contract_first(rows, right).astype(low), left)
+        width = made.shape[1]
+        made = jnp.swapaxes(made.reshape(groups, shards, -1, width), 0, 1).reshape(-1, width)
+        return lax.psum_scatter(made, "fsdp", scatter_dimension=0, tiled=True)
+
+    def slabs_of_rows(values):
+        values = values.reshape(groups, -1, values.shape[1])
+        slabs = lax.all_to_all(values, "seq", split_axis=0, concat_axis=0, tiled=True)
+        return jnp.swapaxes(slabs, 0, 1).astype(wide)
+
+    down_sum = slab_sum(upstream, active)
+
     hidden_grad = order(lambda rows: (contract_last(rows, down_slab) * slope).astype(low), upstream)
-    second_parts = by_slots(lambda rows: contract_last(rows, up_slab).astype(low), hidden_grad, order)
-    if square:
-        second_parts = near(second_parts)
-        order.after(*second_parts)
-    up_sum = order(lambda left: contract_first(left, hidden_grad).astype(low), second)
-    outcome = by_slots(lambda rows: contract(rows, down_slab).astype(low), active, order)
-    second_grad = sum_over_seq(second_parts)
-    middle_part, ln2_gain_grad, ln2_shift_grad = second_back(second_grad)
-    middle_grad = dz + middle_part
-    branch_grad = middle_grad.astype(low)
+
+    def to_second(rows):
+        return contract_last(rows, up_slab).astype(low)
+
+    second_grad = order.add_far(order.scatter(to_second, hidden_grad), to_second)
+    up_sum = slab_sum(second, hidden_grad)
+
+    def to_result(rows):
+        return contract(rows, down_slab).astype(low)
+
+    outcome = order.scatter(to_result, active)
+
+    def to_middle(own, came):
+        middle_part, gain_grad, shift_grad = second_back(summed(own, came))
+        middle_grad = dz + middle_part
+        return middle_grad.astype(low), middle_grad, gain_grad, shift_grad
+
+    branch_grad, middle_grad, ln2_gain_grad, ln2_shift_grad = order(
+        lambda own, *came: to_middle(own, came or None), second_grad[0], *(second_grad[1] or ())
+    )
+    def column_sum(values):
+        return jnp.sum(values.astype(wide), axis=0)
+
+    hidden_sum = lax.dynamic_update_slice_in_dim(
+        jnp.zeros((hidden_width,), wide), column_sum(hidden_grad), me * hidden_slab, axis=0
+    )
+    early = [column_sum(branch_grad), ln2_gain_grad, ln2_shift_grad, hidden_sum, column_sum(dz)]
+    early = jnp.concatenate(early).reshape(-1, PAIR)
     mixed_grad = order(lambda rows: contract_last(rows, full_out).astype(low), branch_grad)
-    mixed_grad = whole(
-        exchange(by_index([mixed_grad[:, j * slab : (j + 1) * slab] for j in range(groups)], me))
-    )
-    out_sum = order(lambda left: contract_first(left, branch_grad).astype(low), mixed_slots)
-    if square:
-        outcome = near([gate(outcome[0], mixed_grad)] + outcome[1:])
-    order.after(mixed_grad)
+    mixed_grad = exchange(by_index([mixed_grad[:, j * slab : (j + 1) * slab] for j in range(groups)], me))
+    branch_pair = jnp.concatenate([branch_grad, pair_swap(branch_grad)], axis=0)
+
+    def to_out(columns):
+        return contract_first(columns, branch_pair).astype(low)
+
+    out_begun = order.scatter(to_out, mixed_half, axis=1)
+    mixed_grad = jnp.concatenate(mixed_grad, axis=0)
+    order.after(down_sum)
     attention = (mask, slopes, qkv, log_totals, attended)
+    out_begun = order.add_far(out_begun, to_out)
     begun = order(lambda rows: attend_backward(*attention, rows, seq_count, local_len, 0, pairs // 2), mixed_grad)
-    if square:
-        order.after(*outcome)
+    early = Total(gate(early, begun))
+    out_sum = order(
+        lambda own, *came: summed(own, came or None).astype(low), out_begun[0], *(out_begun[1] or ())
+    ).reshape(-1, 1, out_rows, model_width)
+    zero = jnp.zeros_like(out_sum)
+    out_sum = jnp.concatenate(
+        [jnp.where(parity == 0, out_sum, zero), jnp.where(parity == 1, out_sum, zero)], axis=1
+    ).reshape(-1, model_width)
+    grad_w_out = lax.psum_scatter(out_sum, "fsdp", scatter_dimension=0, tiled=True).astype(wide)
+    outcome = order.add_far(outcome, to_result)
+    early.step(order)
     qkv_grad = order(
         lambda rows: attend_backward(*attention, rows, seq_count, local_len, pairs // 2, pairs, begun), mixed_grad
     )
-    normed_parts = by_slots(lambda rows: contract_last(rows, qkv_slab).astype(low), qkv_grad, order)
-    outcome = sum_over_seq(outcome)
-    if square:
-        normed_parts = near(normed_parts)
-        order.after(*normed_parts)
-    qkv_sum = order(lambda left: contract_first(left, qkv_grad).astype(low), normed)
-    normed_grad = sum_over_seq(normed_parts)
-    result = (middle + (outcome + down_bias)).astype(low).reshape(tokens.shape)
-    input_part, ln1_gain_grad, ln1_shift_grad = first_back(normed_grad)
-    grad_tokens = (middle_grad + input_part).astype(low).reshape(tokens.shape)
-
-    grad_w_down = scatter_slab(down_sum, me).reshape(-1, hidden_width).T
-    grad_w_up = scatter_slab(up_sum, me).reshape(-1, hidden_width)
-    if square:
-        out_slots = [out_sum[j * slab : (j + 1) * slab] for j in (3, 1, 2, 0)]
-        out_sum = close(*near([gate(out_slots[0], normed_grad)] + out_slots[1:])).astype(low)
-    else:
-        out_sum = lax.psum_scatter(out_sum, "seq", scatter_dimension=0, tiled=True)
-    grad_w_out = lax.psum_scatter(out_sum, "fsdp", scatter_dimension=0, tiled=True).astype(wide)
-    grad_w_qkv = scatter_slab(qkv_sum, me).reshape(-1, groups, pairs, 3, PAIR)
+
+    def to_normed(rows):
+        return contract_last(rows, qkv_slab).astype(low)
+
+    early.step(order)
+    normed_grad = order.scatter(to_normed, qkv_grad)
+    early.step(order)
+    normed_grad = order.add_far(normed_grad, to_normed)
+    early.step(order)
+    order.after(up_sum)
+    qkv_sum = slab_sum(normed, qkv_grad)
+    early.step(order)
+    result = order(
+        lambda own, *came: (middle + (summed(own, came or None) + down_bias)).astype(low),
+        outcome[0],
+        *(outcome[1] or ()),
+    ).reshape(tokens.shape)
+
+    def to_input(own, came):
+        input_part, gain_grad, shift_grad = first_back(summed(own, came))
+        return (middle_grad + input_part).astype(low), gain_grad, shift_grad
+
+    grad_tokens, ln1_gain_grad, ln1_shift_grad = order(
+        lambda own, *came: to_input(own, came or None), normed_grad[0], *(normed_grad[1] or ())
+    )
+    grad_tokens = grad_tokens.reshape(tokens.shape)
+    grad_w_down = slabs_of_rows(down_sum).reshape(-1, hidden_width).T
+    grad_w_up = slabs_of_rows(up_sum).reshape(-1, hidden_width)
+    grad_w_qkv = slabs_of_rows(qkv_sum).reshape(-1, groups, pairs, 3, PAIR)
     grad_w_qkv = jnp.transpose(grad_w_qkv, (0, 3, 1, 2, 4)).reshape(-1, 3 * model_width)
 
-    def column_sum(values):
-        return jnp.sum(values.astype(wide), axis=0)
-
-    hidden_sum = lax.dynamic_update_slice_in_dim(
-        jnp.zeros((hidden_width,), wide), column_sum(hidden_grad), me * hidden_slab, axis=0
-    )
     head_sum = jnp.transpose(column_sum(qkv_grad).reshape(pairs, 3, PAIR), (1, 0, 2)).reshape(3, slab)
     qv_sum = lax.dynamic_update_slice_in_dim(
         jnp.zeros((2, model_width), wide), head_sum[0::2], me * slab, axis=1
     )
-    early = [column_sum(branch_grad), ln2_gain_grad, ln2_shift_grad, hidden_sum, column_sum(dz)]
-    early = total(jnp.concatenate(early).reshape(-1, PAIR)).reshape(-1)
     late = [qv_sum.reshape(-1), ln1_gain_grad, ln1_shift_grad]
-    late = total(jnp.concatenate(late).reshape(-1, PAIR)).reshape(-1)
+    late = Total(jnp.concatenate(late).reshape(-1, PAIR)).done()
+    early = early.done()
 
     def cut(values, at, count):
         return values[at * model_width : (at + count) * model_width]

time: 1170 us -> 947 us (0.81)
  waiting for transfers between devices: 535 us -> 312 us
    ppermute x47 -> x34, waiting for transfers between devices: 378 us -> 206 us  [swap(): return lax.ppermute(values, 'seq', [(i, i ^ bit) for i in range(4)])]
    all_gather x1, waiting for transfers between devices: 67.2 us -> 0.01 us  [local(): qkv_slab = lax.all_gather(head_columns(w_qkv), 'fsdp', axis=0, tiled=True)]
    reduce_scatter x3, waiting for transfers between devices: 65.6 us -> 0.02 us  [slab_sum(): return lax.psum_scatter(made, 'fsdp', scatter_dimension=0, tiled=True)]
    all_to_all x0 -> x3, waiting for transfers between devices: none -> 56.8 us  [slabs_of_rows(): lax.all_to_all(values, 'seq', split_axis=0, concat_axis=0, tiled=True)]
    ppermute x10 -> x12, waiting for transfers between devices: 24.7 us -> 48.9 us  [the longest x10 48.9 us: send(): self.came = lax.ppermute(self.values, axis, other)]
    ppermute x47 -> x34, starting transfers between devices: 53.1 us -> 39.8 us  [swap(): return lax.ppermute(values, 'seq', [(i, i ^ bit) for i in range(4)])]
    unnamed x185 -> x157, local copies, waits for them, and re-layouts: 41.4 us -> 33.3 us
    dot_general x4 -> x7, matrix products: 64.6 us -> 70.2 us  [contract_first(): lax.dot_general(left_side, right_side, (((0,), (0,)), ((), ())), preferre...]
  transfers between devices with their start and end apart: 65 -> 57, of which waited for: 37 -> 22; matrix products, arithmetic and copies ran while one was open for 33% -> 45% of each run, Pallas kernels for 7% -> 9%
where the time goes in v3:
time: 947 us; the launch traced here: 942 us
  waiting for transfers between devices  312 us (33%)
  matrix products  238 us (25%)
  local copies, waits for them, and re-layouts  120 us (13%)
  other arithmetic  111 us (12%)
  Pallas kernels  84.5 us (9%)
  starting transfers between devices  59.7 us (6%)
  between operations  16 us (2%)
    ppermute x34, waiting for transfers between devices, swap(): return lax.ppermute(values, 'seq', [(i, i ^ bit) for i in range(4)])  206 us
    dot_general x10, matrix products, contract_last(): lax.dot_general(left_side, right_side, (((1,), (1,)), ((), ())), preferre...  90 us
    dot_general x7, matrix products, contract(): lax.dot_general(left_side, right_side, (((1,), (0,)), ((), ())), preferre...  77.9 us
    dot_general x7, matrix products, contract_first(): lax.dot_general(left_side, right_side, (((0,), (0,)), ((), ())), preferre...  70.2 us
    all_to_all x3, waiting for transfers between devices, slabs_of_rows(): lax.all_to_all(values, 'seq', split_axis=0, concat_axis=0, tiled=True)  56.8 us
    pallas_call x2, Pallas kernels, attend_backward(): pl.pallas_call(partial(attend_backward_kernel, blocks=blocks, seqs=seqs,...  55.9 us
    ppermute x10, waiting for transfers between devices, send(): self.came = lax.ppermute(self.values, axis, other)  48.9 us
    ppermute x34, starting transfers between devices, swap(): return lax.ppermute(values, 'seq', [(i, i ^ bit) for i in range(4)])  39.8 us
  transfers between devices with their start and end apart: 57, of which 22 were waited for; matrix products, arithmetic and copies ran while one was open for 45% of the time, Pallas kernels for 9%

profile of v3, /device:TPU:0, one launch (start us, length us, event | category | flops | bytes accessed | tf_op | source)
XLA Modules:
  0.0 941.6 jit_solution(6760638905551435158)
XLA Ops:
  25.9 44.1 %collective-permute-done = bf16[512,2048]{1,0:T(8,128)(2,1)S(1)} collective-permute-done((bf16[512,2048]{1,0:T(8,128)(2,1)S(1)}, bf16[512,2048]{1,0:T(8,128)(2,1)S(1)}, u32[]{:S(2)}, u32[]{:S(2)}) %collective-permute-start) | collective-permute-done | bytes 2097184 | tf_op jit(solution)/shard_map/ppermute | solution.py:212
  84.4 16.1 %collective-permute-done.2 = bf16[256,2048]{1,0:T(8,128)(2,1)S(1)} collective-permute-done((bf16[256,2048]{1,0:T(8,128)(2,1)}, bf16[256,2048]{1,0:T(8,128)(2,1)S(1)}, u32[]{:S(2)}, u32[]{:S(2)}) %collective-permute-start.2) | collective-permute-done | bytes 1048608 | tf_op jit(solution)/shard_map/ppermute | solution.py:212
  107.2 17.4 %add_convert_fusion.qkv_ref = bf16[2048,1536]{1,0:T(8,128)(2,1)S(1)} fusion(bf16[2048,2048]{1,0:T(8,128)(2,1)} %constant_dynamic-update-slice_fusion, bf16[2048,1536]{0,1:T(8,128)(2,1)} %all-gather.5.cloned.1.call-done, f32[1536]{0:T(1024)S(1)} %add.211), kind=kOutput, calls=%fused_computation.19 | convolution fusion | flops 12891193344 | bytes 20977664 | tf_op jit(solution)/shard_map/dot_general | solution.py:28
  124.6 28.6 %attend_forward.1 = (bf16[2048,512]{1,0:T(8,128)(2,1)S(1)}, f32[2048,512]{1,0:T(8,128)S(1)}) custom-call(s32[1]{0:T(128)} %bitcast.1.mask_ref, f32[8]{0:T(128)S(1)} %multiply_power_fusion.slope_ref, bf16[2048,1536]{1,0:T(8,128)(2,1)S(1)} %add_convert_fusion.qkv_ref), custom_call_target="tpu_custom_call" | custom-call | flops 10737418240 | bytes 12582912 | tf_op jit(solution)/shard_map/attend_forward/pallas_call | solution.py:163
  162.3 10.2 %collective-permute-done.4 = bf16[512,512]{1,0:T(8,128)(2,1)S(1)} collective-permute-done((bf16[512,512]{1,0:T(8,128)(2,1)}, bf16[512,512]{1,0:T(8,128)(2,1)S(1)}, u32[]{:S(2)}, u32[]{:S(2)}) %collective-permute-start.4) | collective-permute-done | bytes 524320 | tf_op jit(solution)/shard_map/ppermute | solution.py:212
  223.4 43.9 %collective-permute-done.13 = bf16[256,2048]{1,0:T(8,128)(2,1)} collective-permute-done((bf16[256,2048]{1,0:T(8,128)(2,1)S(1)}, bf16[256,2048]{1,0:T(8,128)(2,1)}, u32[]{:S(2)}, u32[]{:S(2)}) %collective-permute-start.13) | collective-permute-done | bytes 1048608 | tf_op jit(solution)/shard_map/ppermute | solution.py:212
  301.8 21.6 %convolution_add_fusion = f32[2048,2048]{1,0:T(8,128)S(1)} fusion(bf16[2048,2048]{1,0:T(8,128)(2,1)} %constant_dynamic-update-slice_fusion.5, bf16[2048,2048]{1,0:T(8,128)(2,1)} %all-gather.9.cloned.1.call-done, f32[2048]{0:T(1024)S(1)} %dynamic-slice-done), kind=kOutput, calls=%fused_computation.20 | convolution fusion | flops 17184063488 | bytes 33562624 | tf_op jit(solution)/shard_map/dot_general | solution.py:28
  323.3 36.9 %multiply_convert_fusion.1 = (bf16[2048,2048]{1,0:T(8,128)(2,1)S(1)}, f32[2048,2048]{1,0:T(8,128)}) fusion(f32[2048,2048]{1,0:T(8,128)S(1)} %convolution_add_fusion), kind=kLoop, calls=%fused_computation.4 | loop fusion | flops 272629760 | bytes 41943040 | tf_op jit(solution)/shard_map/convert_element_type | solution.py:416
  360.3 24.0 %convolution_convert_fusion.1 = bf16[2048,2048]{1,0:T(8,128)(2,1)} fusion(bf16[2048,2048]{1,0:T(8,128)(2,1)} %constant_dynamic-update-slice_fusion.10, bf16[2048,2048]{1,0:T(8,128)(2,1)S(1)} %get-tuple-element.182), kind=kOutput, calls=%fused_computation.22 | convolution fusion | flops 17184063488 | bytes 25165824 | tf_op jit(solution)/shard_map/dot_general | solution.py:40
  392.7 31.7 %convert_reduce_fusion = (f32[2048]{0:T(1024)S(1)}, bf16[2048,2048]{1,0:T(8,128)(2,1)S(1)}) fusion(f32[2048,2048]{1,0:T(8,128)} %get-tuple-element.183, f32[2048,2048]{1,0:T(8,128)} %copy-done.11, bf16[2048,2048]{1,0:T(8,128)(2,1)} %constant_dynamic-update-slice_fusion.10, bf16[2048,2048]{1,0:T(8,128)(2,1)} %all-gather.11.cloned.1.call-done), kind=kOutput, calls=%fused_computation.2 | convolution fusion | flops 17238587392 | bytes 58728448 | tf_op jit(solution)/shard_map/dot_general | solution.py:34
  436.6 10.2 %convolution_convert_fusion.14 = bf16[512,2048]{1,0:T(8,128)(2,1)} fusion(bf16[512,2048]{1,0:T(8,128)(2,1)} %get-tuple-element.108, bf16[2048,2048]{1,0:T(8,128)(2,1)} %all-gather.9.cloned.1.call-done), kind=kOutput, calls=%fused_computation.64 | convolution fusion | flops 4296015872 | bytes 12582912 | tf_op jit(solution)/shard_map/dot_general | solution.py:34
  478.8 9.4 convolution_convert_fusion.12
  488.2 21.6 %convolution_convert_fusion = bf16[2048,2048]{1,0:T(8,128)(2,1)} fusion(bf16[2048,2048]{1,0:T(8,128)(2,1)} %constant_dynamic-update-slice_fusion.5, bf16[2048,2048]{1,0:T(8,128)(2,1)S(1)} %get-tuple-element.237), kind=kOutput, calls=%fused_computation.21 | convolution fusion | flops 17184063488 | bytes 25165824 | tf_op jit(solution)/shard_map/dot_general | solution.py:40
  530.8 10.0 %convolution_convert_fusion.9 = bf16[512,2048]{1,0:T(8,128)(2,1)} fusion(bf16[512,2048]{1,0:T(8,128)(2,1)} %get-tuple-element.116, bf16[2048,2048]{1,0:T(8,128)(2,1)} %all-gather.11.cloned.1.call-done), kind=kOutput, calls=%fused_computation.59 | convolution fusion | flops 4296015872 | bytes 12582912 | tf_op jit(solution)/shard_map/dot_general | solution.py:28
  562.0 11.2 %collective-permute-done.27 = bf16[512,512]{1,0:T(8,128)(2,1)S(1)} collective-permute-done((bf16[512,512]{1,0:T(8,128)(2,1)S(1)}, bf16[512,512]{1,0:T(8,128)(2,1)S(1)}, u32[]{:S(2)}, u32[]{:S(2)}) %collective-permute-start.27) | collective-permute-done | bytes 524320 | tf_op jit(solution)/shard_map/ppermute | solution.py:212
  574.6 11.0 %collective-permute-done.28 = bf16[512,512]{1,0:T(8,128)(2,1)S(1)} collective-permute-done((bf16[512,512]{1,0:T(8,128)(2,1)S(1)}, bf16[512,512]{1,0:T(8,128)(2,1)S(1)}, u32[]{:S(2)}, u32[]{:S(2)}) %collective-permute-start.28) | collective-permute-done | bytes 524320 | tf_op jit(solution)/shard_map/ppermute | solution.py:212
  601.5 17.6 %collective-permute-done.24 = bf16[128,2048]{1,0:T(8,128)(2,1)} collective-permute-done((bf16[128,2048]{1,0:T(8,128)(2,1)S(1)}, bf16[128,2048]{1,0:T(8,128)(2,1)}, u32[]{:S(2)}, u32[]{:S(2)}) %collective-permute-start.24) | collective-permute-done | bytes 524320 | tf_op jit(solution)/shard_map/ppermute | solution.py:212
  627.0 27.9 %attend_backward.2.rest_0_ = bf16[2048,1536]{1,0:T(8,128)(2,1)} custom-call(s32[1]{0:T(128)} %bitcast.1.mask_ref, f32[8]{0:T(128)S(1)} %multiply_power_fusion.slope_ref, bf16[2048,1536]{1,0:T(8,128)(2,1)} %copy-done.1, f32[2048,512]{1,0:T(8,128)S(1)} %copy-done.3, bf16[2048,512]{1,0:T(8,128)(2,1)S(1)} %get-tuple-element.95.mixed_ref, ...), custom_call_target="tpu_custom_call" | custom-call | flops 13421772800 | bytes 10485760 | tf_op jit(solution)/shard_map/attend_backward/pallas_call | solution.py:190
  670.9 28.0 %attend_backward.3 = bf16[2048,1536]{1,0:T(8,128)(2,1)} custom-call(s32[1]{0:T(128)} %bitcast.1.mask_ref, f32[8]{0:T(128)S(1)} %multiply_power_fusion.slope_ref, bf16[2048,1536]{1,0:T(8,128)(2,1)} %copy-done.1, f32[2048,512]{1,0:T(8,128)S(1)} %copy-done.3, bf16[2048,512]{1,0:T(8,128)(2,1)S(1)} %get-tuple-element.95.mixed_ref, ...), custom_call_target="tpu_custom_call", output_to_operand_aliasing={{}: (6, {})} | custom-call | flops 13421772800 | bytes 10485760 | tf_op jit(solution)/shard_map/attend_backward/pallas_call | solution.py:190
  720.7 14.3 %collective-permute-done.36 = bf16[256,2048]{1,0:T(8,128)(2,1)S(1)} collective-permute-done((bf16[256,2048]{1,0:T(8,128)(2,1)S(1)}, bf16[256,2048]{1,0:T(8,128)(2,1)S(1)}, u32[]{:S(2)}, u32[]{:S(2)}) %collective-permute-start.36) | collective-permute-done | bytes 1048608 | tf_op jit(solution)/shard_map/ppermute | solution.py:212
  740.9 17.6 %convolution_convert_fusion.2 = bf16[2048,1536]{1,0:T(8,128)(2,1)S(1)} fusion(bf16[2048,2048]{1,0:T(8,128)(2,1)} %constant_dynamic-update-slice_fusion, bf16[2048,1536]{1,0:T(8,128)(2,1)} %attend_backward.3), kind=kOutput, calls=%fused_computation.23 | convolution fusion | flops 12888047616 | bytes 20971520 | tf_op jit(solution)/shard_map/dot_general | solution.py:40
  765.3 12.6 %all-to-all-done.2 = bf16[4,64,2048]{2,1,0:T(8,128)(2,1)S(1)} async-done(((bf16[4,64,2048]{2,1,0:T(8,128)(2,1)}), bf16[4,64,2048]{2,1,0:T(8,128)(2,1)S(1)}, u32[]{:S(2)}, u32[]{:S(2)}) %all-to-all-start.2) | async-done | bytes 1048608 | tf_op jit(solution)/shard_map/all_to_all | solution.py:429
  798.9 44.2 %all-to-all-done.1 = bf16[4,64,2048]{2,1,0:T(8,128)(2,1)S(1)} async-done(((bf16[4,64,2048]{2,1,0:T(8,128)(2,1)}), bf16[4,64,2048]{2,1,0:T(8,128)(2,1)S(1)}, u32[]{:S(2)}, u32[]{:S(2)}) %all-to-all-start.1) | async-done | bytes 1048608 | tf_op jit(solution)/shard_map/all_to_all | solution.py:429
  844.9 42.1 %collective-permute-done.38 = f32[128,128]{1,0:T(8,128)S(1)} collective-permute-done((f32[128,128]{1,0:T(8,128)S(1)}, f32[128,128]{1,0:T(8,128)S(1)}, u32[]{:S(2)}, u32[]{:S(2)}) %collective-permute-start.38) | collective-permute-done | bytes 65568 | tf_op jit(solution)/shard_map/ppermute | solution.py:310
  (415 shorter events, 373.4 us)
Async XLA Ops:
  7.2 100.1 %all-gather.5.cloned.1.call-start = ((), (), s32[]{:S(2)}) async-start(), calls=%async_computation.7 | async-start | bytes 7077888 | tf_op jit(solution)/shard_map/all_gather | solution.py:378
  17.5 166.6 %all-gather.7.cloned.1.call-start = ((), (), s32[]{:S(2)}) async-start(), calls=%async_computation.8 | async-start | bytes 9437184 | tf_op jit(solution)/shard_map/all_gather | solution.py:385
  71.6 230.1 %all-gather.9.cloned.1.call-start = ((), (), s32[]{:S(2)}) async-start(), calls=%async_computation.9 | async-start | bytes 9437184 | tf_op jit(solution)/shard_map/all_gather | solution.py:386
  74.0 318.6 %all-gather.11.cloned.1.call-start = ((), (), s32[]{:S(2)}) async-start(), calls=%async_computation.10 | async-start | bytes 9437184 | tf_op jit(solution)/shard_map/all_gather | solution.py:387
  104.4 55.6 %collective-permute-start.7 = (bf16[512,2048]{1,0:T(8,128)(2,1)}, bf16[512,2048]{1,0:T(8,128)(2,1)}, u32[]{:S(2)}, u32[]{:S(2)}) collective-permute-start(bf16[512,2048]{1,0:T(8,128)(2,1)} %bitcast.10), channel_id=1, source_target_pairs={{0,8},{8,0},{16,24},{24,16},{1,9},{9,1},{17,25},{25,17},{2,10},{10... | collective-permute-start | bytes 6291464 | tf_op jit(solution)/shard_map/ppermute | solution.py:212
  196.4 73.2 %collective-permute-start.10 = (bf16[512,2048]{1,0:T(8,128)(2,1)}, bf16[512,2048]{1,0:T(8,128)(2,1)}, u32[]{:S(2)}, u32[]{:S(2)}) collective-permute-start(bf16[512,2048]{1,0:T(8,128)(2,1)} %multiply_add_fusion), channel_id=1, source_target_pairs={{0,16},{8,24},{16,0},{24,8},{1,17},{9,25},{17,1},{25,9},{2,18},{10... | collective-permute-start | bytes 6291464 | tf_op jit(solution)/shard_map/ppermute | solution.py:212
  197.4 72.3 %collective-permute-start.9 = (bf16[512,2048]{1,0:T(8,128)(2,1)}, bf16[512,2048]{1,0:T(8,128)(2,1)}, u32[]{:S(2)}, u32[]{:S(2)}) collective-permute-start(bf16[512,2048]{1,0:T(8,128)(2,1)} %multiply_add_fusion), channel_id=1, source_target_pairs={{0,8},{8,0},{16,24},{24,16},{1,9},{9,1},{17,25},{25,17},{2,10},{10... | collective-permute-start | bytes 6291464 | tf_op jit(solution)/shard_map/ppermute | solution.py:212
  200.5 418.5 %reduce-scatter.5.cloned.1.call-start = ((), (), s32[]{:S(2)}) async-start(), calls=%async_computation.11 | async-start | bytes 9437184 | tf_op jit(solution)/shard_map/reduce_scatter | solution.py:425
  200.6 66.8 %collective-permute-start.13 = (bf16[256,2048]{1,0:T(8,128)(2,1)S(1)}, bf16[256,2048]{1,0:T(8,128)(2,1)}, u32[]{:S(2)}, u32[]{:S(2)}) collective-permute-start(bf16[256,2048]{1,0:T(8,128)(2,1)S(1)} %copy-done.28), channel_id=1, source_target_pairs={{0,8},{8,0},{16,24},{24,16},{1,9},{9,1},{17,25},{25,17},{2,10},{10... | collective-permute-start | bytes 3145736 | tf_op jit(solution)/shard_map/ppermute | solution.py:212
  206.7 65.3 %collective-permute-start.14 = (bf16[256,2048]{1,0:T(8,128)(2,1)}, bf16[256,2048]{1,0:T(8,128)(2,1)}, u32[]{:S(2)}, u32[]{:S(2)}) collective-permute-start(bf16[256,2048]{1,0:T(8,128)(2,1)} %slice.231), channel_id=1, source_target_pairs={{0,16},{8,24},{16,0},{24,8},{1,17},{9,25},{17,1},{25,9},{2,18},{10... | collective-permute-start | bytes 3145736 | tf_op jit(solution)/shard_map/ppermute | solution.py:212
  217.0 57.2 %collective-permute-start.19 = (bf16[512,1024]{0,1:T(8,128)(2,1)S(1)}, bf16[512,1024]{0,1:T(8,128)(2,1)S(1)}, u32[]{:S(2)}, u32[]{:S(2)}) collective-permute-start(bf16[512,1024]{0,1:T(8,128)(2,1)S(1)} %bitcast.176), channel_id=1, source_target_pairs={{0,1},{1,0},{2,3},{3,2},{4,5},{5,4},{6,7},{7,6},{8,9},{9,8},{10,11... | collective-permute-start | bytes 3145736 | tf_op jit(solution)/shard_map/ppermute | solution.py:398
  392.6 348.3 %reduce-scatter.7.cloned.1.call-start = ((), (), s32[]{:S(2)}) async-start(), calls=%async_computation.12 | async-start | bytes 9437184 | tf_op jit(solution)/shard_map/reduce_scatter | solution.py:425
  474.6 66.2 %collective-permute-start.21 = (bf16[512,2048]{1,0:T(8,128)(2,1)}, bf16[512,2048]{1,0:T(8,128)(2,1)}, u32[]{:S(2)}, u32[]{:S(2)}) collective-permute-start(bf16[512,2048]{1,0:T(8,128)(2,1)} %pad_maximum_fusion.4), channel_id=1, source_target_pairs={{0,16},{8,24},{16,0},{24,8},{1,17},{9,25},{17,1},{25,9},{2,18},{10... | collective-permute-start | bytes 6291464 | tf_op jit(solution)/shard_map/ppermute | solution.py:212
  477.3 63.5 %collective-permute-start.20 = (bf16[512,2048]{1,0:T(8,128)(2,1)}, bf16[512,2048]{1,0:T(8,128)(2,1)}, u32[]{:S(2)}, u32[]{:S(2)}) collective-permute-start(bf16[512,2048]{1,0:T(8,128)(2,1)} %pad_maximum_fusion.2), channel_id=1, source_target_pairs={{0,8},{8,0},{16,24},{24,16},{1,9},{9,1},{17,25},{25,17},{2,10},{10... | collective-permute-start | bytes 6291464 | tf_op jit(solution)/shard_map/ppermute | solution.py:212
  521.7 135.2 %collective-permute-start.17 = (bf16[256,2048]{1,0:T(8,128)(2,1)}, bf16[256,2048]{1,0:T(8,128)(2,1)S(1)}, u32[]{:S(2)}, u32[]{:S(2)}) collective-permute-start(bf16[256,2048]{1,0:T(8,128)(2,1)} %get-tuple-element.214), channel_id=1, source_target_pairs={{0,8},{8,0},{16,24},{24,16},{1,9},{9,1},{17,25},{25,17},{2,10},{10... | collective-permute-start | bytes 3145736 | tf_op jit(solution)/shard_map/ppermute | solution.py:212
  530.7 381.8 %reduce-scatter.9.cloned.1.call-start = ((), (), s32[]{:S(2)}) async-start(), calls=%async_computation.13 | async-start | bytes 7077888 | tf_op jit(solution)/shard_map/reduce_scatter | solution.py:425
  573.2 83.7 %collective-permute-start.18 = (bf16[256,2048]{1,0:T(8,128)(2,1)}, bf16[256,2048]{1,0:T(8,128)(2,1)}, u32[]{:S(2)}, u32[]{:S(2)}) collective-permute-start(bf16[256,2048]{1,0:T(8,128)(2,1)} %get-tuple-element.213), channel_id=1, source_target_pairs={{0,16},{8,24},{16,0},{24,8},{1,17},{9,25},{17,1},{25,9},{2,18},{10... | collective-permute-start | bytes 3145736 | tf_op jit(solution)/shard_map/ppermute | solution.py:212
  779.7 108.0 %collective-permute-start.30 = (bf16[512,2048]{1,0:T(8,128)(2,1)}, bf16[512,2048]{1,0:T(8,128)(2,1)}, u32[]{:S(2)}, u32[]{:S(2)}) collective-permute-start(bf16[512,2048]{1,0:T(8,128)(2,1)} %pad_maximum_fusion.6), channel_id=1, source_target_pairs={{0,8},{8,0},{16,24},{24,16},{1,9},{9,1},{17,25},{25,17},{2,10},{10... | collective-permute-start | bytes 6291464 | tf_op jit(solution)/shard_map/ppermute | solution.py:212
  783.1 104.6 %collective-permute-start.31 = (bf16[512,2048]{1,0:T(8,128)(2,1)}, bf16[512,2048]{1,0:T(8,128)(2,1)}, u32[]{:S(2)}, u32[]{:S(2)}) collective-permute-start(bf16[512,2048]{1,0:T(8,128)(2,1)} %pad_maximum_fusion.7), channel_id=1, source_target_pairs={{0,16},{8,24},{16,0},{24,8},{1,17},{9,25},{17,1},{25,9},{2,18},{10... | collective-permute-start | bytes 6291464 | tf_op jit(solution)/shard_map/ppermute | solution.py:212
  784.0 59.0 %all-to-all-start.1 = ((bf16[4,64,2048]{2,1,0:T(8,128)(2,1)}), bf16[4,64,2048]{2,1,0:T(8,128)(2,1)S(1)}, u32[]{:S(2)}, u32[]{:S(2)}) async-start(bf16[4,64,2048]{2,1,0:T(8,128)(2,1)} %bitcast.178), calls=%async_computation.5 | async-start | bytes 2097152 | tf_op jit(solution)/shard_map/all_to_all | solution.py:429
  787.6 136.3 %reduce-scatter.11.cloned.1.call-start = ((), (), s32[]{:S(2)}) async-start(), calls=%async_computation.14 | async-start | bytes 2359296 | tf_op jit(solution)/shard_map/reduce_scatter | solution.py:484
  787.7 105.3 %collective-permute-start.39 = (bf16[512,2048]{1,0:T(8,128)(2,1)}, bf16[512,2048]{1,0:T(8,128)(2,1)}, u32[]{:S(2)}, u32[]{:S(2)}) collective-permute-start(bf16[512,2048]{1,0:T(8,128)(2,1)} %pad_maximum_fusion.8), channel_id=1, source_target_pairs={{0,8},{8,0},{16,24},{24,16},{1,9},{9,1},{17,25},{25,17},{2,10},{10... | collective-permute-start | bytes 6291464 | tf_op jit(solution)/shard_map/ppermute | solution.py:212
  793.3 99.7 %collective-permute-start.40 = (bf16[512,2048]{1,0:T(8,128)(2,1)}, bf16[512,2048]{1,0:T(8,128)(2,1)}, u32[]{:S(2)}, u32[]{:S(2)}) collective-permute-start(bf16[512,2048]{1,0:T(8,128)(2,1)} %pad_maximum_fusion.9), channel_id=1, source_target_pairs={{0,16},{8,24},{16,0},{24,8},{1,17},{9,25},{17,1},{25,9},{2,18},{10... | collective-permute-start | bytes 6291464 | tf_op jit(solution)/shard_map/ppermute | solution.py:212
  798.2 88.8 %collective-permute-start.38 = (f32[128,128]{1,0:T(8,128)S(1)}, f32[128,128]{1,0:T(8,128)S(1)}, u32[]{:S(2)}, u32[]{:S(2)}) collective-permute-start(f32[128,128]{1,0:T(8,128)S(1)} %add.240), channel_id=1, source_target_pairs={{0,16},{8,24},{16,0},{24,8},{1,17},{9,25},{17,1},{25,9},{2,18},{10... | collective-permute-start | bytes 196616 | tf_op jit(solution)/shard_map/ppermute | solution.py:310
  (107 other events, 1656.3 us)
Sparse Core Ops, SparseCore 0:
  17.6 67.8 all-gather.4
  87.1 80.2 all-gather.6
  169.6 80.5 all-gather.8
  252.2 81.0 all-gather.10
  392.7 89.6 reduce-scatter.4
  530.8 89.8 reduce-scatter.6
  761.9 67.4 reduce-scatter.8
  831.6 33.9 reduce-scatter.10

commit v4 on v3

--- a/solution.py
+++ b/solution.py
@@ -1,3 +1,4 @@
+import math
 from functools import partial
 
 import jax
@@ -18,10 +19,6 @@
     centred = token_rows - average
     spread = jnp.mean(centred * centred, axis=-1, keepdims=True)
     return centred * lax.rsqrt(spread + 1e-05) * gain_vec + shift_vec
-
-
-def exact_gelu(values):
-    return jax.nn.gelu(values, approximate=False)
 
 
 def contract(left_side, right_side):
@@ -208,6 +205,86 @@
     )(mask, slopes, qkv, lse, mixed, grad, *earlier)
 
 
+def up_kernel(rows_ref, weight_ref, bias_ref, active_ref, slope_ref, *, chunk):
+    rows = rows_ref[...]
+    for at in range(0, weight_ref.shape[1], chunk):
+        columns = slice(at, at + chunk)
+        hidden = contract(rows, weight_ref[:, columns]) + bias_ref[:, columns]
+        below = 0.5 + 0.5 * lax.erf(hidden * 2**-0.5)
+        active_ref[:, columns] = (hidden * below).astype(active_ref.dtype)
+        slope_ref[:, columns] = below + hidden * ((2 * math.pi) ** -0.5 * jnp.exp(-0.5 * hidden * hidden))
+
+
+def hidden_grad_kernel(rows_ref, weight_ref, slope_ref, grad_ref, sum_ref, *, chunk):
+    rows = rows_ref[...]
+    starting = pl.program_id(0) == 0
+    for at in range(0, weight_ref.shape[0], chunk):
+        columns = slice(at, at + chunk)
+        grad = contract_last(rows, weight_ref[columns, :]) * slope_ref[:, columns]
+        grad = grad.astype(grad_ref.dtype)
+        grad_ref[:, columns] = grad
+        part = jnp.sum(grad.astype(jnp.float32), axis=0, keepdims=True)
+        sum_ref[:, columns] = jnp.where(starting, part, sum_ref[:, columns] + part)
+
+
+TILE = 512
+
+
+def up_and_bend(rows, weight, bias):
+    count, depth = rows.shape
+    width = weight.shape[1]
+    tile = pl.BlockSpec((TILE, width), lambda i: (i, 0))
+    return pl.pallas_call(
+        partial(up_kernel, chunk=TILE),
+        grid=(count // TILE,),
+        in_specs=[
+            pl.BlockSpec((TILE, depth), lambda i: (i, 0)),
+            pl.BlockSpec((depth, width), lambda i: (0, 0)),
+            pl.BlockSpec((1, width), lambda i: (0, 0)),
+        ],
+        out_specs=[tile, tile],
+        out_shape=[
+            jax.ShapeDtypeStruct((count, width), jnp.bfloat16),
+            jax.ShapeDtypeStruct((count, width), jnp.float32),
+        ],
+        compiler_params=pltpu.CompilerParams(vmem_limit_bytes=48 * 2**20),
+        cost_estimate=pl.CostEstimate(
+            flops=count * depth * width * 4,
+            bytes_accessed=2 * count * depth + 2 * depth * width + 6 * count * width,
+            transcendentals=2 * count * width,
+        ),
+        name="up_and_bend",
+    )(rows, weight, bias)
+
+
+def hidden_gradient(rows, weight, slope):
+    count, depth = rows.shape
+    width = weight.shape[0]
+    tile = pl.BlockSpec((TILE, width), lambda i: (i, 0))
+    line = pl.BlockSpec((1, width), lambda i: (0, 0))
+    return pl.pallas_call(
+        partial(hidden_grad_kernel, chunk=TILE),
+        grid=(count // TILE,),
+        in_specs=[
+            pl.BlockSpec((TILE, depth), lambda i: (i, 0)),
+            pl.BlockSpec((width, depth), lambda i: (0, 0)),
+            tile,
+        ],
+        out_specs=[tile, line],
+        out_shape=[
+            jax.ShapeDtypeStruct((count, width), jnp.bfloat16),
+            jax.ShapeDtypeStruct((1, width), jnp.float32),
+        ],
+        compiler_params=pltpu.CompilerParams(vmem_limit_bytes=48 * 2**20),
+        cost_estimate=pl.CostEstimate(
+            flops=count * depth * width * 3,
+            bytes_accessed=2 * count * depth + 2 * depth * width + 6 * count * width,
+            transcendentals=0,
+        ),
+        name="hidden_gradient",
+    )(rows, weight, slope)
+
+
 def swap(values, bit):
     return lax.ppermute(values, "seq", [(i, i ^ bit) for i in range(4)])
 
@@ -248,50 +325,70 @@
             count = len(operands)
             operands = lax.optimization_barrier((*operands, *self.pending))[:count]
         made = operation(*operands)
-        self.pending = [jax.tree.leaves(made)[0]]
+        self.pending = jax.tree.leaves(made)
         return made
 
     def gather(self, rows):
         if lax.axis_size("seq") != 4:
-            return lax.all_gather(rows, "seq", axis=0, tiled=True), None
-        return rows, (swap(rows, 1), swap(rows, 2))
+            return lax.all_gather(jnp.concatenate(rows, axis=0), "seq", axis=0, tiled=True), None
+        top, bottom = rows
+        return rows, (swap(bottom, 1), swap(top, 2), swap(top, 1), swap(bottom, 2))
 
     def pass_on(self, begun):
         rows, came = begun
         if came is None:
             return rows
-        half = rows.shape[0] // 2
-        top, bottom = self(lambda first, second: (second[:half], first[half:]), *came)
-        return [rows, *came, swap(top, 1), swap(bottom, 2)]
+        first_bottom, second_top, first_top, second_bottom = came
+        self.after(*came)
+        far = [swap(second_top, 1), swap(first_bottom, 2)]
+        return [*rows, first_top, first_bottom, second_top, second_bottom, *far]
 
     def scatter(self, product, rows, axis=0):
         if lax.axis_size("seq") != 4:
             return lax.psum_scatter(self(product, rows), "seq", scatter_dimension=0, tiled=True), None
         count = rows.shape[axis] // 4
-        cut = [lax.slice_in_dim(rows, j * count, (j + 1) * count, axis=axis) for j in range(4)]
-        far = self(product, cut[3])
-        half = far.shape[0] // 2
-        top, bottom = swap(far[:half], 1), swap(far[half:], 2)
-        return cut, (self(product, cut[1]), self(product, cut[2]), top, bottom)
-
-    def add_far(self, begun, product):
-        cut, parts = begun
+
+        def far_half(values):
+            made = product(lax.slice_in_dim(values, 3 * count, 4 * count, axis=axis))
+            half = made.shape[0] // 2
+            return made[:half], made[half:]
+
+        top, bottom = self(far_half, rows)
+        top, bottom = swap(top, 1), swap(bottom, 2)
+        rest = self(lambda values: product(lax.slice_in_dim(values, 0, 3 * count, axis=axis)), rows)
+        return rest, (top, bottom)
+
+    def add_far(self, begun):
+        rest, parts = begun
         if parts is None:
             return begun
-        half = parts[0].shape[0] // 2
         wide = jnp.float32
 
-        def add(first, second, top, bottom):
-            first_low = (first[half:].astype(wide) + bottom.astype(wide)).astype(first.dtype)
-            second_low = (second[:half].astype(wide) + top.astype(wide)).astype(first.dtype)
+        def add(rest, top, bottom):
+            half = top.shape[0]
+            count = 2 * half
+            first, second = rest[count : 2 * count], rest[2 * count :]
+            first_low = (first[half:].astype(wide) + bottom.astype(wide)).astype(rest.dtype)
+            second_low = (second[:half].astype(wide) + top.astype(wide)).astype(rest.dtype)
             return (
                 jnp.concatenate([first[:half], first_low], axis=0),
                 jnp.concatenate([second_low, second[half:]], axis=0),
             )
 
-        first, second = self(add, *parts)
-        came = swap(first, 1), swap(second, 2)
-        return self(product, cut[0]), came
+        first, second = self(add, rest, *parts)
+        return rest, (swap(first, 1), swap(second, 2))
+
+
+def summed(rest, came):
+    wide = jnp.float32
+    if came is None:
+        return rest.astype(wide)
+    own = rest[: came[0].shape[0]]
+    return own.astype(wide) + came[0].astype(wide) + came[1].astype(wide)
+
+
+def whole(parts):
+    return jnp.concatenate(parts, axis=0) if isinstance(parts, list) else parts
 
 
 class Total:
@@ -319,15 +416,6 @@
         while self.came is not None:
             self.step()
         return self.values.reshape(-1)
-
-
-def summed(own, came):
-    wide = jnp.float32
-    return own.astype(wide) if came is None else own.astype(wide) + came[0].astype(wide) + came[1].astype(wide)
-
-
-def whole(parts):
-    return jnp.concatenate(parts, axis=0) if isinstance(parts, list) else parts
 
 
 def local(
@@ -380,13 +468,18 @@
     up_bias_slab = own_slab(up_bias, 0)
 
     first_norm, first_back = jax.vjp(layer_norm, x, ln1_gain, ln1_shift)
-    normed = order.gather(order(lambda values: values.astype(low), first_norm))
+    half = rows_here // 2
+
+    def halves_of(values):
+        return values[:half].astype(low), values[half:].astype(low)
+
+    normed = order.gather(order(halves_of, first_norm))
     normed = order.pass_on(normed)
-    full_out = lax.all_gather(gate(w_out, *normed[1:3]), "fsdp", axis=0, tiled=True)
+    full_out = lax.all_gather(w_out, "fsdp", axis=0, tiled=True)
     up_slab = lax.all_gather(own_slab(w_up, 1), "fsdp", axis=0, tiled=True)
     down_slab = lax.all_gather(own_slab(w_down, 0), "fsdp", axis=1, tiled=True)
     normed = whole(normed)
-    upstream = order.gather(gate(dz_low, normed))
+    upstream = order.gather(halves_of(gate(dz_low, normed)))
     qkv = order(lambda rows: (contract(rows, qkv_slab) + qkv_bias).astype(low), normed)
     attended, log_totals = order(lambda rows: attend_forward(mask, slopes, rows, seq_count, local_len), qkv)
     mixed_slots = exchange([attended[j * rows_here : (j + 1) * rows_here] for j in range(groups)])
@@ -407,15 +500,9 @@
     mixed_half = jnp.concatenate([mine, pair_swap(theirs)], axis=0)
     middle = order(lambda rows: x + (contract(rows, full_out) + out_bias), mixed_rows)
     second_norm, second_back = jax.vjp(layer_norm, middle, ln2_gain, ln2_shift)
-    second = order.gather(order(lambda values: values.astype(low), second_norm))
+    second = order.gather(order(halves_of, second_norm))
     second = whole(order.pass_on(second))
-    hidden = order(lambda rows: contract(rows, up_slab) + up_bias_slab, second)
-
-    def bend(values):
-        made, back = jax.vjp(exact_gelu, values)
-        return made.astype(low), back(jnp.ones_like(values))[0]
-
-    active, slope = order(bend, hidden)
+    active, slope = order(lambda rows: up_and_bend(rows, up_slab, up_bias_slab[None]), second)
     upstream = whole(upstream)
 
     def slab_sum(left, right):
@@ -431,12 +518,12 @@
 
     down_sum = slab_sum(upstream, active)
 
-    hidden_grad = order(lambda rows: (contract_last(rows, down_slab) * slope).astype(low), upstream)
+    hidden_grad, hidden_sum = order(lambda rows: hidden_gradient(rows, down_slab, slope), upstream)
 
     def to_second(rows):
         return contract_last(rows, up_slab).astype(low)
 
-    second_grad = order.add_far(order.scatter(to_second, hidden_grad), to_second)
+    second_grad = order.add_far(order.scatter(to_second, hidden_grad))
     up_sum = slab_sum(second, hidden_grad)
 
     def to_result(rows):
@@ -456,7 +543,7 @@
         return jnp.sum(values.astype(wide), axis=0)
 
     hidden_sum = lax.dynamic_update_slice_in_dim(
-        jnp.zeros((hidden_width,), wide), column_sum(hidden_grad), me * hidden_slab, axis=0
+        jnp.zeros((hidden_width,), wide), hidden_sum[0], me * hidden_slab, axis=0
     )
     early = [column_sum(branch_grad), ln2_gain_grad, ln2_shift_grad, hidden_sum, column_sum(dz)]
     early = jnp.concatenate(early).reshape(-1, PAIR)
@@ -471,9 +558,15 @@
     mixed_grad = jnp.concatenate(mixed_grad, axis=0)
     order.after(down_sum)
     attention = (mask, slopes, qkv, log_totals, attended)
-    out_begun = order.add_far(out_begun, to_out)
     begun = order(lambda rows: attend_backward(*attention, rows, seq_count, local_len, 0, pairs // 2), mixed_grad)
     early = Total(gate(early, begun))
+    outcome = order.add_far(outcome)
+    out_begun = order.add_far(out_begun)
+    early.step(order)
+    qkv_grad = order(
+        lambda rows: attend_backward(*attention, rows, seq_count, local_len, pairs // 2, pairs, begun), mixed_grad
+    )
+
     out_sum = order(
         lambda own, *came: summed(own, came or None).astype(low), out_begun[0], *(out_begun[1] or ())
     ).reshape(-1, 1, out_rows, model_width)
@@ -482,11 +575,6 @@
         [jnp.where(parity == 0, out_sum, zero), jnp.where(parity == 1, out_sum, zero)], axis=1
     ).reshape(-1, model_width)
     grad_w_out = lax.psum_scatter(out_sum, "fsdp", scatter_dimension=0, tiled=True).astype(wide)
-    outcome = order.add_far(outcome, to_result)
-    early.step(order)
-    qkv_grad = order(
-        lambda rows: attend_backward(*attention, rows, seq_count, local_len, pairs // 2, pairs, begun), mixed_grad
-    )
 
     def to_normed(rows):
         return contract_last(rows, qkv_slab).astype(low)
@@ -494,7 +582,7 @@
     early.step(order)
     normed_grad = order.scatter(to_normed, qkv_grad)
     early.step(order)
-    normed_grad = order.add_far(normed_grad, to_normed)
+    normed_grad = order.add_far(normed_grad)
     early.step(order)
     order.after(up_sum)
     qkv_sum = slab_sum(normed, qkv_grad)

time: 947 us -> 840 us (0.89)
  matrix products: 238 us -> 169 us
  Pallas kernels: 84.5 us -> 140 us
  waiting for transfers between devices: 312 us -> 264 us
  other arithmetic: 111 us -> 71.1 us
  local copies, waits for them, and re-layouts: 120 us -> 107 us
    pallas_call x0 -> x2, Pallas kernels: none -> 55.6 us  [the longest x1 30 us: up_and_bend(): pl.pallas_call(partial(up_kernel, chunk=TILE), grid=(count // TILE,), in_...]
    ppermute x34 -> x40, waiting for transfers between devices: 206 us -> 160 us  [swap(): return lax.ppermute(values, 'seq', [(i, i ^ bit) for i in range(4)])]
    dot_general x10 -> x5, matrix products: 90 us -> 46.2 us  [contract_last(): lax.dot_general(left_side, right_side, (((1,), (1,)), ((), ())), preferre...]
    convert_element_type x9 -> x4, other arithmetic: 45.7 us -> 6.25 us  [add(): (second[:half].astype(wide) + top.astype(wide)).astype(rest.dtype)]
    dot_general x7 -> x4, matrix products: 77.9 us -> 51.6 us  [contract(): lax.dot_general(left_side, right_side, (((1,), (0,)), ((), ())), preferre...]
    slice x19 -> x7, local copies, waits for them, and re-layouts: 25.8 us -> 6.14 us  [the longest x3 3.2 us: halves_of(): return (values[:half].astype(low), values[half:].astype(low))]
    ppermute x34 -> x40, starting transfers between devices: 39.8 us -> 47.7 us  [swap(): return lax.ppermute(values, 'seq', [(i, i ^ bit) for i in range(4)])]
    unnamed x157 -> x143, local copies, waits for them, and re-layouts: 33.3 us -> 36.9 us
  transfers between devices with their start and end apart: 57 -> 63, of which waited for: 22 -> 23; matrix products, arithmetic and copies ran while one was open for 45% -> 36% of each run, Pallas kernels for 9% -> 17%
where the time goes in v4:
time: 840 us; the launch traced here: 835 us
  waiting for transfers between devices  264 us (31%)
  matrix products  169 us (20%)
  Pallas kernels  140 us (17%)
  local copies, waits for them, and re-layouts  107 us (13%)
  other arithmetic  71.1 us (8%)
  starting transfers between devices  69 us (8%)
  between operations  15.8 us (2%)
    ppermute x40, waiting for transfers between devices, swap(): return lax.ppermute(values, 'seq', [(i, i ^ bit) for i in range(4)])  160 us
    dot_general x5, matrix products, contract_first(): lax.dot_general(left_side, right_side, (((0,), (0,)), ((), ())), preferre...  70.8 us
    pallas_call x2, Pallas kernels, attend_backward(): pl.pallas_call(partial(attend_backward_kernel, blocks=blocks, seqs=seqs,...  55.7 us
    all_to_all x3, waiting for transfers between devices, slabs_of_rows(): lax.all_to_all(values, 'seq', split_axis=0, concat_axis=0, tiled=True)  53 us
    dot_general x4, matrix products, contract(): lax.dot_general(left_side, right_side, (((1,), (0,)), ((), ())), preferre...  51.6 us
    ppermute x10, waiting for transfers between devices, send(): self.came = lax.ppermute(self.values, axis, other)  48.1 us
    ppermute x40, starting transfers between devices, swap(): return lax.ppermute(values, 'seq', [(i, i ^ bit) for i in range(4)])  47.7 us
    dot_general x5, matrix products, contract_last(): lax.dot_general(left_side, right_side, (((1,), (1,)), ((), ())), preferre...  46.2 us
  transfers between devices with their start and end apart: 63, of which 23 were waited for; matrix products, arithmetic and copies ran while one was open for 36% of the time, Pallas kernels for 17%

profile of v4, /device:TPU:0, one launch (start us, length us, event | category | flops | bytes accessed | tf_op | source)
XLA Modules:
  0.0 834.9 jit_solution(10433730611448126636)
XLA Ops:
  33.8 19.5 %collective-permute-done.2 = bf16[256,2048]{1,0:T(8,128)(2,1)} collective-permute-done((bf16[256,2048]{1,0:T(8,128)(2,1)}, bf16[256,2048]{1,0:T(8,128)(2,1)}, u32[]{:S(2)}, u32[]{:S(2)}) %collective-permute-start.2) | collective-permute-done | bytes 1048608 | tf_op jit(solution)/shard_map/ppermute | solution.py:289
  57.6 20.3 %collective-permute-done = bf16[256,2048]{1,0:T(8,128)(2,1)} collective-permute-done((bf16[256,2048]{1,0:T(8,128)(2,1)}, bf16[256,2048]{1,0:T(8,128)(2,1)}, u32[]{:S(2)}, u32[]{:S(2)}) %collective-permute-start) | collective-permute-done | bytes 1048608 | tf_op jit(solution)/shard_map/ppermute | solution.py:289
  86.2 12.7 %collective-permute-done.4 = bf16[256,2048]{1,0:T(8,128)(2,1)} collective-permute-done((bf16[256,2048]{1,0:T(8,128)(2,1)}, bf16[256,2048]{1,0:T(8,128)(2,1)}, u32[]{:S(2)}, u32[]{:S(2)}) %collective-permute-start.4) | collective-permute-done | bytes 1048608 | tf_op jit(solution)/shard_map/ppermute | solution.py:289
  107.8 17.4 %add_convert_fusion.qkv_ref = bf16[2048,1536]{1,0:T(8,128)(2,1)S(1)} fusion(bf16[2048,2048]{1,0:T(8,128)(2,1)} %constant_dynamic-update-slice_fusion, bf16[2048,1536]{0,1:T(8,128)(2,1)} %all-gather.5.cloned.1.call-done, f32[1536]{0:T(1024)S(1)} %add.203), kind=kOutput, calls=%fused_computation.1 | convolution fusion | flops 12891193344 | bytes 20977664 | tf_op jit(solution)/shard_map/dot_general | solution.py:25
  125.3 28.6 %attend_forward.1 = (bf16[2048,512]{1,0:T(8,128)(2,1)S(1)}, f32[2048,512]{1,0:T(8,128)S(1)}) custom-call(s32[1]{0:T(128)} %bitcast.1.mask_ref, f32[8]{0:T(128)S(1)} %multiply_power_fusion.slope_ref, bf16[2048,1536]{1,0:T(8,128)(2,1)S(1)} %add_convert_fusion.qkv_ref), custom_call_target="tpu_custom_call" | custom-call | flops 10737418240 | bytes 12582912 | tf_op jit(solution)/shard_map/attend_forward/pallas_call | solution.py:160
  160.8 9.1 %collective-permute-done.6 = bf16[512,512]{1,0:T(8,128)(2,1)S(1)} collective-permute-done((bf16[512,512]{1,0:T(8,128)(2,1)S(1)}, bf16[512,512]{1,0:T(8,128)(2,1)S(1)}, u32[]{:S(2)}, u32[]{:S(2)}) %collective-permute-start.6) | collective-permute-done | bytes 524320 | tf_op jit(solution)/shard_map/ppermute | solution.py:289
  209.5 13.1 %collective-permute-done.15 = bf16[256,2048]{1,0:T(8,128)(2,1)S(1)} collective-permute-done((bf16[256,2048]{1,0:T(8,128)(2,1)S(1)}, bf16[256,2048]{1,0:T(8,128)(2,1)S(1)}, u32[]{:S(2)}, u32[]{:S(2)}) %collective-permute-start.15) | collective-permute-done | bytes 1048608 | tf_op jit(solution)/shard_map/ppermute | solution.py:289
  225.8 21.0 %collective-permute-done.14 = bf16[256,2048]{1,0:T(8,128)(2,1)S(1)} collective-permute-done((bf16[256,2048]{1,0:T(8,128)(2,1)S(1)}, bf16[256,2048]{1,0:T(8,128)(2,1)S(1)}, u32[]{:S(2)}, u32[]{:S(2)}) %collective-permute-start.14) | collective-permute-done | bytes 1048608 | tf_op jit(solution)/shard_map/ppermute | solution.py:289
  252.4 14.4 %collective-permute-done.17 = bf16[256,2048]{1,0:T(8,128)(2,1)S(1)} collective-permute-done((bf16[256,2048]{1,0:T(8,128)(2,1)S(1)}, bf16[256,2048]{1,0:T(8,128)(2,1)S(1)}, u32[]{:S(2)}, u32[]{:S(2)}) %collective-permute-start.17) | collective-permute-done | bytes 1048608 | tf_op jit(solution)/shard_map/ppermute | solution.py:289
  268.9 30.0 %up_and_bend.1 = (bf16[2048,2048]{1,0:T(8,128)(2,1)}, f32[2048,2048]{1,0:T(8,128)}) custom-call(bf16[2048,2048]{1,0:T(8,128)(2,1)} %constant_dynamic-update-slice_fusion.7.rows_ref, bf16[2048,2048]{1,0:T(8,128)(2,1)} %all-gather.9.cloned.1.call-done.weight_ref, f32[1,2048]{1,0:T(1,128)S(1)} %bitcast.130), custom_call_target="tpu_custom_call" | custom-call | flops 34359738368 | bytes 41943040 | tf_op jit(solution)/shard_map/up_and_bend/pallas_call | solution.py:237
  298.9 24.0 %convolution_convert_fusion.4 = bf16[2048,2048]{1,0:T(8,128)(2,1)} fusion(bf16[2048,2048]{1,0:T(8,128)(2,1)} %constant_dynamic-update-slice_fusion.14.rows_ref, bf16[2048,2048]{1,0:T(8,128)(2,1)} %get-tuple-element.97), kind=kOutput, calls=%fused_computation.6 | convolution fusion | flops 17184063488 | bytes 25165824 | tf_op jit(solution)/shard_map/dot_general | solution.py:37
  347.3 25.6 %hidden_gradient.1 = (bf16[2048,2048]{1,0:T(8,128)(2,1)}, f32[1,2048]{1,0:T(1,128)S(1)}) custom-call(bf16[2048,2048]{1,0:T(8,128)(2,1)} %constant_dynamic-update-slice_fusion.14.rows_ref, bf16[2048,2048]{1,0:T(8,128)(2,1)} %all-gather.11.cloned.1.call-done.weight_ref, f32[2048,2048]{1,0:T(8,128)} %get-tuple-element.85.slope_ref), custom_call_target="tpu_custom_call" | custom-call | flops 25769803776 | bytes 41943040 | tf_op jit(solution)/shard_map/hidden_gradient/pallas_call | solution.py:265
  384.4 17.5 %convolution_convert_fusion.3 = bf16[1536,2048]{1,0:T(8,128)(2,1)S(1)} fusion(bf16[2048,2048]{1,0:T(8,128)(2,1)} %all-gather.9.cloned.1.call-done.weight_ref, bf16[2048,2048]{1,0:T(8,128)(2,1)} %get-tuple-element.91), kind=kOutput, calls=%fused_computation.5 | convolution fusion | flops 12888047616 | bytes 20971520 | tf_op jit(solution)/shard_map/dot_general | solution.py:31
  413.9 23.0 %convolution_convert_fusion.2 = bf16[2048,2048]{1,0:T(8,128)(2,1)} fusion(bf16[2048,2048]{1,0:T(8,128)(2,1)} %constant_dynamic-update-slice_fusion.7.rows_ref, bf16[2048,2048]{1,0:T(8,128)(2,1)S(1)} %bitcast.178), kind=kOutput, calls=%fused_computation.4 | convolution fusion | flops 17184063488 | bytes 25165824 | tf_op jit(solution)/shard_map/dot_general | solution.py:37
  454.5 19.5 %convolution_convert_fusion.1 = bf16[1536,2048]{1,0:T(8,128)(2,1)} fusion(bf16[2048,2048]{1,0:T(8,128)(2,1)} %all-gather.11.cloned.1.call-done.weight_ref, bf16[2048,2048]{1,0:T(8,128)(2,1)} %get-tuple-element.97), kind=kOutput, calls=%fused_computation.3 | convolution fusion | flops 12888047616 | bytes 20971520 | tf_op jit(solution)/shard_map/dot_general | solution.py:25
  494.8 11.2 %collective-permute-done.27 = bf16[512,512]{1,0:T(8,128)(2,1)S(1)} collective-permute-done((bf16[512,512]{1,0:T(8,128)(2,1)S(1)}, bf16[512,512]{1,0:T(8,128)(2,1)S(1)}, u32[]{:S(2)}, u32[]{:S(2)}) %collective-permute-start.27) | collective-permute-done | bytes 524320 | tf_op jit(solution)/shard_map/ppermute | solution.py:289
  506.8 11.0 %collective-permute-done.28 = bf16[512,512]{1,0:T(8,128)(2,1)S(1)} collective-permute-done((bf16[512,512]{1,0:T(8,128)(2,1)S(1)}, bf16[512,512]{1,0:T(8,128)(2,1)S(1)}, u32[]{:S(2)}, u32[]{:S(2)}) %collective-permute-start.28) | collective-permute-done | bytes 524320 | tf_op jit(solution)/shard_map/ppermute | solution.py:289
  532.1 27.8 %attend_backward.2.rest_0_ = bf16[2048,1536]{1,0:T(8,128)(2,1)} custom-call(s32[1]{0:T(128)} %bitcast.1.mask_ref, f32[8]{0:T(128)S(1)} %copy-done.4, bf16[2048,1536]{1,0:T(8,128)(2,1)} %copy-done.5, f32[2048,512]{1,0:T(8,128)S(1)} %copy-done.7, bf16[2048,512]{1,0:T(8,128)(2,1)S(1)} %copy-done.1, bf16[2048,512]{1,0:T(8,128)(2,1)S(1)} %copy-done.2), custom_call_target="tpu_custom_call" | custom-call | flops 13421772800 | bytes 10485760 | tf_op jit(solution)/shard_map/attend_backward/pallas_call | solution.py:187
  574.2 27.9 %attend_backward.3 = bf16[2048,1536]{1,0:T(8,128)(2,1)} custom-call(s32[1]{0:T(128)} %bitcast.1.mask_ref, f32[8]{0:T(128)S(1)} %copy-done.4, bf16[2048,1536]{1,0:T(8,128)(2,1)} %copy-done.5, f32[2048,512]{1,0:T(8,128)S(1)} %copy-done.7, bf16[2048,512]{1,0:T(8,128)(2,1)S(1)} %copy-done.1, ...), custom_call_target="tpu_custom_call", output_to_operand_aliasing={{}: (6, {})} | custom-call | flops 13421772800 | bytes 10485760 | tf_op jit(solution)/shard_map/attend_backward/pallas_call | solution.py:187
  613.3 10.3 %convolution_convert_fusion = bf16[1536,2048]{1,0:T(8,128)(2,1)S(1)} fusion(bf16[2048,1536]{0,1:T(8,128)(2,1)S(1)} %bitcast.176, bf16[2048,1536]{1,0:T(8,128)(2,1)S(1)} %bitcast.145), kind=kOutput, calls=%fused_computation.2 | convolution fusion | flops 9666822144 | bytes 17301504 | tf_op jit(solution)/shard_map/dot_general | solution.py:31
  624.8 12.3 %collective-permute-done.42 = bf16[256,2048]{1,0:T(8,128)(2,1)S(1)} collective-permute-done((bf16[256,2048]{1,0:T(8,128)(2,1)S(1)}, bf16[256,2048]{1,0:T(8,128)(2,1)S(1)}, u32[]{:S(2)}, u32[]{:S(2)}) %collective-permute-start.42) | collective-permute-done | bytes 1048608 | tf_op jit(solution)/shard_map/ppermute | solution.py:289
  641.7 17.6 %convolution_convert_fusion.5 = bf16[2048,1536]{1,0:T(8,128)(2,1)S(1)} fusion(bf16[2048,2048]{1,0:T(8,128)(2,1)} %constant_dynamic-update-slice_fusion, bf16[2048,1536]{1,0:T(8,128)(2,1)} %attend_backward.3), kind=kOutput, calls=%fused_computation.7 | convolution fusion | flops 12888047616 | bytes 20971520 | tf_op jit(solution)/shard_map/dot_general | solution.py:37
  692.4 45.1 %all-to-all-done.1 = bf16[4,64,2048]{2,1,0:T(8,128)(2,1)S(1)} async-done(((bf16[4,64,2048]{2,1,0:T(8,128)(2,1)}), bf16[4,64,2048]{2,1,0:T(8,128)(2,1)S(1)}, u32[]{:S(2)}, u32[]{:S(2)}) %all-to-all-start.1) | async-done | bytes 1048608 | tf_op jit(solution)/shard_map/all_to_all | solution.py:516
  739.3 41.6 %collective-permute-done.44 = f32[128,128]{1,0:T(8,128)S(1)} collective-permute-done((f32[128,128]{1,0:T(8,128)S(1)}, f32[128,128]{1,0:T(8,128)S(1)}, u32[]{:S(2)}, u32[]{:S(2)}) %collective-permute-start.44) | collective-permute-done | bytes 65568 | tf_op jit(solution)/shard_map/ppermute | solution.py:407
  (387 shorter events, 318.7 us)
Async XLA Ops:
  7.2 100.6 %all-gather.5.cloned.1.call-start = ((), (), s32[]{:S(2)}) async-start(), calls=%async_computation.7 | async-start | bytes 7077888 | tf_op jit(solution)/shard_map/all_gather | solution.py:466
  17.5 165.1 %all-gather.7.cloned.1.call-start = ((), (), s32[]{:S(2)}) async-start(), calls=%async_computation.8 | async-start | bytes 9437184 | tf_op jit(solution)/shard_map/all_gather | solution.py:478
  18.2 250.7 %all-gather.9.cloned.1.call-start = ((), (), s32[]{:S(2)}) async-start(), calls=%async_computation.9 | async-start | bytes 9437184 | tf_op jit(solution)/shard_map/all_gather | solution.py:479
  20.6 326.7 %all-gather.11.cloned.1.call-start = ((), (), s32[]{:S(2)}) async-start(), calls=%async_computation.10 | async-start | bytes 9437184 | tf_op jit(solution)/shard_map/all_gather | solution.py:480
  31.1 52.8 %collective-permute-start.3 = (bf16[256,2048]{1,0:T(8,128)(2,1)}, bf16[256,2048]{1,0:T(8,128)(2,1)}, u32[]{:S(2)}, u32[]{:S(2)}) collective-permute-start(bf16[256,2048]{1,0:T(8,128)(2,1)} %get-tuple-element.193), channel_id=1, source_target_pairs={{0,16},{8,24},{16,0},{24,8},{1,17},{9,25},{17,1},{25,9},{2,18},{10... | collective-permute-start | bytes 3145736 | tf_op jit(solution)/shard_map/ppermute | solution.py:289
  33.5 494.8 %reduce-scatter.5.cloned.1.call-start = ((), (), s32[]{:S(2)}) async-start(), calls=%async_computation.11 | async-start | bytes 9437184 | tf_op jit(solution)/shard_map/reduce_scatter | solution.py:512
  103.7 51.7 %collective-permute-start.11 = (bf16[256,2048]{1,0:T(8,128)(2,1)}, bf16[256,2048]{1,0:T(8,128)(2,1)}, u32[]{:S(2)}, u32[]{:S(2)}) collective-permute-start(bf16[256,2048]{1,0:T(8,128)(2,1)} %get-tuple-element.188), channel_id=1, source_target_pairs={{0,8},{8,0},{16,24},{24,16},{1,9},{9,1},{17,25},{25,17},{2,10},{10... | collective-permute-start | bytes 3145736 | tf_op jit(solution)/shard_map/ppermute | solution.py:289
  105.2 54.0 %collective-permute-start.10 = (bf16[256,2048]{1,0:T(8,128)(2,1)}, bf16[256,2048]{1,0:T(8,128)(2,1)}, u32[]{:S(2)}, u32[]{:S(2)}) collective-permute-start(bf16[256,2048]{1,0:T(8,128)(2,1)} %get-tuple-element.188), channel_id=1, source_target_pairs={{0,16},{8,24},{16,0},{24,8},{1,17},{9,25},{17,1},{25,9},{2,18},{10... | collective-permute-start | bytes 3145736 | tf_op jit(solution)/shard_map/ppermute | solution.py:289
  105.7 51.3 %collective-permute-start.9 = (bf16[256,2048]{1,0:T(8,128)(2,1)}, bf16[256,2048]{1,0:T(8,128)(2,1)}, u32[]{:S(2)}, u32[]{:S(2)}) collective-permute-start(bf16[256,2048]{1,0:T(8,128)(2,1)} %get-tuple-element.189), channel_id=1, source_target_pairs={{0,8},{8,0},{16,24},{24,16},{1,9},{9,1},{17,25},{25,17},{2,10},{10... | collective-permute-start | bytes 3145736 | tf_op jit(solution)/shard_map/ppermute | solution.py:289
  106.1 76.4 %collective-permute-start.12 = (bf16[256,2048]{1,0:T(8,128)(2,1)}, bf16[256,2048]{1,0:T(8,128)(2,1)}, u32[]{:S(2)}, u32[]{:S(2)}) collective-permute-start(bf16[256,2048]{1,0:T(8,128)(2,1)} %get-tuple-element.189), channel_id=1, source_target_pairs={{0,16},{8,24},{16,0},{24,8},{1,17},{9,25},{17,1},{25,9},{2,18},{10... | collective-permute-start | bytes 3145736 | tf_op jit(solution)/shard_map/ppermute | solution.py:289
  197.9 50.3 %collective-permute-start.13 = (bf16[256,2048]{1,0:T(8,128)(2,1)S(1)}, bf16[256,2048]{1,0:T(8,128)(2,1)S(1)}, u32[]{:S(2)}, u32[]{:S(2)}) collective-permute-start(bf16[256,2048]{1,0:T(8,128)(2,1)S(1)} %get-tuple-element.187), channel_id=1, source_target_pairs={{0,8},{8,0},{16,24},{24,16},{1,9},{9,1},{17,25},{25,17},{2,10},{10... | collective-permute-start | bytes 3145736 | tf_op jit(solution)/shard_map/ppermute | solution.py:289
  331.3 310.5 %reduce-scatter.7.cloned.1.call-start = ((), (), s32[]{:S(2)}) async-start(), calls=%async_computation.12 | async-start | bytes 9437184 | tf_op jit(solution)/shard_map/reduce_scatter | solution.py:512
  410.5 63.5 %collective-permute-start.26 = (bf16[512,2048]{1,0:T(8,128)(2,1)}, bf16[512,2048]{1,0:T(8,128)(2,1)}, u32[]{:S(2)}, u32[]{:S(2)}) collective-permute-start(bf16[512,2048]{1,0:T(8,128)(2,1)} %pad_maximum_fusion.7), channel_id=1, source_target_pairs={{0,16},{8,24},{16,0},{24,8},{1,17},{9,25},{17,1},{25,9},{2,18},{10... | collective-permute-start | bytes 6291464 | tf_op jit(solution)/shard_map/ppermute | solution.py:289
  413.4 60.5 %collective-permute-start.25 = (bf16[512,2048]{1,0:T(8,128)(2,1)}, bf16[512,2048]{1,0:T(8,128)(2,1)}, u32[]{:S(2)}, u32[]{:S(2)}) collective-permute-start(bf16[512,2048]{1,0:T(8,128)(2,1)} %pad_maximum_fusion.6), channel_id=1, source_target_pairs={{0,8},{8,0},{16,24},{24,16},{1,9},{9,1},{17,25},{25,17},{2,10},{10... | collective-permute-start | bytes 6291464 | tf_op jit(solution)/shard_map/ppermute | solution.py:289
  445.0 114.9 %collective-permute-start.23 = (bf16[256,2048]{1,0:T(8,128)(2,1)}, bf16[256,2048]{1,0:T(8,128)(2,1)S(1)}, u32[]{:S(2)}, u32[]{:S(2)}) collective-permute-start(bf16[256,2048]{1,0:T(8,128)(2,1)} %get-tuple-element.183), channel_id=1, source_target_pairs={{0,8},{8,0},{16,24},{24,16},{1,9},{9,1},{17,25},{25,17},{2,10},{10... | collective-permute-start | bytes 3145736 | tf_op jit(solution)/shard_map/ppermute | solution.py:289
  454.4 352.0 %reduce-scatter.9.cloned.1.call-start = ((), (), s32[]{:S(2)}) async-start(), calls=%async_computation.13 | async-start | bytes 7077888 | tf_op jit(solution)/shard_map/reduce_scatter | solution.py:512
  505.9 53.9 %collective-permute-start.24 = (bf16[256,2048]{1,0:T(8,128)(2,1)}, bf16[256,2048]{1,0:T(8,128)(2,1)}, u32[]{:S(2)}, u32[]{:S(2)}) collective-permute-start(bf16[256,2048]{1,0:T(8,128)(2,1)} %get-tuple-element.182), channel_id=1, source_target_pairs={{0,16},{8,24},{16,0},{24,8},{1,17},{9,25},{17,1},{25,9},{2,18},{10... | collective-permute-start | bytes 3145736 | tf_op jit(solution)/shard_map/ppermute | solution.py:289
  666.3 114.7 %collective-permute-start.33 = (bf16[512,2048]{1,0:T(8,128)(2,1)}, bf16[512,2048]{1,0:T(8,128)(2,1)}, u32[]{:S(2)}, u32[]{:S(2)}) collective-permute-start(bf16[512,2048]{1,0:T(8,128)(2,1)} %pad_maximum_fusion.12), channel_id=1, source_target_pairs={{0,16},{8,24},{16,0},{24,8},{1,17},{9,25},{17,1},{25,9},{2,18},{10... | collective-permute-start | bytes 6291464 | tf_op jit(solution)/shard_map/ppermute | solution.py:289
  668.3 112.7 %collective-permute-start.32 = (bf16[512,2048]{1,0:T(8,128)(2,1)}, bf16[512,2048]{1,0:T(8,128)(2,1)}, u32[]{:S(2)}, u32[]{:S(2)}) collective-permute-start(bf16[512,2048]{1,0:T(8,128)(2,1)} %pad_maximum_fusion.11), channel_id=1, source_target_pairs={{0,8},{8,0},{16,24},{24,16},{1,9},{9,1},{17,25},{25,17},{2,10},{10... | collective-permute-start | bytes 6291464 | tf_op jit(solution)/shard_map/ppermute | solution.py:289
  681.3 56.2 %all-to-all-start.1 = ((bf16[4,64,2048]{2,1,0:T(8,128)(2,1)}), bf16[4,64,2048]{2,1,0:T(8,128)(2,1)S(1)}, u32[]{:S(2)}, u32[]{:S(2)}) async-start(bf16[4,64,2048]{2,1,0:T(8,128)(2,1)} %bitcast.42), calls=%async_computation.5 | async-start | bytes 2097152 | tf_op jit(solution)/shard_map/all_to_all | solution.py:516
  684.9 132.2 %reduce-scatter.11.cloned.1.call-start = ((), (), s32[]{:S(2)}) async-start(), calls=%async_computation.14 | async-start | bytes 2359296 | tf_op jit(solution)/shard_map/reduce_scatter | solution.py:577
  686.6 101.0 %collective-permute-start.46 = (bf16[512,2048]{1,0:T(8,128)(2,1)}, bf16[512,2048]{1,0:T(8,128)(2,1)S(1)}, u32[]{:S(2)}, u32[]{:S(2)}) collective-permute-start(bf16[512,2048]{1,0:T(8,128)(2,1)} %pad_maximum_fusion.14), channel_id=1, source_target_pairs={{0,16},{8,24},{16,0},{24,8},{1,17},{9,25},{17,1},{25,9},{2,18},{10... | collective-permute-start | bytes 6291464 | tf_op jit(solution)/shard_map/ppermute | solution.py:289
  688.6 99.1 %collective-permute-start.45 = (bf16[512,2048]{1,0:T(8,128)(2,1)}, bf16[512,2048]{1,0:T(8,128)(2,1)}, u32[]{:S(2)}, u32[]{:S(2)}) collective-permute-start(bf16[512,2048]{1,0:T(8,128)(2,1)} %pad_maximum_fusion.13), channel_id=1, source_target_pairs={{0,8},{8,0},{16,24},{24,16},{1,9},{9,1},{17,25},{25,17},{2,10},{10... | collective-permute-start | bytes 6291464 | tf_op jit(solution)/shard_map/ppermute | solution.py:289
  691.8 89.2 %collective-permute-start.44 = (f32[128,128]{1,0:T(8,128)S(1)}, f32[128,128]{1,0:T(8,128)S(1)}, u32[]{:S(2)}, u32[]{:S(2)}) collective-permute-start(f32[128,128]{1,0:T(8,128)S(1)} %add.231), channel_id=1, source_target_pairs={{0,16},{8,24},{16,0},{24,8},{1,17},{9,25},{17,1},{25,9},{2,18},{10... | collective-permute-start | bytes 196616 | tf_op jit(solution)/shard_map/ppermute | solution.py:407
  (98 other events, 1817.6 us)
Sparse Core Ops, SparseCore 0:
  17.6 67.8 all-gather.4
  87.1 80.2 all-gather.6
  169.5 80.5 all-gather.8
  251.6 81.0 all-gather.10
  334.8 87.8 reduce-scatter.4
  454.5 89.3 reduce-scatter.6
  662.9 66.5 reduce-scatter.8
  731.7 33.9 reduce-scatter.10

commit v5 on v4

--- a/solution.py
+++ b/solution.py
@@ -334,18 +334,20 @@
         top, bottom = rows
         return rows, (swap(bottom, 1), swap(top, 2), swap(top, 1), swap(bottom, 2))
 
-    def pass_on(self, begun):
+    def pass_on(self, begun, *before):
         rows, came = begun
         if came is None:
             return rows
         first_bottom, second_top, first_top, second_bottom = came
         self.after(*came)
+        if before:
+            second_top, first_bottom = gate((second_top, first_bottom), *before)
         far = [swap(second_top, 1), swap(first_bottom, 2)]
         return [*rows, first_top, first_bottom, second_top, second_bottom, *far]
 
-    def scatter(self, product, rows, axis=0):
+    def send_far(self, product, rows, axis=0):
         if lax.axis_size("seq") != 4:
-            return lax.psum_scatter(self(product, rows), "seq", scatter_dimension=0, tiled=True), None
+            return product, rows, axis, None
         count = rows.shape[axis] // 4
 
         def far_half(values):
@@ -354,9 +356,14 @@
             return made[:half], made[half:]
 
         top, bottom = self(far_half, rows)
-        top, bottom = swap(top, 1), swap(bottom, 2)
-        rest = self(lambda values: product(lax.slice_in_dim(values, 0, 3 * count, axis=axis)), rows)
-        return rest, (top, bottom)
+        return product, rows, axis, (swap(top, 1), swap(bottom, 2))
+
+    def make_rest(self, begun):
+        product, rows, axis, parts = begun
+        if parts is None:
+            return lax.psum_scatter(self(product, rows), "seq", scatter_dimension=0, tiled=True), None
+        count = rows.shape[axis] // 4
+        return self(lambda values: product(lax.slice_in_dim(values, 0, 3 * count, axis=axis)), rows), parts
 
     def add_far(self, begun):
         rest, parts = begun
@@ -391,31 +398,13 @@
     return jnp.concatenate(parts, axis=0) if isinstance(parts, list) else parts
 
 
-class Total:
-    def __init__(self, values):
-        self.values = values
-        self.steps = [
-            (axis, 1 << bit) for axis in ("fsdp", "seq") for bit in range(lax.axis_size(axis).bit_length() - 1)
-        ]
-        self.send()
-
-    def send(self):
-        self.came = None
-        if self.steps:
-            axis, bit = self.steps.pop(0)
-            other = [(i, i ^ bit) for i in range(lax.axis_size(axis))]
-            self.came = lax.ppermute(self.values, axis, other)
-
-    def step(self, order=None):
-        if self.came is not None:
-            add = lambda own, other: own + other
-            self.values = (order or (lambda operation, *operands: operation(*operands)))(add, self.values, self.came)
-            self.send()
-
-    def done(self):
-        while self.came is not None:
-            self.step()
-        return self.values.reshape(-1)
+def total(values):
+    for axis in ("fsdp", "seq"):
+        count, bit = lax.axis_size(axis), 1
+        while bit < count:
+            values = values + lax.ppermute(values, axis, [(i, i ^ bit) for i in range(count)])
+            bit *= 2
+    return values
 
 
 def local(
@@ -482,8 +471,9 @@
     upstream = order.gather(halves_of(gate(dz_low, normed)))
     qkv = order(lambda rows: (contract(rows, qkv_slab) + qkv_bias).astype(low), normed)
     attended, log_totals = order(lambda rows: attend_forward(mask, slopes, rows, seq_count, local_len), qkv)
+    if square:
+        attended = gate(attended, *upstream[1])
     mixed_slots = exchange([attended[j * rows_here : (j + 1) * rows_here] for j in range(groups)])
-    upstream = order.pass_on(upstream)
     mixed_rows = jnp.concatenate(by_index(mixed_slots, me), axis=1)
     mixed_slots = jnp.concatenate(mixed_slots, axis=1)
 
@@ -492,16 +482,21 @@
 
     parity = lax.axis_index("fsdp") & 1
     out_rows = model_width // (groups * shards)
-    halves = mixed_slots.reshape(rows_here, -1, 2, out_rows)
-    mine, theirs = (
-        lax.dynamic_index_in_dim(halves, index, axis=2, keepdims=False).reshape(rows_here, -1)
-        for index in (parity, 1 - parity)
-    )
-    mixed_half = jnp.concatenate([mine, pair_swap(theirs)], axis=0)
+
+    def pair_halves(values):
+        halves = values.reshape(rows_here, -1, 2, out_rows)
+        return tuple(
+            lax.dynamic_index_in_dim(halves, index, axis=2, keepdims=False).reshape(rows_here, -1)
+            for index in (parity, 1 - parity)
+        )
+
     middle = order(lambda rows: x + (contract(rows, full_out) + out_bias), mixed_rows)
     second_norm, second_back = jax.vjp(layer_norm, middle, ln2_gain, ln2_shift)
     second = order.gather(order(halves_of, second_norm))
+    mine, theirs = order(pair_halves, mixed_slots)
+    mixed_half = jnp.concatenate([mine, pair_swap(theirs)], axis=0)
     second = whole(order.pass_on(second))
+    upstream = order.pass_on(upstream, second)
     active, slope = order(lambda rows: up_and_bend(rows, up_slab, up_bias_slab[None]), second)
     upstream = whole(upstream)
 
@@ -511,7 +506,8 @@
         made = jnp.swapaxes(made.reshape(groups, shards, -1, width), 0, 1).reshape(-1, width)
         return lax.psum_scatter(made, "fsdp", scatter_dimension=0, tiled=True)
 
-    def slabs_of_rows(values):
+    def slabs_of_rows(values, *before):
+        values = gate(values, *before) if before else values
         values = values.reshape(groups, -1, values.shape[1])
         slabs = lax.all_to_all(values, "seq", split_axis=0, concat_axis=0, tiled=True)
         return jnp.swapaxes(slabs, 0, 1).astype(wide)
@@ -523,13 +519,13 @@
     def to_second(rows):
         return contract_last(rows, up_slab).astype(low)
 
-    second_grad = order.add_far(order.scatter(to_second, hidden_grad))
+    second_grad = order.add_far(order.make_rest(order.send_far(to_second, hidden_grad)))
     up_sum = slab_sum(second, hidden_grad)
 
     def to_result(rows):
         return contract(rows, down_slab).astype(low)
 
-    outcome = order.scatter(to_result, active)
+    outcome = order.send_far(to_result, active)
 
     def to_middle(own, came):
         middle_part, gain_grad, shift_grad = second_back(summed(own, came))
@@ -546,27 +542,34 @@
         jnp.zeros((hidden_width,), wide), hidden_sum[0], me * hidden_slab, axis=0
     )
     early = [column_sum(branch_grad), ln2_gain_grad, ln2_shift_grad, hidden_sum, column_sum(dz)]
-    early = jnp.concatenate(early).reshape(-1, PAIR)
     mixed_grad = order(lambda rows: contract_last(rows, full_out).astype(low), branch_grad)
     mixed_grad = exchange(by_index([mixed_grad[:, j * slab : (j + 1) * slab] for j in range(groups)], me))
-    branch_pair = jnp.concatenate([branch_grad, pair_swap(branch_grad)], axis=0)
-
-    def to_out(columns):
-        return contract_first(columns, branch_pair).astype(low)
-
-    out_begun = order.scatter(to_out, mixed_half, axis=1)
+    outcome = order.add_far(order.make_rest(outcome))
     mixed_grad = jnp.concatenate(mixed_grad, axis=0)
     order.after(down_sum)
     attention = (mask, slopes, qkv, log_totals, attended)
     begun = order(lambda rows: attend_backward(*attention, rows, seq_count, local_len, 0, pairs // 2), mixed_grad)
-    early = Total(gate(early, begun))
-    outcome = order.add_far(outcome)
-    out_begun = order.add_far(out_begun)
-    early.step(order)
+    branch_pair = jnp.concatenate([branch_grad, pair_swap(gate(branch_grad, mixed_grad))], axis=0)
+
+    def to_out(columns):
+        return contract_first(columns, branch_pair).astype(low)
+
+    out_begun = order.make_rest(order.send_far(to_out, mixed_half, axis=1))
     qkv_grad = order(
         lambda rows: attend_backward(*attention, rows, seq_count, local_len, pairs // 2, pairs, begun), mixed_grad
     )
-
+    if square:
+        order.after(*outcome[1])
+    out_begun = order.add_far(out_begun)
+    order.after(up_sum)
+    qkv_sum = slab_sum(normed, qkv_grad)
+
+    def to_normed(rows):
+        return contract_last(rows, qkv_slab).astype(low)
+
+    normed_grad = order.send_far(to_normed, qkv_grad)
+    normed_grad = order.make_rest(normed_grad)
+    normed_grad = order.add_far(normed_grad)
     out_sum = order(
         lambda own, *came: summed(own, came or None).astype(low), out_begun[0], *(out_begun[1] or ())
     ).reshape(-1, 1, out_rows, model_width)
@@ -574,19 +577,8 @@
     out_sum = jnp.concatenate(
         [jnp.where(parity == 0, out_sum, zero), jnp.where(parity == 1, out_sum, zero)], axis=1
     ).reshape(-1, model_width)
+
     grad_w_out = lax.psum_scatter(out_sum, "fsdp", scatter_dimension=0, tiled=True).astype(wide)
-
-    def to_normed(rows):
-        return contract_last(rows, qkv_slab).astype(low)
-
-    early.step(order)
-    normed_grad = order.scatter(to_normed, qkv_grad)
-    early.step(order)
-    normed_grad = order.add_far(normed_grad)
-    early.step(order)
-    order.after(up_sum)
-    qkv_sum = slab_sum(normed, qkv_grad)
-    early.step(order)
     result = order(
         lambda own, *came: (middle + (summed(own, came or None) + down_bias)).astype(low),
         outcome[0],
@@ -601,8 +593,8 @@
         lambda own, *came: to_input(own, came or None), normed_grad[0], *(normed_grad[1] or ())
     )
     grad_tokens = grad_tokens.reshape(tokens.shape)
-    grad_w_down = slabs_of_rows(down_sum).reshape(-1, hidden_width).T
-    grad_w_up = slabs_of_rows(up_sum).reshape(-1, hidden_width)
+    grad_w_down = slabs_of_rows(down_sum, grad_tokens).reshape(-1, hidden_width).T
+    grad_w_up = slabs_of_rows(up_sum, grad_tokens).reshape(-1, hidden_width)
     grad_w_qkv = slabs_of_rows(qkv_sum).reshape(-1, groups, pairs, 3, PAIR)
     grad_w_qkv = jnp.transpose(grad_w_qkv, (0, 3, 1, 2, 4)).reshape(-1, 3 * model_width)
 
@@ -611,28 +603,27 @@
         jnp.zeros((2, model_width), wide), head_sum[0::2], me * slab, axis=1
     )
     late = [qv_sum.reshape(-1), ln1_gain_grad, ln1_shift_grad]
-    late = Total(jnp.concatenate(late).reshape(-1, PAIR)).done()
-    early = early.done()
-
-    def cut(values, at, count):
-        return values[at * model_width : (at + count) * model_width]
+    sums = total(jnp.concatenate(early + late).reshape(-1, PAIR)).reshape(-1)
+
+    def cut(at, count):
+        return sums[at * model_width : (at + count) * model_width]
 
     ratio = hidden_width // model_width
     return (
         result,
         grad_tokens,
         grad_w_qkv,
-        cut(late, 0, 2).reshape(2, model_width),
+        cut(4 + ratio, 2).reshape(2, model_width),
         grad_w_out,
-        cut(early, 0, 1),
-        cut(late, 2, 1),
-        cut(late, 3, 1),
-        cut(early, 1, 1),
-        cut(early, 2, 1),
+        cut(0, 1),
+        cut(6 + ratio, 1),
+        cut(7 + ratio, 1),
+        cut(1, 1),
+        cut(2, 1),
         grad_w_up,
-        cut(early, 3, ratio),
+        cut(3, ratio),
         grad_w_down,
-        cut(early, 3 + ratio, 1),
+        cut(3 + ratio, 1),
     )
 
 

time: 840 us -> 830 us (0.988)
  waiting for transfers between devices: 264 us -> 249 us
    ppermute x40, waiting for transfers between devices: 160 us -> 223 us  [swap(): return lax.ppermute(values, 'seq', [(i, i ^ bit) for i in range(4)])]
    all_to_all x3, waiting for transfers between devices: 53 us -> 10.7 us  [slabs_of_rows(): lax.all_to_all(values, 'seq', split_axis=0, concat_axis=0, tiled=True)]
    ppermute x10 -> x5, waiting for transfers between devices: 48.1 us -> 14.9 us  [total(): lax.ppermute(values, axis, [(i, i ^ bit) for i in range(count)])]
    unnamed x143 -> x142, local copies, waits for them, and re-layouts: 36.9 us -> 42.9 us
  transfers between devices with their start and end apart: 63 -> 58, of which waited for: 23 -> 22; matrix products, arithmetic and copies ran while one was open for 36% -> 37% of each run, Pallas kernels for 17% -> 17%
where the time goes in v5:
time: 830 us; the launch traced here: 819 us
  waiting for transfers between devices  249 us (30%)
  matrix products  176 us (21%)
  Pallas kernels  141 us (17%)
  local copies, waits for them, and re-layouts  110 us (13%)
  starting transfers between devices  64 us (8%)
  other arithmetic  63.4 us (8%)
  between operations  15.5 us (2%)
    ppermute x40, waiting for transfers between devices, swap(): return lax.ppermute(values, 'seq', [(i, i ^ bit) for i in range(4)])  223 us
    dot_general x5, matrix products, contract_first(): lax.dot_general(left_side, right_side, (((0,), (0,)), ((), ())), preferre...  70.7 us
    pallas_call x2, Pallas kernels, attend_backward(): pl.pallas_call(partial(attend_backward_kernel, blocks=blocks, seqs=seqs,...  56.2 us
    dot_general x4, matrix products, contract(): lax.dot_general(left_side, right_side, (((1,), (0,)), ((), ())), preferre...  53.5 us
    dot_general x5, matrix products, contract_last(): lax.dot_general(left_side, right_side, (((1,), (1,)), ((), ())), preferre...  51.4 us
    ppermute x40, starting transfers between devices, swap(): return lax.ppermute(values, 'seq', [(i, i ^ bit) for i in range(4)])  44.7 us
    unnamed x142, local copies, waits for them, and re-layouts  42.9 us
    pallas_call x1, Pallas kernels, up_and_bend(): pl.pallas_call(partial(up_kernel, chunk=TILE), grid=(count // TILE,), in_...  30.1 us
  transfers between devices with their start and end apart: 58, of which 22 were waited for; matrix products, arithmetic and copies ran while one was open for 37% of the time, Pallas kernels for 17%

profile of v5, /device:TPU:0, one launch (start us, length us, event | category | flops | bytes accessed | tf_op | source)
XLA Modules:
  0.0 818.7 jit_solution(9919160583740694101)
XLA Ops:
  31.2 22.0 %collective-permute-done.2 = bf16[256,2048]{1,0:T(8,128)(2,1)S(1)} collective-permute-done((bf16[256,2048]{1,0:T(8,128)(2,1)}, bf16[256,2048]{1,0:T(8,128)(2,1)S(1)}, u32[]{:S(2)}, u32[]{:S(2)}) %collective-permute-start.2) | collective-permute-done | bytes 1048608 | tf_op jit(solution)/shard_map/ppermute | solution.py:289
  56.9 21.0 %collective-permute-done = bf16[256,2048]{1,0:T(8,128)(2,1)} collective-permute-done((bf16[256,2048]{1,0:T(8,128)(2,1)}, bf16[256,2048]{1,0:T(8,128)(2,1)}, u32[]{:S(2)}, u32[]{:S(2)}) %collective-permute-start) | collective-permute-done | bytes 1048608 | tf_op jit(solution)/shard_map/ppermute | solution.py:289
  83.4 15.5 %collective-permute-done.4 = bf16[256,2048]{1,0:T(8,128)(2,1)} collective-permute-done((bf16[256,2048]{1,0:T(8,128)(2,1)S(1)}, bf16[256,2048]{1,0:T(8,128)(2,1)}, u32[]{:S(2)}, u32[]{:S(2)}) %collective-permute-start.4) | collective-permute-done | bytes 1048608 | tf_op jit(solution)/shard_map/ppermute | solution.py:289
  107.8 17.4 %add_convert_fusion.qkv_ref = bf16[2048,1536]{1,0:T(8,128)(2,1)S(1)} fusion(bf16[2048,2048]{1,0:T(8,128)(2,1)} %constant_dynamic-update-slice_fusion, bf16[2048,1536]{0,1:T(8,128)(2,1)} %all-gather.5.cloned.1.call-done, f32[1536]{0:T(1024)S(1)} %add.188), kind=kOutput, calls=%fused_computation.1 | convolution fusion | flops 12891193344 | bytes 20977664 | tf_op jit(solution)/shard_map/dot_general | solution.py:25
  125.3 28.6 %attend_forward.1 = (bf16[2048,512]{1,0:T(8,128)(2,1)S(1)}, f32[2048,512]{1,0:T(8,128)S(1)}) custom-call(s32[1]{0:T(128)} %bitcast.1.mask_ref, f32[8]{0:T(128)S(1)} %multiply_power_fusion.slope_ref, bf16[2048,1536]{1,0:T(8,128)(2,1)S(1)} %add_convert_fusion.qkv_ref), custom_call_target="tpu_custom_call" | custom-call | flops 10737418240 | bytes 12582912 | tf_op jit(solution)/shard_map/attend_forward/pallas_call | solution.py:160
  163.7 9.8 %collective-permute-done.10 = bf16[512,512]{1,0:T(8,128)(2,1)S(1)} collective-permute-done((bf16[512,512]{1,0:T(8,128)(2,1)}, bf16[512,512]{1,0:T(8,128)(2,1)S(1)}, u32[]{:S(2)}, u32[]{:S(2)}) %collective-permute-start.10) | collective-permute-done | bytes 524320 | tf_op jit(solution)/shard_map/ppermute | solution.py:289
  185.7 9.4 %fusion.42 = (f32[512]{0:T(512)S(1)}, f32[512,2048]{1,0:T(8,128)S(1)}) fusion(f32[2048]{0:T(1024)S(1)} %copy-done.45, bf16[512,2048]{1,0:T(8,128)(2,1)} %get-tuple-element.78, bf16[2048,2048]{1,0:T(8,128)(2,1)} %all-gather.7.cloned.1.call-done, bf16[2,256,2048]{2,1,0:T(8,128)(2,1)} %param.14), kind=kOutput, calls=%fused_computation.170 | convolution fusion | flops 4299161088 | bytes 16787456 | tf_op jit(solution)/shard_map/dot_general | solution.py:25
  213.5 11.9 %collective-permute-done.15 = bf16[256,2048]{1,0:T(8,128)(2,1)} collective-permute-done((bf16[256,2048]{1,0:T(8,128)(2,1)}, bf16[256,2048]{1,0:T(8,128)(2,1)}, u32[]{:S(2)}, u32[]{:S(2)}) %collective-permute-start.15) | collective-permute-done | bytes 1048608 | tf_op jit(solution)/shard_map/ppermute | solution.py:289
  230.8 17.7 %collective-permute-done.13 = bf16[256,2048]{1,0:T(8,128)(2,1)S(1)} collective-permute-done((bf16[256,2048]{1,0:T(8,128)(2,1)}, bf16[256,2048]{1,0:T(8,128)(2,1)S(1)}, u32[]{:S(2)}, u32[]{:S(2)}) %collective-permute-start.13) | collective-permute-done | bytes 1048608 | tf_op jit(solution)/shard_map/ppermute | solution.py:289
  256.6 13.2 %collective-permute-done.17 = bf16[256,2048]{1,0:T(8,128)(2,1)S(1)} collective-permute-done((bf16[256,2048]{1,0:T(8,128)(2,1)}, bf16[256,2048]{1,0:T(8,128)(2,1)S(1)}, u32[]{:S(2)}, u32[]{:S(2)}) %collective-permute-start.17) | collective-permute-done | bytes 1048608 | tf_op jit(solution)/shard_map/ppermute | solution.py:289
  273.7 30.1 %up_and_bend.1 = (bf16[2048,2048]{1,0:T(8,128)(2,1)}, f32[2048,2048]{1,0:T(8,128)}) custom-call(bf16[2048,2048]{1,0:T(8,128)(2,1)} %constant_dynamic-update-slice_fusion.7.rows_ref, bf16[2048,2048]{1,0:T(8,128)(2,1)} %all-gather.9.cloned.1.call-done.weight_ref, f32[1,2048]{1,0:T(1,128)S(1)} %bitcast.128), custom_call_target="tpu_custom_call" | custom-call | flops 34359738368 | bytes 41943040 | tf_op jit(solution)/shard_map/up_and_bend/pallas_call | solution.py:237
  315.0 22.0 %convolution_convert_fusion.4 = bf16[2048,2048]{1,0:T(8,128)(2,1)} fusion(bf16[2048,2048]{1,0:T(8,128)(2,1)} %constant_dynamic-update-slice_fusion.14.rows_ref, bf16[2048,2048]{1,0:T(8,128)(2,1)S(1)} %copy-done.46), kind=kOutput, calls=%fused_computation.6 | convolution fusion | flops 17184063488 | bytes 25165824 | tf_op jit(solution)/shard_map/dot_general | solution.py:37
  345.5 25.7 %hidden_gradient.1 = (bf16[2048,2048]{1,0:T(8,128)(2,1)}, f32[1,2048]{1,0:T(1,128)S(1)}) custom-call(bf16[2048,2048]{1,0:T(8,128)(2,1)} %constant_dynamic-update-slice_fusion.14.rows_ref, bf16[2048,2048]{1,0:T(8,128)(2,1)} %all-gather.11.cloned.1.call-done.weight_ref, f32[2048,2048]{1,0:T(8,128)} %get-tuple-element.85.slope_ref), custom_call_target="tpu_custom_call" | custom-call | flops 25769803776 | bytes 41943040 | tf_op jit(solution)/shard_map/hidden_gradient/pallas_call | solution.py:265
  382.5 17.5 %convolution_convert_fusion.3 = bf16[1536,2048]{1,0:T(8,128)(2,1)S(1)} fusion(bf16[2048,2048]{1,0:T(8,128)(2,1)} %all-gather.9.cloned.1.call-done.weight_ref, bf16[2048,2048]{1,0:T(8,128)(2,1)} %get-tuple-element.91), kind=kOutput, calls=%fused_computation.5 | convolution fusion | flops 12888047616 | bytes 20971520 | tf_op jit(solution)/shard_map/dot_general | solution.py:31
  412.0 22.3 %convolution_convert_fusion.2 = bf16[2048,2048]{1,0:T(8,128)(2,1)} fusion(bf16[2048,2048]{1,0:T(8,128)(2,1)} %constant_dynamic-update-slice_fusion.7.rows_ref, bf16[2048,2048]{1,0:T(8,128)(2,1)S(1)} %bitcast.170), kind=kOutput, calls=%fused_computation.4 | convolution fusion | flops 17184063488 | bytes 25165824 | tf_op jit(solution)/shard_map/dot_general | solution.py:37
  447.7 9.4 %convolution_convert_fusion.9 = bf16[512,2048]{1,0:T(8,128)(2,1)S(1)} fusion(bf16[2048,2048]{1,0:T(8,128)(2,1)} %all-gather.11.cloned.1.call-done.weight_ref, bf16[2048,2048]{1,0:T(8,128)(2,1)} %get-tuple-element.101), kind=kOutput, calls=%fused_computation.43 | convolution fusion | flops 4296015872 | bytes 12582912 | tf_op jit(solution)/shard_map/dot_general | solution.py:25
  459.6 32.0 %collective-permute-done.24 = bf16[512,2048]{1,0:T(8,128)(2,1)S(1)} collective-permute-done((bf16[512,2048]{1,0:T(8,128)(2,1)}, bf16[512,2048]{1,0:T(8,128)(2,1)S(1)}, u32[]{:S(2)}, u32[]{:S(2)}) %collective-permute-start.24) | collective-permute-done | bytes 2097184 | tf_op jit(solution)/shard_map/ppermute | solution.py:289
  511.7 17.3 %convolution_convert_fusion.1 = bf16[1536,2048]{1,0:T(8,128)(2,1)S(1)} fusion(bf16[2048,2048]{1,0:T(8,128)(2,1)} %all-gather.11.cloned.1.call-done.weight_ref, bf16[2048,2048]{1,0:T(8,128)(2,1)} %get-tuple-element.101), kind=kOutput, calls=%fused_computation.3 | convolution fusion | flops 12888047616 | bytes 20971520 | tf_op jit(solution)/shard_map/dot_general | solution.py:25
  546.6 27.9 %attend_backward.2.rest_0_ = bf16[2048,1536]{1,0:T(8,128)(2,1)} custom-call(s32[1]{0:T(128)} %bitcast.1.mask_ref, f32[8]{0:T(128)S(1)} %copy-done.2, bf16[2048,1536]{1,0:T(8,128)(2,1)} %copy-done.3, f32[2048,512]{1,0:T(8,128)S(1)} %copy-done.5, bf16[2048,512]{1,0:T(8,128)(2,1)S(1)} %get-tuple-element.76.mixed_ref, bf16[2048,512]{1,0:T(8,128)(2,1)S(1)} %copy-done), custom_call_target="tpu_custom_call" | custom-call | flops 13421772800 | bytes 10485760 | tf_op jit(solution)/shard_map/attend_backward/pallas_call | solution.py:187
  585.6 28.2 %attend_backward.3 = bf16[2048,1536]{1,0:T(8,128)(2,1)} custom-call(s32[1]{0:T(128)} %bitcast.1.mask_ref, f32[8]{0:T(128)S(1)} %copy-done.2, bf16[2048,1536]{1,0:T(8,128)(2,1)} %copy-done.3, f32[2048,512]{1,0:T(8,128)S(1)} %copy-done.5, bf16[2048,512]{1,0:T(8,128)(2,1)S(1)} %get-tuple-element.76.mixed_ref, ...), custom_call_target="tpu_custom_call", output_to_operand_aliasing={{}: (6, {})} | custom-call | flops 13421772800 | bytes 10485760 | tf_op jit(solution)/shard_map/attend_backward/pallas_call | solution.py:187
  615.5 17.3 %convolution_convert_fusion.5 = bf16[2048,1536]{1,0:T(8,128)(2,1)S(1)} fusion(bf16[2048,2048]{1,0:T(8,128)(2,1)} %constant_dynamic-update-slice_fusion, bf16[2048,1536]{1,0:T(8,128)(2,1)} %attend_backward.3), kind=kOutput, calls=%fused_computation.7 | convolution fusion | flops 12888047616 | bytes 20971520 | tf_op jit(solution)/shard_map/dot_general | solution.py:37
  653.8 12.3 %convolution_convert_fusion = bf16[1536,2048]{1,0:T(8,128)(2,1)S(1)} fusion(bf16[2048,1536]{0,1:T(8,128)(2,1)} %all-gather.5.cloned.1.call-done, bf16[2048,1536]{1,0:T(8,128)(2,1)S(1)} %bitcast.144), kind=kOutput, calls=%fused_computation.2 | convolution fusion | flops 9666822144 | bytes 17301504 | tf_op jit(solution)/shard_map/dot_general | solution.py:31
  666.1 24.7 %collective-permute-done.38 = bf16[256,2048]{1,0:T(8,128)(2,1)S(1)} collective-permute-done((bf16[256,2048]{1,0:T(8,128)(2,1)S(1)}, bf16[256,2048]{1,0:T(8,128)(2,1)S(1)}, u32[]{:S(2)}, u32[]{:S(2)}) %collective-permute-start.38) | collective-permute-done | bytes 1048608 | tf_op jit(solution)/shard_map/ppermute | solution.py:289
  708.0 31.8 %collective-permute-done.41 = bf16[512,2048]{1,0:T(8,128)(2,1)} collective-permute-done((bf16[512,2048]{1,0:T(8,128)(2,1)}, bf16[512,2048]{1,0:T(8,128)(2,1)}, u32[]{:S(2)}, u32[]{:S(2)}) %collective-permute-start.41) | collective-permute-done | bytes 2097184 | tf_op jit(solution)/shard_map/ppermute | solution.py:289
  (367 shorter events, 318.0 us)
Async XLA Ops:
  7.2 100.7 %all-gather.5.cloned.1.call-start = ((), (), s32[]{:S(2)}) async-start(), calls=%async_computation.7 | async-start | bytes 7077888 | tf_op jit(solution)/shard_map/all_gather | solution.py:455
  17.5 168.2 %all-gather.7.cloned.1.call-start = ((), (), s32[]{:S(2)}) async-start(), calls=%async_computation.8 | async-start | bytes 9437184 | tf_op jit(solution)/shard_map/all_gather | solution.py:467
  18.2 255.5 %all-gather.9.cloned.1.call-start = ((), (), s32[]{:S(2)}) async-start(), calls=%async_computation.9 | async-start | bytes 9437184 | tf_op jit(solution)/shard_map/all_gather | solution.py:468
  20.6 324.9 %all-gather.11.cloned.1.call-start = ((), (), s32[]{:S(2)}) async-start(), calls=%async_computation.10 | async-start | bytes 9437184 | tf_op jit(solution)/shard_map/all_gather | solution.py:469
  30.6 47.4 %collective-permute-start = (bf16[256,2048]{1,0:T(8,128)(2,1)}, bf16[256,2048]{1,0:T(8,128)(2,1)}, u32[]{:S(2)}, u32[]{:S(2)}) collective-permute-start(bf16[256,2048]{1,0:T(8,128)(2,1)} %get-tuple-element.186), channel_id=1, source_target_pairs={{0,8},{8,0},{16,24},{24,16},{1,9},{9,1},{17,25},{25,17},{2,10},{10... | collective-permute-start | bytes 3145736 | tf_op jit(solution)/shard_map/ppermute | solution.py:289
  31.1 51.3 %collective-permute-start.3 = (bf16[256,2048]{1,0:T(8,128)(2,1)}, bf16[256,2048]{1,0:T(8,128)(2,1)S(1)}, u32[]{:S(2)}, u32[]{:S(2)}) collective-permute-start(bf16[256,2048]{1,0:T(8,128)(2,1)} %get-tuple-element.185), channel_id=1, source_target_pairs={{0,16},{8,24},{16,0},{24,8},{1,17},{9,25},{17,1},{25,9},{2,18},{10... | collective-permute-start | bytes 3145736 | tf_op jit(solution)/shard_map/ppermute | solution.py:289
  103.8 52.2 %collective-permute-start.7 = (bf16[256,2048]{1,0:T(8,128)(2,1)}, bf16[256,2048]{1,0:T(8,128)(2,1)S(1)}, u32[]{:S(2)}, u32[]{:S(2)}) collective-permute-start(bf16[256,2048]{1,0:T(8,128)(2,1)} %get-tuple-element.183), channel_id=1, source_target_pairs={{0,16},{8,24},{16,0},{24,8},{1,17},{9,25},{17,1},{25,9},{2,18},{10... | collective-permute-start | bytes 3145736 | tf_op jit(solution)/shard_map/ppermute | solution.py:289
  104.1 51.9 %collective-permute-start.8 = (bf16[256,2048]{1,0:T(8,128)(2,1)}, bf16[256,2048]{1,0:T(8,128)(2,1)}, u32[]{:S(2)}, u32[]{:S(2)}) collective-permute-start(bf16[256,2048]{1,0:T(8,128)(2,1)} %get-tuple-element.183), channel_id=1, source_target_pairs={{0,8},{8,0},{16,24},{24,16},{1,9},{9,1},{17,25},{25,17},{2,10},{10... | collective-permute-start | bytes 3145736 | tf_op jit(solution)/shard_map/ppermute | solution.py:289
  105.8 50.2 %collective-permute-start.6 = (bf16[256,2048]{1,0:T(8,128)(2,1)}, bf16[256,2048]{1,0:T(8,128)(2,1)}, u32[]{:S(2)}, u32[]{:S(2)}) collective-permute-start(bf16[256,2048]{1,0:T(8,128)(2,1)} %get-tuple-element.184), channel_id=1, source_target_pairs={{0,8},{8,0},{16,24},{24,16},{1,9},{9,1},{17,25},{25,17},{2,10},{10... | collective-permute-start | bytes 3145736 | tf_op jit(solution)/shard_map/ppermute | solution.py:289
  106.2 49.8 %collective-permute-start.9 = (bf16[256,2048]{1,0:T(8,128)(2,1)}, bf16[256,2048]{1,0:T(8,128)(2,1)}, u32[]{:S(2)}, u32[]{:S(2)}) collective-permute-start(bf16[256,2048]{1,0:T(8,128)(2,1)} %get-tuple-element.184), channel_id=1, source_target_pairs={{0,16},{8,24},{16,0},{24,8},{1,17},{9,25},{17,1},{25,9},{2,18},{10... | collective-permute-start | bytes 3145736 | tf_op jit(solution)/shard_map/ppermute | solution.py:289
  163.3 379.6 %reduce-scatter.5.cloned.1.call-start = ((), (), s32[]{:S(2)}) async-start(), calls=%async_computation.11 | async-start | bytes 9437184 | tf_op jit(solution)/shard_map/reduce_scatter | solution.py:507
  205.7 48.6 %collective-permute-start.16 = (bf16[256,2048]{1,0:T(8,128)(2,1)}, bf16[256,2048]{1,0:T(8,128)(2,1)}, u32[]{:S(2)}, u32[]{:S(2)}) collective-permute-start(bf16[256,2048]{1,0:T(8,128)(2,1)} %get-tuple-element.178), channel_id=1, source_target_pairs={{0,16},{8,24},{16,0},{24,8},{1,17},{9,25},{17,1},{25,9},{2,18},{10... | collective-permute-start | bytes 3145736 | tf_op jit(solution)/shard_map/ppermute | solution.py:289
  345.4 270.1 %reduce-scatter.7.cloned.1.call-start = ((), (), s32[]{:S(2)}) async-start(), calls=%async_computation.12 | async-start | bytes 9437184 | tf_op jit(solution)/shard_map/reduce_scatter | solution.py:507
  345.4 99.3 %collective-permute-start.29 = (bf16[512,1024]{0,1:T(8,128)(2,1)}, bf16[512,1024]{0,1:T(8,128)(2,1)}, u32[]{:S(2)}, u32[]{:S(2)}) collective-permute-start(bf16[512,1024]{0,1:T(8,128)(2,1)} %bitcast.13), channel_id=1, source_target_pairs={{0,1},{1,0},{2,3},{3,2},{4,5},{5,4},{6,7},{7,6},{8,9},{9,8},{10,11... | collective-permute-start | bytes 3145736 | tf_op jit(solution)/shard_map/ppermute | solution.py:481
  442.7 348.7 %reduce-scatter.9.cloned.1.call-start = ((), (), s32[]{:S(2)}) async-start(), calls=%async_computation.13 | async-start | bytes 7077888 | tf_op jit(solution)/shard_map/reduce_scatter | solution.py:507
  442.7 48.8 %collective-permute-start.24 = (bf16[512,2048]{1,0:T(8,128)(2,1)}, bf16[512,2048]{1,0:T(8,128)(2,1)S(1)}, u32[]{:S(2)}, u32[]{:S(2)}) collective-permute-start(bf16[512,2048]{1,0:T(8,128)(2,1)} %pad_maximum_fusion.8), channel_id=1, source_target_pairs={{0,16},{8,24},{16,0},{24,8},{1,17},{9,25},{17,1},{25,9},{2,18},{10... | collective-permute-start | bytes 6291464 | tf_op jit(solution)/shard_map/ppermute | solution.py:289
  443.6 48.8 %collective-permute-start.23 = (bf16[512,2048]{1,0:T(8,128)(2,1)}, bf16[512,2048]{1,0:T(8,128)(2,1)S(1)}, u32[]{:S(2)}, u32[]{:S(2)}) collective-permute-start(bf16[512,2048]{1,0:T(8,128)(2,1)} %pad_maximum_fusion.7), channel_id=1, source_target_pairs={{0,8},{8,0},{16,24},{24,16},{1,9},{9,1},{17,25},{25,17},{2,10},{10... | collective-permute-start | bytes 6291464 | tf_op jit(solution)/shard_map/ppermute | solution.py:289
  457.3 71.8 %collective-permute-start.25 = (bf16[256,2048]{1,0:T(8,128)(2,1)S(1)}, bf16[256,2048]{1,0:T(8,128)(2,1)S(1)}, u32[]{:S(2)}, u32[]{:S(2)}) collective-permute-start(bf16[256,2048]{1,0:T(8,128)(2,1)S(1)} %get-tuple-element.172), channel_id=1, source_target_pairs={{0,8},{8,0},{16,24},{24,16},{1,9},{9,1},{17,25},{25,17},{2,10},{10... | collective-permute-start | bytes 3145736 | tf_op jit(solution)/shard_map/ppermute | solution.py:289
  458.3 70.8 %collective-permute-start.26 = (bf16[256,2048]{1,0:T(8,128)(2,1)S(1)}, bf16[256,2048]{1,0:T(8,128)(2,1)S(1)}, u32[]{:S(2)}, u32[]{:S(2)}) collective-permute-start(bf16[256,2048]{1,0:T(8,128)(2,1)S(1)} %get-tuple-element.171), channel_id=1, source_target_pairs={{0,16},{8,24},{16,0},{24,8},{1,17},{9,25},{17,1},{25,9},{2,18},{10... | collective-permute-start | bytes 3145736 | tf_op jit(solution)/shard_map/ppermute | solution.py:289
  538.9 74.9 %collective-permute-start.28 = (bf16[512,2048]{1,0:T(8,128)(2,1)}, bf16[512,2048]{1,0:T(8,128)(2,1)}, u32[]{:S(2)}, u32[]{:S(2)}) collective-permute-start(bf16[512,2048]{1,0:T(8,128)(2,1)} %pad_maximum_fusion.10), channel_id=1, source_target_pairs={{0,16},{8,24},{16,0},{24,8},{1,17},{9,25},{17,1},{25,9},{2,18},{10... | collective-permute-start | bytes 6291464 | tf_op jit(solution)/shard_map/ppermute | solution.py:289
  541.6 72.2 %collective-permute-start.27 = (bf16[512,2048]{1,0:T(8,128)(2,1)}, bf16[512,2048]{1,0:T(8,128)(2,1)}, u32[]{:S(2)}, u32[]{:S(2)}) collective-permute-start(bf16[512,2048]{1,0:T(8,128)(2,1)} %pad_maximum_fusion.9), channel_id=1, source_target_pairs={{0,8},{8,0},{16,24},{24,16},{1,9},{9,1},{17,25},{25,17},{2,10},{10... | collective-permute-start | bytes 6291464 | tf_op jit(solution)/shard_map/ppermute | solution.py:289
  636.1 162.2 %reduce-scatter.11.cloned.1.call-start = ((), (), s32[]{:S(2)}) async-start(), calls=%async_computation.14 | async-start | bytes 2359296 | tf_op jit(solution)/shard_map/reduce_scatter | solution.py:581
  642.8 54.2 %collective-permute-start.37 = (bf16[256,2048]{1,0:T(8,128)(2,1)S(1)}, bf16[256,2048]{1,0:T(8,128)(2,1)S(1)}, u32[]{:S(2)}, u32[]{:S(2)}) collective-permute-start(bf16[256,2048]{1,0:T(8,128)(2,1)S(1)} %pad_maximum_fusion.17), channel_id=1, source_target_pairs={{0,16},{8,24},{16,0},{24,8},{1,17},{9,25},{17,1},{25,9},{2,18},{10... | collective-permute-start | bytes 3145736 | tf_op jit(solution)/shard_map/ppermute | solution.py:289
  643.9 53.1 %collective-permute-start.36 = (bf16[256,2048]{1,0:T(8,128)(2,1)}, bf16[256,2048]{1,0:T(8,128)(2,1)S(1)}, u32[]{:S(2)}, u32[]{:S(2)}) collective-permute-start(bf16[256,2048]{1,0:T(8,128)(2,1)} %pad_maximum_fusion.16), channel_id=1, source_target_pairs={{0,8},{8,0},{16,24},{24,16},{1,9},{9,1},{17,25},{25,17},{2,10},{10... | collective-permute-start | bytes 3145736 | tf_op jit(solution)/shard_map/ppermute | solution.py:289
  (91 other events, 1906.3 us)
Sparse Core Ops, SparseCore 0:
  17.6 67.8 all-gather.4
  87.1 80.2 all-gather.6
  169.0 80.5 all-gather.8
  251.6 81.0 all-gather.10
  345.5 89.9 reduce-scatter.4
  442.8 89.5 reduce-scatter.6
  636.2 70.2 reduce-scatter.8
  708.9 33.9 reduce-scatter.10

commit v6 on v5

--- a/solution.py
+++ b/solution.py
@@ -169,7 +169,7 @@
             jax.ShapeDtypeStruct((rows, pairs * PAIR), jnp.bfloat16),
             jax.ShapeDtypeStruct((rows, pairs * PAIR), jnp.float32),
         ],
-        compiler_params=pltpu.CompilerParams(vmem_limit_bytes=40 * 2**20),
+        compiler_params=pltpu.CompilerParams(vmem_limit_bytes=24 * 2**20),
         cost_estimate=pl.CostEstimate(
             flops=scored * 2 * 512, bytes_accessed=rows * pairs * PAIR * 12, transcendentals=scored
         ),
@@ -195,7 +195,7 @@
         ),
         out_shape=jax.ShapeDtypeStruct((rows, width), jnp.bfloat16),
         input_output_aliases={6: 0} if earlier else {},
-        compiler_params=pltpu.CompilerParams(vmem_limit_bytes=40 * 2**20),
+        compiler_params=pltpu.CompilerParams(vmem_limit_bytes=24 * 2**20),
         cost_estimate=pl.CostEstimate(
             flops=scored * 2 * 1280,
             bytes_accessed=rows * (stop - start) * PAIR * 20,
@@ -203,6 +203,16 @@
         ),
         name="attend_backward",
     )(mask, slopes, qkv, lse, mixed, grad, *earlier)
+
+
+def head_columns_kernel(at_ref, in_ref, out_ref):
+    for t in range(3):
+
+        @pl.when(pl.program_id(0) == t)
+        def _():
+            for pair in range(in_ref.shape[1] // PAIR):
+                at = (pair * 3 + t) * PAIR
+                out_ref[:, at : at + PAIR] = in_ref[:, pair * PAIR : (pair + 1) * PAIR]
 
 
 def up_kernel(rows_ref, weight_ref, bias_ref, active_ref, slope_ref, *, chunk):
@@ -227,7 +237,7 @@
         sum_ref[:, columns] = jnp.where(starting, part, sum_ref[:, columns] + part)
 
 
-TILE = 512
+TILE = 256
 
 
 def up_and_bend(rows, weight, bias):
@@ -235,11 +245,11 @@
     width = weight.shape[1]
     tile = pl.BlockSpec((TILE, width), lambda i: (i, 0))
     return pl.pallas_call(
-        partial(up_kernel, chunk=TILE),
+        partial(up_kernel, chunk=512),
         grid=(count // TILE,),
         in_specs=[
             pl.BlockSpec((TILE, depth), lambda i: (i, 0)),
-            pl.BlockSpec((depth, width), lambda i: (0, 0)),
+            pl.BlockSpec((depth, width), lambda i: (0, 0), pipeline_mode=pl.Buffered(1)),
             pl.BlockSpec((1, width), lambda i: (0, 0)),
         ],
         out_specs=[tile, tile],
@@ -247,7 +257,7 @@
             jax.ShapeDtypeStruct((count, width), jnp.bfloat16),
             jax.ShapeDtypeStruct((count, width), jnp.float32),
         ],
-        compiler_params=pltpu.CompilerParams(vmem_limit_bytes=48 * 2**20),
+        compiler_params=pltpu.CompilerParams(vmem_limit_bytes=28 * 2**20),
         cost_estimate=pl.CostEstimate(
             flops=count * depth * width * 4,
             bytes_accessed=2 * count * depth + 2 * depth * width + 6 * count * width,
@@ -263,11 +273,11 @@
     tile = pl.BlockSpec((TILE, width), lambda i: (i, 0))
     line = pl.BlockSpec((1, width), lambda i: (0, 0))
     return pl.pallas_call(
-        partial(hidden_grad_kernel, chunk=TILE),
+        partial(hidden_grad_kernel, chunk=512),
         grid=(count // TILE,),
         in_specs=[
             pl.BlockSpec((TILE, depth), lambda i: (i, 0)),
-            pl.BlockSpec((width, depth), lambda i: (0, 0)),
+            pl.BlockSpec((width, depth), lambda i: (0, 0), pipeline_mode=pl.Buffered(1)),
             tile,
         ],
         out_specs=[tile, line],
@@ -275,7 +285,7 @@
             jax.ShapeDtypeStruct((count, width), jnp.bfloat16),
             jax.ShapeDtypeStruct((1, width), jnp.float32),
         ],
-        compiler_params=pltpu.CompilerParams(vmem_limit_bytes=48 * 2**20),
+        compiler_params=pltpu.CompilerParams(vmem_limit_bytes=28 * 2**20),
         cost_estimate=pl.CostEstimate(
             flops=count * depth * width * 3,
             bytes_accessed=2 * count * depth + 2 * depth * width + 6 * count * width,
@@ -283,6 +293,39 @@
         ),
         name="hidden_gradient",
     )(rows, weight, slope)
+
+
+def outer_kernel(left_ref, right_ref, out_ref, *, chunk):
+    left = left_ref[...]
+    shards = out_ref.shape[0]
+    for at in range(0, right_ref.shape[1], chunk):
+        columns = slice(at, at + chunk)
+        made = contract_first(left, right_ref[:, columns]).astype(out_ref.dtype)
+        out_ref[:, 0, :, columns] = made.reshape(shards, -1, made.shape[1])
+
+
+def outer(left, right, groups, shards):
+    tokens, rows = left.shape
+    width = right.shape[1]
+    part = rows // groups
+    made = pl.pallas_call(
+        partial(outer_kernel, chunk=512 if width % 512 == 0 else 256),
+        grid=(groups,),
+        in_specs=[
+            pl.BlockSpec((tokens, part), lambda i: (0, i)),
+            pl.BlockSpec((tokens, width), lambda i: (0, 0), pipeline_mode=pl.Buffered(1)),
+        ],
+        out_specs=pl.BlockSpec((shards, 1, part // shards, width), lambda i: (0, i, 0, 0)),
+        out_shape=jax.ShapeDtypeStruct((shards, groups, part // shards, width), jnp.bfloat16),
+        compiler_params=pltpu.CompilerParams(vmem_limit_bytes=28 * 2**20),
+        cost_estimate=pl.CostEstimate(
+            flops=2 * tokens * rows * width,
+            bytes_accessed=2 * (tokens * rows + tokens * width + rows * width),
+            transcendentals=0,
+        ),
+        name="outer",
+    )(left, right)
+    return made.reshape(rows, width)
 
 
 def swap(values, bit):
@@ -334,6 +377,20 @@
         top, bottom = rows
         return rows, (swap(bottom, 1), swap(top, 2), swap(top, 1), swap(bottom, 2))
 
+    def fill(self, pieces):
+        if not isinstance(pieces, list):
+            return pieces
+        count = sum(piece.shape[0] for piece in pieces[:-2])
+        rows = pieces[-1].shape[0]
+        room = jnp.zeros((2 * rows, pieces[0].shape[1]), pieces[0].dtype)
+        made = self(lambda *parts: jnp.concatenate([*parts, room], axis=0), *pieces[:-2])
+
+        def put(before, first, second):
+            before = lax.dynamic_update_slice_in_dim(before, first, count, axis=0)
+            return lax.dynamic_update_slice_in_dim(before, second, count + rows, axis=0)
+
+        return lambda: self(put, made, *pieces[-2:])
+
     def pass_on(self, begun, *before):
         rows, came = begun
         if came is None:
@@ -345,7 +402,7 @@
         far = [swap(second_top, 1), swap(first_bottom, 2)]
         return [*rows, first_top, first_bottom, second_top, second_bottom, *far]
 
-    def send_far(self, product, rows, axis=0):
+    def send_far(self, product, rows, axis=0, held=False):
         if lax.axis_size("seq") != 4:
             return product, rows, axis, None
         count = rows.shape[axis] // 4
@@ -356,7 +413,14 @@
             return made[:half], made[half:]
 
         top, bottom = self(far_half, rows)
-        return product, rows, axis, (swap(top, 1), swap(bottom, 2))
+        return product, rows, axis, (top, bottom) if held else (swap(top, 1), swap(bottom, 2))
+
+    def send_held(self, begun, *before):
+        if begun[1] is None:
+            return begun
+        rest, parts = begun
+        top, bottom = gate(parts, *before)
+        return rest, (swap(top, 1), swap(bottom, 2))
 
     def make_rest(self, begun):
         product, rows, axis, parts = begun
@@ -401,9 +465,13 @@
 def total(values):
     for axis in ("fsdp", "seq"):
         count, bit = lax.axis_size(axis), 1
+        bits = count.bit_length() - 1
         while bit < count:
-            values = values + lax.ppermute(values, axis, [(i, i ^ bit) for i in range(count)])
-            bit *= 2
+            masks = [bit] if bits % 2 else [bit, 2 * bit, 3 * bit]
+            came = [lax.ppermute(values, axis, [(i, i ^ mask) for i in range(count)]) for mask in masks]
+            values = sum(came, values)
+            bit <<= 1 if bits % 2 else 2
+            bits -= bits % 2
     return values
 
 
@@ -439,9 +507,18 @@
     slopes = 2.0 ** (-8.0 * head_index.astype(wide) / HEADS)
 
     def head_columns(values):
-        split = values.reshape(-1, 3, groups, pairs, PAIR)
-        mine = lax.dynamic_index_in_dim(split, me, axis=2, keepdims=False)
-        return jnp.swapaxes(mine, 1, 2).reshape(values.shape[0], -1)
+        rows = values.shape[0]
+        return pl.pallas_call(
+            head_columns_kernel,
+            grid_spec=pltpu.PrefetchScalarGridSpec(
+                num_scalar_prefetch=1,
+                grid=(3,),
+                in_specs=[pl.BlockSpec((rows, slab), lambda t, at: (0, t * groups + at[0]))],
+                out_specs=pl.BlockSpec((rows, 3 * slab), lambda t, at: (0, 0)),
+            ),
+            out_shape=jax.ShapeDtypeStruct((rows, 3 * slab), values.dtype),
+            name="head_columns",
+        )(jnp.reshape(me, (1,)).astype(jnp.int32), values)
 
     def own_slab(values, axis):
         width = values.shape[axis] // groups
@@ -465,8 +542,8 @@
     normed = order.gather(order(halves_of, first_norm))
     normed = order.pass_on(normed)
     full_out = lax.all_gather(w_out, "fsdp", axis=0, tiled=True)
-    up_slab = lax.all_gather(own_slab(w_up, 1), "fsdp", axis=0, tiled=True)
-    down_slab = lax.all_gather(own_slab(w_down, 0), "fsdp", axis=1, tiled=True)
+    up_slab = lax.all_gather(own_slab(gate(w_up, normed[0]) if square else w_up, 1), "fsdp", axis=0, tiled=True)
+    down_slab = lax.all_gather(own_slab(gate(w_down, normed[0]) if square else w_down, 0), "fsdp", axis=1, tiled=True)
     normed = whole(normed)
     upstream = order.gather(halves_of(gate(dz_low, normed)))
     qkv = order(lambda rows: (contract(rows, qkv_slab) + qkv_bias).astype(low), normed)
@@ -494,16 +571,17 @@
     second_norm, second_back = jax.vjp(layer_norm, middle, ln2_gain, ln2_shift)
     second = order.gather(order(halves_of, second_norm))
     mine, theirs = order(pair_halves, mixed_slots)
-    mixed_half = jnp.concatenate([mine, pair_swap(theirs)], axis=0)
+    theirs = pair_swap(theirs)
     second = whole(order.pass_on(second))
-    upstream = order.pass_on(upstream, second)
+    upstream = order.fill(order.pass_on(upstream, second))
+    mixed_half = order(lambda *parts: jnp.concatenate(parts, axis=0), mine, theirs)
     active, slope = order(lambda rows: up_and_bend(rows, up_slab, up_bias_slab[None]), second)
-    upstream = whole(upstream)
-
-    def slab_sum(left, right):
-        made = order(lambda rows: contract_first(rows, right).astype(low), left)
-        width = made.shape[1]
-        made = jnp.swapaxes(made.reshape(groups, shards, -1, width), 0, 1).reshape(-1, width)
+    upstream = upstream() if callable(upstream) else upstream
+
+    def slab_product(left, right):
+        return order(lambda rows: outer(rows, right, groups, shards), left)
+
+    def slab_sum(made):
         return lax.psum_scatter(made, "fsdp", scatter_dimension=0, tiled=True)
 
     def slabs_of_rows(values, *before):
@@ -512,7 +590,7 @@
         slabs = lax.all_to_all(values, "seq", split_axis=0, concat_axis=0, tiled=True)
         return jnp.swapaxes(slabs, 0, 1).astype(wide)
 
-    down_sum = slab_sum(upstream, active)
+    down_sum = slab_sum(slab_product(upstream, active))
 
     hidden_grad, hidden_sum = order(lambda rows: hidden_gradient(rows, down_slab, slope), upstream)
 
@@ -520,12 +598,15 @@
         return contract_last(rows, up_slab).astype(low)
 
     second_grad = order.add_far(order.make_rest(order.send_far(to_second, hidden_grad)))
-    up_sum = slab_sum(second, hidden_grad)
-
     def to_result(rows):
         return contract(rows, down_slab).astype(low)
 
-    outcome = order.send_far(to_result, active)
+    outcome = order.send_far(to_result, active, held=True)
+    up_sum = slab_product(second, hidden_grad)
+    if square:
+        up_sum = gate(up_sum, *second_grad[1])
+    up_sum = slab_sum(up_sum)
+
 
     def to_middle(own, came):
         middle_part, gain_grad, shift_grad = second_back(summed(own, came))
@@ -544,32 +625,22 @@
     early = [column_sum(branch_grad), ln2_gain_grad, ln2_shift_grad, hidden_sum, column_sum(dz)]
     mixed_grad = order(lambda rows: contract_last(rows, full_out).astype(low), branch_grad)
     mixed_grad = exchange(by_index([mixed_grad[:, j * slab : (j + 1) * slab] for j in range(groups)], me))
-    outcome = order.add_far(order.make_rest(outcome))
+    outcome = order.make_rest(outcome)
+    branch_pair = jnp.concatenate([branch_grad, pair_swap(branch_grad)], axis=0)
+
+    def to_out(columns):
+        return contract_first(columns, branch_pair).astype(low)
+    out_begun = order.make_rest(order.send_far(to_out, mixed_half, axis=1))
     mixed_grad = jnp.concatenate(mixed_grad, axis=0)
+    outcome = order.send_held(outcome, mixed_grad)
     order.after(down_sum)
     attention = (mask, slopes, qkv, log_totals, attended)
     begun = order(lambda rows: attend_backward(*attention, rows, seq_count, local_len, 0, pairs // 2), mixed_grad)
-    branch_pair = jnp.concatenate([branch_grad, pair_swap(gate(branch_grad, mixed_grad))], axis=0)
-
-    def to_out(columns):
-        return contract_first(columns, branch_pair).astype(low)
-
-    out_begun = order.make_rest(order.send_far(to_out, mixed_half, axis=1))
+    outcome = order.add_far(outcome)
+    out_begun = order.add_far(out_begun)
     qkv_grad = order(
         lambda rows: attend_backward(*attention, rows, seq_count, local_len, pairs // 2, pairs, begun), mixed_grad
     )
-    if square:
-        order.after(*outcome[1])
-    out_begun = order.add_far(out_begun)
-    order.after(up_sum)
-    qkv_sum = slab_sum(normed, qkv_grad)
-
-    def to_normed(rows):
-        return contract_last(rows, qkv_slab).astype(low)
-
-    normed_grad = order.send_far(to_normed, qkv_grad)
-    normed_grad = order.make_rest(normed_grad)
-    normed_grad = order.add_far(normed_grad)
     out_sum = order(
         lambda own, *came: summed(own, came or None).astype(low), out_begun[0], *(out_begun[1] or ())
     ).reshape(-1, 1, out_rows, model_width)
@@ -577,8 +648,18 @@
     out_sum = jnp.concatenate(
         [jnp.where(parity == 0, out_sum, zero), jnp.where(parity == 1, out_sum, zero)], axis=1
     ).reshape(-1, model_width)
-
     grad_w_out = lax.psum_scatter(out_sum, "fsdp", scatter_dimension=0, tiled=True).astype(wide)
+    order.after(up_sum)
+
+    def to_normed(rows):
+        return contract_last(rows, qkv_slab).astype(low)
+
+    normed_grad = order.send_far(to_normed, qkv_grad)
+    qkv_sum = slab_product(normed, qkv_grad)
+    qkv_sum = slab_sum(gate(qkv_sum, grad_w_out, *(outcome[1] or ())))
+    order.after(grad_w_out, *(outcome[1] or ()))
+    normed_grad = order.make_rest(normed_grad)
+    normed_grad = order.add_far(normed_grad)
     result = order(
         lambda own, *came: (middle + (summed(own, came or None) + down_bias)).astype(low),
         outcome[0],
@@ -593,8 +674,8 @@
         lambda own, *came: to_input(own, came or None), normed_grad[0], *(normed_grad[1] or ())
     )
     grad_tokens = grad_tokens.reshape(tokens.shape)
-    grad_w_down = slabs_of_rows(down_sum, grad_tokens).reshape(-1, hidden_width).T
-    grad_w_up = slabs_of_rows(up_sum, grad_tokens).reshape(-1, hidden_width)
+    grad_w_down = slabs_of_rows(down_sum, *(normed_grad[1] or ())).reshape(-1, hidden_width).T
+    grad_w_up = slabs_of_rows(up_sum, *(normed_grad[1] or ())).reshape(-1, hidden_width)
     grad_w_qkv = slabs_of_rows(qkv_sum).reshape(-1, groups, pairs, 3, PAIR)
     grad_w_qkv = jnp.transpose(grad_w_qkv, (0, 3, 1, 2, 4)).reshape(-1, 3 * model_width)
 

time: 830 us -> 803 us (0.967)
  matrix products: 176 us -> 112 us
  Pallas kernels: 141 us -> 189 us
  waiting for transfers between devices: 249 us -> 218 us
  local copies, waits for them, and re-layouts: 110 us -> 125 us
    dot_general x5 -> x2, matrix products: 70.7 us -> 11.5 us  [contract_first(): lax.dot_general(left_side, right_side, (((0,), (0,)), ((), ())), preferre...]
    pallas_call x2 -> x7, Pallas kernels: 55.8 us -> 108 us  [the longest x3 54.6 us: outer(): pl.pallas_call(partial(outer_kernel, chunk=512 if width % 512 == 0 else 2...]
    unnamed x142 -> x160, local copies, waits for them, and re-layouts: 42.9 us -> 75.7 us
    ppermute x40, waiting for transfers between devices: 223 us -> 192 us  [swap(): return lax.ppermute(values, 'seq', [(i, i ^ bit) for i in range(4)])]
    reshape x5 -> x1, local copies, waits for them, and re-layouts: 28.8 us -> 1.47 us  [local(): slabs_of_rows(up_sum, *(normed_grad[1] or ())).reshape(-1, hidden_width)]
  transfers between devices with their start and end apart: 58 -> 60, of which waited for: 22 -> 24; matrix products, arithmetic and copies ran while one was open for 37% -> 32% of each run, Pallas kernels for 17% -> 23%
where the time goes in v6:
time: 803 us; the launch traced here: 793 us
  waiting for transfers between devices  218 us (27%)
  Pallas kernels  189 us (24%)
  local copies, waits for them, and re-layouts  125 us (16%)
  matrix products  112 us (14%)
  other arithmetic  68.9 us (9%)
  starting transfers between devices  64.3 us (8%)
  between operations  15.6 us (2%)
    ppermute x40, waiting for transfers between devices, swap(): return lax.ppermute(values, 'seq', [(i, i ^ bit) for i in range(4)])  192 us
    unnamed x160, local copies, waits for them, and re-layouts  75.7 us
    pallas_call x3, Pallas kernels, outer(): pl.pallas_call(partial(outer_kernel, chunk=512 if width % 512 == 0 else 2...  54.6 us
    pallas_call x2, Pallas kernels, attend_backward(): pl.pallas_call(partial(attend_backward_kernel, blocks=blocks, seqs=seqs,...  52.7 us
    dot_general x5, matrix products, contract_last(): lax.dot_general(left_side, right_side, (((1,), (1,)), ((), ())), preferre...  51.6 us
    dot_general x4, matrix products, contract(): lax.dot_general(left_side, right_side, (((1,), (0,)), ((), ())), preferre...  48.5 us
    ppermute x40, starting transfers between devices, swap(): return lax.ppermute(values, 'seq', [(i, i ^ bit) for i in range(4)])  44.4 us
    pallas_call x1, Pallas kernels, attend_forward(): pl.pallas_call(partial(attend_forward_kernel, blocks=blocks, seqs=seqs, l...  28.6 us
  transfers between devices with their start and end apart: 60, of which 24 were waited for; matrix products, arithmetic and copies ran while one was open for 32% of the time, Pallas kernels for 23%

profile of v6, /device:TPU:0, one launch (start us, length us, event | category | flops | bytes accessed | tf_op | source)
XLA Modules:
  0.0 792.6 jit_solution(3322647774467920768)
XLA Ops:
  27.1 19.1 %collective-permute-done.2 = bf16[256,2048]{1,0:T(8,128)(2,1)S(1)} collective-permute-done((bf16[256,2048]{1,0:T(8,128)(2,1)}, bf16[256,2048]{1,0:T(8,128)(2,1)S(1)}, u32[]{:S(2)}, u32[]{:S(2)}) %collective-permute-start.2) | collective-permute-done | bytes 1048608 | tf_op jit(solution)/shard_map/ppermute | solution.py:332
  52.5 18.3 %collective-permute-done = bf16[256,2048]{1,0:T(8,128)(2,1)} collective-permute-done((bf16[256,2048]{1,0:T(8,128)(2,1)}, bf16[256,2048]{1,0:T(8,128)(2,1)}, u32[]{:S(2)}, u32[]{:S(2)}) %collective-permute-start) | collective-permute-done | bytes 1048608 | tf_op jit(solution)/shard_map/ppermute | solution.py:332
  76.4 15.5 %collective-permute-done.4 = bf16[256,2048]{1,0:T(8,128)(2,1)} collective-permute-done((bf16[256,2048]{1,0:T(8,128)(2,1)S(1)}, bf16[256,2048]{1,0:T(8,128)(2,1)}, u32[]{:S(2)}, u32[]{:S(2)}) %collective-permute-start.4) | collective-permute-done | bytes 1048608 | tf_op jit(solution)/shard_map/ppermute | solution.py:332
  100.5 17.3 %add_convert_fusion.qkv_ref = bf16[2048,1536]{1,0:T(8,128)(2,1)S(1)} fusion(bf16[2048,2048]{1,0:T(8,128)(2,1)} %constant_dynamic-update-slice_fusion.left_ref, bf16[2048,1536]{1,0:T(8,128)(2,1)} %all-gather.5.cloned.1.call-done, f32[1536]{0:T(1024)S(1)} %reduce.3), kind=kOutput, calls=%fused_computation.1 | convolution fusion | flops 12891193344 | bytes 20977664 | tf_op jit(solution)/shard_map/dot_general | solution.py:25
  117.8 28.6 %attend_forward.1 = (bf16[2048,512]{1,0:T(8,128)(2,1)S(1)}, f32[2048,512]{1,0:T(8,128)S(1)}) custom-call(s32[1]{0:T(128)} %bitcast.1.at_ref.mask_ref, f32[8]{0:T(128)S(1)} %multiply_power_fusion.slope_ref, bf16[2048,1536]{1,0:T(8,128)(2,1)S(1)} %add_convert_fusion.qkv_ref), custom_call_target="tpu_custom_call" | custom-call | flops 10737418240 | bytes 12582912 | tf_op jit(solution)/shard_map/attend_forward/pallas_call | solution.py:160
  153.1 12.6 %collective-permute-done.10 = bf16[512,512]{1,0:T(8,128)(2,1)} collective-permute-done((bf16[512,512]{1,0:T(8,128)(2,1)}, bf16[512,512]{1,0:T(8,128)(2,1)}, u32[]{:S(2)}, u32[]{:S(2)}) %collective-permute-start.10) | collective-permute-done | bytes 524320 | tf_op jit(solution)/shard_map/ppermute | solution.py:332
  178.6 9.4 %fusion.42 = (f32[512]{0:T(512)S(1)}, f32[512,2048]{1,0:T(8,128)S(1)}) fusion(f32[2048]{0:T(1024)S(1)} %copy-done.53, bf16[512,2048]{1,0:T(8,128)(2,1)} %get-tuple-element.94, bf16[2048,2048]{1,0:T(8,128)(2,1)} %all-gather.7.cloned.1.call-done, bf16[2,256,2048]{2,1,0:T(8,128)(2,1)} %param.14), kind=kOutput, calls=%fused_computation.170 | convolution fusion | flops 4299161088 | bytes 16787456 | tf_op jit(solution)/shard_map/dot_general | solution.py:25
  203.9 14.5 %collective-permute-done.15 = bf16[256,2048]{1,0:T(8,128)(2,1)} collective-permute-done((bf16[256,2048]{1,0:T(8,128)(2,1)}, bf16[256,2048]{1,0:T(8,128)(2,1)}, u32[]{:S(2)}, u32[]{:S(2)}) %collective-permute-start.15) | collective-permute-done | bytes 1048608 | tf_op jit(solution)/shard_map/ppermute | solution.py:332
  222.4 19.1 %collective-permute-done.13 = bf16[256,2048]{1,0:T(8,128)(2,1)} collective-permute-done((bf16[256,2048]{1,0:T(8,128)(2,1)}, bf16[256,2048]{1,0:T(8,128)(2,1)}, u32[]{:S(2)}, u32[]{:S(2)}) %collective-permute-start.13) | collective-permute-done | bytes 1048608 | tf_op jit(solution)/shard_map/ppermute | solution.py:332
  250.9 11.7 %collective-permute-done.17 = bf16[256,2048]{1,0:T(8,128)(2,1)S(1)} collective-permute-done((bf16[256,2048]{1,0:T(8,128)(2,1)}, bf16[256,2048]{1,0:T(8,128)(2,1)S(1)}, u32[]{:S(2)}, u32[]{:S(2)}) %collective-permute-start.17) | collective-permute-done | bytes 1048608 | tf_op jit(solution)/shard_map/ppermute | solution.py:332
  289.8 26.4 %up_and_bend.1 = (bf16[2048,2048]{1,0:T(8,128)(2,1)S(1)}, f32[2048,2048]{1,0:T(8,128)}) custom-call(bf16[2048,2048]{1,0:T(8,128)(2,1)S(1)} %copy-done.6, bf16[2048,2048]{1,0:T(8,128)(2,1)S(1)} %copy-done.9, f32[1,2048]{1,0:T(1,128)S(1)} %bitcast.111), custom_call_target="tpu_custom_call" | custom-call | flops 34359738368 | bytes 41943040 | tf_op jit(solution)/shard_map/up_and_bend/pallas_call | solution.py:247
  322.1 20.2 %outer.3 = bf16[8,4,64,2048]{3,2,1,0:T(8,128)(2,1)S(1)} custom-call(bf16[2048,2048]{1,0:T(8,128)(2,1)} %constant_dynamic-update-slice_fusion.31.left_ref.rows_ref, bf16[2048,2048]{1,0:T(8,128)(2,1)S(1)} %get-tuple-element.130.right_ref), custom_call_target="tpu_custom_call" | custom-call | flops 17179869184 | bytes 25165824 | tf_op jit(solution)/shard_map/outer/pallas_call | solution.py:311
  349.1 21.9 %hidden_gradient.1 = (bf16[2048,2048]{1,0:T(8,128)(2,1)S(1)}, f32[1,2048]{1,0:T(1,128)S(1)}) custom-call(bf16[2048,2048]{1,0:T(8,128)(2,1)} %constant_dynamic-update-slice_fusion.31.left_ref.rows_ref, bf16[2048,2048]{1,0:T(8,128)(2,1)S(1)} %copy-done.8, f32[2048,2048]{1,0:T(8,128)} %get-tuple-element.110.slope_ref), custom_call_target="tpu_custom_call" | custom-call | flops 25769803776 | bytes 41943040 | tf_op jit(solution)/shard_map/hidden_gradient/pallas_call | solution.py:275
  381.8 16.6 %convolution_convert_fusion.2 = bf16[1536,2048]{1,0:T(8,128)(2,1)} fusion(bf16[2048,2048]{1,0:T(8,128)(2,1)S(1)} %copy-done.10, bf16[2048,2048]{1,0:T(8,128)(2,1)} %copy-done.13), kind=kOutput, calls=%fused_computation.4 | convolution fusion | flops 12888047616 | bytes 20971520 | tf_op jit(solution)/shard_map/dot_general | solution.py:31
  422.5 19.4 %outer.4 = bf16[8,4,64,2048]{3,2,1,0:T(8,128)(2,1)S(1)} custom-call(bf16[2048,2048]{1,0:T(8,128)(2,1)S(1)} %bitcast.109, bf16[2048,2048]{1,0:T(8,128)(2,1)S(1)} %copy-done.14), custom_call_target="tpu_custom_call" | custom-call | flops 17179869184 | bytes 25165824 | tf_op jit(solution)/shard_map/outer/pallas_call | solution.py:311
  445.3 8.7 %collective-permute-done.25 = bf16[512,2048]{1,0:T(8,128)(2,1)} collective-permute-done((bf16[512,2048]{1,0:T(8,128)(2,1)S(1)}, bf16[512,2048]{1,0:T(8,128)(2,1)}, u32[]{:S(2)}, u32[]{:S(2)}) %collective-permute-start.25) | collective-permute-done | bytes 2097184 | tf_op jit(solution)/shard_map/ppermute | solution.py:332
  470.2 8.9 %convolution_convert_fusion.5 = bf16[512,2048]{1,0:T(8,128)(2,1)S(1)} fusion(bf16[512,2048]{1,0:T(8,128)(2,1)} %get-tuple-element.129, bf16[2048,2048]{1,0:T(8,128)(2,1)} %all-gather.7.cloned.1.call-done), kind=kOutput, calls=%fused_computation.39 | convolution fusion | flops 4296015872 | bytes 12582912 | tf_op jit(solution)/shard_map/dot_general | solution.py:31
  482.9 15.2 %convolution_convert_fusion.1 = bf16[1536,2048]{1,0:T(8,128)(2,1)} fusion(bf16[2048,2048]{1,0:T(8,128)(2,1)S(1)} %bitcast.115, bf16[2048,2048]{1,0:T(8,128)(2,1)S(1)} %bitcast.119), kind=kOutput, calls=%fused_computation.3 | convolution fusion | flops 12888047616 | bytes 20971520 | tf_op jit(solution)/shard_map/dot_general | solution.py:25
  530.5 26.5 %attend_backward.2.rest_0_ = bf16[2048,1536]{1,0:T(8,128)(2,1)S(1)} custom-call(s32[1]{0:T(128)} %bitcast.1.at_ref.mask_ref, f32[8]{0:T(128)S(1)} %copy-done.12, bf16[2048,1536]{1,0:T(8,128)(2,1)S(1)} %copy-done.16, f32[2048,512]{1,0:T(8,128)S(1)} %copy-done.19, bf16[2048,512]{1,0:T(8,128)(2,1)S(1)} %get-tuple-element.92.mixed_ref, ...), custom_call_target="tpu_custom_call" | custom-call | flops 13421772800 | bytes 10485760 | tf_op jit(solution)/shard_map/attend_backward/pallas_call | solution.py:187
  567.1 26.1 %attend_backward.3.right_ref = bf16[2048,1536]{1,0:T(8,128)(2,1)S(1)} custom-call(s32[1]{0:T(128)} %bitcast.1.at_ref.mask_ref, f32[8]{0:T(128)S(1)} %copy-done.12, bf16[2048,1536]{1,0:T(8,128)(2,1)S(1)} %bitcast.117, f32[2048,512]{1,0:T(8,128)S(1)} %copy-done.19, bf16[2048,512]{1,0:T(8,128)(2,1)S(1)} %get-tuple-element.92.mixed_ref, ...), custom_call_target="tpu_custom_call", output_to_operand_aliasing={{}: (6, {})} | custom-call | flops 13421772800 | bytes 10485760 | tf_op jit(solution)/shard_map/attend_backward/pallas_call | solution.py:187
  611.6 15.0 %outer.5 = bf16[8,4,64,1536]{3,2,1,0:T(8,128)(2,1)S(1)} custom-call(bf16[2048,2048]{1,0:T(8,128)(2,1)S(1)} %copy-done.7, bf16[2048,1536]{1,0:T(8,128)(2,1)S(1)} %copy-done.4), custom_call_target="tpu_custom_call" | custom-call | flops 12884901888 | bytes 20971520 | tf_op jit(solution)/shard_map/outer/pallas_call | solution.py:311
  635.1 8.4 %collective-permute-done.33 = bf16[512,2048]{1,0:T(8,128)(2,1)} collective-permute-done((bf16[512,2048]{1,0:T(8,128)(2,1)S(1)}, bf16[512,2048]{1,0:T(8,128)(2,1)}, u32[]{:S(2)}, u32[]{:S(2)}) %collective-permute-start.33) | collective-permute-done | bytes 2097184 | tf_op jit(solution)/shard_map/ppermute | solution.py:332
  646.9 13.5 %convolution_convert_fusion = bf16[1536,2048]{1,0:T(8,128)(2,1)S(1)} fusion(bf16[2048,1536]{1,0:T(8,128)(2,1)} %all-gather.5.cloned.1.call-done, bf16[2048,1536]{1,0:T(8,128)(2,1)} %copy-done.3), kind=kOutput, calls=%fused_computation.2 | convolution fusion | flops 9666822144 | bytes 17301504 | tf_op jit(solution)/shard_map/dot_general | solution.py:31
  682.2 30.9 %collective-permute-done.41 = bf16[512,2048]{1,0:T(8,128)(2,1)} collective-permute-done((bf16[512,2048]{1,0:T(8,128)(2,1)}, bf16[512,2048]{1,0:T(8,128)(2,1)}, u32[]{:S(2)}, u32[]{:S(2)}) %collective-permute-start.41) | collective-permute-done | bytes 2097184 | tf_op jit(solution)/shard_map/ppermute | solution.py:332
  (385 shorter events, 353.2 us)
Async XLA Ops:
  7.2 93.3 %all-gather.5.cloned.1.call-start = ((), (), s32[]{:S(2)}) async-start(), calls=%async_computation.7 | async-start | bytes 7077888 | tf_op jit(solution)/shard_map/all_gather | solution.py:532
  10.3 168.3 %all-gather.7.cloned.1.call-start = ((), (), s32[]{:S(2)}) async-start(), calls=%async_computation.8 | async-start | bytes 9437184 | tf_op jit(solution)/shard_map/all_gather | solution.py:544
  11.1 271.9 %all-gather.9.cloned.1.call-start = ((), (), s32[]{:S(2)}) async-start(), calls=%async_computation.9 | async-start | bytes 9437184 | tf_op jit(solution)/shard_map/all_gather | solution.py:545
  18.9 326.8 %all-gather.11.cloned.1.call-start = ((), (), s32[]{:S(2)}) async-start(), calls=%async_computation.10 | async-start | bytes 9437184 | tf_op jit(solution)/shard_map/all_gather | solution.py:546
  23.5 47.4 %collective-permute-start = (bf16[256,2048]{1,0:T(8,128)(2,1)}, bf16[256,2048]{1,0:T(8,128)(2,1)}, u32[]{:S(2)}, u32[]{:S(2)}) collective-permute-start(bf16[256,2048]{1,0:T(8,128)(2,1)} %get-tuple-element.218), channel_id=1, source_target_pairs={{0,8},{8,0},{16,24},{24,16},{1,9},{9,1},{17,25},{25,17},{2,10},{10... | collective-permute-start | bytes 3145736 | tf_op jit(solution)/shard_map/ppermute | solution.py:332
  24.0 51.3 %collective-permute-start.3 = (bf16[256,2048]{1,0:T(8,128)(2,1)}, bf16[256,2048]{1,0:T(8,128)(2,1)S(1)}, u32[]{:S(2)}, u32[]{:S(2)}) collective-permute-start(bf16[256,2048]{1,0:T(8,128)(2,1)} %get-tuple-element.217), channel_id=1, source_target_pairs={{0,16},{8,24},{16,0},{24,8},{1,17},{9,25},{17,1},{25,9},{2,18},{10... | collective-permute-start | bytes 3145736 | tf_op jit(solution)/shard_map/ppermute | solution.py:332
  26.4 497.5 %reduce-scatter.5.cloned.1.call-start = ((), (), s32[]{:S(2)}) async-start(), calls=%async_computation.11 | async-start | bytes 9437184 | tf_op jit(solution)/shard_map/reduce_scatter | solution.py:585
  46.2 45.7 %collective-permute-start.4 = (bf16[256,2048]{1,0:T(8,128)(2,1)S(1)}, bf16[256,2048]{1,0:T(8,128)(2,1)}, u32[]{:S(2)}, u32[]{:S(2)}) collective-permute-start(bf16[256,2048]{1,0:T(8,128)(2,1)S(1)} %collective-permute-done.2), channel_id=1, source_target_pairs={{0,8},{8,0},{16,24},{24,16},{1,9},{9,1},{17,25},{25,17},{2,10},{10... | collective-permute-start | bytes 3145736 | tf_op jit(solution)/shard_map/ppermute | solution.py:332
  96.4 52.0 %collective-permute-start.7 = (bf16[256,2048]{1,0:T(8,128)(2,1)}, bf16[256,2048]{1,0:T(8,128)(2,1)}, u32[]{:S(2)}, u32[]{:S(2)}) collective-permute-start(bf16[256,2048]{1,0:T(8,128)(2,1)} %get-tuple-element.99), channel_id=1, source_target_pairs={{0,16},{8,24},{16,0},{24,8},{1,17},{9,25},{17,1},{25,9},{2,18},{10... | collective-permute-start | bytes 3145736 | tf_op jit(solution)/shard_map/ppermute | solution.py:332
  96.8 51.6 %collective-permute-start.8 = (bf16[256,2048]{1,0:T(8,128)(2,1)}, bf16[256,2048]{1,0:T(8,128)(2,1)}, u32[]{:S(2)}, u32[]{:S(2)}) collective-permute-start(bf16[256,2048]{1,0:T(8,128)(2,1)} %get-tuple-element.99), channel_id=1, source_target_pairs={{0,8},{8,0},{16,24},{24,16},{1,9},{9,1},{17,25},{25,17},{2,10},{10... | collective-permute-start | bytes 3145736 | tf_op jit(solution)/shard_map/ppermute | solution.py:332
  98.4 50.0 %collective-permute-start.6 = (bf16[256,2048]{1,0:T(8,128)(2,1)S(1)}, bf16[256,2048]{1,0:T(8,128)(2,1)}, u32[]{:S(2)}, u32[]{:S(2)}) collective-permute-start(bf16[256,2048]{1,0:T(8,128)(2,1)S(1)} %get-tuple-element.100), channel_id=1, source_target_pairs={{0,8},{8,0},{16,24},{24,16},{1,9},{9,1},{17,25},{25,17},{2,10},{10... | collective-permute-start | bytes 3145736 | tf_op jit(solution)/shard_map/ppermute | solution.py:332
  98.8 49.6 %collective-permute-start.9 = (bf16[256,2048]{1,0:T(8,128)(2,1)S(1)}, bf16[256,2048]{1,0:T(8,128)(2,1)}, u32[]{:S(2)}, u32[]{:S(2)}) collective-permute-start(bf16[256,2048]{1,0:T(8,128)(2,1)S(1)} %get-tuple-element.100), channel_id=1, source_target_pairs={{0,16},{8,24},{16,0},{24,8},{1,17},{9,25},{17,1},{25,9},{2,18},{10... | collective-permute-start | bytes 3145736 | tf_op jit(solution)/shard_map/ppermute | solution.py:332
  194.1 47.5 %collective-permute-start.13 = (bf16[256,2048]{1,0:T(8,128)(2,1)}, bf16[256,2048]{1,0:T(8,128)(2,1)}, u32[]{:S(2)}, u32[]{:S(2)}) collective-permute-start(bf16[256,2048]{1,0:T(8,128)(2,1)} %get-tuple-element.211), channel_id=1, source_target_pairs={{0,8},{8,0},{16,24},{24,16},{1,9},{9,1},{17,25},{25,17},{2,10},{10... | collective-permute-start | bytes 3145736 | tf_op jit(solution)/shard_map/ppermute | solution.py:332
  195.4 53.1 %collective-permute-start.16 = (bf16[256,2048]{1,0:T(8,128)(2,1)}, bf16[256,2048]{1,0:T(8,128)(2,1)}, u32[]{:S(2)}, u32[]{:S(2)}) collective-permute-start(bf16[256,2048]{1,0:T(8,128)(2,1)} %get-tuple-element.210), channel_id=1, source_target_pairs={{0,16},{8,24},{16,0},{24,8},{1,17},{9,25},{17,1},{25,9},{2,18},{10... | collective-permute-start | bytes 3145736 | tf_op jit(solution)/shard_map/ppermute | solution.py:332
  221.2 59.8 %collective-permute-start.19 = (bf16[512,1024]{0,1:T(8,128)(2,1)S(1)}, bf16[512,1024]{0,1:T(8,128)(2,1)S(1)}, u32[]{:S(2)}, u32[]{:S(2)}) collective-permute-start(bf16[512,1024]{0,1:T(8,128)(2,1)S(1)} %bitcast.131), channel_id=1, source_target_pairs={{0,1},{1,0},{2,3},{3,2},{4,5},{5,4},{6,7},{7,6},{8,9},{9,8},{10,11... | collective-permute-start | bytes 3145736 | tf_op jit(solution)/shard_map/ppermute | solution.py:558
  264.8 51.4 %collective-permute-start.20 = (bf16[256,2048]{1,0:T(8,128)(2,1)}, bf16[256,2048]{1,0:T(8,128)(2,1)}, u32[]{:S(2)}, u32[]{:S(2)}) collective-permute-start(bf16[256,2048]{1,0:T(8,128)(2,1)} %collective-permute-done.7), channel_id=1, source_target_pairs={{0,8},{8,0},{16,24},{24,16},{1,9},{9,1},{17,25},{25,17},{2,10},{10... | collective-permute-start | bytes 3145736 | tf_op jit(solution)/shard_map/ppermute | solution.py:332
  266.1 50.1 %collective-permute-start.21 = (bf16[256,2048]{1,0:T(8,128)(2,1)}, bf16[256,2048]{1,0:T(8,128)(2,1)}, u32[]{:S(2)}, u32[]{:S(2)}) collective-permute-start(bf16[256,2048]{1,0:T(8,128)(2,1)} %collective-permute-done.6), channel_id=1, source_target_pairs={{0,16},{8,24},{16,0},{24,8},{1,17},{9,25},{17,1},{25,9},{2,18},{10... | collective-permute-start | bytes 3145736 | tf_op jit(solution)/shard_map/ppermute | solution.py:332
  345.7 254.5 %reduce-scatter.7.cloned.1.call-start = ((), (), s32[]{:S(2)}) async-start(), calls=%async_computation.12 | async-start | bytes 9437184 | tf_op jit(solution)/shard_map/reduce_scatter | solution.py:585
  455.2 178.2 %reduce-scatter.9.cloned.1.call-start = ((), (), s32[]{:S(2)}) async-start(), calls=%async_computation.13 | async-start | bytes 2359296 | tf_op jit(solution)/shard_map/reduce_scatter | solution.py:651
  507.2 49.9 %collective-permute-start.29 = (bf16[256,2048]{1,0:T(8,128)(2,1)}, bf16[256,2048]{1,0:T(8,128)(2,1)}, u32[]{:S(2)}, u32[]{:S(2)}) collective-permute-start(bf16[256,2048]{1,0:T(8,128)(2,1)} %get-tuple-element.131), channel_id=1, source_target_pairs={{0,8},{8,0},{16,24},{24,16},{1,9},{9,1},{17,25},{25,17},{2,10},{10... | collective-permute-start | bytes 3145736 | tf_op jit(solution)/shard_map/ppermute | solution.py:332
  508.0 49.0 %collective-permute-start.30 = (bf16[256,2048]{1,0:T(8,128)(2,1)S(1)}, bf16[256,2048]{1,0:T(8,128)(2,1)}, u32[]{:S(2)}, u32[]{:S(2)}) collective-permute-start(bf16[256,2048]{1,0:T(8,128)(2,1)S(1)} %get-tuple-element.132), channel_id=1, source_target_pairs={{0,16},{8,24},{16,0},{24,8},{1,17},{9,25},{17,1},{25,9},{2,18},{10... | collective-permute-start | bytes 3145736 | tf_op jit(solution)/shard_map/ppermute | solution.py:332
  514.0 48.7 %collective-permute-start.34 = (bf16[128,2048]{1,0:T(8,128)(2,1)}, bf16[128,2048]{1,0:T(8,128)(2,1)}, u32[]{:S(2)}, u32[]{:S(2)}) collective-permute-start(bf16[128,2048]{1,0:T(8,128)(2,1)} %get-tuple-element.220), channel_id=1, source_target_pairs={{0,8},{8,0},{16,24},{24,16},{1,9},{9,1},{17,25},{25,17},{2,10},{10... | collective-permute-start | bytes 1572872 | tf_op jit(solution)/shard_map/ppermute | solution.py:332
  514.8 47.9 %collective-permute-start.35 = (bf16[128,2048]{1,0:T(8,128)(2,1)}, bf16[128,2048]{1,0:T(8,128)(2,1)}, u32[]{:S(2)}, u32[]{:S(2)}) collective-permute-start(bf16[128,2048]{1,0:T(8,128)(2,1)} %get-tuple-element.219), channel_id=1, source_target_pairs={{0,16},{8,24},{16,0},{24,8},{1,17},{9,25},{17,1},{25,9},{2,18},{10... | collective-permute-start | bytes 1572872 | tf_op jit(solution)/shard_map/ppermute | solution.py:332
  597.4 164.8 %reduce-scatter.11.cloned.1.call-start = ((), (), s32[]{:S(2)}) async-start(), calls=%async_computation.14 | async-start | bytes 7077888 | tf_op jit(solution)/shard_map/reduce_scatter | solution.py:585
  (102 other events, 1588.2 us)
Sparse Core Ops, SparseCore 0:
  10.4 67.4 all-gather.4
  79.5 80.6 all-gather.6
  161.9 80.5 all-gather.8
  244.5 81.0 all-gather.10
  345.8 90.1 reduce-scatter.4
  455.3 90.0 reduce-scatter.6
  597.5 35.8 reduce-scatter.8
  644.5 70.3 reduce-scatter.10

commit v7 on v6

--- a/solution.py
+++ b/solution.py
@@ -12,6 +12,10 @@
 HEAD_DIM = 64
 BLOCK = 256
 PAIR = 2 * HEAD_DIM
+
+
+def estimate(flops, transcendentals=0):
+    return pl.CostEstimate(flops=flops // 4, bytes_accessed=flops // 4096, transcendentals=transcendentals // 4)
 
 
 def layer_norm(token_rows, gain_vec, shift_vec):
@@ -170,9 +174,7 @@
             jax.ShapeDtypeStruct((rows, pairs * PAIR), jnp.float32),
         ],
         compiler_params=pltpu.CompilerParams(vmem_limit_bytes=24 * 2**20),
-        cost_estimate=pl.CostEstimate(
-            flops=scored * 2 * 512, bytes_accessed=rows * pairs * PAIR * 12, transcendentals=scored
-        ),
+        cost_estimate=estimate(scored * 2 * 512, scored),
         name="attend_forward",
     )(mask, slopes, qkv)
 
@@ -196,11 +198,7 @@
         out_shape=jax.ShapeDtypeStruct((rows, width), jnp.bfloat16),
         input_output_aliases={6: 0} if earlier else {},
         compiler_params=pltpu.CompilerParams(vmem_limit_bytes=24 * 2**20),
-        cost_estimate=pl.CostEstimate(
-            flops=scored * 2 * 1280,
-            bytes_accessed=rows * (stop - start) * PAIR * 20,
-            transcendentals=scored,
-        ),
+        cost_estimate=estimate(scored * 2 * 1280, scored),
         name="attend_backward",
     )(mask, slopes, qkv, lse, mixed, grad, *earlier)
 
@@ -258,11 +256,7 @@
             jax.ShapeDtypeStruct((count, width), jnp.float32),
         ],
         compiler_params=pltpu.CompilerParams(vmem_limit_bytes=28 * 2**20),
-        cost_estimate=pl.CostEstimate(
-            flops=count * depth * width * 4,
-            bytes_accessed=2 * count * depth + 2 * depth * width + 6 * count * width,
-            transcendentals=2 * count * width,
-        ),
+        cost_estimate=estimate(count * depth * width * 4, 2 * count * width),
         name="up_and_bend",
     )(rows, weight, bias)
 
@@ -286,13 +280,54 @@
             jax.ShapeDtypeStruct((1, width), jnp.float32),
         ],
         compiler_params=pltpu.CompilerParams(vmem_limit_bytes=28 * 2**20),
-        cost_estimate=pl.CostEstimate(
-            flops=count * depth * width * 3,
-            bytes_accessed=2 * count * depth + 2 * depth * width + 6 * count * width,
-            transcendentals=0,
-        ),
+        cost_estimate=estimate(count * depth * width * 3, 0),
         name="hidden_gradient",
     )(rows, weight, slope)
+
+
+def norm_back_kernel(rest_ref, values_ref, base_ref, gain_ref, *refs, parts):
+    came, (low_ref, wide_ref, sums_ref) = refs[:parts], refs[parts:]
+    wide = jnp.float32
+    starting = pl.program_id(0) == 0
+    grad = rest_ref[...].astype(wide)
+    for top, bottom in zip(came[0::2], came[1::2]):
+        grad = grad + jnp.where(starting, top[...], bottom[...]).astype(wide)
+    values = values_ref[...].astype(wide)
+    base = base_ref[...].astype(wide)
+    centred = values - jnp.mean(values, axis=-1, keepdims=True)
+    scale = lax.rsqrt(jnp.mean(centred * centred, axis=-1, keepdims=True) + 1e-05)
+    normal = centred * scale
+    gained = grad * gain_ref[...]
+    along = jnp.mean(gained * normal, axis=-1, keepdims=True)
+    made = base + scale * (gained - jnp.mean(gained, axis=-1, keepdims=True) - normal * along)
+    low = made.astype(low_ref.dtype)
+    low_ref[...] = low
+    wide_ref[...] = made
+    for row, part in enumerate((grad * normal, grad, low.astype(wide), base)):
+        line = jnp.sum(part, axis=0, keepdims=True)
+        sums_ref[row : row + 1, :] = jnp.where(starting, line, sums_ref[row : row + 1, :] + line)
+
+
+def norm_back(rest, values, base, gain, came):
+    rows, width = values.shape
+    half = rows // 2
+    came = list(came or ())
+    tile = pl.BlockSpec((half, width), lambda i: (i, 0))
+    every = pl.BlockSpec((half, width), lambda i: (0, 0), pipeline_mode=pl.Buffered(1))
+    return pl.pallas_call(
+        partial(norm_back_kernel, parts=len(came)),
+        grid=(2,),
+        in_specs=[tile, tile, tile, pl.BlockSpec((1, width), lambda i: (0, 0))] + [every] * len(came),
+        out_specs=[tile, tile, pl.BlockSpec((8, width), lambda i: (0, 0))],
+        out_shape=[
+            jax.ShapeDtypeStruct((rows, width), jnp.bfloat16),
+            jax.ShapeDtypeStruct((rows, width), jnp.float32),
+            jax.ShapeDtypeStruct((8, width), jnp.float32),
+        ],
+        compiler_params=pltpu.CompilerParams(vmem_limit_bytes=40 * 2**20),
+        cost_estimate=estimate(30 * rows * width, rows),
+        name="norm_back",
+    )(rest, values, base, gain[None], *came)
 
 
 def outer_kernel(left_ref, right_ref, out_ref, *, chunk):
@@ -318,11 +353,7 @@
         out_specs=pl.BlockSpec((shards, 1, part // shards, width), lambda i: (0, i, 0, 0)),
         out_shape=jax.ShapeDtypeStruct((shards, groups, part // shards, width), jnp.bfloat16),
         compiler_params=pltpu.CompilerParams(vmem_limit_bytes=28 * 2**20),
-        cost_estimate=pl.CostEstimate(
-            flops=2 * tokens * rows * width,
-            bytes_accessed=2 * (tokens * rows + tokens * width + rows * width),
-            transcendentals=0,
-        ),
+        cost_estimate=estimate(2 * tokens * rows * width, 0),
         name="outer",
     )(left, right)
     return made.reshape(rows, width)
@@ -377,19 +408,25 @@
         top, bottom = rows
         return rows, (swap(bottom, 1), swap(top, 2), swap(top, 1), swap(bottom, 2))
 
-    def fill(self, pieces):
+    def fill(self, begun):
+        rows, came = begun
+        if came is None:
+            return rows
+        first_bottom, second_top, first_top, second_bottom = came
+        room = jnp.zeros_like(rows[0])
+        parts = (*rows, first_top, first_bottom, second_top, second_bottom, room, room)
+        return self(lambda *parts: jnp.concatenate(parts, axis=0), *parts)
+
+    def complete(self, made, pieces):
         if not isinstance(pieces, list):
-            return pieces
-        count = sum(piece.shape[0] for piece in pieces[:-2])
+            return made
         rows = pieces[-1].shape[0]
-        room = jnp.zeros((2 * rows, pieces[0].shape[1]), pieces[0].dtype)
-        made = self(lambda *parts: jnp.concatenate([*parts, room], axis=0), *pieces[:-2])
 
         def put(before, first, second):
-            before = lax.dynamic_update_slice_in_dim(before, first, count, axis=0)
-            return lax.dynamic_update_slice_in_dim(before, second, count + rows, axis=0)
-
-        return lambda: self(put, made, *pieces[-2:])
+            before = lax.dynamic_update_slice_in_dim(before, first, 6 * rows, axis=0)
+            return lax.dynamic_update_slice_in_dim(before, second, 7 * rows, axis=0)
+
+        return self(put, made, *pieces[-2:])
 
     def pass_on(self, begun, *before):
         rows, came = begun
@@ -415,47 +452,53 @@
         top, bottom = self(far_half, rows)
         return product, rows, axis, (top, bottom) if held else (swap(top, 1), swap(bottom, 2))
 
-    def send_held(self, begun, *before):
-        if begun[1] is None:
-            return begun
-        rest, parts = begun
-        top, bottom = gate(parts, *before)
-        return rest, (swap(top, 1), swap(bottom, 2))
-
-    def make_rest(self, begun):
-        product, rows, axis, parts = begun
-        if parts is None:
-            return lax.psum_scatter(self(product, rows), "seq", scatter_dimension=0, tiled=True), None
+    def make_rest(self, begun, held=False):
+        product, rows, axis, far = begun
+        if far is None:
+            return lax.psum_scatter(self(product, rows), "seq", scatter_dimension=0, tiled=True), None, None
         count = rows.shape[axis] // 4
-        return self(lambda values: product(lax.slice_in_dim(values, 0, 3 * count, axis=axis)), rows), parts
-
-    def add_far(self, begun):
-        rest, parts = begun
-        if parts is None:
-            return begun
+        rest = self(lambda values: product(lax.slice_in_dim(values, 0, 3 * count, axis=axis)), rows)
+        count = rest.shape[0] // 3
+        half = count // 2
+        direct = rest[count : count + half], rest[2 * count + half :]
+        return rest, far, direct if held else (swap(direct[0], 1), swap(direct[1], 2))
+
+    def send_held(self, begun, which, *before):
+        rest, *parts = begun
+        if parts[which] is not None:
+            first, second = gate(parts[which], *before) if before else parts[which]
+            parts[which] = swap(first, 1), swap(second, 2)
+        return rest, *parts
+
+    def add_far(self, begun, *before):
+        rest, far, direct = begun
+        if far is None:
+            return rest, None
         wide = jnp.float32
 
         def add(rest, top, bottom):
             half = top.shape[0]
-            count = 2 * half
-            first, second = rest[count : 2 * count], rest[2 * count :]
-            first_low = (first[half:].astype(wide) + bottom.astype(wide)).astype(rest.dtype)
-            second_low = (second[:half].astype(wide) + top.astype(wide)).astype(rest.dtype)
+            first, second = rest[3 * half : 4 * half], rest[4 * half : 5 * half]
             return (
-                jnp.concatenate([first[:half], first_low], axis=0),
-                jnp.concatenate([second_low, second[half:]], axis=0),
+                (first.astype(wide) + bottom.astype(wide)).astype(rest.dtype),
+                (second.astype(wide) + top.astype(wide)).astype(rest.dtype),
             )
 
-        first, second = self(add, rest, *parts)
-        return rest, (swap(first, 1), swap(second, 2))
+        first, second = self(add, rest, *far)
+        if before:
+            first, second = gate((first, second), *before)
+        return rest, (direct[0], swap(first, 1), swap(second, 2), direct[1])
 
 
 def summed(rest, came):
     wide = jnp.float32
     if came is None:
         return rest.astype(wide)
-    own = rest[: came[0].shape[0]]
-    return own.astype(wide) + came[0].astype(wide) + came[1].astype(wide)
+    half = came[0].shape[0]
+    first_top, first_bottom, second_top, second_bottom = (part.astype(wide) for part in came)
+    top = rest[:half].astype(wide) + first_top + second_top
+    bottom = rest[half : 2 * half].astype(wide) + first_bottom + second_bottom
+    return jnp.concatenate([top, bottom], axis=0)
 
 
 def whole(parts):
@@ -528,12 +571,11 @@
     x_low = tokens.reshape(rows_here, model_width)
     x = x_low.astype(wide)
     dz_low = cotangent.reshape(rows_here, model_width)
-    dz = dz_low.astype(wide)
     qkv_slab = lax.all_gather(head_columns(w_qkv), "fsdp", axis=0, tiled=True)
     qkv_bias = head_columns(jnp.concatenate([qv_bias[0], jnp.zeros_like(qv_bias[0]), qv_bias[1]])[None])
     up_bias_slab = own_slab(up_bias, 0)
 
-    first_norm, first_back = jax.vjp(layer_norm, x, ln1_gain, ln1_shift)
+    first_norm = layer_norm(x, ln1_gain, ln1_shift)
     half = rows_here // 2
 
     def halves_of(values):
@@ -568,15 +610,16 @@
         )
 
     middle = order(lambda rows: x + (contract(rows, full_out) + out_bias), mixed_rows)
-    second_norm, second_back = jax.vjp(layer_norm, middle, ln2_gain, ln2_shift)
+    second_norm = layer_norm(middle, ln2_gain, ln2_shift)
     second = order.gather(order(halves_of, second_norm))
     mine, theirs = order(pair_halves, mixed_slots)
+    upstream_made = order.fill(upstream)
     theirs = pair_swap(theirs)
     second = whole(order.pass_on(second))
-    upstream = order.fill(order.pass_on(upstream, second))
+    upstream = order.pass_on(upstream, second)
     mixed_half = order(lambda *parts: jnp.concatenate(parts, axis=0), mine, theirs)
     active, slope = order(lambda rows: up_and_bend(rows, up_slab, up_bias_slab[None]), second)
-    upstream = upstream() if callable(upstream) else upstream
+    upstream = order.complete(upstream_made, upstream)
 
     def slab_product(left, right):
         return order(lambda rows: outer(rows, right, groups, shards), left)
@@ -584,13 +627,13 @@
     def slab_sum(made):
         return lax.psum_scatter(made, "fsdp", scatter_dimension=0, tiled=True)
 
-    def slabs_of_rows(values, *before):
-        values = gate(values, *before) if before else values
-        values = values.reshape(groups, -1, values.shape[1])
-        slabs = lax.all_to_all(values, "seq", split_axis=0, concat_axis=0, tiled=True)
-        return jnp.swapaxes(slabs, 0, 1).astype(wide)
-
-    down_sum = slab_sum(slab_product(upstream, active))
+    def slabs_of_rows(*sums):
+        parts = [part.reshape(groups, -1, part.shape[1]) for part in sums]
+        slabs = lax.all_to_all(jnp.concatenate(parts, axis=1), "seq", split_axis=0, concat_axis=0, tiled=True)
+        count = parts[0].shape[1]
+        return [
+            jnp.swapaxes(slabs[:, at : at + count], 0, 1).astype(wide) for at in range(0, slabs.shape[1], count)
+        ]
 
     hidden_grad, hidden_sum = order(lambda rows: hidden_gradient(rows, down_slab, slope), upstream)
 
@@ -602,45 +645,60 @@
         return contract(rows, down_slab).astype(low)
 
     outcome = order.send_far(to_result, active, held=True)
+    down_sum = slab_product(upstream, active)
+    if square:
+        down_sum = gate(down_sum, *second_grad[1][0::3])
+    down_sum = slab_sum(down_sum)
     up_sum = slab_product(second, hidden_grad)
     if square:
         up_sum = gate(up_sum, *second_grad[1])
     up_sum = slab_sum(up_sum)
 
 
-    def to_middle(own, came):
-        middle_part, gain_grad, shift_grad = second_back(summed(own, came))
-        middle_grad = dz + middle_part
-        return middle_grad.astype(low), middle_grad, gain_grad, shift_grad
-
-    branch_grad, middle_grad, ln2_gain_grad, ln2_shift_grad = order(
-        lambda own, *came: to_middle(own, came or None), second_grad[0], *(second_grad[1] or ())
-    )
+    branch_grad, middle_grad, middle_sums = order(
+        lambda rest, *came: norm_back(rest, middle, dz_low, ln2_gain, came), second_grad[0], *(second_grad[1] or ())
+    )
+
     def column_sum(values):
         return jnp.sum(values.astype(wide), axis=0)
 
     hidden_sum = lax.dynamic_update_slice_in_dim(
         jnp.zeros((hidden_width,), wide), hidden_sum[0], me * hidden_slab, axis=0
     )
-    early = [column_sum(branch_grad), ln2_gain_grad, ln2_shift_grad, hidden_sum, column_sum(dz)]
+    early = [middle_sums[2], middle_sums[0], middle_sums[1], hidden_sum, middle_sums[3]]
     mixed_grad = order(lambda rows: contract_last(rows, full_out).astype(low), branch_grad)
     mixed_grad = exchange(by_index([mixed_grad[:, j * slab : (j + 1) * slab] for j in range(groups)], me))
-    outcome = order.make_rest(outcome)
+    outcome = order.make_rest(outcome, held=True)
+    mixed_grad = order(lambda *parts: jnp.concatenate(parts, axis=0), *mixed_grad)
+    outcome = order.send_held(order.send_held(outcome, 0, mixed_grad), 1, mixed_grad)
     branch_pair = jnp.concatenate([branch_grad, pair_swap(branch_grad)], axis=0)
 
     def to_out(columns):
         return contract_first(columns, branch_pair).astype(low)
-    out_begun = order.make_rest(order.send_far(to_out, mixed_half, axis=1))
-    mixed_grad = jnp.concatenate(mixed_grad, axis=0)
-    outcome = order.send_held(outcome, mixed_grad)
+
     order.after(down_sum)
     attention = (mask, slopes, qkv, log_totals, attended)
     begun = order(lambda rows: attend_backward(*attention, rows, seq_count, local_len, 0, pairs // 2), mixed_grad)
-    outcome = order.add_far(outcome)
-    out_begun = order.add_far(out_begun)
+    out_begun = order.make_rest(order.send_far(to_out, mixed_half, axis=1))
     qkv_grad = order(
         lambda rows: attend_backward(*attention, rows, seq_count, local_len, pairs // 2, pairs, begun), mixed_grad
     )
+    out_begun = order.add_far(out_begun)
+    if square:
+        order.after(*outcome[1], *outcome[2])
+    order.after(up_sum)
+
+    def to_normed(rows):
+        return contract_last(rows, qkv_slab).astype(low)
+
+    normed_grad = order.send_far(to_normed, qkv_grad)
+    qkv_sum = slab_product(normed, qkv_grad)
+    if square:
+        qkv_sum = gate(qkv_sum, *normed_grad[3], *out_begun[1])
+    qkv_sum = slab_sum(qkv_sum)
+    normed_grad = order.make_rest(normed_grad)
+    normed_grad = order.add_far(normed_grad)
+    outcome = order.add_far(outcome)
     out_sum = order(
         lambda own, *came: summed(own, came or None).astype(low), out_begun[0], *(out_begun[1] or ())
     ).reshape(-1, 1, out_rows, model_width)
@@ -649,41 +707,31 @@
         [jnp.where(parity == 0, out_sum, zero), jnp.where(parity == 1, out_sum, zero)], axis=1
     ).reshape(-1, model_width)
     grad_w_out = lax.psum_scatter(out_sum, "fsdp", scatter_dimension=0, tiled=True).astype(wide)
-    order.after(up_sum)
-
-    def to_normed(rows):
-        return contract_last(rows, qkv_slab).astype(low)
-
-    normed_grad = order.send_far(to_normed, qkv_grad)
-    qkv_sum = slab_product(normed, qkv_grad)
-    qkv_sum = slab_sum(gate(qkv_sum, grad_w_out, *(outcome[1] or ())))
-    order.after(grad_w_out, *(outcome[1] or ()))
-    normed_grad = order.make_rest(normed_grad)
-    normed_grad = order.add_far(normed_grad)
+    grad_tokens, _, input_sums = order(
+        lambda rest, *came: norm_back(rest, x_low, middle_grad, ln1_gain, came),
+        normed_grad[0],
+        *(normed_grad[1] or ()),
+    )
+    grad_tokens = grad_tokens.reshape(tokens.shape)
     result = order(
         lambda own, *came: (middle + (summed(own, came or None) + down_bias)).astype(low),
         outcome[0],
         *(outcome[1] or ()),
     ).reshape(tokens.shape)
-
-    def to_input(own, came):
-        input_part, gain_grad, shift_grad = first_back(summed(own, came))
-        return (middle_grad + input_part).astype(low), gain_grad, shift_grad
-
-    grad_tokens, ln1_gain_grad, ln1_shift_grad = order(
-        lambda own, *came: to_input(own, came or None), normed_grad[0], *(normed_grad[1] or ())
-    )
-    grad_tokens = grad_tokens.reshape(tokens.shape)
-    grad_w_down = slabs_of_rows(down_sum, *(normed_grad[1] or ())).reshape(-1, hidden_width).T
-    grad_w_up = slabs_of_rows(up_sum, *(normed_grad[1] or ())).reshape(-1, hidden_width)
-    grad_w_qkv = slabs_of_rows(qkv_sum).reshape(-1, groups, pairs, 3, PAIR)
+    sums = down_sum, up_sum
+    if square:
+        sums = gate(sums, *normed_grad[1])
+    grad_w_down, grad_w_up = slabs_of_rows(*sums)
+    grad_w_down = grad_w_down.reshape(-1, hidden_width).T
+    grad_w_up = grad_w_up.reshape(-1, hidden_width)
+    grad_w_qkv = slabs_of_rows(qkv_sum)[0].reshape(-1, groups, pairs, 3, PAIR)
     grad_w_qkv = jnp.transpose(grad_w_qkv, (0, 3, 1, 2, 4)).reshape(-1, 3 * model_width)
 
     head_sum = jnp.transpose(column_sum(qkv_grad).reshape(pairs, 3, PAIR), (1, 0, 2)).reshape(3, slab)
     qv_sum = lax.dynamic_update_slice_in_dim(
         jnp.zeros((2, model_width), wide), head_sum[0::2], me * slab, axis=1
     )
-    late = [qv_sum.reshape(-1), ln1_gain_grad, ln1_shift_grad]
+    late = [qv_sum.reshape(-1), input_sums[0], input_sums[1]]
     sums = total(jnp.concatenate(early + late).reshape(-1, PAIR)).reshape(-1)
 
     def cut(at, count):

time: 803 us -> 808 us (level)
  other arithmetic: 68.9 us -> 41.3 us
  local copies, waits for them, and re-layouts: 125 us -> 147 us
  waiting for transfers between devices: 218 us -> 198 us
  Pallas kernels: 189 us -> 208 us
  starting transfers between devices: 64.3 us -> 80.3 us
    reduce_sum x4 -> x0, other arithmetic: 19.6 us -> none  [the longest x2 9.82 us: layer_norm(): centred = token_rows - average]
    unnamed x160 -> x177, local copies, waits for them, and re-layouts: 75.7 us -> 95 us
    pallas_call x0 -> x2, Pallas kernels: none -> 18.6 us  [norm_back(): pl.pallas_call(partial(norm_back_kernel, parts=len(came)), grid=(2,), in_...]
    all_gather x1, waiting for transfers between devices: 0.02 us -> 13.1 us  [local(): lax.all_gather(own_slab(gate(w_down, normed[0]) if square else w_down, 0)...]
    ppermute x40 -> x48, waiting for transfers between devices: 192 us -> 179 us  [swap(): return lax.ppermute(values, 'seq', [(i, i ^ bit) for i in range(4)])]
    all_to_all x3 -> x2, waiting for transfers between devices: 13.3 us -> 1.73 us  [slabs_of_rows(): lax.all_to_all(jnp.concatenate(parts, axis=1), 'seq', split_axis=0, conca...]
    ppermute x7, starting transfers between devices: 8.12 us -> 19.6 us  [total(): lax.ppermute(values, axis, [(i, i ^ mask) for i in range(count)])]
    ppermute x40 -> x48, starting transfers between devices: 44.4 us -> 52.9 us  [swap(): return lax.ppermute(values, 'seq', [(i, i ^ bit) for i in range(4)])]
  transfers between devices with their start and end apart: 60 -> 67, of which waited for: 24 -> 25; matrix products, arithmetic and copies ran while one was open for 32% -> 28% of each run, Pallas kernels for 23% -> 23%
where the time goes in v7:
time: 808 us; the launch traced here: 803 us
  Pallas kernels  208 us (26%)
  waiting for transfers between devices  198 us (25%)
  local copies, waits for them, and re-layouts  147 us (18%)
  matrix products  113 us (14%)
  starting transfers between devices  80.3 us (10%)
  other arithmetic  41.3 us (5%)
  between operations  15.6 us (2%)
    ppermute x48, waiting for transfers between devices, swap(): return lax.ppermute(values, 'seq', [(i, i ^ bit) for i in range(4)])  179 us
    unnamed x177, local copies, waits for them, and re-layouts  95 us
    pallas_call x3, Pallas kernels, outer(): pl.pallas_call(partial(outer_kernel, chunk=512 if width % 512 == 0 else 2...  54.7 us
    dot_general x5, matrix products, contract_last(): lax.dot_general(left_side, right_side, (((1,), (1,)), ((), ())), preferre...  54.6 us
    ppermute x48, starting transfers between devices, swap(): return lax.ppermute(values, 'seq', [(i, i ^ bit) for i in range(4)])  52.9 us
    pallas_call x2, Pallas kernels, attend_backward(): pl.pallas_call(partial(attend_backward_kernel, blocks=blocks, seqs=seqs,...  52.8 us
    dot_general x4, matrix products, contract(): lax.dot_general(left_side, right_side, (((1,), (0,)), ((), ())), preferre...  48.9 us
    pallas_call x1, Pallas kernels, attend_forward(): pl.pallas_call(partial(attend_forward_kernel, blocks=blocks, seqs=seqs, l...  28.6 us
  transfers between devices with their start and end apart: 67, of which 25 were waited for; matrix products, arithmetic and copies ran while one was open for 28% of the time, Pallas kernels for 23%

profile of v7, /device:TPU:0, one launch (start us, length us, event | category | flops | bytes accessed | tf_op | source)
XLA Modules:
  0.0 803.3 jit_solution(13294376411511022657)
XLA Ops:
  26.9 18.9 %collective-permute-done.2 = bf16[256,2048]{1,0:T(8,128)(2,1)} collective-permute-done((bf16[256,2048]{1,0:T(8,128)(2,1)}, bf16[256,2048]{1,0:T(8,128)(2,1)}, u32[]{:S(2)}, u32[]{:S(2)}) %collective-permute-start.2) | collective-permute-done | bytes 1048608 | tf_op jit(solution)/shard_map/ppermute | solution.py:363
  52.1 18.2 %collective-permute-done = bf16[256,2048]{1,0:T(8,128)(2,1)} collective-permute-done((bf16[256,2048]{1,0:T(8,128)(2,1)}, bf16[256,2048]{1,0:T(8,128)(2,1)}, u32[]{:S(2)}, u32[]{:S(2)}) %collective-permute-start) | collective-permute-done | bytes 1048608 | tf_op jit(solution)/shard_map/ppermute | solution.py:363
  78.5 12.8 %collective-permute-done.4 = bf16[256,2048]{1,0:T(8,128)(2,1)} collective-permute-done((bf16[256,2048]{1,0:T(8,128)(2,1)}, bf16[256,2048]{1,0:T(8,128)(2,1)}, u32[]{:S(2)}, u32[]{:S(2)}) %collective-permute-start.4) | collective-permute-done | bytes 1048608 | tf_op jit(solution)/shard_map/ppermute | solution.py:363
  100.1 17.3 %add_convert_fusion.qkv_ref = bf16[2048,1536]{1,0:T(8,128)(2,1)S(1)} fusion(bf16[2048,2048]{1,0:T(8,128)(2,1)} %constant_dynamic-update-slice_fusion.left_ref, bf16[2048,1536]{1,0:T(8,128)(2,1)} %all-gather.5.cloned.1.call-done, f32[1536]{0:T(1024)S(1)} %reduce.2), kind=kOutput, calls=%fused_computation.1 | convolution fusion | flops 12891193344 | bytes 20977664 | tf_op jit(solution)/shard_map/dot_general | solution.py:29
  117.4 28.6 %attend_forward.1 = (bf16[2048,512]{1,0:T(8,128)(2,1)S(1)}, f32[2048,512]{1,0:T(8,128)S(1)}) custom-call(s32[1]{0:T(128)} %bitcast.1.at_ref.mask_ref, f32[8]{0:T(128)S(1)} %multiply_power_fusion.slope_ref, bf16[2048,1536]{1,0:T(8,128)(2,1)S(1)} %add_convert_fusion.qkv_ref), custom_call_target="tpu_custom_call" | custom-call | flops 2684354560 | bytes 2621440 | tf_op jit(solution)/shard_map/attend_forward/pallas_call | solution.py:164
  154.7 11.8 %collective-permute-done.10 = bf16[512,512]{1,0:T(8,128)(2,1)S(1)} collective-permute-done((bf16[512,512]{1,0:T(8,128)(2,1)}, bf16[512,512]{1,0:T(8,128)(2,1)S(1)}, u32[]{:S(2)}, u32[]{:S(2)}) %collective-permute-start.10) | collective-permute-done | bytes 524320 | tf_op jit(solution)/shard_map/ppermute | solution.py:363
  220.2 19.4 %collective-permute-done.14 = bf16[256,2048]{1,0:T(8,128)(2,1)} collective-permute-done((bf16[256,2048]{1,0:T(8,128)(2,1)}, bf16[256,2048]{1,0:T(8,128)(2,1)}, u32[]{:S(2)}, u32[]{:S(2)}) %collective-permute-start.14) | collective-permute-done | bytes 1048608 | tf_op jit(solution)/shard_map/ppermute | solution.py:363
  245.5 15.6 %collective-permute-done.17 = bf16[256,2048]{1,0:T(8,128)(2,1)S(1)} collective-permute-done((bf16[256,2048]{1,0:T(8,128)(2,1)}, bf16[256,2048]{1,0:T(8,128)(2,1)S(1)}, u32[]{:S(2)}, u32[]{:S(2)}) %collective-permute-start.17) | collective-permute-done | bytes 1048608 | tf_op jit(solution)/shard_map/ppermute | solution.py:363
  277.6 26.4 %up_and_bend.1 = (bf16[2048,2048]{1,0:T(8,128)(2,1)S(1)}, f32[2048,2048]{1,0:T(8,128)}) custom-call(bf16[2048,2048]{1,0:T(8,128)(2,1)S(1)} %copy-done.13, bf16[2048,2048]{1,0:T(8,128)(2,1)S(1)} %copy-done.35, f32[1,2048]{1,0:T(1,128)S(1)} %bitcast.107), custom_call_target="tpu_custom_call" | custom-call | flops 8589934592 | bytes 8388608 | tf_op jit(solution)/shard_map/up_and_bend/pallas_call | solution.py:245
  311.9 13.1 %all-gather.11.cloned.1.call-done.weight_ref = bf16[2048,2048]{1,0:T(8,128)(2,1)} async-done(((bf16[2048,256]{1,0:T(8,128)(2,1)}), bf16[2048,2048]{1,0:T(8,128)(2,1)}) %all-gather.11.cloned.1.call-update) | async-done | bytes 8388624 | tf_op jit(solution)/shard_map/all_gather | solution.py:588
  328.4 21.5 %hidden_gradient.1 = (bf16[2048,2048]{1,0:T(8,128)(2,1)S(1)}, f32[1,2048]{1,0:T(1,128)S(1)}) custom-call(bf16[2048,2048]{1,0:T(8,128)(2,1)} %constant_dynamic-update-slice_fusion.39.rows_ref.left_ref, bf16[2048,2048]{1,0:T(8,128)(2,1)S(1)} %copy-done.20, f32[2048,2048]{1,0:T(8,128)} %get-tuple-element.134.slope_ref), custom_call_target="tpu_custom_call" | custom-call | flops 6442450944 | bytes 6291456 | tf_op jit(solution)/shard_map/hidden_gradient/pallas_call | solution.py:269
  361.7 19.9 %convolution_convert_fusion.2.rest_ref = bf16[1536,2048]{1,0:T(8,128)(2,1)} fusion(bf16[2048,2048]{1,0:T(8,128)(2,1)} %all-gather.9.cloned.1.call-done.weight_ref, bf16[2048,2048]{1,0:T(8,128)(2,1)} %copy-done.18), kind=kOutput, calls=%fused_computation.4 | convolution fusion | flops 12888047616 | bytes 20971520 | tf_op jit(solution)/shard_map/dot_general | solution.py:35
  398.8 20.2 %outer.3 = bf16[8,4,64,2048]{3,2,1,0:T(8,128)(2,1)S(1)} custom-call(bf16[2048,2048]{1,0:T(8,128)(2,1)} %constant_dynamic-update-slice_fusion.39.rows_ref.left_ref, bf16[2048,2048]{1,0:T(8,128)(2,1)S(1)} %bitcast.99), custom_call_target="tpu_custom_call" | custom-call | flops 4294967296 | bytes 4194304 | tf_op jit(solution)/shard_map/outer/pallas_call | solution.py:346
  433.5 19.5 %outer.4 = bf16[8,4,64,2048]{3,2,1,0:T(8,128)(2,1)S(1)} custom-call(bf16[2048,2048]{1,0:T(8,128)(2,1)S(1)} %copy-done.14, bf16[2048,2048]{1,0:T(8,128)(2,1)S(1)} %copy-done.19), custom_call_target="tpu_custom_call" | custom-call | flops 4294967296 | bytes 4194304 | tf_op jit(solution)/shard_map/outer/pallas_call | solution.py:346
  486.0 15.7 %convolution_convert_fusion.1 = bf16[1536,2048]{1,0:T(8,128)(2,1)S(1)} fusion(bf16[2048,2048]{1,0:T(8,128)(2,1)} %all-gather.11.cloned.1.call-done.weight_ref, bf16[2048,2048]{1,0:T(8,128)(2,1)S(1)} %bitcast.101), kind=kOutput, calls=%fused_computation.3 | convolution fusion | flops 12888047616 | bytes 20971520 | tf_op jit(solution)/shard_map/dot_general | solution.py:29
  525.5 26.5 %attend_backward.2.rest_0_ = bf16[2048,1536]{1,0:T(8,128)(2,1)S(1)} custom-call(s32[1]{0:T(128)} %bitcast.1.at_ref.mask_ref, f32[8]{0:T(128)S(1)} %copy-done.34, bf16[2048,1536]{1,0:T(8,128)(2,1)S(1)} %copy-done.6, f32[2048,512]{1,0:T(8,128)S(1)} %copy-done.11, bf16[2048,512]{1,0:T(8,128)(2,1)S(1)} %copy-done.8, bf16[2048,512]{1,0:T(8,128)(2,1)S(1)} %copy-done.16), custom_call_target="tpu_custom_call" | custom-call | flops 3355443200 | bytes 3276800 | tf_op jit(solution)/shard_map/attend_backward/pallas_call | solution.py:189
  570.0 26.3 %attend_backward.3.right_ref = bf16[2048,1536]{1,0:T(8,128)(2,1)S(1)} custom-call(s32[1]{0:T(128)} %bitcast.1.at_ref.mask_ref, f32[8]{0:T(128)S(1)} %copy-done.34, bf16[2048,1536]{1,0:T(8,128)(2,1)S(1)} %copy-done.6, f32[2048,512]{1,0:T(8,128)S(1)} %copy-done.11, bf16[2048,512]{1,0:T(8,128)(2,1)S(1)} %copy-done.9, ...), custom_call_target="tpu_custom_call", output_to_operand_aliasing={{}: (6, {})} | custom-call | flops 3355443200 | bytes 3276800 | tf_op jit(solution)/shard_map/attend_backward/pallas_call | solution.py:189
  616.4 15.0 %outer.5 = bf16[8,4,64,1536]{3,2,1,0:T(8,128)(2,1)S(1)} custom-call(bf16[2048,2048]{1,0:T(8,128)(2,1)S(1)} %bitcast.97, bf16[2048,1536]{1,0:T(8,128)(2,1)S(1)} %bitcast.90), custom_call_target="tpu_custom_call" | custom-call | flops 3221225472 | bytes 3145728 | tf_op jit(solution)/shard_map/outer/pallas_call | solution.py:346
  634.1 14.2 %collective-permute-done.49 = bf16[128,2048]{1,0:T(8,128)(2,1)S(1)} collective-permute-done((bf16[128,2048]{1,0:T(8,128)(2,1)S(1)}, bf16[128,2048]{1,0:T(8,128)(2,1)S(1)}, u32[]{:S(2)}, u32[]{:S(2)}) %collective-permute-start.49) | collective-permute-done | bytes 524320 | tf_op jit(solution)/shard_map/ppermute | solution.py:363
  648.3 8.5 %collective-permute-done.48 = bf16[128,2048]{1,0:T(8,128)(2,1)S(1)} collective-permute-done((bf16[128,2048]{1,0:T(8,128)(2,1)S(1)}, bf16[128,2048]{1,0:T(8,128)(2,1)S(1)}, u32[]{:S(2)}, u32[]{:S(2)}) %collective-permute-start.48) | collective-permute-done | bytes 524320 | tf_op jit(solution)/shard_map/ppermute | solution.py:363
  662.0 13.5 %convolution_convert_fusion.rest_ref = bf16[1536,2048]{1,0:T(8,128)(2,1)S(1)} fusion(bf16[2048,1536]{1,0:T(8,128)(2,1)} %all-gather.5.cloned.1.call-done, bf16[2048,1536]{1,0:T(8,128)(2,1)} %copy-done), kind=kOutput, calls=%fused_computation.2 | convolution fusion | flops 9666822144 | bytes 17301504 | tf_op jit(solution)/shard_map/dot_general | solution.py:35
  705.2 20.8 %collective-permute-done.43.refs_1_ = bf16[256,2048]{1,0:T(8,128)(2,1)} collective-permute-done((bf16[256,2048]{1,0:T(8,128)(2,1)}, bf16[256,2048]{1,0:T(8,128)(2,1)}, u32[]{:S(2)}, u32[]{:S(2)}) %collective-permute-start.43) | collective-permute-done | bytes 1048608 | tf_op jit(solution)/shard_map/ppermute | solution.py:363
  727.7 10.3 %norm_back.3 = (bf16[512,2048]{1,0:T(8,128)(2,1)}, f32[512,2048]{1,0:T(8,128)}, f32[8,2048]{1,0:T(8,128)S(1)}) custom-call(bf16[1536,2048]{1,0:T(8,128)(2,1)} %copy-done.41, bf16[512,2048]{1,0:T(8,128)(2,1)S(1)} %bitcast.94, f32[512,2048]{1,0:T(8,128)} %copy-done.23, f32[1,2048]{1,0:T(1,128)S(1)} %bitcast.105, ...), custom_call_target="tpu_custom_call" | custom-call | flops 7864320 | bytes 7680 | tf_op jit(solution)/shard_map/norm_back/pallas_call | solution.py:317
  746.8 13.0 %collective-permute-start.51 = (f32[192,128]{1,0:T(8,128)S(1)}, f32[192,128]{1,0:T(8,128)S(1)}, u32[]{:S(2)}, u32[]{:S(2)}) collective-permute-start(f32[192,128]{1,0:T(8,128)S(1)} %bitcast_add_fusion), channel_id=1, source_target_pairs={{0,2},{1,3},{2,0},{3,1},{4,6},{5,7},{6,4},{7,5},{8,10},{9,11},{10,... | collective-permute-start | bytes 294920 | tf_op jit(solution)/shard_map/ppermute | solution.py:514
  (401 shorter events, 360.6 us)
Async XLA Ops:
  7.2 92.9 %all-gather.5.cloned.1.call-start = ((), (), s32[]{:S(2)}) async-start(), calls=%async_computation.6 | async-start | bytes 7077888 | tf_op jit(solution)/shard_map/all_gather | solution.py:574
  10.3 168.6 %all-gather.7.cloned.1.call-start = ((), (), s32[]{:S(2)}) async-start(), calls=%async_computation.7 | async-start | bytes 9437184 | tf_op jit(solution)/shard_map/all_gather | solution.py:586
  11.1 259.7 %all-gather.9.cloned.1.call-start = ((), (), s32[]{:S(2)}) async-start(), calls=%async_computation.8 | async-start | bytes 9437184 | tf_op jit(solution)/shard_map/all_gather | solution.py:587
  18.4 306.6 %all-gather.11.cloned.1.call-start = ((), (), s32[]{:S(2)}) async-start(), calls=%async_computation.9 | async-start | bytes 9437184 | tf_op jit(solution)/shard_map/all_gather | solution.py:588
  23.0 47.4 %collective-permute-start = (bf16[256,2048]{1,0:T(8,128)(2,1)}, bf16[256,2048]{1,0:T(8,128)(2,1)}, u32[]{:S(2)}, u32[]{:S(2)}) collective-permute-start(bf16[256,2048]{1,0:T(8,128)(2,1)} %get-tuple-element.253), channel_id=1, source_target_pairs={{0,8},{8,0},{16,24},{24,16},{1,9},{9,1},{17,25},{25,17},{2,10},{10... | collective-permute-start | bytes 3145736 | tf_op jit(solution)/shard_map/ppermute | solution.py:363
  23.5 52.7 %collective-permute-start.3 = (bf16[256,2048]{1,0:T(8,128)(2,1)}, bf16[256,2048]{1,0:T(8,128)(2,1)}, u32[]{:S(2)}, u32[]{:S(2)}) collective-permute-start(bf16[256,2048]{1,0:T(8,128)(2,1)} %get-tuple-element.252), channel_id=1, source_target_pairs={{0,16},{8,24},{16,0},{24,8},{1,17},{9,25},{17,1},{25,9},{2,18},{10... | collective-permute-start | bytes 3145736 | tf_op jit(solution)/shard_map/ppermute | solution.py:363
  25.9 490.7 %reduce-scatter.5.cloned.1.call-start = ((), (), s32[]{:S(2)}) async-start(), calls=%async_computation.10 | async-start | bytes 9437184 | tf_op jit(solution)/shard_map/reduce_scatter | solution.py:628
  96.0 52.0 %collective-permute-start.7 = (bf16[256,2048]{1,0:T(8,128)(2,1)}, bf16[256,2048]{1,0:T(8,128)(2,1)}, u32[]{:S(2)}, u32[]{:S(2)}) collective-permute-start(bf16[256,2048]{1,0:T(8,128)(2,1)} %get-tuple-element.119), channel_id=1, source_target_pairs={{0,16},{8,24},{16,0},{24,8},{1,17},{9,25},{17,1},{25,9},{2,18},{10... | collective-permute-start | bytes 3145736 | tf_op jit(solution)/shard_map/ppermute | solution.py:363
  96.4 51.6 %collective-permute-start.8 = (bf16[256,2048]{1,0:T(8,128)(2,1)}, bf16[256,2048]{1,0:T(8,128)(2,1)}, u32[]{:S(2)}, u32[]{:S(2)}) collective-permute-start(bf16[256,2048]{1,0:T(8,128)(2,1)} %get-tuple-element.119), channel_id=1, source_target_pairs={{0,8},{8,0},{16,24},{24,16},{1,9},{9,1},{17,25},{25,17},{2,10},{10... | collective-permute-start | bytes 3145736 | tf_op jit(solution)/shard_map/ppermute | solution.py:363
  98.0 50.0 %collective-permute-start.6 = (bf16[256,2048]{1,0:T(8,128)(2,1)S(1)}, bf16[256,2048]{1,0:T(8,128)(2,1)}, u32[]{:S(2)}, u32[]{:S(2)}) collective-permute-start(bf16[256,2048]{1,0:T(8,128)(2,1)S(1)} %get-tuple-element.120), channel_id=1, source_target_pairs={{0,8},{8,0},{16,24},{24,16},{1,9},{9,1},{17,25},{25,17},{2,10},{10... | collective-permute-start | bytes 3145736 | tf_op jit(solution)/shard_map/ppermute | solution.py:363
  98.4 49.6 %collective-permute-start.9 = (bf16[256,2048]{1,0:T(8,128)(2,1)S(1)}, bf16[256,2048]{1,0:T(8,128)(2,1)}, u32[]{:S(2)}, u32[]{:S(2)}) collective-permute-start(bf16[256,2048]{1,0:T(8,128)(2,1)S(1)} %get-tuple-element.120), channel_id=1, source_target_pairs={{0,16},{8,24},{16,0},{24,8},{1,17},{9,25},{17,1},{25,9},{2,18},{10... | collective-permute-start | bytes 3145736 | tf_op jit(solution)/shard_map/ppermute | solution.py:363
  190.8 49.5 %collective-permute-start.13 = (bf16[256,2048]{1,0:T(8,128)(2,1)}, bf16[256,2048]{1,0:T(8,128)(2,1)}, u32[]{:S(2)}, u32[]{:S(2)}) collective-permute-start(bf16[256,2048]{1,0:T(8,128)(2,1)} %get-tuple-element.246), channel_id=1, source_target_pairs={{0,8},{8,0},{16,24},{24,16},{1,9},{9,1},{17,25},{25,17},{2,10},{10... | collective-permute-start | bytes 3145736 | tf_op jit(solution)/shard_map/ppermute | solution.py:363
  193.0 46.6 %collective-permute-start.14 = (bf16[256,2048]{1,0:T(8,128)(2,1)}, bf16[256,2048]{1,0:T(8,128)(2,1)}, u32[]{:S(2)}, u32[]{:S(2)}) collective-permute-start(bf16[256,2048]{1,0:T(8,128)(2,1)} %get-tuple-element.245), channel_id=1, source_target_pairs={{0,8},{8,0},{16,24},{24,16},{1,9},{9,1},{17,25},{25,17},{2,10},{10... | collective-permute-start | bytes 3145736 | tf_op jit(solution)/shard_map/ppermute | solution.py:363
  193.5 48.1 %collective-permute-start.16 = (bf16[256,2048]{1,0:T(8,128)(2,1)}, bf16[256,2048]{1,0:T(8,128)(2,1)}, u32[]{:S(2)}, u32[]{:S(2)}) collective-permute-start(bf16[256,2048]{1,0:T(8,128)(2,1)} %get-tuple-element.245), channel_id=1, source_target_pairs={{0,16},{8,24},{16,0},{24,8},{1,17},{9,25},{17,1},{25,9},{2,18},{10... | collective-permute-start | bytes 3145736 | tf_op jit(solution)/shard_map/ppermute | solution.py:363
  423.4 179.7 %reduce-scatter.7.cloned.1.call-start = ((), (), s32[]{:S(2)}) async-start(), calls=%async_computation.11 | async-start | bytes 9437184 | tf_op jit(solution)/shard_map/reduce_scatter | solution.py:628
  458.2 317.6 %reduce-scatter.9.cloned.1.call-start = ((), (), s32[]{:S(2)}) async-start(), calls=%async_computation.12 | async-start | bytes 7077888 | tf_op jit(solution)/shard_map/reduce_scatter | solution.py:628
  511.1 92.0 %collective-permute-start.32 = (bf16[256,2048]{1,0:T(8,128)(2,1)}, bf16[256,2048]{1,0:T(8,128)(2,1)}, u32[]{:S(2)}, u32[]{:S(2)}) collective-permute-start(bf16[256,2048]{1,0:T(8,128)(2,1)} %get-tuple-element.165), channel_id=1, source_target_pairs={{0,8},{8,0},{16,24},{24,16},{1,9},{9,1},{17,25},{25,17},{2,10},{10... | collective-permute-start | bytes 3145736 | tf_op jit(solution)/shard_map/ppermute | solution.py:363
  511.4 91.6 %collective-permute-start.33 = (bf16[256,2048]{1,0:T(8,128)(2,1)}, bf16[256,2048]{1,0:T(8,128)(2,1)}, u32[]{:S(2)}, u32[]{:S(2)}) collective-permute-start(bf16[256,2048]{1,0:T(8,128)(2,1)} %get-tuple-element.166), channel_id=1, source_target_pairs={{0,16},{8,24},{16,0},{24,8},{1,17},{9,25},{17,1},{25,9},{2,18},{10... | collective-permute-start | bytes 3145736 | tf_op jit(solution)/shard_map/ppermute | solution.py:363
  512.8 90.2 %collective-permute-start.31 = (bf16[256,2048]{1,0:T(8,128)(2,1)}, bf16[256,2048]{1,0:T(8,128)(2,1)S(1)}, u32[]{:S(2)}, u32[]{:S(2)}) collective-permute-start(bf16[256,2048]{1,0:T(8,128)(2,1)} %get-tuple-element.164), channel_id=1, source_target_pairs={{0,8},{8,0},{16,24},{24,16},{1,9},{9,1},{17,25},{25,17},{2,10},{10... | collective-permute-start | bytes 3145736 | tf_op jit(solution)/shard_map/ppermute | solution.py:363
  513.4 89.7 %collective-permute-start.37 = (bf16[256,2048]{1,0:T(8,128)(2,1)}, bf16[256,2048]{1,0:T(8,128)(2,1)}, u32[]{:S(2)}, u32[]{:S(2)}) collective-permute-start(bf16[256,2048]{1,0:T(8,128)(2,1)} %get-tuple-element.175), channel_id=1, source_target_pairs={{0,16},{8,24},{16,0},{24,8},{1,17},{9,25},{17,1},{25,9},{2,18},{10... | collective-permute-start | bytes 3145736 | tf_op jit(solution)/shard_map/ppermute | solution.py:363
  610.5 46.2 %collective-permute-start.38 = (bf16[256,2048]{1,0:T(8,128)(2,1)S(1)}, bf16[256,2048]{1,0:T(8,128)(2,1)}, u32[]{:S(2)}, u32[]{:S(2)}) collective-permute-start(bf16[256,2048]{1,0:T(8,128)(2,1)S(1)} %get-tuple-element.233), channel_id=1, source_target_pairs={{0,8},{8,0},{16,24},{24,16},{1,9},{9,1},{17,25},{25,17},{2,10},{10... | collective-permute-start | bytes 3145736 | tf_op jit(solution)/shard_map/ppermute | solution.py:363
  610.9 45.8 %collective-permute-start.39 = (bf16[256,2048]{1,0:T(8,128)(2,1)S(1)}, bf16[256,2048]{1,0:T(8,128)(2,1)}, u32[]{:S(2)}, u32[]{:S(2)}) collective-permute-start(bf16[256,2048]{1,0:T(8,128)(2,1)S(1)} %get-tuple-element.232), channel_id=1, source_target_pairs={{0,16},{8,24},{16,0},{24,8},{1,17},{9,25},{17,1},{25,9},{2,18},{10... | collective-permute-start | bytes 3145736 | tf_op jit(solution)/shard_map/ppermute | solution.py:363
  657.6 126.5 %reduce-scatter.11.cloned.1.call-start = ((), (), s32[]{:S(2)}) async-start(), calls=%async_computation.13 | async-start | bytes 2359296 | tf_op jit(solution)/shard_map/reduce_scatter | solution.py:709
  693.5 51.9 %collective-permute-start.40 = (bf16[256,2048]{1,0:T(8,128)(2,1)}, bf16[256,2048]{1,0:T(8,128)(2,1)}, u32[]{:S(2)}, u32[]{:S(2)}) collective-permute-start(bf16[256,2048]{1,0:T(8,128)(2,1)} %get-tuple-element.211), channel_id=1, source_target_pairs={{0,8},{8,0},{16,24},{24,16},{1,9},{9,1},{17,25},{25,17},{2,10},{10... | collective-permute-start | bytes 3145736 | tf_op jit(solution)/shard_map/ppermute | solution.py:363
  (115 other events, 1866.7 us)
Sparse Core Ops, SparseCore 0:
  10.4 67.4 all-gather.4
  79.5 80.6 all-gather.6
  161.9 80.5 all-gather.8
  243.9 81.0 all-gather.10
  423.5 87.5 reduce-scatter.4
  513.3 87.9 reduce-scatter.6
  657.7 67.5 reduce-scatter.8
  727.6 35.3 reduce-scatter.10

commit v8 on v7

--- a/solution.py
+++ b/solution.py
@@ -12,6 +12,7 @@
 HEAD_DIM = 64
 BLOCK = 256
 PAIR = 2 * HEAD_DIM
+GRANT = 58 * 2**20
 
 
 def estimate(flops, transcendentals=0):
@@ -173,7 +174,7 @@
             jax.ShapeDtypeStruct((rows, pairs * PAIR), jnp.bfloat16),
             jax.ShapeDtypeStruct((rows, pairs * PAIR), jnp.float32),
         ],
-        compiler_params=pltpu.CompilerParams(vmem_limit_bytes=24 * 2**20),
+        compiler_params=pltpu.CompilerParams(vmem_limit_bytes=GRANT),
         cost_estimate=estimate(scored * 2 * 512, scored),
         name="attend_forward",
     )(mask, slopes, qkv)
@@ -197,7 +198,7 @@
         ),
         out_shape=jax.ShapeDtypeStruct((rows, width), jnp.bfloat16),
         input_output_aliases={6: 0} if earlier else {},
-        compiler_params=pltpu.CompilerParams(vmem_limit_bytes=24 * 2**20),
+        compiler_params=pltpu.CompilerParams(vmem_limit_bytes=GRANT),
         cost_estimate=estimate(scored * 2 * 1280, scored),
         name="attend_backward",
     )(mask, slopes, qkv, lse, mixed, grad, *earlier)
@@ -255,7 +256,7 @@
             jax.ShapeDtypeStruct((count, width), jnp.bfloat16),
             jax.ShapeDtypeStruct((count, width), jnp.float32),
         ],
-        compiler_params=pltpu.CompilerParams(vmem_limit_bytes=28 * 2**20),
+        compiler_params=pltpu.CompilerParams(vmem_limit_bytes=GRANT),
         cost_estimate=estimate(count * depth * width * 4, 2 * count * width),
         name="up_and_bend",
     )(rows, weight, bias)
@@ -279,7 +280,7 @@
             jax.ShapeDtypeStruct((count, width), jnp.bfloat16),
             jax.ShapeDtypeStruct((1, width), jnp.float32),
         ],
-        compiler_params=pltpu.CompilerParams(vmem_limit_bytes=28 * 2**20),
+        compiler_params=pltpu.CompilerParams(vmem_limit_bytes=GRANT),
         cost_estimate=estimate(count * depth * width * 3, 0),
         name="hidden_gradient",
     )(rows, weight, slope)
@@ -324,7 +325,7 @@
             jax.ShapeDtypeStruct((rows, width), jnp.float32),
             jax.ShapeDtypeStruct((8, width), jnp.float32),
         ],
-        compiler_params=pltpu.CompilerParams(vmem_limit_bytes=40 * 2**20),
+        compiler_params=pltpu.CompilerParams(vmem_limit_bytes=GRANT),
         cost_estimate=estimate(30 * rows * width, rows),
         name="norm_back",
     )(rest, values, base, gain[None], *came)
@@ -352,7 +353,7 @@
         ],
         out_specs=pl.BlockSpec((shards, 1, part // shards, width), lambda i: (0, i, 0, 0)),
         out_shape=jax.ShapeDtypeStruct((shards, groups, part // shards, width), jnp.bfloat16),
-        compiler_params=pltpu.CompilerParams(vmem_limit_bytes=28 * 2**20),
+        compiler_params=pltpu.CompilerParams(vmem_limit_bytes=GRANT),
         cost_estimate=estimate(2 * tokens * rows * width, 0),
         name="outer",
     )(left, right)
@@ -452,23 +453,33 @@
         top, bottom = self(far_half, rows)
         return product, rows, axis, (top, bottom) if held else (swap(top, 1), swap(bottom, 2))
 
-    def make_rest(self, begun, held=False):
+    def make_rest(self, begun, later=False):
         product, rows, axis, far = begun
         if far is None:
             return lax.psum_scatter(self(product, rows), "seq", scatter_dimension=0, tiled=True), None, None
         count = rows.shape[axis] // 4
         rest = self(lambda values: product(lax.slice_in_dim(values, 0, 3 * count, axis=axis)), rows)
+        if later:
+            return rest, far, None
         count = rest.shape[0] // 3
         half = count // 2
-        direct = rest[count : count + half], rest[2 * count + half :]
-        return rest, far, direct if held else (swap(direct[0], 1), swap(direct[1], 2))
-
-    def send_held(self, begun, which, *before):
-        rest, *parts = begun
-        if parts[which] is not None:
-            first, second = gate(parts[which], *before) if before else parts[which]
-            parts[which] = swap(first, 1), swap(second, 2)
-        return rest, *parts
+        return rest, far, (swap(rest[count : count + half], 1), swap(rest[2 * count + half :], 2))
+
+    def send_direct(self, begun, *before):
+        rest, far, _ = begun
+        if far is None:
+            return begun
+        count = rest.shape[0] // 3
+        half = count // 2
+        first, second = gate((rest[count : count + half], rest[2 * count + half :]), *before)
+        return rest, far, (swap(first, 1), swap(second, 2))
+
+    def send_held(self, begun, *before):
+        rest, far, direct = begun
+        if far is not None:
+            first, second = gate(far, *before)
+            far = swap(first, 1), swap(second, 2)
+        return rest, far, direct
 
     def add_far(self, begun, *before):
         rest, far, direct = begun
@@ -479,14 +490,18 @@
         def add(rest, top, bottom):
             half = top.shape[0]
             first, second = rest[3 * half : 4 * half], rest[4 * half : 5 * half]
-            return (
-                (first.astype(wide) + bottom.astype(wide)).astype(rest.dtype),
-                (second.astype(wide) + top.astype(wide)).astype(rest.dtype),
-            )
+            first = (first.astype(wide) + bottom.astype(wide)).astype(rest.dtype)
+            second = (second.astype(wide) + top.astype(wide)).astype(rest.dtype)
+            if direct is None:
+                first = jnp.concatenate([rest[2 * half : 3 * half], first], axis=0)
+                second = jnp.concatenate([second, rest[5 * half :]], axis=0)
+            return first, second
 
         first, second = self(add, rest, *far)
         if before:
             first, second = gate((first, second), *before)
+        if direct is None:
+            return rest, (swap(first, 1), swap(second, 2))
         return rest, (direct[0], swap(first, 1), swap(second, 2), direct[1])
 
 
@@ -494,6 +509,8 @@
     wide = jnp.float32
     if came is None:
         return rest.astype(wide)
+    if len(came) == 2:
+        return rest[: came[0].shape[0]].astype(wide) + came[0].astype(wide) + came[1].astype(wide)
     half = came[0].shape[0]
     first_top, first_bottom, second_top, second_bottom = (part.astype(wide) for part in came)
     top = rest[:half].astype(wide) + first_top + second_top
@@ -614,10 +631,9 @@
     second = order.gather(order(halves_of, second_norm))
     mine, theirs = order(pair_halves, mixed_slots)
     upstream_made = order.fill(upstream)
-    theirs = pair_swap(theirs)
+    mixed_half = order(lambda *parts: jnp.concatenate(parts, axis=0), mine, pair_swap(theirs))
     second = whole(order.pass_on(second))
     upstream = order.pass_on(upstream, second)
-    mixed_half = order(lambda *parts: jnp.concatenate(parts, axis=0), mine, theirs)
     active, slope = order(lambda rows: up_and_bend(rows, up_slab, up_bias_slab[None]), second)
     upstream = order.complete(upstream_made, upstream)
 
@@ -635,26 +651,26 @@
             jnp.swapaxes(slabs[:, at : at + count], 0, 1).astype(wide) for at in range(0, slabs.shape[1], count)
         ]
 
+    down_sum = slab_sum(slab_product(upstream, active))
+
+    def to_result(rows):
+        return contract(rows, down_slab).astype(low)
+
+    outcome = order.send_far(to_result, active)
     hidden_grad, hidden_sum = order(lambda rows: hidden_gradient(rows, down_slab, slope), upstream)
 
     def to_second(rows):
         return contract_last(rows, up_slab).astype(low)
 
+    if square:
+        order.after(*outcome[3])
     second_grad = order.add_far(order.make_rest(order.send_far(to_second, hidden_grad)))
-    def to_result(rows):
-        return contract(rows, down_slab).astype(low)
-
-    outcome = order.send_far(to_result, active, held=True)
-    down_sum = slab_product(upstream, active)
-    if square:
-        down_sum = gate(down_sum, *second_grad[1][0::3])
-    down_sum = slab_sum(down_sum)
+    outcome = order.make_rest(outcome, later=True)
     up_sum = slab_product(second, hidden_grad)
     if square:
         up_sum = gate(up_sum, *second_grad[1])
+        outcome = order.send_direct(outcome, *second_grad[1])
     up_sum = slab_sum(up_sum)
-
-
     branch_grad, middle_grad, middle_sums = order(
         lambda rest, *came: norm_back(rest, middle, dz_low, ln2_gain, came), second_grad[0], *(second_grad[1] or ())
     )
@@ -668,37 +684,27 @@
     early = [middle_sums[2], middle_sums[0], middle_sums[1], hidden_sum, middle_sums[3]]
     mixed_grad = order(lambda rows: contract_last(rows, full_out).astype(low), branch_grad)
     mixed_grad = exchange(by_index([mixed_grad[:, j * slab : (j + 1) * slab] for j in range(groups)], me))
-    outcome = order.make_rest(outcome, held=True)
+    branch_pair = jnp.concatenate([branch_grad, pair_swap(branch_grad)], axis=0)
+    out_sum = order(lambda columns: outer(columns, branch_pair, groups, 1), mixed_half)
+    if square:
+        order.after(*outcome[2])
     mixed_grad = order(lambda *parts: jnp.concatenate(parts, axis=0), *mixed_grad)
-    outcome = order.send_held(order.send_held(outcome, 0, mixed_grad), 1, mixed_grad)
-    branch_pair = jnp.concatenate([branch_grad, pair_swap(branch_grad)], axis=0)
-
-    def to_out(columns):
-        return contract_first(columns, branch_pair).astype(low)
-
+    if square:
+        count = out_sum.shape[0] // 4
+        far = out_sum[3 * count : 3 * count + count // 2], out_sum[3 * count + count // 2 :]
+        out_begun = order.send_held((out_sum[: 3 * count], far, None), mixed_grad)
+    else:
+        out_begun = lax.psum_scatter(out_sum, "seq", scatter_dimension=0, tiled=True), None, None
     order.after(down_sum)
     attention = (mask, slopes, qkv, log_totals, attended)
     begun = order(lambda rows: attend_backward(*attention, rows, seq_count, local_len, 0, pairs // 2), mixed_grad)
-    out_begun = order.make_rest(order.send_far(to_out, mixed_half, axis=1))
+    out_begun = order.add_far(out_begun)
+    outcome = order.add_far(outcome, begun)
     qkv_grad = order(
         lambda rows: attend_backward(*attention, rows, seq_count, local_len, pairs // 2, pairs, begun), mixed_grad
     )
-    out_begun = order.add_far(out_begun)
     if square:
-        order.after(*outcome[1], *outcome[2])
-    order.after(up_sum)
-
-    def to_normed(rows):
-        return contract_last(rows, qkv_slab).astype(low)
-
-    normed_grad = order.send_far(to_normed, qkv_grad)
-    qkv_sum = slab_product(normed, qkv_grad)
-    if square:
-        qkv_sum = gate(qkv_sum, *normed_grad[3], *out_begun[1])
-    qkv_sum = slab_sum(qkv_sum)
-    normed_grad = order.make_rest(normed_grad)
-    normed_grad = order.add_far(normed_grad)
-    outcome = order.add_far(outcome)
+        order.after(*out_begun[1])
     out_sum = order(
         lambda own, *came: summed(own, came or None).astype(low), out_begun[0], *(out_begun[1] or ())
     ).reshape(-1, 1, out_rows, model_width)
@@ -707,6 +713,18 @@
         [jnp.where(parity == 0, out_sum, zero), jnp.where(parity == 1, out_sum, zero)], axis=1
     ).reshape(-1, model_width)
     grad_w_out = lax.psum_scatter(out_sum, "fsdp", scatter_dimension=0, tiled=True).astype(wide)
+    order.after(up_sum, *(out_begun[1] or ()))
+
+    def to_normed(rows):
+        return contract_last(rows, qkv_slab).astype(low)
+
+    normed_grad = order.send_far(to_normed, qkv_grad)
+    qkv_sum = slab_product(normed, qkv_grad)
+    if square:
+        qkv_sum = gate(qkv_sum, *normed_grad[3], *outcome[1])
+    qkv_sum = slab_sum(qkv_sum)
+    normed_grad = order.make_rest(normed_grad)
+    normed_grad = order.add_far(normed_grad)
     grad_tokens, _, input_sums = order(
         lambda rest, *came: norm_back(rest, x_low, middle_grad, ln1_gain, came),
         normed_grad[0],

time: 808 us -> 783 us (0.969)
  local copies, waits for them, and re-layouts: 147 us -> 100 us
  Pallas kernels: 208 us -> 246 us
  starting transfers between devices: 80.3 us -> 66.6 us
    unnamed x177 -> x103, local copies, waits for them, and re-layouts: 95 us -> 45.8 us
    pallas_call x3 -> x4, Pallas kernels: 54.7 us -> 74.6 us  [outer(): pl.pallas_call(partial(outer_kernel, chunk=512 if width % 512 == 0 else 2...]
    ppermute x7, waiting for transfers between devices: 2.81 us -> 16.8 us  [total(): lax.ppermute(values, axis, [(i, i ^ mask) for i in range(count)])]
    ppermute x7, starting transfers between devices: 19.6 us -> 7.18 us  [total(): lax.ppermute(values, axis, [(i, i ^ mask) for i in range(count)])]
    all_gather x1, waiting for transfers between devices: 13.1 us -> 0.89 us  [local(): lax.all_gather(own_slab(gate(w_down, normed[0]) if square else w_down, 0)...]
    dot_general x2 -> x0, matrix products: 9.95 us -> none  [contract_first(): lax.dot_general(left_side, right_side, (((0,), (0,)), ((), ())), preferre...]
    ppermute x48 -> x46, waiting for transfers between devices: 179 us -> 175 us  [swap(): return lax.ppermute(values, 'seq', [(i, i ^ bit) for i in range(4)])]
    ppermute x48 -> x46, starting transfers between devices: 52.9 us -> 51.4 us  [swap(): return lax.ppermute(values, 'seq', [(i, i ^ bit) for i in range(4)])]
  transfers between devices with their start and end apart: 67 -> 65, of which waited for: 25 -> 24; matrix products, arithmetic and copies ran while one was open for 28% -> 30% of each run, Pallas kernels for 23% -> 31%
where the time goes in v8:
time: 783 us; the launch traced here: 778 us
  Pallas kernels  246 us (31%)
  waiting for transfers between devices  200 us (26%)
  matrix products  110 us (14%)
  local copies, waits for them, and re-layouts  100 us (13%)
  starting transfers between devices  66.6 us (9%)
  other arithmetic  41.1 us (5%)
  between operations  15.2 us (2%)
    ppermute x46, waiting for transfers between devices, swap(): return lax.ppermute(values, 'seq', [(i, i ^ bit) for i in range(4)])  175 us
    pallas_call x4, Pallas kernels, outer(): pl.pallas_call(partial(outer_kernel, chunk=512 if width % 512 == 0 else 2...  74.6 us
    pallas_call x2, Pallas kernels, attend_backward(): pl.pallas_call(partial(attend_backward_kernel, blocks=blocks, seqs=seqs,...  57.4 us
    dot_general x5, matrix products, contract_last(): lax.dot_general(left_side, right_side, (((1,), (1,)), ((), ())), preferre...  55.8 us
    dot_general x4, matrix products, contract(): lax.dot_general(left_side, right_side, (((1,), (0,)), ((), ())), preferre...  54.2 us
    ppermute x46, starting transfers between devices, swap(): return lax.ppermute(values, 'seq', [(i, i ^ bit) for i in range(4)])  51.4 us
    unnamed x103, local copies, waits for them, and re-layouts  45.8 us
    pallas_call x1, Pallas kernels, up_and_bend(): pl.pallas_call(partial(up_kernel, chunk=512), grid=(count // TILE,), in_s...  30.7 us
  transfers between devices with their start and end apart: 65, of which 24 were waited for; matrix products, arithmetic and copies ran while one was open for 30% of the time, Pallas kernels for 31%

profile of v8, /device:TPU:0, one launch (start us, length us, event | category | flops | bytes accessed | tf_op | source)
XLA Modules:
  0.0 778.3 jit_solution(16722265843389346458)
XLA Ops:
  27.1 18.7 %collective-permute-done.2 = bf16[256,2048]{1,0:T(8,128)(2,1)} collective-permute-done((bf16[256,2048]{1,0:T(8,128)(2,1)}, bf16[256,2048]{1,0:T(8,128)(2,1)}, u32[]{:S(2)}, u32[]{:S(2)}) %collective-permute-start.2) | collective-permute-done | bytes 1048608 | tf_op jit(solution)/shard_map/ppermute | solution.py:364
  52.6 17.7 %collective-permute-done = bf16[256,2048]{1,0:T(8,128)(2,1)} collective-permute-done((bf16[256,2048]{1,0:T(8,128)(2,1)}, bf16[256,2048]{1,0:T(8,128)(2,1)}, u32[]{:S(2)}, u32[]{:S(2)}) %collective-permute-start) | collective-permute-done | bytes 1048608 | tf_op jit(solution)/shard_map/ppermute | solution.py:364
  78.5 12.8 %collective-permute-done.4 = bf16[256,2048]{1,0:T(8,128)(2,1)} collective-permute-done((bf16[256,2048]{1,0:T(8,128)(2,1)}, bf16[256,2048]{1,0:T(8,128)(2,1)}, u32[]{:S(2)}, u32[]{:S(2)}) %collective-permute-start.4) | collective-permute-done | bytes 1048608 | tf_op jit(solution)/shard_map/ppermute | solution.py:364
  100.0 18.6 %add_convert_fusion.qkv_ref = bf16[2048,1536]{1,0:T(8,128)(2,1)} fusion(bf16[2048,2048]{1,0:T(8,128)(2,1)} %constant_dynamic-update-slice_fusion.left_ref, bf16[2048,1536]{1,0:T(8,128)(2,1)} %all-gather.5.cloned.1.call-done, f32[1536]{0:T(1024)S(1)} %reduce.2), kind=kOutput, calls=%fused_computation.1 | convolution fusion | flops 12891193344 | bytes 20977664 | tf_op jit(solution)/shard_map/dot_general | solution.py:30
  118.6 29.7 %attend_forward.1 = (bf16[2048,512]{1,0:T(8,128)(2,1)}, f32[2048,512]{1,0:T(8,128)}) custom-call(s32[1]{0:T(128)} %bitcast.1.at_ref.mask_ref, f32[8]{0:T(128)} %multiply_power_fusion.slope_ref, bf16[2048,1536]{1,0:T(8,128)(2,1)} %add_convert_fusion.qkv_ref), custom_call_target="tpu_custom_call" | custom-call | flops 2684354560 | bytes 2621440 | tf_op jit(solution)/shard_map/attend_forward/pallas_call | solution.py:165
  220.0 15.1 %collective-permute-done.15 = bf16[256,2048]{1,0:T(8,128)(2,1)} collective-permute-done((bf16[256,2048]{1,0:T(8,128)(2,1)}, bf16[256,2048]{1,0:T(8,128)(2,1)}, u32[]{:S(2)}, u32[]{:S(2)}) %collective-permute-start.15) | collective-permute-done | bytes 1048608 | tf_op jit(solution)/shard_map/ppermute | solution.py:364
  266.9 30.7 %up_and_bend.1 = (bf16[2048,2048]{1,0:T(8,128)(2,1)}, f32[2048,2048]{1,0:T(8,128)}) custom-call(bf16[2048,2048]{1,0:T(8,128)(2,1)} %constant_dynamic-update-slice_fusion.7.rows_ref.left_ref, bf16[2048,2048]{1,0:T(8,128)(2,1)} %all-gather.9.cloned.1.call-done.weight_ref, f32[1,2048]{1,0:T(1,128)} %bitcast.133), custom_call_target="tpu_custom_call" | custom-call | flops 8589934592 | bytes 8388608 | tf_op jit(solution)/shard_map/up_and_bend/pallas_call | solution.py:246
  301.0 23.6 %outer.4 = bf16[8,4,64,2048]{3,2,1,0:T(8,128)(2,1)} custom-call(bf16[2048,2048]{1,0:T(8,128)(2,1)} %constant_dynamic-update-slice_fusion.35.left_ref.rows_ref, bf16[2048,2048]{1,0:T(8,128)(2,1)} %get-tuple-element.147.right_ref), custom_call_target="tpu_custom_call" | custom-call | flops 4294967296 | bytes 4194304 | tf_op jit(solution)/shard_map/outer/pallas_call | solution.py:347
  337.4 25.4 %hidden_gradient.1 = (bf16[2048,2048]{1,0:T(8,128)(2,1)}, f32[1,2048]{1,0:T(1,128)}) custom-call(bf16[2048,2048]{1,0:T(8,128)(2,1)} %constant_dynamic-update-slice_fusion.35.left_ref.rows_ref, bf16[2048,2048]{1,0:T(8,128)(2,1)} %all-gather.11.cloned.1.call-done.weight_ref, f32[2048,2048]{1,0:T(8,128)} %get-tuple-element.132.slope_ref), custom_call_target="tpu_custom_call" | custom-call | flops 6442450944 | bytes 6291456 | tf_op jit(solution)/shard_map/hidden_gradient/pallas_call | solution.py:270
  374.1 17.5 %convolution_convert_fusion.2.rest_ref = bf16[1536,2048]{1,0:T(8,128)(2,1)S(1)} fusion(bf16[2048,2048]{1,0:T(8,128)(2,1)} %all-gather.9.cloned.1.call-done.weight_ref, bf16[2048,2048]{1,0:T(8,128)(2,1)} %get-tuple-element.143.right_ref), kind=kOutput, calls=%fused_computation.4 | convolution fusion | flops 12888047616 | bytes 20971520 | tf_op jit(solution)/shard_map/dot_general | solution.py:36
  402.6 19.3 %convolution_convert_fusion.1 = bf16[1536,2048]{1,0:T(8,128)(2,1)} fusion(bf16[2048,2048]{1,0:T(8,128)(2,1)} %all-gather.11.cloned.1.call-done.weight_ref, bf16[2048,2048]{1,0:T(8,128)(2,1)} %get-tuple-element.147.right_ref), kind=kOutput, calls=%fused_computation.3 | convolution fusion | flops 12888047616 | bytes 20971520 | tf_op jit(solution)/shard_map/dot_general | solution.py:30
  421.9 23.6 %outer.5 = bf16[8,4,64,2048]{3,2,1,0:T(8,128)(2,1)} custom-call(bf16[2048,2048]{1,0:T(8,128)(2,1)} %constant_dynamic-update-slice_fusion.7.rows_ref.left_ref, bf16[2048,2048]{1,0:T(8,128)(2,1)} %get-tuple-element.143.right_ref), custom_call_target="tpu_custom_call" | custom-call | flops 4294967296 | bytes 4194304 | tf_op jit(solution)/shard_map/outer/pallas_call | solution.py:347
  446.4 11.9 %norm_back.2 = (bf16[512,2048]{1,0:T(8,128)(2,1)}, f32[512,2048]{1,0:T(8,128)}, f32[8,2048]{1,0:T(8,128)}) custom-call(bf16[1536,2048]{1,0:T(8,128)(2,1)} %copy-done.4, f32[512,2048]{1,0:T(8,128)} %copy-done, bf16[512,2048]{1,0:T(8,128)(2,1)} %bitcast.103, f32[1,2048]{1,0:T(1,128)} %bitcast.119, bf16[256,2048]{1,0:T(8,128)(2,1)} %collective-permute-done.26.refs_0_, ...), custom_call_target="tpu_custom_call" | custom-call | flops 7864320 | bytes 7680 | tf_op jit(solution)/shard_map/norm_back/pallas_call | solution.py:318
  487.0 11.2 %collective-permute-done.34 = bf16[512,512]{1,0:T(8,128)(2,1)S(1)} collective-permute-done((bf16[512,512]{1,0:T(8,128)(2,1)}, bf16[512,512]{1,0:T(8,128)(2,1)S(1)}, u32[]{:S(2)}, u32[]{:S(2)}) %collective-permute-start.34) | collective-permute-done | bytes 524320 | tf_op jit(solution)/shard_map/ppermute | solution.py:364
  498.2 11.3 %collective-permute-done.32 = bf16[512,512]{1,0:T(8,128)(2,1)S(1)} collective-permute-done((bf16[512,512]{1,0:T(8,128)(2,1)}, bf16[512,512]{1,0:T(8,128)(2,1)S(1)}, u32[]{:S(2)}, u32[]{:S(2)}) %collective-permute-start.32) | collective-permute-done | bytes 524320 | tf_op jit(solution)/shard_map/ppermute | solution.py:364
  518.8 28.7 %attend_backward.2.rest_0_ = bf16[2048,1536]{1,0:T(8,128)(2,1)} custom-call(s32[1]{0:T(128)} %bitcast.1.at_ref.mask_ref, f32[8]{0:T(128)} %multiply_power_fusion.slope_ref, bf16[2048,1536]{1,0:T(8,128)(2,1)} %add_convert_fusion.qkv_ref, f32[2048,512]{1,0:T(8,128)} %get-tuple-element.113.lse_ref, bf16[2048,512]{1,0:T(8,128)(2,1)} %get-tuple-element.112.mixed_ref, ...), custom_call_target="tpu_custom_call" | custom-call | flops 3355443200 | bytes 3276800 | tf_op jit(solution)/shard_map/attend_backward/pallas_call | solution.py:190
  556.7 28.7 %attend_backward.3.right_ref = bf16[2048,1536]{1,0:T(8,128)(2,1)} custom-call(s32[1]{0:T(128)} %bitcast.1.at_ref.mask_ref, f32[8]{0:T(128)} %multiply_power_fusion.slope_ref, bf16[2048,1536]{1,0:T(8,128)(2,1)} %add_convert_fusion.qkv_ref, f32[2048,512]{1,0:T(8,128)} %get-tuple-element.113.lse_ref, ...), custom_call_target="tpu_custom_call", output_to_operand_aliasing={{}: (6, {})} | custom-call | flops 3355443200 | bytes 3276800 | tf_op jit(solution)/shard_map/attend_backward/pallas_call | solution.py:190
  601.0 18.7 %outer.7 = bf16[8,4,64,1536]{3,2,1,0:T(8,128)(2,1)} custom-call(bf16[2048,2048]{1,0:T(8,128)(2,1)} %constant_dynamic-update-slice_fusion.left_ref, bf16[2048,1536]{1,0:T(8,128)(2,1)} %attend_backward.3.right_ref), custom_call_target="tpu_custom_call" | custom-call | flops 3221225472 | bytes 3145728 | tf_op jit(solution)/shard_map/outer/pallas_call | solution.py:347
  619.7 16.8 %collective-permute-done.44 = bf16[256,2048]{1,0:T(8,128)(2,1)S(1)} collective-permute-done((bf16[256,2048]{1,0:T(8,128)(2,1)S(1)}, bf16[256,2048]{1,0:T(8,128)(2,1)S(1)}, u32[]{:S(2)}, u32[]{:S(2)}) %collective-permute-start.44) | collective-permute-done | bytes 1048608 | tf_op jit(solution)/shard_map/ppermute | solution.py:364
  637.0 14.6 %convolution_convert_fusion.rest_ref = bf16[1536,2048]{1,0:T(8,128)(2,1)S(1)} fusion(bf16[2048,1536]{1,0:T(8,128)(2,1)} %all-gather.5.cloned.1.call-done, bf16[2048,1536]{1,0:T(8,128)(2,1)} %attend_backward.3.right_ref), kind=kOutput, calls=%fused_computation.2 | convolution fusion | flops 9666822144 | bytes 17301504 | tf_op jit(solution)/shard_map/dot_general | solution.py:36
  661.8 17.7 %collective-permute-done.47.refs_3_ = bf16[256,2048]{1,0:T(8,128)(2,1)} collective-permute-done((bf16[256,2048]{1,0:T(8,128)(2,1)}, bf16[256,2048]{1,0:T(8,128)(2,1)}, u32[]{:S(2)}, u32[]{:S(2)}) %collective-permute-start.47) | collective-permute-done | bytes 1048608 | tf_op jit(solution)/shard_map/ppermute | solution.py:364
  679.9 18.2 %collective-permute-done.46.refs_2_ = bf16[256,2048]{1,0:T(8,128)(2,1)S(1)} collective-permute-done((bf16[256,2048]{1,0:T(8,128)(2,1)}, bf16[256,2048]{1,0:T(8,128)(2,1)S(1)}, u32[]{:S(2)}, u32[]{:S(2)}) %collective-permute-start.46) | collective-permute-done | bytes 1048608 | tf_op jit(solution)/shard_map/ppermute | solution.py:364
  700.1 11.2 %norm_back.3 = (bf16[512,2048]{1,0:T(8,128)(2,1)}, f32[512,2048]{1,0:T(8,128)}, f32[8,2048]{1,0:T(8,128)}) custom-call(bf16[1536,2048]{1,0:T(8,128)(2,1)} %copy-done.3, bf16[512,2048]{1,0:T(8,128)(2,1)} %bitcast.93, f32[512,2048]{1,0:T(8,128)} %get-tuple-element.156.base_ref, f32[1,2048]{1,0:T(1,128)} %bitcast.120, ...), custom_call_target="tpu_custom_call" | custom-call | flops 7864320 | bytes 7680 | tf_op jit(solution)/shard_map/norm_back/pallas_call | solution.py:318
  734.7 12.0 %collective-permute-done.54 = f32[192,128]{1,0:T(8,128)S(1)} collective-permute-done((f32[192,128]{1,0:T(8,128)S(1)}, f32[192,128]{1,0:T(8,128)S(1)}, u32[]{:S(2)}, u32[]{:S(2)}) %collective-permute-start.54) | collective-permute-done | bytes 98336 | tf_op jit(solution)/shard_map/ppermute | solution.py:531
  (324 shorter events, 309.4 us)
Async XLA Ops:
  7.2 92.8 %all-gather.5.cloned.1.call-start = ((), (), s32[]{:S(2)}) async-start(), calls=%async_computation.6 | async-start | bytes 7077888 | tf_op jit(solution)/shard_map/all_gather | solution.py:591
  10.3 169.3 %all-gather.7.cloned.1.call-start = ((), (), s32[]{:S(2)}) async-start(), calls=%async_computation.7 | async-start | bytes 9437184 | tf_op jit(solution)/shard_map/all_gather | solution.py:603
  11.1 255.8 %all-gather.9.cloned.1.call-start = ((), (), s32[]{:S(2)}) async-start(), calls=%async_computation.8 | async-start | bytes 9437184 | tf_op jit(solution)/shard_map/all_gather | solution.py:604
  18.4 307.2 %all-gather.11.cloned.1.call-start = ((), (), s32[]{:S(2)}) async-start(), calls=%async_computation.9 | async-start | bytes 9437184 | tf_op jit(solution)/shard_map/all_gather | solution.py:605
  22.9 47.4 %collective-permute-start = (bf16[256,2048]{1,0:T(8,128)(2,1)}, bf16[256,2048]{1,0:T(8,128)(2,1)}, u32[]{:S(2)}, u32[]{:S(2)}) collective-permute-start(bf16[256,2048]{1,0:T(8,128)(2,1)} %get-tuple-element.251), channel_id=1, source_target_pairs={{0,8},{8,0},{16,24},{24,16},{1,9},{9,1},{17,25},{25,17},{2,10},{10... | collective-permute-start | bytes 3145736 | tf_op jit(solution)/shard_map/ppermute | solution.py:364
  23.5 52.8 %collective-permute-start.3 = (bf16[256,2048]{1,0:T(8,128)(2,1)}, bf16[256,2048]{1,0:T(8,128)(2,1)}, u32[]{:S(2)}, u32[]{:S(2)}) collective-permute-start(bf16[256,2048]{1,0:T(8,128)(2,1)} %get-tuple-element.250), channel_id=1, source_target_pairs={{0,16},{8,24},{16,0},{24,8},{1,17},{9,25},{17,1},{25,9},{2,18},{10... | collective-permute-start | bytes 3145736 | tf_op jit(solution)/shard_map/ppermute | solution.py:364
  25.8 492.9 %reduce-scatter.5.cloned.1.call-start = ((), (), s32[]{:S(2)}) async-start(), calls=%async_computation.10 | async-start | bytes 9437184 | tf_op jit(solution)/shard_map/reduce_scatter | solution.py:644
  45.8 45.6 %collective-permute-start.4 = (bf16[256,2048]{1,0:T(8,128)(2,1)}, bf16[256,2048]{1,0:T(8,128)(2,1)}, u32[]{:S(2)}, u32[]{:S(2)}) collective-permute-start(bf16[256,2048]{1,0:T(8,128)(2,1)} %collective-permute-done.2), channel_id=1, source_target_pairs={{0,8},{8,0},{16,24},{24,16},{1,9},{9,1},{17,25},{25,17},{2,10},{10... | collective-permute-start | bytes 3145736 | tf_op jit(solution)/shard_map/ppermute | solution.py:364
  96.0 52.3 %collective-permute-start.8 = (bf16[256,2048]{1,0:T(8,128)(2,1)}, bf16[256,2048]{1,0:T(8,128)(2,1)}, u32[]{:S(2)}, u32[]{:S(2)}) collective-permute-start(bf16[256,2048]{1,0:T(8,128)(2,1)} %get-tuple-element.117), channel_id=1, source_target_pairs={{0,8},{8,0},{16,24},{24,16},{1,9},{9,1},{17,25},{25,17},{2,10},{10... | collective-permute-start | bytes 3145736 | tf_op jit(solution)/shard_map/ppermute | solution.py:364
  97.5 50.8 %collective-permute-start.7 = (bf16[256,2048]{1,0:T(8,128)(2,1)}, bf16[256,2048]{1,0:T(8,128)(2,1)}, u32[]{:S(2)}, u32[]{:S(2)}) collective-permute-start(bf16[256,2048]{1,0:T(8,128)(2,1)} %get-tuple-element.117), channel_id=1, source_target_pairs={{0,16},{8,24},{16,0},{24,8},{1,17},{9,25},{17,1},{25,9},{2,18},{10... | collective-permute-start | bytes 3145736 | tf_op jit(solution)/shard_map/ppermute | solution.py:364
  98.0 50.4 %collective-permute-start.9 = (bf16[256,2048]{1,0:T(8,128)(2,1)S(1)}, bf16[256,2048]{1,0:T(8,128)(2,1)}, u32[]{:S(2)}, u32[]{:S(2)}) collective-permute-start(bf16[256,2048]{1,0:T(8,128)(2,1)S(1)} %get-tuple-element.118), channel_id=1, source_target_pairs={{0,16},{8,24},{16,0},{24,8},{1,17},{9,25},{17,1},{25,9},{2,18},{10... | collective-permute-start | bytes 3145736 | tf_op jit(solution)/shard_map/ppermute | solution.py:364
  99.5 48.8 %collective-permute-start.6 = (bf16[256,2048]{1,0:T(8,128)(2,1)S(1)}, bf16[256,2048]{1,0:T(8,128)(2,1)}, u32[]{:S(2)}, u32[]{:S(2)}) collective-permute-start(bf16[256,2048]{1,0:T(8,128)(2,1)S(1)} %get-tuple-element.118), channel_id=1, source_target_pairs={{0,8},{8,0},{16,24},{24,16},{1,9},{9,1},{17,25},{25,17},{2,10},{10... | collective-permute-start | bytes 3145736 | tf_op jit(solution)/shard_map/ppermute | solution.py:364
  191.2 54.8 %collective-permute-start.16 = (bf16[256,2048]{1,0:T(8,128)(2,1)}, bf16[256,2048]{1,0:T(8,128)(2,1)}, u32[]{:S(2)}, u32[]{:S(2)}) collective-permute-start(bf16[256,2048]{1,0:T(8,128)(2,1)} %get-tuple-element.243), channel_id=1, source_target_pairs={{0,16},{8,24},{16,0},{24,8},{1,17},{9,25},{17,1},{25,9},{2,18},{10... | collective-permute-start | bytes 3145736 | tf_op jit(solution)/shard_map/ppermute | solution.py:364
  191.8 45.8 %collective-permute-start.14 = (bf16[256,2048]{1,0:T(8,128)(2,1)}, bf16[256,2048]{1,0:T(8,128)(2,1)}, u32[]{:S(2)}, u32[]{:S(2)}) collective-permute-start(bf16[256,2048]{1,0:T(8,128)(2,1)} %get-tuple-element.243), channel_id=1, source_target_pairs={{0,8},{8,0},{16,24},{24,16},{1,9},{9,1},{17,25},{25,17},{2,10},{10... | collective-permute-start | bytes 3145736 | tf_op jit(solution)/shard_map/ppermute | solution.py:364
  193.8 45.1 %collective-permute-start.13 = (bf16[256,2048]{1,0:T(8,128)(2,1)}, bf16[256,2048]{1,0:T(8,128)(2,1)}, u32[]{:S(2)}, u32[]{:S(2)}) collective-permute-start(bf16[256,2048]{1,0:T(8,128)(2,1)} %get-tuple-element.244), channel_id=1, source_target_pairs={{0,8},{8,0},{16,24},{24,16},{1,9},{9,1},{17,25},{25,17},{2,10},{10... | collective-permute-start | bytes 3145736 | tf_op jit(solution)/shard_map/ppermute | solution.py:364
  204.4 59.2 %collective-permute-start.19 = (bf16[512,1024]{1,0:T(8,128)(2,1)}, bf16[512,1024]{1,0:T(8,128)(2,1)}, u32[]{:S(2)}, u32[]{:S(2)}) collective-permute-start(bf16[512,1024]{1,0:T(8,128)(2,1)} %copy.51), channel_id=1, source_target_pairs={{0,1},{1,0},{2,3},{3,2},{4,5},{5,4},{6,7},{7,6},{8,9},{9,8},{10,11... | collective-permute-start | bytes 3145736 | tf_op jit(solution)/shard_map/ppermute | solution.py:617
  324.7 266.3 %reduce-scatter.7.cloned.1.call-start = ((), (), s32[]{:S(2)}) async-start(), calls=%async_computation.11 | async-start | bytes 9437184 | tf_op jit(solution)/shard_map/reduce_scatter | solution.py:644
  391.9 53.6 %collective-permute-start.29 = (bf16[256,2048]{1,0:T(8,128)(2,1)S(1)}, bf16[256,2048]{1,0:T(8,128)(2,1)S(1)}, u32[]{:S(2)}, u32[]{:S(2)}) collective-permute-start(bf16[256,2048]{1,0:T(8,128)(2,1)S(1)} %get-tuple-element.212), channel_id=1, source_target_pairs={{0,16},{8,24},{16,0},{24,8},{1,17},{9,25},{17,1},{25,9},{2,18},{10... | collective-permute-start | bytes 3145736 | tf_op jit(solution)/shard_map/ppermute | solution.py:364
  393.5 52.0 %collective-permute-start.26 = (bf16[256,2048]{1,0:T(8,128)(2,1)S(1)}, bf16[256,2048]{1,0:T(8,128)(2,1)}, u32[]{:S(2)}, u32[]{:S(2)}) collective-permute-start(bf16[256,2048]{1,0:T(8,128)(2,1)S(1)} %get-tuple-element.213), channel_id=1, source_target_pairs={{0,8},{8,0},{16,24},{24,16},{1,9},{9,1},{17,25},{25,17},{2,10},{10... | collective-permute-start | bytes 3145736 | tf_op jit(solution)/shard_map/ppermute | solution.py:364
  400.5 44.9 %collective-permute-start.28 = (bf16[256,2048]{1,0:T(8,128)(2,1)S(1)}, bf16[256,2048]{1,0:T(8,128)(2,1)}, u32[]{:S(2)}, u32[]{:S(2)}) collective-permute-start(bf16[256,2048]{1,0:T(8,128)(2,1)S(1)} %get-tuple-element.216), channel_id=1, source_target_pairs={{0,16},{8,24},{16,0},{24,8},{1,17},{9,25},{17,1},{25,9},{2,18},{10... | collective-permute-start | bytes 3145736 | tf_op jit(solution)/shard_map/ppermute | solution.py:364
  446.4 213.6 %reduce-scatter.11.cloned.1.call-start = ((), (), s32[]{:S(2)}) async-start(), calls=%async_computation.13 | async-start | bytes 2359296 | tf_op jit(solution)/shard_map/reduce_scatter | solution.py:715
  461.3 48.8 %collective-permute-start.30 = (bf16[256,2048]{1,0:T(8,128)(2,1)}, bf16[256,2048]{1,0:T(8,128)(2,1)S(1)}, u32[]{:S(2)}, u32[]{:S(2)}) collective-permute-start(bf16[256,2048]{1,0:T(8,128)(2,1)} %get-tuple-element.148), channel_id=1, source_target_pairs={{0,8},{8,0},{16,24},{24,16},{1,9},{9,1},{17,25},{25,17},{2,10},{10... | collective-permute-start | bytes 3145736 | tf_op jit(solution)/shard_map/ppermute | solution.py:364
  462.5 47.6 %collective-permute-start.35 = (bf16[256,2048]{1,0:T(8,128)(2,1)S(1)}, bf16[256,2048]{1,0:T(8,128)(2,1)S(1)}, u32[]{:S(2)}, u32[]{:S(2)}) collective-permute-start(bf16[256,2048]{1,0:T(8,128)(2,1)S(1)} %get-tuple-element.160), channel_id=1, source_target_pairs={{0,16},{8,24},{16,0},{24,8},{1,17},{9,25},{17,1},{25,9},{2,18},{10... | collective-permute-start | bytes 3145736 | tf_op jit(solution)/shard_map/ppermute | solution.py:364
  589.8 158.4 %reduce-scatter.9.cloned.1.call-start = ((), (), s32[]{:S(2)}) async-start(), calls=%async_computation.12 | async-start | bytes 7077888 | tf_op jit(solution)/shard_map/reduce_scatter | solution.py:644
  (77 other events, 1472.1 us)
Sparse Core Ops, SparseCore 0:
  10.4 67.4 all-gather.4
  79.5 80.6 all-gather.6
  161.9 80.5 all-gather.8
  244.5 81.0 all-gather.10
  327.7 87.7 reduce-scatter.4
  445.6 88.0 reduce-scatter.6
  589.9 33.4 reduce-scatter.10
  636.7 67.8 reduce-scatter.8

commit v9 on v8

--- a/solution.py
+++ b/solution.py
@@ -262,20 +262,20 @@
     )(rows, weight, bias)
 
 
-def hidden_gradient(rows, weight, slope):
-    count, depth = rows.shape
+def hidden_gradient(rows, weight, slope, start, count):
+    depth = rows.shape[1]
     width = weight.shape[0]
-    tile = pl.BlockSpec((TILE, width), lambda i: (i, 0))
+    first = start // TILE
     line = pl.BlockSpec((1, width), lambda i: (0, 0))
     return pl.pallas_call(
         partial(hidden_grad_kernel, chunk=512),
         grid=(count // TILE,),
         in_specs=[
-            pl.BlockSpec((TILE, depth), lambda i: (i, 0)),
+            pl.BlockSpec((TILE, depth), lambda i: (i + first, 0)),
             pl.BlockSpec((width, depth), lambda i: (0, 0), pipeline_mode=pl.Buffered(1)),
-            tile,
+            pl.BlockSpec((TILE, width), lambda i: (i + first, 0)),
         ],
-        out_specs=[tile, line],
+        out_specs=[pl.BlockSpec((TILE, width), lambda i: (i, 0)), line],
         out_shape=[
             jax.ShapeDtypeStruct((count, width), jnp.bfloat16),
             jax.ShapeDtypeStruct((1, width), jnp.float32),
@@ -289,10 +289,11 @@
 def norm_back_kernel(rest_ref, values_ref, base_ref, gain_ref, *refs, parts):
     came, (low_ref, wide_ref, sums_ref) = refs[:parts], refs[parts:]
     wide = jnp.float32
-    starting = pl.program_id(0) == 0
+    step = pl.program_id(0)
+    upper = step < pl.num_programs(0) // 2
     grad = rest_ref[...].astype(wide)
     for top, bottom in zip(came[0::2], came[1::2]):
-        grad = grad + jnp.where(starting, top[...], bottom[...]).astype(wide)
+        grad = grad + jnp.where(upper, top[...], bottom[...]).astype(wide)
     values = values_ref[...].astype(wide)
     base = base_ref[...].astype(wide)
     centred = values - jnp.mean(values, axis=-1, keepdims=True)
@@ -306,19 +307,22 @@
     wide_ref[...] = made
     for row, part in enumerate((grad * normal, grad, low.astype(wide), base)):
         line = jnp.sum(part, axis=0, keepdims=True)
-        sums_ref[row : row + 1, :] = jnp.where(starting, line, sums_ref[row : row + 1, :] + line)
+        sums_ref[row : row + 1, :] = jnp.where(step == 0, line, sums_ref[row : row + 1, :] + line)
 
 
 def norm_back(rest, values, base, gain, came):
     rows, width = values.shape
-    half = rows // 2
+    steps = 8
+    half = steps // 2
     came = list(came or ())
-    tile = pl.BlockSpec((half, width), lambda i: (i, 0))
-    every = pl.BlockSpec((half, width), lambda i: (0, 0), pipeline_mode=pl.Buffered(1))
+    count = rows // steps
+    tile = pl.BlockSpec((count, width), lambda i: (i, 0))
+    top = pl.BlockSpec((count, width), lambda i: (jnp.minimum(i, half - 1), 0))
+    bottom = pl.BlockSpec((count, width), lambda i: (jnp.maximum(i - half, 0), 0))
     return pl.pallas_call(
         partial(norm_back_kernel, parts=len(came)),
-        grid=(2,),
-        in_specs=[tile, tile, tile, pl.BlockSpec((1, width), lambda i: (0, 0))] + [every] * len(came),
+        grid=(steps,),
+        in_specs=[tile, tile, tile, pl.BlockSpec((1, width), lambda i: (0, 0))] + [top, bottom] * (len(came) // 2),
         out_specs=[tile, tile, pl.BlockSpec((8, width), lambda i: (0, 0))],
         out_shape=[
             jax.ShapeDtypeStruct((rows, width), jnp.bfloat16),
@@ -331,32 +335,39 @@
     )(rest, values, base, gain[None], *came)
 
 
-def outer_kernel(left_ref, right_ref, out_ref, *, chunk):
-    left = left_ref[...]
+def outer_kernel(left_ref, *refs, chunk):
+    right_refs, out_ref = refs[:-1], refs[-1]
     shards = out_ref.shape[0]
-    for at in range(0, right_ref.shape[1], chunk):
+    for at in range(0, out_ref.shape[3], chunk):
         columns = slice(at, at + chunk)
-        made = contract_first(left, right_ref[:, columns]).astype(out_ref.dtype)
-        out_ref[:, 0, :, columns] = made.reshape(shards, -1, made.shape[1])
-
-
-def outer(left, right, groups, shards):
+        made, row = None, 0
+        for right_ref in right_refs:
+            count = right_ref.shape[0]
+            part = contract_first(left_ref[row : row + count, :], right_ref[:, columns])
+            made = part if made is None else made + part
+            row += count
+        out_ref[:, 0, :, columns] = made.astype(out_ref.dtype).reshape(shards, -1, made.shape[1])
+
+
+def outer(left, rights, groups, shards):
+    rights = rights if isinstance(rights, (list, tuple)) else [rights]
     tokens, rows = left.shape
-    width = right.shape[1]
+    width = rights[0].shape[1]
     part = rows // groups
     made = pl.pallas_call(
         partial(outer_kernel, chunk=512 if width % 512 == 0 else 256),
         grid=(groups,),
-        in_specs=[
-            pl.BlockSpec((tokens, part), lambda i: (0, i)),
-            pl.BlockSpec((tokens, width), lambda i: (0, 0), pipeline_mode=pl.Buffered(1)),
+        in_specs=[pl.BlockSpec((tokens, part), lambda i: (0, i))]
+        + [
+            pl.BlockSpec((right.shape[0], width), lambda i: (0, 0), pipeline_mode=pl.Buffered(1))
+            for right in rights
         ],
         out_specs=pl.BlockSpec((shards, 1, part // shards, width), lambda i: (0, i, 0, 0)),
         out_shape=jax.ShapeDtypeStruct((shards, groups, part // shards, width), jnp.bfloat16),
         compiler_params=pltpu.CompilerParams(vmem_limit_bytes=GRANT),
         cost_estimate=estimate(2 * tokens * rows * width, 0),
         name="outer",
-    )(left, right)
+    )(left, *rights)
     return made.reshape(rows, width)
 
 
@@ -440,82 +451,46 @@
         far = [swap(second_top, 1), swap(first_bottom, 2)]
         return [*rows, first_top, first_bottom, second_top, second_bottom, *far]
 
-    def send_far(self, product, rows, axis=0, held=False):
-        if lax.axis_size("seq") != 4:
-            return product, rows, axis, None
-        count = rows.shape[axis] // 4
-
-        def far_half(values):
-            made = product(lax.slice_in_dim(values, 3 * count, 4 * count, axis=axis))
+    def halves(self, product, rows):
+        def cut(values):
+            made = product(values)
             half = made.shape[0] // 2
             return made[:half], made[half:]
 
-        top, bottom = self(far_half, rows)
-        return product, rows, axis, (top, bottom) if held else (swap(top, 1), swap(bottom, 2))
-
-    def make_rest(self, begun, later=False):
-        product, rows, axis, far = begun
-        if far is None:
-            return lax.psum_scatter(self(product, rows), "seq", scatter_dimension=0, tiled=True), None, None
-        count = rows.shape[axis] // 4
-        rest = self(lambda values: product(lax.slice_in_dim(values, 0, 3 * count, axis=axis)), rows)
-        if later:
-            return rest, far, None
-        count = rest.shape[0] // 3
-        half = count // 2
-        return rest, far, (swap(rest[count : count + half], 1), swap(rest[2 * count + half :], 2))
-
-    def send_direct(self, begun, *before):
-        rest, far, _ = begun
-        if far is None:
-            return begun
-        count = rest.shape[0] // 3
-        half = count // 2
-        first, second = gate((rest[count : count + half], rest[2 * count + half :]), *before)
-        return rest, far, (swap(first, 1), swap(second, 2))
-
-    def send_held(self, begun, *before):
-        rest, far, direct = begun
-        if far is not None:
-            first, second = gate(far, *before)
-            far = swap(first, 1), swap(second, 2)
-        return rest, far, direct
-
-    def add_far(self, begun, *before):
-        rest, far, direct = begun
-        if far is None:
-            return rest, None
+        return self(cut, rows)
+
+    def add_far(self, near, far, direct, *before):
         wide = jnp.float32
 
-        def add(rest, top, bottom):
+        def add(near, top, bottom):
             half = top.shape[0]
-            first, second = rest[3 * half : 4 * half], rest[4 * half : 5 * half]
-            first = (first.astype(wide) + bottom.astype(wide)).astype(rest.dtype)
-            second = (second.astype(wide) + top.astype(wide)).astype(rest.dtype)
+            first = (near[half : 2 * half].astype(wide) + bottom.astype(wide)).astype(near.dtype)
+            second = (near[2 * half : 3 * half].astype(wide) + top.astype(wide)).astype(near.dtype)
             if direct is None:
-                first = jnp.concatenate([rest[2 * half : 3 * half], first], axis=0)
-                second = jnp.concatenate([second, rest[5 * half :]], axis=0)
+                first = jnp.concatenate([near[:half], first], axis=0)
+                second = jnp.concatenate([second, near[3 * half :]], axis=0)
             return first, second
 
-        first, second = self(add, rest, *far)
+        first, second = self(add, near, *far)
         if before:
             first, second = gate((first, second), *before)
-        if direct is None:
-            return rest, (swap(first, 1), swap(second, 2))
-        return rest, (direct[0], swap(first, 1), swap(second, 2), direct[1])
-
-
-def summed(rest, came):
+        first, second = swap(first, 1), swap(second, 2)
+        return (first, second) if direct is None else (direct[0], first, second, direct[1])
+
+
+def swap_far(halves):
+    return swap(halves[0], 1), swap(halves[1], 2)
+
+
+def swap_direct(near):
+    half = near.shape[0] // 4
+    return swap(near[:half], 1), swap(near[3 * half :], 2)
+
+
+def summed(own, came):
     wide = jnp.float32
-    if came is None:
-        return rest.astype(wide)
-    if len(came) == 2:
-        return rest[: came[0].shape[0]].astype(wide) + came[0].astype(wide) + came[1].astype(wide)
-    half = came[0].shape[0]
-    first_top, first_bottom, second_top, second_bottom = (part.astype(wide) for part in came)
-    top = rest[:half].astype(wide) + first_top + second_top
-    bottom = rest[half : 2 * half].astype(wide) + first_bottom + second_bottom
-    return jnp.concatenate([top, bottom], axis=0)
+    own = own.astype(wide)
+    return sum((part.astype(wide) for part in came), own)
 
 
 def whole(parts):
@@ -652,27 +627,48 @@
         ]
 
     down_sum = slab_sum(slab_product(upstream, active))
+    count = rows_here
+
+    def slots(values, start, stop):
+        return values[start * count : stop * count]
+
+    def to_hidden(start, stop):
+        return order(
+            lambda rows: hidden_gradient(rows, down_slab, slope, start * count, (stop - start) * count), upstream
+        )
+
+    def to_second(rows):
+        return contract_last(rows, up_slab).astype(low)
 
     def to_result(rows):
         return contract(rows, down_slab).astype(low)
 
-    outcome = order.send_far(to_result, active)
-    hidden_grad, hidden_sum = order(lambda rows: hidden_gradient(rows, down_slab, slope), upstream)
-
-    def to_second(rows):
-        return contract_last(rows, up_slab).astype(low)
+    def to_normed(rows):
+        return contract_last(rows, qkv_slab).astype(low)
+
+    def scatter(product, rows):
+        return lax.psum_scatter(order(product, rows), "seq", scatter_dimension=0, tiled=True)
 
     if square:
-        order.after(*outcome[3])
-    second_grad = order.add_far(order.make_rest(order.send_far(to_second, hidden_grad)))
-    outcome = order.make_rest(outcome, later=True)
-    up_sum = slab_product(second, hidden_grad)
-    if square:
-        up_sum = gate(up_sum, *second_grad[1])
-        outcome = order.send_direct(outcome, *second_grad[1])
-    up_sum = slab_sum(up_sum)
+        grad_far, sum_far = to_hidden(3, 4)
+        far = swap_far(order.halves(to_second, grad_far))
+        grad_near, sum_near = to_hidden(1, 3)
+        near = order(to_second, grad_near)
+        direct = swap_direct(near)
+        came = order.add_far(near, far, direct)
+        grad_own, sum_own = to_hidden(0, 1)
+        second_own = order(to_second, grad_own)
+        hidden_grad = [grad_own, grad_near, grad_far]
+        hidden_sum = sum_own + sum_near + sum_far
+        result_far = order.halves(to_result, slots(active, 3, 4))
+        up_sum = slab_sum(gate(slab_product(second, hidden_grad), *came))
+        result_far = swap_far(gate(result_far, *came))
+    else:
+        hidden_grad, hidden_sum = to_hidden(0, groups)
+        second_own, came = scatter(to_second, hidden_grad), ()
+        up_sum = slab_sum(slab_product(second, hidden_grad))
     branch_grad, middle_grad, middle_sums = order(
-        lambda rest, *came: norm_back(rest, middle, dz_low, ln2_gain, came), second_grad[0], *(second_grad[1] or ())
+        lambda own, *came: norm_back(own, middle, dz_low, ln2_gain, came), second_own, *came
     )
 
     def column_sum(values):
@@ -684,64 +680,65 @@
     early = [middle_sums[2], middle_sums[0], middle_sums[1], hidden_sum, middle_sums[3]]
     mixed_grad = order(lambda rows: contract_last(rows, full_out).astype(low), branch_grad)
     mixed_grad = exchange(by_index([mixed_grad[:, j * slab : (j + 1) * slab] for j in range(groups)], me))
-    branch_pair = jnp.concatenate([branch_grad, pair_swap(branch_grad)], axis=0)
+    if square:
+        order.after(*result_far)
+        result_rest = order(to_result, slots(active, 0, 3))
+    branch_other = pair_swap(gate(branch_grad, *result_far) if square else branch_grad)
+    branch_pair = jnp.concatenate([branch_grad, branch_other], axis=0)
     out_sum = order(lambda columns: outer(columns, branch_pair, groups, 1), mixed_half)
+    mixed_grad = order(lambda *parts: jnp.concatenate(parts, axis=0), *mixed_grad)
+    attention = (mask, slopes, qkv, log_totals, attended)
     if square:
-        order.after(*outcome[2])
-    mixed_grad = order(lambda *parts: jnp.concatenate(parts, axis=0), *mixed_grad)
+        part = out_sum.shape[0] // 4
+        out_far = out_sum[3 * part : 3 * part + part // 2], out_sum[3 * part + part // 2 :]
+        out_far = swap_far(gate(out_far, mixed_grad))
+        result_near = result_rest[count:]
+        result_came = order.add_far(result_near, result_far, None, mixed_grad)
+    order.after(down_sum)
+    begun = order(lambda rows: attend_backward(*attention, rows, seq_count, local_len, 0, pairs // 2), mixed_grad)
     if square:
-        count = out_sum.shape[0] // 4
-        far = out_sum[3 * count : 3 * count + count // 2], out_sum[3 * count + count // 2 :]
-        out_begun = order.send_held((out_sum[: 3 * count], far, None), mixed_grad)
-    else:
-        out_begun = lax.psum_scatter(out_sum, "seq", scatter_dimension=0, tiled=True), None, None
-    order.after(down_sum)
-    attention = (mask, slopes, qkv, log_totals, attended)
-    begun = order(lambda rows: attend_backward(*attention, rows, seq_count, local_len, 0, pairs // 2), mixed_grad)
-    out_begun = order.add_far(out_begun)
-    outcome = order.add_far(outcome, begun)
+        out_came = order.add_far(out_sum[part : 3 * part], out_far, None)
     qkv_grad = order(
         lambda rows: attend_backward(*attention, rows, seq_count, local_len, pairs // 2, pairs, begun), mixed_grad
     )
     if square:
-        order.after(*out_begun[1])
-    out_sum = order(
-        lambda own, *came: summed(own, came or None).astype(low), out_begun[0], *(out_begun[1] or ())
-    ).reshape(-1, 1, out_rows, model_width)
+        order.after(*out_came, *result_came)
+        out_sum = order(lambda own, *came: summed(own, came).astype(low), out_sum[:part], *out_came)
+        order.after(*out_came)
+    else:
+        out_sum = lax.psum_scatter(out_sum, "seq", scatter_dimension=0, tiled=True)
+    out_sum = out_sum.reshape(-1, 1, out_rows, model_width)
     zero = jnp.zeros_like(out_sum)
     out_sum = jnp.concatenate(
         [jnp.where(parity == 0, out_sum, zero), jnp.where(parity == 1, out_sum, zero)], axis=1
     ).reshape(-1, model_width)
     grad_w_out = lax.psum_scatter(out_sum, "fsdp", scatter_dimension=0, tiled=True).astype(wide)
-    order.after(up_sum, *(out_begun[1] or ()))
-
-    def to_normed(rows):
-        return contract_last(rows, qkv_slab).astype(low)
-
-    normed_grad = order.send_far(to_normed, qkv_grad)
-    qkv_sum = slab_product(normed, qkv_grad)
+    order.after(up_sum)
     if square:
-        qkv_sum = gate(qkv_sum, *normed_grad[3], *outcome[1])
-    qkv_sum = slab_sum(qkv_sum)
-    normed_grad = order.make_rest(normed_grad)
-    normed_grad = order.add_far(normed_grad)
+        far = swap_far(order.halves(to_normed, slots(qkv_grad, 3, 4)))
+        near = order(to_normed, slots(qkv_grad, 1, 3))
+        direct = swap_direct(near)
+        qkv_sum = slab_sum(gate(slab_product(normed, qkv_grad), *far))
+        came = order.add_far(near, far, direct)
+        normed_own = order(to_normed, slots(qkv_grad, 0, 1))
+    else:
+        qkv_sum = slab_sum(slab_product(normed, qkv_grad))
+        normed_own, came = scatter(to_normed, qkv_grad), ()
     grad_tokens, _, input_sums = order(
-        lambda rest, *came: norm_back(rest, x_low, middle_grad, ln1_gain, came),
-        normed_grad[0],
-        *(normed_grad[1] or ()),
+        lambda own, *came: norm_back(own, x_low, middle_grad, ln1_gain, came), normed_own, *came
     )
     grad_tokens = grad_tokens.reshape(tokens.shape)
-    result = order(
-        lambda own, *came: (middle + (summed(own, came or None) + down_bias)).astype(low),
-        outcome[0],
-        *(outcome[1] or ()),
-    ).reshape(tokens.shape)
-    sums = down_sum, up_sum
     if square:
-        sums = gate(sums, *normed_grad[1])
-    grad_w_down, grad_w_up = slabs_of_rows(*sums)
+        outcome = summed(result_rest[:count], result_came)
+    else:
+        outcome = scatter(to_result, active).astype(wide)
+    result = (middle + (outcome + down_bias)).astype(low).reshape(tokens.shape)
+    if square:
+        up_sum, down_sum = gate((up_sum, down_sum), *came)
+    grad_w_down = slabs_of_rows(down_sum)[0]
+    order.after(grad_w_down)
     grad_w_down = grad_w_down.reshape(-1, hidden_width).T
-    grad_w_up = grad_w_up.reshape(-1, hidden_width)
+    grad_w_up = slabs_of_rows(up_sum)[0].reshape(-1, hidden_width)
     grad_w_qkv = slabs_of_rows(qkv_sum)[0].reshape(-1, groups, pairs, 3, PAIR)
     grad_w_qkv = jnp.transpose(grad_w_qkv, (0, 3, 1, 2, 4)).reshape(-1, 3 * model_width)
 
@@ -750,7 +747,8 @@
         jnp.zeros((2, model_width), wide), head_sum[0::2], me * slab, axis=1
     )
     late = [qv_sum.reshape(-1), input_sums[0], input_sums[1]]
-    sums = total(jnp.concatenate(early + late).reshape(-1, PAIR)).reshape(-1)
+    sums = order(lambda *parts: jnp.concatenate(parts).reshape(-1, PAIR), *early, *late)
+    sums = total(sums).reshape(-1)
 
     def cut(at, count):
         return sums[at * model_width : (at + count) * model_width]

time: 783 us -> 804 us (1.027)
  waiting for transfers between devices: 200 us -> 174 us
  local copies, waits for them, and re-layouts: 100 us -> 123 us
  Pallas kernels: 246 us -> 256 us
    ppermute x46 -> x44, waiting for transfers between devices: 175 us -> 153 us  [swap(): return lax.ppermute(values, 'seq', [(i, i ^ bit) for i in range(4)])]
    slice x9 -> x15, local copies, waits for them, and re-layouts: 8.85 us -> 28.6 us  [the longest x4 14.3 us: slots(): return values[start * count:stop * count]]
    pallas_call x1 -> x3, Pallas kernels: 25.4 us -> 36.8 us  [hidden_gradient(): pl.pallas_call(partial(hidden_grad_kernel, chunk=512), grid=(count // TIL...]
    dot_general x5 -> x7, matrix products: 55.8 us -> 65.4 us  [contract_last(): lax.dot_general(left_side, right_side, (((1,), (1,)), ((), ())), preferre...]
    unnamed x103 -> x89, local copies, waits for them, and re-layouts: 45.8 us -> 48.2 us
    ppermute x46 -> x44, starting transfers between devices: 51.4 us -> 49.3 us  [swap(): return lax.ppermute(values, 'seq', [(i, i ^ bit) for i in range(4)])]
  transfers between devices with their start and end apart: 65 -> 64, of which waited for: 24 -> 20; matrix products, arithmetic and copies ran while one was open for 30% -> 33% of each run, Pallas kernels for 31% -> 32%
where the time goes in v9:
time: 804 us; the launch traced here: 797 us
  Pallas kernels  256 us (32%)
  waiting for transfers between devices  174 us (22%)
  local copies, waits for them, and re-layouts  123 us (15%)
  matrix products  114 us (14%)
  starting transfers between devices  68.6 us (9%)
  other arithmetic  46.8 us (6%)
  between operations  15.3 us (2%)
    ppermute x44, waiting for transfers between devices, swap(): return lax.ppermute(values, 'seq', [(i, i ^ bit) for i in range(4)])  153 us
    pallas_call x4, Pallas kernels, outer(): pl.pallas_call(partial(outer_kernel, chunk=512 if width % 512 == 0 else 2...  74.8 us
    dot_general x7, matrix products, contract_last(): lax.dot_general(left_side, right_side, (((1,), (1,)), ((), ())), preferre...  65.4 us
    pallas_call x2, Pallas kernels, attend_backward(): pl.pallas_call(partial(attend_backward_kernel, blocks=blocks, seqs=seqs,...  56.8 us
    ppermute x44, starting transfers between devices, swap(): return lax.ppermute(values, 'seq', [(i, i ^ bit) for i in range(4)])  49.3 us
    unnamed x89, local copies, waits for them, and re-layouts  48.2 us
    dot_general x4, matrix products, contract(): lax.dot_general(left_side, right_side, (((1,), (0,)), ((), ())), preferre...  48.2 us
    pallas_call x3, Pallas kernels, hidden_gradient(): pl.pallas_call(partial(hidden_grad_kernel, chunk=512), grid=(count // TIL...  36.8 us
  transfers between devices with their start and end apart: 64, of which 20 were waited for; matrix products, arithmetic and copies ran while one was open for 33% of the time, Pallas kernels for 32%

profile of v9, /device:TPU:0, one launch (start us, length us, event | category | flops | bytes accessed | tf_op | source)
XLA Modules:
  0.0 797.0 jit_solution(17561676294070956085)
XLA Ops:
  26.7 19.0 %collective-permute-done.2 = bf16[256,2048]{1,0:T(8,128)(2,1)} collective-permute-done((bf16[256,2048]{1,0:T(8,128)(2,1)}, bf16[256,2048]{1,0:T(8,128)(2,1)}, u32[]{:S(2)}, u32[]{:S(2)}) %collective-permute-start.2) | collective-permute-done | bytes 1048608 | tf_op jit(solution)/shard_map/ppermute | solution.py:375
  52.5 17.7 %collective-permute-done = bf16[256,2048]{1,0:T(8,128)(2,1)} collective-permute-done((bf16[256,2048]{1,0:T(8,128)(2,1)}, bf16[256,2048]{1,0:T(8,128)(2,1)}, u32[]{:S(2)}, u32[]{:S(2)}) %collective-permute-start) | collective-permute-done | bytes 1048608 | tf_op jit(solution)/shard_map/ppermute | solution.py:375
  78.5 12.8 %collective-permute-done.4 = bf16[256,2048]{1,0:T(8,128)(2,1)} collective-permute-done((bf16[256,2048]{1,0:T(8,128)(2,1)}, bf16[256,2048]{1,0:T(8,128)(2,1)}, u32[]{:S(2)}, u32[]{:S(2)}) %collective-permute-start.4) | collective-permute-done | bytes 1048608 | tf_op jit(solution)/shard_map/ppermute | solution.py:375
  99.9 18.6 %add_convert_fusion.qkv_ref = bf16[2048,1536]{1,0:T(8,128)(2,1)} fusion(bf16[2048,2048]{1,0:T(8,128)(2,1)} %constant_dynamic-update-slice_fusion.left_ref, bf16[2048,1536]{1,0:T(8,128)(2,1)} %all-gather.5.cloned.1.call-done, f32[1536]{0:T(1024)S(1)} %reduce.2), kind=kOutput, calls=%fused_computation.1 | convolution fusion | flops 12891193344 | bytes 20977664 | tf_op jit(solution)/shard_map/dot_general | solution.py:30
  118.5 29.7 %attend_forward.1 = (bf16[2048,512]{1,0:T(8,128)(2,1)}, f32[2048,512]{1,0:T(8,128)}) custom-call(s32[1]{0:T(128)} %bitcast.1.at_ref.mask_ref, f32[8]{0:T(128)} %multiply_power_fusion.slope_ref, bf16[2048,1536]{1,0:T(8,128)(2,1)} %add_convert_fusion.qkv_ref), custom_call_target="tpu_custom_call" | custom-call | flops 2684354560 | bytes 2621440 | tf_op jit(solution)/shard_map/attend_forward/pallas_call | solution.py:165
  155.6 10.3 %collective-permute-done.12 = bf16[512,512]{1,0:T(8,128)(2,1)S(1)} collective-permute-done((bf16[512,512]{1,0:T(8,128)(2,1)}, bf16[512,512]{1,0:T(8,128)(2,1)S(1)}, u32[]{:S(2)}, u32[]{:S(2)}) %collective-permute-start.12) | collective-permute-done | bytes 524320 | tf_op jit(solution)/shard_map/ppermute | solution.py:375
  219.5 15.3 %collective-permute-done.15 = bf16[256,2048]{1,0:T(8,128)(2,1)} collective-permute-done((bf16[256,2048]{1,0:T(8,128)(2,1)}, bf16[256,2048]{1,0:T(8,128)(2,1)}, u32[]{:S(2)}, u32[]{:S(2)}) %collective-permute-start.15) | collective-permute-done | bytes 1048608 | tf_op jit(solution)/shard_map/ppermute | solution.py:375
  266.5 30.6 %up_and_bend.1 = (bf16[2048,2048]{1,0:T(8,128)(2,1)}, f32[2048,2048]{1,0:T(8,128)}) custom-call(bf16[2048,2048]{1,0:T(8,128)(2,1)} %constant_dynamic-update-slice_fusion.7.rows_ref.left_ref, bf16[2048,2048]{1,0:T(8,128)(2,1)} %all-gather.9.cloned.1.call-done.weight_ref, f32[1,2048]{1,0:T(1,128)} %bitcast.143), custom_call_target="tpu_custom_call" | custom-call | flops 8589934592 | bytes 8388608 | tf_op jit(solution)/shard_map/up_and_bend/pallas_call | solution.py:246
  300.5 23.6 %outer.4 = bf16[8,4,64,2048]{3,2,1,0:T(8,128)(2,1)} custom-call(bf16[2048,2048]{1,0:T(8,128)(2,1)} %constant_dynamic-update-slice_fusion.35.left_ref.rows_ref, bf16[2048,2048]{1,0:T(8,128)(2,1)} %get-tuple-element.141.refs_0_), custom_call_target="tpu_custom_call" | custom-call | flops 4294967296 | bytes 4194304 | tf_op jit(solution)/shard_map/outer/pallas_call | solution.py:357
  325.9 10.9 %hidden_gradient.3 = (bf16[512,2048]{1,0:T(8,128)(2,1)}, f32[1,2048]{1,0:T(1,128)}) custom-call(bf16[2048,2048]{1,0:T(8,128)(2,1)} %constant_dynamic-update-slice_fusion.35.left_ref.rows_ref, bf16[2048,2048]{1,0:T(8,128)(2,1)} %all-gather.11.cloned.1.call-done.weight_ref, f32[2048,2048]{1,0:T(8,128)} %get-tuple-element.144.slope_ref), custom_call_target="tpu_custom_call" | custom-call | flops 1610612736 | bytes 1572864 | tf_op jit(solution)/shard_map/hidden_gradient/pallas_call | solution.py:270
  349.3 15.2 %hidden_gradient.4 = (bf16[1024,2048]{1,0:T(8,128)(2,1)}, f32[1,2048]{1,0:T(1,128)}) custom-call(bf16[2048,2048]{1,0:T(8,128)(2,1)} %constant_dynamic-update-slice_fusion.35.left_ref.rows_ref, bf16[2048,2048]{1,0:T(8,128)(2,1)} %all-gather.11.cloned.1.call-done.weight_ref, f32[2048,2048]{1,0:T(8,128)} %get-tuple-element.144.slope_ref), custom_call_target="tpu_custom_call" | custom-call | flops 3221225472 | bytes 3145728 | tf_op jit(solution)/shard_map/hidden_gradient/pallas_call | solution.py:270
  364.5 12.8 %convolution_convert_fusion.2 = bf16[1024,2048]{1,0:T(8,128)(2,1)S(1)} fusion(bf16[1024,2048]{1,0:T(8,128)(2,1)} %get-tuple-element.157.refs_1_, bf16[2048,2048]{1,0:T(8,128)(2,1)} %all-gather.9.cloned.1.call-done.weight_ref), kind=kOutput, calls=%fused_computation.18 | convolution fusion | flops 8592031744 | bytes 16777216 | tf_op jit(solution)/shard_map/dot_general | solution.py:36
  385.8 10.6 %hidden_gradient.5 = (bf16[512,2048]{1,0:T(8,128)(2,1)}, f32[1,2048]{1,0:T(1,128)}) custom-call(bf16[2048,2048]{1,0:T(8,128)(2,1)} %constant_dynamic-update-slice_fusion.35.left_ref.rows_ref, bf16[2048,2048]{1,0:T(8,128)(2,1)} %all-gather.11.cloned.1.call-done.weight_ref, f32[2048,2048]{1,0:T(8,128)} %get-tuple-element.144.slope_ref), custom_call_target="tpu_custom_call" | custom-call | flops 1610612736 | bytes 1572864 | tf_op jit(solution)/shard_map/hidden_gradient/pallas_call | solution.py:270
  416.1 23.5 %outer.5 = bf16[8,4,64,2048]{3,2,1,0:T(8,128)(2,1)} custom-call(bf16[2048,2048]{1,0:T(8,128)(2,1)} %constant_dynamic-update-slice_fusion.7.rows_ref.left_ref, bf16[512,2048]{1,0:T(8,128)(2,1)} %get-tuple-element.164.refs_0_, bf16[1024,2048]{1,0:T(8,128)(2,1)} %get-tuple-element.157.refs_1_, bf16[512,2048]{1,0:T(8,128)(2,1)} %get-tuple-element.153.refs_2_), custom_call_target="tpu_custom_call" | custom-call | flops 4294967296 | bytes 4194304 | tf_op jit(solution)/shard_map/outer/pallas_call | solution.py:357
  446.5 11.5 %norm_back.2 = (bf16[512,2048]{1,0:T(8,128)(2,1)}, f32[512,2048]{1,0:T(8,128)}, f32[8,2048]{1,0:T(8,128)}) custom-call(bf16[512,2048]{1,0:T(8,128)(2,1)} %convolution_convert_fusion.7.rest_ref, f32[512,2048]{1,0:T(8,128)} %copy-done.1, bf16[512,2048]{1,0:T(8,128)(2,1)} %bitcast.115, f32[1,2048]{1,0:T(1,128)} %bitcast.138, ...), custom_call_target="tpu_custom_call" | custom-call | flops 7864320 | bytes 7680 | tf_op jit(solution)/shard_map/norm_back/pallas_call | solution.py:322
  473.9 10.5 %collective-permute-done.28 = bf16[256,2048]{1,0:T(8,128)(2,1)S(1)} collective-permute-done((bf16[256,2048]{1,0:T(8,128)(2,1)}, bf16[256,2048]{1,0:T(8,128)(2,1)S(1)}, u32[]{:S(2)}, u32[]{:S(2)}) %collective-permute-start.28) | collective-permute-done | bytes 1048608 | tf_op jit(solution)/shard_map/ppermute | solution.py:375
  484.4 12.4 %collective-permute-done.29 = bf16[256,2048]{1,0:T(8,128)(2,1)S(1)} collective-permute-done((bf16[256,2048]{1,0:T(8,128)(2,1)}, bf16[256,2048]{1,0:T(8,128)(2,1)S(1)}, u32[]{:S(2)}, u32[]{:S(2)}) %collective-permute-start.29) | collective-permute-done | bytes 1048608 | tf_op jit(solution)/shard_map/ppermute | solution.py:375
  496.8 13.6 %convolution_convert_fusion = bf16[1536,2048]{1,0:T(8,128)(2,1)S(1)} fusion(bf16[1536,2048]{1,0:T(8,128)(2,1)S(1)} %copy-done.5, bf16[2048,2048]{1,0:T(8,128)(2,1)S(1)} %bitcast.103), kind=kOutput, calls=%fused_computation.2 | convolution fusion | flops 12888047616 | bytes 20971520 | tf_op jit(solution)/shard_map/dot_general | solution.py:30
  545.0 28.3 %attend_backward.2.rest_0_ = bf16[2048,1536]{1,0:T(8,128)(2,1)} custom-call(s32[1]{0:T(128)} %bitcast.1.at_ref.mask_ref, f32[8]{0:T(128)} %multiply_power_fusion.slope_ref, bf16[2048,1536]{1,0:T(8,128)(2,1)} %add_convert_fusion.qkv_ref, f32[2048,512]{1,0:T(8,128)} %get-tuple-element.125.lse_ref, bf16[2048,512]{1,0:T(8,128)(2,1)} %get-tuple-element.124.mixed_ref, ...), custom_call_target="tpu_custom_call" | custom-call | flops 3355443200 | bytes 3276800 | tf_op jit(solution)/shard_map/attend_backward/pallas_call | solution.py:190
  578.6 28.5 %attend_backward.3.refs_0_ = bf16[2048,1536]{1,0:T(8,128)(2,1)} custom-call(s32[1]{0:T(128)} %bitcast.1.at_ref.mask_ref, f32[8]{0:T(128)} %multiply_power_fusion.slope_ref, bf16[2048,1536]{1,0:T(8,128)(2,1)} %add_convert_fusion.qkv_ref, f32[2048,512]{1,0:T(8,128)} %get-tuple-element.125.lse_ref, ...), custom_call_target="tpu_custom_call", output_to_operand_aliasing={{}: (6, {})} | custom-call | flops 3355443200 | bytes 3276800 | tf_op jit(solution)/shard_map/attend_backward/pallas_call | solution.py:190
  630.2 11.0 %convolution_convert_fusion.1 = bf16[1024,2048]{1,0:T(8,128)(2,1)} fusion(bf16[1024,1536]{1,0:T(8,128)(2,1)S(1)} %copy-done.9, bf16[2048,1536]{1,0:T(8,128)(2,1)} %all-gather.5.cloned.1.call-done), kind=kOutput, calls=%fused_computation.17 | convolution fusion | flops 6444548096 | bytes 13631488 | tf_op jit(solution)/shard_map/dot_general | solution.py:36
  641.3 18.6 %outer.7 = bf16[8,4,64,1536]{3,2,1,0:T(8,128)(2,1)} custom-call(bf16[2048,2048]{1,0:T(8,128)(2,1)} %constant_dynamic-update-slice_fusion.left_ref, bf16[2048,1536]{1,0:T(8,128)(2,1)} %attend_backward.3.refs_0_), custom_call_target="tpu_custom_call" | custom-call | flops 3221225472 | bytes 3145728 | tf_op jit(solution)/shard_map/outer/pallas_call | solution.py:357
  695.7 19.0 %collective-permute-done.44.refs_2_ = bf16[256,2048]{1,0:T(8,128)(2,1)S(1)} collective-permute-done((bf16[256,2048]{1,0:T(8,128)(2,1)}, bf16[256,2048]{1,0:T(8,128)(2,1)S(1)}, u32[]{:S(2)}, u32[]{:S(2)}) %collective-permute-start.44) | collective-permute-done | bytes 1048608 | tf_op jit(solution)/shard_map/ppermute | solution.py:375
  719.2 11.2 %norm_back.3 = (bf16[512,2048]{1,0:T(8,128)(2,1)}, f32[512,2048]{1,0:T(8,128)}, f32[8,2048]{1,0:T(8,128)}) custom-call(bf16[512,2048]{1,0:T(8,128)(2,1)} %convolution_convert_fusion.3.rest_ref, bf16[512,2048]{1,0:T(8,128)(2,1)} %bitcast.106, f32[512,2048]{1,0:T(8,128)} %get-tuple-element.173.base_ref, f32[1,2048]{1,0:T(1,128)} %bitcast.139, ...), custom_call_target="tpu_custom_call" | custom-call | flops 7864320 | bytes 7680 | tf_op jit(solution)/shard_map/norm_back/pallas_call | solution.py:322
  (320 shorter events, 366.2 us)
Async XLA Ops:
  7.2 92.7 %all-gather.5.cloned.1.call-start = ((), (), s32[]{:S(2)}) async-start(), calls=%async_computation.7 | async-start | bytes 7077888 | tf_op jit(solution)/shard_map/all_gather | solution.py:566
  10.3 169.2 %all-gather.7.cloned.1.call-start = ((), (), s32[]{:S(2)}) async-start(), calls=%async_computation.8 | async-start | bytes 9437184 | tf_op jit(solution)/shard_map/all_gather | solution.py:578
  11.1 255.4 %all-gather.9.cloned.1.call-start = ((), (), s32[]{:S(2)}) async-start(), calls=%async_computation.9 | async-start | bytes 9437184 | tf_op jit(solution)/shard_map/all_gather | solution.py:579
  18.3 307.6 %all-gather.11.cloned.1.call-start = ((), (), s32[]{:S(2)}) async-start(), calls=%async_computation.10 | async-start | bytes 9437184 | tf_op jit(solution)/shard_map/all_gather | solution.py:580
  23.4 52.7 %collective-permute-start.3 = (bf16[256,2048]{1,0:T(8,128)(2,1)}, bf16[256,2048]{1,0:T(8,128)(2,1)}, u32[]{:S(2)}, u32[]{:S(2)}) collective-permute-start(bf16[256,2048]{1,0:T(8,128)(2,1)} %get-tuple-element.272), channel_id=1, source_target_pairs={{0,16},{8,24},{16,0},{24,8},{1,17},{9,25},{17,1},{25,9},{2,18},{10... | collective-permute-start | bytes 3145736 | tf_op jit(solution)/shard_map/ppermute | solution.py:375
  25.8 519.2 %reduce-scatter.5.cloned.1.call-start = ((), (), s32[]{:S(2)}) async-start(), calls=%async_computation.11 | async-start | bytes 9437184 | tf_op jit(solution)/shard_map/reduce_scatter | solution.py:619
  95.8 52.4 %collective-permute-start.8 = (bf16[256,2048]{1,0:T(8,128)(2,1)}, bf16[256,2048]{1,0:T(8,128)(2,1)}, u32[]{:S(2)}, u32[]{:S(2)}) collective-permute-start(bf16[256,2048]{1,0:T(8,128)(2,1)} %get-tuple-element.129), channel_id=1, source_target_pairs={{0,8},{8,0},{16,24},{24,16},{1,9},{9,1},{17,25},{25,17},{2,10},{10... | collective-permute-start | bytes 3145736 | tf_op jit(solution)/shard_map/ppermute | solution.py:375
  97.3 50.9 %collective-permute-start.7 = (bf16[256,2048]{1,0:T(8,128)(2,1)}, bf16[256,2048]{1,0:T(8,128)(2,1)}, u32[]{:S(2)}, u32[]{:S(2)}) collective-permute-start(bf16[256,2048]{1,0:T(8,128)(2,1)} %get-tuple-element.129), channel_id=1, source_target_pairs={{0,16},{8,24},{16,0},{24,8},{1,17},{9,25},{17,1},{25,9},{2,18},{10... | collective-permute-start | bytes 3145736 | tf_op jit(solution)/shard_map/ppermute | solution.py:375
  97.8 50.4 %collective-permute-start.9 = (bf16[256,2048]{1,0:T(8,128)(2,1)S(1)}, bf16[256,2048]{1,0:T(8,128)(2,1)}, u32[]{:S(2)}, u32[]{:S(2)}) collective-permute-start(bf16[256,2048]{1,0:T(8,128)(2,1)S(1)} %get-tuple-element.130), channel_id=1, source_target_pairs={{0,16},{8,24},{16,0},{24,8},{1,17},{9,25},{17,1},{25,9},{2,18},{10... | collective-permute-start | bytes 3145736 | tf_op jit(solution)/shard_map/ppermute | solution.py:375
  99.3 48.9 %collective-permute-start.6 = (bf16[256,2048]{1,0:T(8,128)(2,1)S(1)}, bf16[256,2048]{1,0:T(8,128)(2,1)}, u32[]{:S(2)}, u32[]{:S(2)}) collective-permute-start(bf16[256,2048]{1,0:T(8,128)(2,1)S(1)} %get-tuple-element.130), channel_id=1, source_target_pairs={{0,8},{8,0},{16,24},{24,16},{1,9},{9,1},{17,25},{25,17},{2,10},{10... | collective-permute-start | bytes 3145736 | tf_op jit(solution)/shard_map/ppermute | solution.py:375
  190.9 54.5 %collective-permute-start.16 = (bf16[256,2048]{1,0:T(8,128)(2,1)}, bf16[256,2048]{1,0:T(8,128)(2,1)}, u32[]{:S(2)}, u32[]{:S(2)}) collective-permute-start(bf16[256,2048]{1,0:T(8,128)(2,1)} %get-tuple-element.265), channel_id=1, source_target_pairs={{0,16},{8,24},{16,0},{24,8},{1,17},{9,25},{17,1},{25,9},{2,18},{10... | collective-permute-start | bytes 3145736 | tf_op jit(solution)/shard_map/ppermute | solution.py:375
  204.0 59.2 %collective-permute-start.19 = (bf16[512,1024]{1,0:T(8,128)(2,1)}, bf16[512,1024]{1,0:T(8,128)(2,1)}, u32[]{:S(2)}, u32[]{:S(2)}) collective-permute-start(bf16[512,1024]{1,0:T(8,128)(2,1)} %copy.51), channel_id=1, source_target_pairs={{0,1},{1,0},{2,3},{3,2},{4,5},{5,4},{6,7},{7,6},{8,9},{9,8},{10,11... | collective-permute-start | bytes 3145736 | tf_op jit(solution)/shard_map/ppermute | solution.py:592
  324.1 297.1 %reduce-scatter.7.cloned.1.call-start = ((), (), s32[]{:S(2)}) async-start(), calls=%async_computation.12 | async-start | bytes 9437184 | tf_op jit(solution)/shard_map/reduce_scatter | solution.py:619
  377.5 62.2 %collective-permute-start.27 = (bf16[256,2048]{1,0:T(8,128)(2,1)S(1)}, bf16[256,2048]{1,0:T(8,128)(2,1)}, u32[]{:S(2)}, u32[]{:S(2)}) collective-permute-start(bf16[256,2048]{1,0:T(8,128)(2,1)S(1)} %get-tuple-element.240), channel_id=1, source_target_pairs={{0,16},{8,24},{16,0},{24,8},{1,17},{9,25},{17,1},{25,9},{2,18},{10... | collective-permute-start | bytes 3145736 | tf_op jit(solution)/shard_map/ppermute | solution.py:375
  378.3 61.3 %collective-permute-start.24 = (bf16[256,2048]{1,0:T(8,128)(2,1)S(1)}, bf16[256,2048]{1,0:T(8,128)(2,1)}, u32[]{:S(2)}, u32[]{:S(2)}) collective-permute-start(bf16[256,2048]{1,0:T(8,128)(2,1)S(1)} %get-tuple-element.241), channel_id=1, source_target_pairs={{0,8},{8,0},{16,24},{24,16},{1,9},{9,1},{17,25},{25,17},{2,10},{10... | collective-permute-start | bytes 3145736 | tf_op jit(solution)/shard_map/ppermute | solution.py:375
  383.5 56.1 %collective-permute-start.26 = (bf16[256,2048]{1,0:T(8,128)(2,1)}, bf16[256,2048]{1,0:T(8,128)(2,1)}, u32[]{:S(2)}, u32[]{:S(2)}) collective-permute-start(bf16[256,2048]{1,0:T(8,128)(2,1)} %get-tuple-element.242), channel_id=1, source_target_pairs={{0,16},{8,24},{16,0},{24,8},{1,17},{9,25},{17,1},{25,9},{2,18},{10... | collective-permute-start | bytes 3145736 | tf_op jit(solution)/shard_map/ppermute | solution.py:375
  385.0 54.6 %collective-permute-start.25 = (bf16[256,2048]{1,0:T(8,128)(2,1)S(1)}, bf16[256,2048]{1,0:T(8,128)(2,1)}, u32[]{:S(2)}, u32[]{:S(2)}) collective-permute-start(bf16[256,2048]{1,0:T(8,128)(2,1)S(1)} %get-tuple-element.243), channel_id=1, source_target_pairs={{0,8},{8,0},{16,24},{24,16},{1,9},{9,1},{17,25},{25,17},{2,10},{10... | collective-permute-start | bytes 3145736 | tf_op jit(solution)/shard_map/ppermute | solution.py:375
  439.7 327.4 %reduce-scatter.9.cloned.1.call-start = ((), (), s32[]{:S(2)}) async-start(), calls=%async_computation.13 | async-start | bytes 7077888 | tf_op jit(solution)/shard_map/reduce_scatter | solution.py:619
  470.4 57.5 %collective-permute-start.32 = (bf16[512,512]{1,0:T(8,128)(2,1)}, bf16[512,512]{1,0:T(8,128)(2,1)}, u32[]{:S(2)}, u32[]{:S(2)}) collective-permute-start(bf16[512,512]{1,0:T(8,128)(2,1)} %get-tuple-element.254), channel_id=1, source_target_pairs={{0,24},{8,16},{16,8},{24,0},{1,25},{9,17},{17,9},{25,1},{2,26},{10... | collective-permute-start | bytes 1572872 | tf_op jit(solution)/shard_map/ppermute | solution.py:375
  471.8 56.1 %collective-permute-start.30 = (bf16[512,512]{1,0:T(8,128)(2,1)}, bf16[512,512]{1,0:T(8,128)(2,1)}, u32[]{:S(2)}, u32[]{:S(2)}) collective-permute-start(bf16[512,512]{1,0:T(8,128)(2,1)} %get-tuple-element.256), channel_id=1, source_target_pairs={{0,8},{8,0},{16,24},{24,16},{1,9},{9,1},{17,25},{25,17},{2,10},{10... | collective-permute-start | bytes 1572872 | tf_op jit(solution)/shard_map/ppermute | solution.py:375
  472.9 54.9 %collective-permute-start.31 = (bf16[512,512]{1,0:T(8,128)(2,1)}, bf16[512,512]{1,0:T(8,128)(2,1)}, u32[]{:S(2)}, u32[]{:S(2)}) collective-permute-start(bf16[512,512]{1,0:T(8,128)(2,1)} %get-tuple-element.257), channel_id=1, source_target_pairs={{0,16},{8,24},{16,0},{24,8},{1,17},{9,25},{17,1},{25,9},{2,18},{10... | collective-permute-start | bytes 1572872 | tf_op jit(solution)/shard_map/ppermute | solution.py:375
  542.9 71.0 %collective-permute-start.34 = (bf16[512,2048]{1,0:T(8,128)(2,1)}, bf16[512,2048]{1,0:T(8,128)(2,1)}, u32[]{:S(2)}, u32[]{:S(2)}) collective-permute-start(bf16[512,2048]{1,0:T(8,128)(2,1)} %pad_maximum_fusion.4), channel_id=1, source_target_pairs={{0,8},{8,0},{16,24},{24,16},{1,9},{9,1},{17,25},{25,17},{2,10},{10... | collective-permute-start | bytes 6291464 | tf_op jit(solution)/shard_map/ppermute | solution.py:375
  543.9 69.9 %collective-permute-start.35 = (bf16[512,2048]{1,0:T(8,128)(2,1)}, bf16[512,2048]{1,0:T(8,128)(2,1)}, u32[]{:S(2)}, u32[]{:S(2)}) collective-permute-start(bf16[512,2048]{1,0:T(8,128)(2,1)} %pad_maximum_fusion.5), channel_id=1, source_target_pairs={{0,16},{8,24},{16,0},{24,8},{1,17},{9,25},{17,1},{25,9},{2,18},{10... | collective-permute-start | bytes 6291464 | tf_op jit(solution)/shard_map/ppermute | solution.py:375
  659.9 114.4 %reduce-scatter.11.cloned.1.call-start = ((), (), s32[]{:S(2)}) async-start(), calls=%async_computation.14 | async-start | bytes 2359296 | tf_op jit(solution)/shard_map/reduce_scatter | solution.py:715
  (69 other events, 1485.9 us)
Sparse Core Ops, SparseCore 0:
  10.4 67.4 all-gather.4
  79.5 80.6 all-gather.6
  161.9 80.5 all-gather.8
  243.9 81.0 all-gather.10
  327.2 87.7 reduce-scatter.4
  439.8 89.6 reduce-scatter.6
  660.0 69.5 reduce-scatter.8
  731.9 37.2 reduce-scatter.10

commit v10 on v9

--- a/solution.py
+++ b/solution.py
@@ -286,28 +286,58 @@
     )(rows, weight, slope)
 
 
-def norm_back_kernel(rest_ref, values_ref, base_ref, gain_ref, *refs, parts):
+def mixed_grad_kernel(rows_ref, weight_ref, out_ref):
+    out_ref[...] = contract_last(rows_ref[...], weight_ref[...]).astype(out_ref.dtype)
+
+
+def mixed_gradient(rows, weight, slab):
+    count, depth = rows.shape
+    width = weight.shape[0]
+    return pl.pallas_call(
+        mixed_grad_kernel,
+        grid=(width // slab,),
+        in_specs=[
+            pl.BlockSpec((count, depth), lambda i: (0, 0), pipeline_mode=pl.Buffered(1)),
+            pl.BlockSpec((slab, depth), lambda i: (i, 0)),
+        ],
+        out_specs=pl.BlockSpec((count, slab), lambda i: (0, i)),
+        out_shape=jax.ShapeDtypeStruct((count, width), jnp.bfloat16),
+        compiler_params=pltpu.CompilerParams(vmem_limit_bytes=GRANT),
+        cost_estimate=estimate(2 * count * depth * width, 0),
+        name="mixed_gradient",
+    )(rows, weight)
+
+
+def norm_back_kernel(own_ref, values_ref, base_ref, gain_ref, *refs, parts):
     came, (low_ref, wide_ref, sums_ref) = refs[:parts], refs[parts:]
     wide = jnp.float32
     step = pl.program_id(0)
+
+    def make(came):
+        grad = own_ref[...].astype(wide)
+        for part in came:
+            grad = grad + part[...].astype(wide)
+        values = values_ref[...].astype(wide)
+        centred = values - jnp.mean(values, axis=-1, keepdims=True)
+        scale = lax.rsqrt(jnp.mean(centred * centred, axis=-1, keepdims=True) + 1e-05)
+        normal = centred * scale
+        gained = grad * gain_ref[...]
+        along = jnp.mean(gained * normal, axis=-1, keepdims=True)
+        made = gained - jnp.mean(gained, axis=-1, keepdims=True) - normal * along
+        made = base_ref[...].astype(wide) + scale * made
+        low = made.astype(low_ref.dtype)
+        low_ref[...] = low
+        wide_ref[...] = made
+        for row, part in enumerate((grad * normal, grad, low.astype(wide))):
+            line = jnp.sum(part, axis=0, keepdims=True)
+            sums_ref[row : row + 1, :] = jnp.where(step == 0, line, sums_ref[row : row + 1, :] + line)
+
+    if not came:
+        make(())
+        return
     upper = step < pl.num_programs(0) // 2
-    grad = rest_ref[...].astype(wide)
-    for top, bottom in zip(came[0::2], came[1::2]):
-        grad = grad + jnp.where(upper, top[...], bottom[...]).astype(wide)
-    values = values_ref[...].astype(wide)
-    base = base_ref[...].astype(wide)
-    centred = values - jnp.mean(values, axis=-1, keepdims=True)
-    scale = lax.rsqrt(jnp.mean(centred * centred, axis=-1, keepdims=True) + 1e-05)
-    normal = centred * scale
-    gained = grad * gain_ref[...]
-    along = jnp.mean(gained * normal, axis=-1, keepdims=True)
-    made = base + scale * (gained - jnp.mean(gained, axis=-1, keepdims=True) - normal * along)
-    low = made.astype(low_ref.dtype)
-    low_ref[...] = low
-    wide_ref[...] = made
-    for row, part in enumerate((grad * normal, grad, low.astype(wide), base)):
-        line = jnp.sum(part, axis=0, keepdims=True)
-        sums_ref[row : row + 1, :] = jnp.where(step == 0, line, sums_ref[row : row + 1, :] + line)
+    pl.when(upper)(lambda: make(came[0::2]))
+    pl.when(jnp.logical_not(upper))(lambda: make(came[1::2]))
 
 
 def norm_back(rest, values, base, gain, came):
@@ -459,19 +489,21 @@
 
         return self(cut, rows)
 
-    def add_far(self, near, far, direct, *before):
+    def add_far(self, made, far, direct, *before, at=None):
         wide = jnp.float32
-
-        def add(near, top, bottom):
-            half = top.shape[0]
-            first = (near[half : 2 * half].astype(wide) + bottom.astype(wide)).astype(near.dtype)
-            second = (near[2 * half : 3 * half].astype(wide) + top.astype(wide)).astype(near.dtype)
+        half = far[0].shape[0]
+        start = made.shape[0] - 4 * half if at is None else at
+
+        def add(made, top, bottom):
+            at = start
+            first = (made[at + half : at + 2 * half].astype(wide) + bottom.astype(wide)).astype(made.dtype)
+            second = (made[at + 2 * half : at + 3 * half].astype(wide) + top.astype(wide)).astype(made.dtype)
             if direct is None:
-                first = jnp.concatenate([near[:half], first], axis=0)
-                second = jnp.concatenate([second, near[3 * half :]], axis=0)
+                first = jnp.concatenate([made[at : at + half], first], axis=0)
+                second = jnp.concatenate([second, made[at + 3 * half : at + 4 * half]], axis=0)
             return first, second
 
-        first, second = self(add, near, *far)
+        first, second = self(add, made, *far)
         if before:
             first, second = gate((first, second), *before)
         first, second = swap(first, 1), swap(second, 2)
@@ -482,9 +514,9 @@
     return swap(halves[0], 1), swap(halves[1], 2)
 
 
-def swap_direct(near):
-    half = near.shape[0] // 4
-    return swap(near[:half], 1), swap(near[3 * half :], 2)
+def swap_direct(made, half):
+    at = made.shape[0] - 4 * half
+    return swap(made[at : at + half], 1), swap(made[at + 3 * half :], 2)
 
 
 def summed(own, came):
@@ -497,17 +529,16 @@
     return jnp.concatenate(parts, axis=0) if isinstance(parts, list) else parts
 
 
-def total(values):
+def total_stages():
+    stages = []
     for axis in ("fsdp", "seq"):
         count, bit = lax.axis_size(axis), 1
         bits = count.bit_length() - 1
         while bit < count:
-            masks = [bit] if bits % 2 else [bit, 2 * bit, 3 * bit]
-            came = [lax.ppermute(values, axis, [(i, i ^ mask) for i in range(count)]) for mask in masks]
-            values = sum(came, values)
+            stages.append((axis, [bit] if bits % 2 else [bit, 2 * bit, 3 * bit]))
             bit <<= 1 if bits % 2 else 2
             bits -= bits % 2
-    return values
+    return stages
 
 
 def local(
@@ -607,6 +638,7 @@
     mine, theirs = order(pair_halves, mixed_slots)
     upstream_made = order.fill(upstream)
     mixed_half = order(lambda *parts: jnp.concatenate(parts, axis=0), mine, pair_swap(theirs))
+    dz_sum = order(lambda values: jnp.sum(values.astype(wide), axis=0), dz_low)
     second = whole(order.pass_on(second))
     upstream = order.pass_on(upstream, second)
     active, slope = order(lambda rows: up_and_bend(rows, up_slab, up_bias_slab[None]), second)
@@ -618,24 +650,16 @@
     def slab_sum(made):
         return lax.psum_scatter(made, "fsdp", scatter_dimension=0, tiled=True)
 
-    def slabs_of_rows(*sums):
-        parts = [part.reshape(groups, -1, part.shape[1]) for part in sums]
-        slabs = lax.all_to_all(jnp.concatenate(parts, axis=1), "seq", split_axis=0, concat_axis=0, tiled=True)
-        count = parts[0].shape[1]
-        return [
-            jnp.swapaxes(slabs[:, at : at + count], 0, 1).astype(wide) for at in range(0, slabs.shape[1], count)
-        ]
+    def slabs_of_rows(values):
+        return lax.all_to_all(
+            values.reshape(groups, -1, values.shape[1]), "seq", split_axis=0, concat_axis=0, tiled=True
+        )
 
     down_sum = slab_sum(slab_product(upstream, active))
     count = rows_here
 
-    def slots(values, start, stop):
-        return values[start * count : stop * count]
-
-    def to_hidden(start, stop):
-        return order(
-            lambda rows: hidden_gradient(rows, down_slab, slope, start * count, (stop - start) * count), upstream
-        )
+    def slots(product, start, stop):
+        return lambda values: product(values[start * count : stop * count])
 
     def to_second(rows):
         return contract_last(rows, up_slab).astype(low)
@@ -649,22 +673,17 @@
     def scatter(product, rows):
         return lax.psum_scatter(order(product, rows), "seq", scatter_dimension=0, tiled=True)
 
+    hidden_grad, hidden_sum = order(lambda rows: hidden_gradient(rows, down_slab, slope, 0, groups * count), upstream)
     if square:
-        grad_far, sum_far = to_hidden(3, 4)
-        far = swap_far(order.halves(to_second, grad_far))
-        grad_near, sum_near = to_hidden(1, 3)
-        near = order(to_second, grad_near)
-        direct = swap_direct(near)
-        came = order.add_far(near, far, direct)
-        grad_own, sum_own = to_hidden(0, 1)
-        second_own = order(to_second, grad_own)
-        hidden_grad = [grad_own, grad_near, grad_far]
-        hidden_sum = sum_own + sum_near + sum_far
-        result_far = order.halves(to_result, slots(active, 3, 4))
+        far = swap_far(order.halves(slots(to_second, 3, 4), hidden_grad))
+        rest = order(slots(to_second, 0, 3), hidden_grad)
+        second_own = rest
+        direct = swap_direct(rest, half)
+        came = order.add_far(rest, far, direct)
+        result_far = order.halves(slots(to_result, 3, 4), active)
         up_sum = slab_sum(gate(slab_product(second, hidden_grad), *came))
         result_far = swap_far(gate(result_far, *came))
     else:
-        hidden_grad, hidden_sum = to_hidden(0, groups)
         second_own, came = scatter(to_second, hidden_grad), ()
         up_sum = slab_sum(slab_product(second, hidden_grad))
     branch_grad, middle_grad, middle_sums = order(
@@ -677,13 +696,14 @@
     hidden_sum = lax.dynamic_update_slice_in_dim(
         jnp.zeros((hidden_width,), wide), hidden_sum[0], me * hidden_slab, axis=0
     )
-    early = [middle_sums[2], middle_sums[0], middle_sums[1], hidden_sum, middle_sums[3]]
-    mixed_grad = order(lambda rows: contract_last(rows, full_out).astype(low), branch_grad)
+    early = [middle_sums[2], middle_sums[0], middle_sums[1], hidden_sum, dz_sum]
+    mixed_grad = order(lambda rows: mixed_gradient(rows, full_out, slab), branch_grad)
+    if square:
+        mixed_grad = gate(mixed_grad, *result_far)
     mixed_grad = exchange(by_index([mixed_grad[:, j * slab : (j + 1) * slab] for j in range(groups)], me))
     if square:
-        order.after(*result_far)
-        result_rest = order(to_result, slots(active, 0, 3))
-    branch_other = pair_swap(gate(branch_grad, *result_far) if square else branch_grad)
+        result_rest = order(slots(to_result, 0, 3), active)
+    branch_other = pair_swap(branch_grad)
     branch_pair = jnp.concatenate([branch_grad, branch_other], axis=0)
     out_sum = order(lambda columns: outer(columns, branch_pair, groups, 1), mixed_half)
     mixed_grad = order(lambda *parts: jnp.concatenate(parts, axis=0), *mixed_grad)
@@ -692,18 +712,19 @@
         part = out_sum.shape[0] // 4
         out_far = out_sum[3 * part : 3 * part + part // 2], out_sum[3 * part + part // 2 :]
         out_far = swap_far(gate(out_far, mixed_grad))
-        result_near = result_rest[count:]
-        result_came = order.add_far(result_near, result_far, None, mixed_grad)
+        result_came = order.add_far(result_rest, result_far, None, mixed_grad)
     order.after(down_sum)
     begun = order(lambda rows: attend_backward(*attention, rows, seq_count, local_len, 0, pairs // 2), mixed_grad)
     if square:
-        out_came = order.add_far(out_sum[part : 3 * part], out_far, None)
+        out_came = order.add_far(out_sum, out_far, None, at=part)
+    down_slabs = slabs_of_rows(gate(down_sum, begun))
     qkv_grad = order(
         lambda rows: attend_backward(*attention, rows, seq_count, local_len, pairs // 2, pairs, begun), mixed_grad
     )
+    order.after(down_slabs)
     if square:
         order.after(*out_came, *result_came)
-        out_sum = order(lambda own, *came: summed(own, came).astype(low), out_sum[:part], *out_came)
+        out_sum = order(lambda own, *came: summed(own[:part], came).astype(low), out_sum, *out_came)
         order.after(*out_came)
     else:
         out_sum = lax.psum_scatter(out_sum, "seq", scatter_dimension=0, tiled=True)
@@ -715,12 +736,12 @@
     grad_w_out = lax.psum_scatter(out_sum, "fsdp", scatter_dimension=0, tiled=True).astype(wide)
     order.after(up_sum)
     if square:
-        far = swap_far(order.halves(to_normed, slots(qkv_grad, 3, 4)))
-        near = order(to_normed, slots(qkv_grad, 1, 3))
-        direct = swap_direct(near)
+        far = swap_far(order.halves(slots(to_normed, 3, 4), qkv_grad))
+        near = order(slots(to_normed, 1, 3), qkv_grad)
+        direct = swap_direct(near, half)
         qkv_sum = slab_sum(gate(slab_product(normed, qkv_grad), *far))
         came = order.add_far(near, far, direct)
-        normed_own = order(to_normed, slots(qkv_grad, 0, 1))
+        normed_own = order(slots(to_normed, 0, 1), qkv_grad)
     else:
         qkv_sum = slab_sum(slab_product(normed, qkv_grad))
         normed_own, came = scatter(to_normed, qkv_grad), ()
@@ -733,13 +754,15 @@
     else:
         outcome = scatter(to_result, active).astype(wide)
     result = (middle + (outcome + down_bias)).astype(low).reshape(tokens.shape)
-    if square:
-        up_sum, down_sum = gate((up_sum, down_sum), *came)
-    grad_w_down = slabs_of_rows(down_sum)[0]
-    order.after(grad_w_down)
-    grad_w_down = grad_w_down.reshape(-1, hidden_width).T
-    grad_w_up = slabs_of_rows(up_sum)[0].reshape(-1, hidden_width)
-    grad_w_qkv = slabs_of_rows(qkv_sum)[0].reshape(-1, groups, pairs, 3, PAIR)
+    up_slabs = slabs_of_rows(gate(up_sum, *came, normed_own))
+    qkv_slabs = slabs_of_rows(qkv_sum)
+
+    def rows_of(slabs):
+        return jnp.swapaxes(slabs, 0, 1).astype(wide)
+
+    grad_w_down = rows_of(down_slabs).reshape(-1, hidden_width).T
+    grad_w_up = rows_of(up_slabs).reshape(-1, hidden_width)
+    grad_w_qkv = rows_of(qkv_slabs).reshape(-1, groups, pairs, 3, PAIR)
     grad_w_qkv = jnp.transpose(grad_w_qkv, (0, 3, 1, 2, 4)).reshape(-1, 3 * model_width)
 
     head_sum = jnp.transpose(column_sum(qkv_grad).reshape(pairs, 3, PAIR), (1, 0, 2)).reshape(3, slab)
@@ -747,8 +770,16 @@
         jnp.zeros((2, model_width), wide), head_sum[0::2], me * slab, axis=1
     )
     late = [qv_sum.reshape(-1), input_sums[0], input_sums[1]]
+    order.after(up_slabs)
     sums = order(lambda *parts: jnp.concatenate(parts).reshape(-1, PAIR), *early, *late)
-    sums = total(sums).reshape(-1)
+    stages = total_stages()
+    for axis, masks in stages:
+        others = range(lax.axis_size(axis))
+        came = [lax.ppermute(sums, axis, [(i, i ^ mask) for i in others]) for mask in masks]
+        if (axis, masks) == stages[-1]:
+            order.after(qkv_slabs)
+        sums = order(lambda *parts: sum(parts[1:], parts[0]), sums, *came)
+    sums = sums.reshape(-1)
 
     def cut(at, count):
         return sums[at * model_width : (at + count) * model_width]

time: 804 us -> 777 us (0.966)
  local copies, waits for them, and re-layouts: 123 us -> 102 us
    slice x12 -> x5, local copies, waits for them, and re-layouts: 23.2 us -> 6.23 us  [the longest x2 2.94 us: swap_direct(): return (swap(made[at:at + half], 1), swap(made[at + 3 * half:], 2))]
    ppermute x44, waiting for transfers between devices: 153 us -> 138 us  [swap(): return lax.ppermute(values, 'seq', [(i, i ^ bit) for i in range(4)])]
    dot_general x7 -> x5, matrix products: 65.4 us -> 51.1 us  [contract_last(): lax.dot_general(left_side, right_side, (((1,), (1,)), ((), ())), preferre...]
    pallas_call x3 -> x1, Pallas kernels: 36.8 us -> 25.3 us  [hidden_gradient(): pl.pallas_call(partial(hidden_grad_kernel, chunk=512), grid=(count // TIL...]
    all_to_all x3, waiting for transfers between devices: 8.02 us -> 17.5 us  [slabs_of_rows(): lax.all_to_all(values.reshape(groups, -1, values.shape[1]), 'seq', split_...]
    pallas_call x0 -> x1, Pallas kernels: none -> 8.87 us  [mixed_gradient(): pl.pallas_call(mixed_grad_kernel, grid=(width // slab,), in_specs=[pl.Blo...]
    unnamed x89 -> x77, local copies, waits for them, and re-layouts: 48.2 us -> 43.3 us
  transfers between devices with their start and end apart: 64 -> 64, of which waited for: 20 -> 22; matrix products, arithmetic and copies ran while one was open for 33% -> 31% of each run, Pallas kernels for 32% -> 33%
where the time goes in v10:
time: 777 us; the launch traced here: 772 us
  Pallas kernels  255 us (33%)
  waiting for transfers between devices  175 us (23%)
  matrix products  106 us (14%)
  local copies, waits for them, and re-layouts  102 us (13%)
  starting transfers between devices  68.2 us (9%)
  other arithmetic  50.3 us (6%)
  between operations  15.2 us (2%)
    ppermute x44, waiting for transfers between devices, swap(): return lax.ppermute(values, 'seq', [(i, i ^ bit) for i in range(4)])  138 us
    pallas_call x4, Pallas kernels, outer(): pl.pallas_call(partial(outer_kernel, chunk=512 if width % 512 == 0 else 2...  74.6 us
    pallas_call x2, Pallas kernels, attend_backward(): pl.pallas_call(partial(attend_backward_kernel, blocks=blocks, seqs=seqs,...  57.2 us
    dot_general x4, matrix products, contract(): lax.dot_general(left_side, right_side, (((1,), (0,)), ((), ())), preferre...  54.4 us
    dot_general x5, matrix products, contract_last(): lax.dot_general(left_side, right_side, (((1,), (1,)), ((), ())), preferre...  51.1 us
    ppermute x44, starting transfers between devices, swap(): return lax.ppermute(values, 'seq', [(i, i ^ bit) for i in range(4)])  48 us
    unnamed x77, local copies, waits for them, and re-layouts  43.3 us
    pallas_call x1, Pallas kernels, up_and_bend(): pl.pallas_call(partial(up_kernel, chunk=512), grid=(count // TILE,), in_s...  30.6 us
  transfers between devices with their start and end apart: 64, of which 22 were waited for; matrix products, arithmetic and copies ran while one was open for 31% of the time, Pallas kernels for 33%

profile of v10, /device:TPU:0, one launch (start us, length us, event | category | flops | bytes accessed | tf_op | source)
XLA Modules:
  0.0 771.6 jit_solution(2524966096297862479)
XLA Ops:
  26.8 18.9 %collective-permute-done.2 = bf16[256,2048]{1,0:T(8,128)(2,1)} collective-permute-done((bf16[256,2048]{1,0:T(8,128)(2,1)}, bf16[256,2048]{1,0:T(8,128)(2,1)}, u32[]{:S(2)}, u32[]{:S(2)}) %collective-permute-start.2) | collective-permute-done | bytes 1048608 | tf_op jit(solution)/shard_map/ppermute | solution.py:405
  52.5 17.7 %collective-permute-done = bf16[256,2048]{1,0:T(8,128)(2,1)} collective-permute-done((bf16[256,2048]{1,0:T(8,128)(2,1)}, bf16[256,2048]{1,0:T(8,128)(2,1)}, u32[]{:S(2)}, u32[]{:S(2)}) %collective-permute-start) | collective-permute-done | bytes 1048608 | tf_op jit(solution)/shard_map/ppermute | solution.py:405
  78.4 12.9 %collective-permute-done.4 = bf16[256,2048]{1,0:T(8,128)(2,1)} collective-permute-done((bf16[256,2048]{1,0:T(8,128)(2,1)}, bf16[256,2048]{1,0:T(8,128)(2,1)}, u32[]{:S(2)}, u32[]{:S(2)}) %collective-permute-start.4) | collective-permute-done | bytes 1048608 | tf_op jit(solution)/shard_map/ppermute | solution.py:405
  99.8 18.6 %add_convert_fusion.qkv_ref = bf16[2048,1536]{1,0:T(8,128)(2,1)} fusion(bf16[2048,2048]{1,0:T(8,128)(2,1)} %constant_dynamic-update-slice_fusion.left_ref, bf16[2048,1536]{1,0:T(8,128)(2,1)} %all-gather.5.cloned.1.call-done, f32[1536]{0:T(1024)S(1)} %reduce.2), kind=kOutput, calls=%fused_computation.1 | convolution fusion | flops 12891193344 | bytes 20977664 | tf_op jit(solution)/shard_map/dot_general | solution.py:30
  118.4 29.7 %attend_forward.1 = (bf16[2048,512]{1,0:T(8,128)(2,1)}, f32[2048,512]{1,0:T(8,128)}) custom-call(s32[1]{0:T(128)} %bitcast.1.at_ref.mask_ref, f32[8]{0:T(128)} %multiply_power_fusion.slope_ref, bf16[2048,1536]{1,0:T(8,128)(2,1)} %add_convert_fusion.qkv_ref), custom_call_target="tpu_custom_call" | custom-call | flops 2684354560 | bytes 2621440 | tf_op jit(solution)/shard_map/attend_forward/pallas_call | solution.py:165
  155.5 11.2 %collective-permute-done.10 = bf16[512,512]{1,0:T(8,128)(2,1)S(1)} collective-permute-done((bf16[512,512]{1,0:T(8,128)(2,1)}, bf16[512,512]{1,0:T(8,128)(2,1)S(1)}, u32[]{:S(2)}, u32[]{:S(2)}) %collective-permute-start.10) | collective-permute-done | bytes 524320 | tf_op jit(solution)/shard_map/ppermute | solution.py:405
  222.6 16.7 %collective-permute-done.14 = bf16[256,2048]{1,0:T(8,128)(2,1)} collective-permute-done((bf16[256,2048]{1,0:T(8,128)(2,1)}, bf16[256,2048]{1,0:T(8,128)(2,1)}, u32[]{:S(2)}, u32[]{:S(2)}) %collective-permute-start.14) | collective-permute-done | bytes 1048608 | tf_op jit(solution)/shard_map/ppermute | solution.py:405
  249.8 11.0 %collective-permute-done.17 = bf16[256,2048]{1,0:T(8,128)(2,1)S(1)} collective-permute-done((bf16[256,2048]{1,0:T(8,128)(2,1)}, bf16[256,2048]{1,0:T(8,128)(2,1)S(1)}, u32[]{:S(2)}, u32[]{:S(2)}) %collective-permute-start.17) | collective-permute-done | bytes 1048608 | tf_op jit(solution)/shard_map/ppermute | solution.py:405
  271.1 30.6 %up_and_bend.1 = (bf16[2048,2048]{1,0:T(8,128)(2,1)}, f32[2048,2048]{1,0:T(8,128)}) custom-call(bf16[2048,2048]{1,0:T(8,128)(2,1)} %constant_dynamic-update-slice_fusion.7.rows_ref.left_ref, bf16[2048,2048]{1,0:T(8,128)(2,1)} %all-gather.9.cloned.1.call-done.weight_ref, f32[1,2048]{1,0:T(1,128)} %bitcast.126), custom_call_target="tpu_custom_call" | custom-call | flops 8589934592 | bytes 8388608 | tf_op jit(solution)/shard_map/up_and_bend/pallas_call | solution.py:246
  303.8 23.7 %outer.4 = bf16[8,4,64,2048]{3,2,1,0:T(8,128)(2,1)} custom-call(bf16[2048,2048]{1,0:T(8,128)(2,1)} %constant_dynamic-update-slice_fusion.35.left_ref.rows_ref, bf16[2048,2048]{1,0:T(8,128)(2,1)} %get-tuple-element.174.refs_0_), custom_call_target="tpu_custom_call" | custom-call | flops 4294967296 | bytes 4194304 | tf_op jit(solution)/shard_map/outer/pallas_call | solution.py:387
  327.5 25.3 %hidden_gradient.1 = (bf16[2048,2048]{1,0:T(8,128)(2,1)}, f32[1,2048]{1,0:T(1,128)}) custom-call(bf16[2048,2048]{1,0:T(8,128)(2,1)} %constant_dynamic-update-slice_fusion.35.left_ref.rows_ref, bf16[2048,2048]{1,0:T(8,128)(2,1)} %all-gather.11.cloned.1.call-done.weight_ref, f32[2048,2048]{1,0:T(8,128)} %get-tuple-element.149.slope_ref), custom_call_target="tpu_custom_call" | custom-call | flops 6442450944 | bytes 6291456 | tf_op jit(solution)/shard_map/hidden_gradient/pallas_call | solution.py:270
  365.3 16.3 %convolution_convert_fusion.1.own_ref = bf16[1536,2048]{1,0:T(8,128)(2,1)S(1)} fusion(bf16[2048,2048]{1,0:T(8,128)(2,1)} %all-gather.9.cloned.1.call-done.weight_ref, bf16[2048,2048]{1,0:T(8,128)(2,1)S(1)} %copy-done.6), kind=kOutput, calls=%fused_computation.3 | convolution fusion | flops 12888047616 | bytes 20971520 | tf_op jit(solution)/shard_map/dot_general | solution.py:36
  403.9 23.5 %outer.5 = bf16[8,4,64,2048]{3,2,1,0:T(8,128)(2,1)} custom-call(bf16[2048,2048]{1,0:T(8,128)(2,1)} %constant_dynamic-update-slice_fusion.7.rows_ref.left_ref, bf16[2048,2048]{1,0:T(8,128)(2,1)} %get-tuple-element.159.refs_0_), custom_call_target="tpu_custom_call" | custom-call | flops 4294967296 | bytes 4194304 | tf_op jit(solution)/shard_map/outer/pallas_call | solution.py:387
  434.8 12.2 %norm_back.2 = (bf16[512,2048]{1,0:T(8,128)(2,1)}, f32[512,2048]{1,0:T(8,128)}, f32[8,2048]{1,0:T(8,128)}) custom-call(bf16[1536,2048]{1,0:T(8,128)(2,1)} %copy-done.4, f32[512,2048]{1,0:T(8,128)} %copy-done, bf16[512,2048]{1,0:T(8,128)(2,1)} %bitcast.90, f32[1,2048]{1,0:T(1,128)} %bitcast.113, bf16[256,2048]{1,0:T(8,128)(2,1)} %collective-permute-done.22.refs_0_, ...), custom_call_target="tpu_custom_call" | custom-call | flops 7864320 | bytes 7680 | tf_op jit(solution)/shard_map/norm_back/pallas_call | solution.py:352
  447.0 8.9 %mixed_gradient.1 = bf16[512,2048]{1,0:T(8,128)(2,1)} custom-call(bf16[512,2048]{1,0:T(8,128)(2,1)} %get-tuple-element.173.rows_ref, bf16[2048,2048]{1,0:T(8,128)(2,1)} %all-gather.7.cloned.1.call-done.weight_ref), custom_call_target="tpu_custom_call" | custom-call | flops 1073741824 | bytes 1048576 | tf_op jit(solution)/shard_map/mixed_gradient/pallas_call | solution.py:296
  461.9 19.3 %convolution_convert_fusion = bf16[1536,2048]{1,0:T(8,128)(2,1)} fusion(bf16[2048,2048]{1,0:T(8,128)(2,1)} %all-gather.11.cloned.1.call-done.weight_ref, bf16[2048,2048]{1,0:T(8,128)(2,1)} %get-tuple-element.174.refs_0_), kind=kOutput, calls=%fused_computation.2 | convolution fusion | flops 12888047616 | bytes 20971520 | tf_op jit(solution)/shard_map/dot_general | solution.py:30
  512.8 28.9 %attend_backward.2.rest_0_ = bf16[2048,1536]{1,0:T(8,128)(2,1)} custom-call(s32[1]{0:T(128)} %bitcast.1.at_ref.mask_ref, f32[8]{0:T(128)} %multiply_power_fusion.slope_ref, bf16[2048,1536]{1,0:T(8,128)(2,1)} %add_convert_fusion.qkv_ref, f32[2048,512]{1,0:T(8,128)} %get-tuple-element.129.lse_ref, bf16[2048,512]{1,0:T(8,128)(2,1)} %get-tuple-element.128.mixed_ref, ...), custom_call_target="tpu_custom_call" | custom-call | flops 3355443200 | bytes 3276800 | tf_op jit(solution)/shard_map/attend_backward/pallas_call | solution.py:190
  549.0 28.3 %attend_backward.3.refs_0_ = bf16[2048,1536]{1,0:T(8,128)(2,1)} custom-call(s32[1]{0:T(128)} %bitcast.1.at_ref.mask_ref, f32[8]{0:T(128)} %multiply_power_fusion.slope_ref, bf16[2048,1536]{1,0:T(8,128)(2,1)} %add_convert_fusion.qkv_ref, f32[2048,512]{1,0:T(8,128)} %get-tuple-element.129.lse_ref, ...), custom_call_target="tpu_custom_call", output_to_operand_aliasing={{}: (6, {})} | custom-call | flops 3355443200 | bytes 3276800 | tf_op jit(solution)/shard_map/attend_backward/pallas_call | solution.py:190
  577.2 17.5 %all-to-all-done = bf16[4,64,2048]{2,1,0:T(8,128)(2,1)S(1)} async-done(((bf16[4,64,2048]{2,1,0:T(8,128)(2,1)}), bf16[4,64,2048]{2,1,0:T(8,128)(2,1)S(1)}, u32[]{:S(2)}, u32[]{:S(2)}) %all-to-all-start) | async-done | bytes 1048608 | tf_op jit(solution)/shard_map/all_to_all | solution.py:654
  608.9 11.1 %convolution_convert_fusion.2 = bf16[1024,2048]{1,0:T(8,128)(2,1)} fusion(bf16[2048,1536]{1,0:T(8,128)(2,1)} %all-gather.5.cloned.1.call-done, bf16[2048,1536]{1,0:T(8,128)(2,1)S(1)} %bitcast.84), kind=kOutput, calls=%fused_computation.21 | convolution fusion | flops 6444548096 | bytes 13631488 | tf_op jit(solution)/shard_map/dot_general | solution.py:36
  620.0 18.6 %outer.7 = bf16[8,4,64,1536]{3,2,1,0:T(8,128)(2,1)} custom-call(bf16[2048,2048]{1,0:T(8,128)(2,1)} %constant_dynamic-update-slice_fusion.left_ref, bf16[2048,1536]{1,0:T(8,128)(2,1)} %attend_backward.3.refs_0_), custom_call_target="tpu_custom_call" | custom-call | flops 3221225472 | bytes 3145728 | tf_op jit(solution)/shard_map/outer/pallas_call | solution.py:387
  661.2 8.9 %collective-permute-done.42.refs_0_ = bf16[256,2048]{1,0:T(8,128)(2,1)} collective-permute-done((bf16[256,2048]{1,0:T(8,128)(2,1)}, bf16[256,2048]{1,0:T(8,128)(2,1)}, u32[]{:S(2)}, u32[]{:S(2)}) %collective-permute-start.42) | collective-permute-done | bytes 1048608 | tf_op jit(solution)/shard_map/ppermute | solution.py:405
  670.5 19.1 %collective-permute-done.43.refs_1_ = bf16[256,2048]{1,0:T(8,128)(2,1)} collective-permute-done((bf16[256,2048]{1,0:T(8,128)(2,1)}, bf16[256,2048]{1,0:T(8,128)(2,1)}, u32[]{:S(2)}, u32[]{:S(2)}) %collective-permute-start.43) | collective-permute-done | bytes 1048608 | tf_op jit(solution)/shard_map/ppermute | solution.py:405
  697.0 11.7 %norm_back.3 = (bf16[512,2048]{1,0:T(8,128)(2,1)}, f32[512,2048]{1,0:T(8,128)}, f32[8,2048]{1,0:T(8,128)}) custom-call(bf16[512,2048]{1,0:T(8,128)(2,1)} %convolution_convert_fusion.3.own_ref, bf16[512,2048]{1,0:T(8,128)(2,1)} %bitcast.87, f32[512,2048]{1,0:T(8,128)} %get-tuple-element.171.base_ref, f32[1,2048]{1,0:T(1,128)} %bitcast.121, ...), custom_call_target="tpu_custom_call" | custom-call | flops 7864320 | bytes 7680 | tf_op jit(solution)/shard_map/norm_back/pallas_call | solution.py:352
  (298 shorter events, 315.9 us)
Async XLA Ops:
  7.2 92.7 %all-gather.5.cloned.1.call-start = ((), (), s32[]{:S(2)}) async-start(), calls=%async_computation.7 | async-start | bytes 7077888 | tf_op jit(solution)/shard_map/all_gather | solution.py:597
  10.3 168.8 %all-gather.7.cloned.1.call-start = ((), (), s32[]{:S(2)}) async-start(), calls=%async_computation.8 | async-start | bytes 9437184 | tf_op jit(solution)/shard_map/all_gather | solution.py:609
  11.1 260.0 %all-gather.9.cloned.1.call-start = ((), (), s32[]{:S(2)}) async-start(), calls=%async_computation.9 | async-start | bytes 9437184 | tf_op jit(solution)/shard_map/all_gather | solution.py:610
  18.3 309.2 %all-gather.11.cloned.1.call-start = ((), (), s32[]{:S(2)}) async-start(), calls=%async_computation.10 | async-start | bytes 9437184 | tf_op jit(solution)/shard_map/all_gather | solution.py:611
  22.9 47.4 %collective-permute-start = (bf16[256,2048]{1,0:T(8,128)(2,1)}, bf16[256,2048]{1,0:T(8,128)(2,1)}, u32[]{:S(2)}, u32[]{:S(2)}) collective-permute-start(bf16[256,2048]{1,0:T(8,128)(2,1)} %get-tuple-element.279), channel_id=1, source_target_pairs={{0,8},{8,0},{16,24},{24,16},{1,9},{9,1},{17,25},{25,17},{2,10},{10... | collective-permute-start | bytes 3145736 | tf_op jit(solution)/shard_map/ppermute | solution.py:405
  23.4 52.7 %collective-permute-start.3 = (bf16[256,2048]{1,0:T(8,128)(2,1)}, bf16[256,2048]{1,0:T(8,128)(2,1)}, u32[]{:S(2)}, u32[]{:S(2)}) collective-permute-start(bf16[256,2048]{1,0:T(8,128)(2,1)} %get-tuple-element.278), channel_id=1, source_target_pairs={{0,16},{8,24},{16,0},{24,8},{1,17},{9,25},{17,1},{25,9},{2,18},{10... | collective-permute-start | bytes 3145736 | tf_op jit(solution)/shard_map/ppermute | solution.py:405
  25.8 487.0 %reduce-scatter.5.cloned.1.call-start = ((), (), s32[]{:S(2)}) async-start(), calls=%async_computation.11 | async-start | bytes 9437184 | tf_op jit(solution)/shard_map/reduce_scatter | solution.py:651
  45.7 45.6 %collective-permute-start.4 = (bf16[256,2048]{1,0:T(8,128)(2,1)}, bf16[256,2048]{1,0:T(8,128)(2,1)}, u32[]{:S(2)}, u32[]{:S(2)}) collective-permute-start(bf16[256,2048]{1,0:T(8,128)(2,1)} %collective-permute-done.2), channel_id=1, source_target_pairs={{0,8},{8,0},{16,24},{24,16},{1,9},{9,1},{17,25},{25,17},{2,10},{10... | collective-permute-start | bytes 3145736 | tf_op jit(solution)/shard_map/ppermute | solution.py:405
  95.8 52.3 %collective-permute-start.7 = (bf16[256,2048]{1,0:T(8,128)(2,1)}, bf16[256,2048]{1,0:T(8,128)(2,1)}, u32[]{:S(2)}, u32[]{:S(2)}) collective-permute-start(bf16[256,2048]{1,0:T(8,128)(2,1)} %get-tuple-element.133), channel_id=1, source_target_pairs={{0,16},{8,24},{16,0},{24,8},{1,17},{9,25},{17,1},{25,9},{2,18},{10... | collective-permute-start | bytes 3145736 | tf_op jit(solution)/shard_map/ppermute | solution.py:405
  96.2 52.0 %collective-permute-start.8 = (bf16[256,2048]{1,0:T(8,128)(2,1)}, bf16[256,2048]{1,0:T(8,128)(2,1)}, u32[]{:S(2)}, u32[]{:S(2)}) collective-permute-start(bf16[256,2048]{1,0:T(8,128)(2,1)} %get-tuple-element.133), channel_id=1, source_target_pairs={{0,8},{8,0},{16,24},{24,16},{1,9},{9,1},{17,25},{25,17},{2,10},{10... | collective-permute-start | bytes 3145736 | tf_op jit(solution)/shard_map/ppermute | solution.py:405
  97.8 50.3 %collective-permute-start.6 = (bf16[256,2048]{1,0:T(8,128)(2,1)S(1)}, bf16[256,2048]{1,0:T(8,128)(2,1)}, u32[]{:S(2)}, u32[]{:S(2)}) collective-permute-start(bf16[256,2048]{1,0:T(8,128)(2,1)S(1)} %get-tuple-element.134), channel_id=1, source_target_pairs={{0,8},{8,0},{16,24},{24,16},{1,9},{9,1},{17,25},{25,17},{2,10},{10... | collective-permute-start | bytes 3145736 | tf_op jit(solution)/shard_map/ppermute | solution.py:405
  98.2 50.0 %collective-permute-start.9 = (bf16[256,2048]{1,0:T(8,128)(2,1)S(1)}, bf16[256,2048]{1,0:T(8,128)(2,1)}, u32[]{:S(2)}, u32[]{:S(2)}) collective-permute-start(bf16[256,2048]{1,0:T(8,128)(2,1)S(1)} %get-tuple-element.134), channel_id=1, source_target_pairs={{0,16},{8,24},{16,0},{24,8},{1,17},{9,25},{17,1},{25,9},{2,18},{10... | collective-permute-start | bytes 3145736 | tf_op jit(solution)/shard_map/ppermute | solution.py:405
  190.5 49.5 %collective-permute-start.13 = (bf16[256,2048]{1,0:T(8,128)(2,1)}, bf16[256,2048]{1,0:T(8,128)(2,1)}, u32[]{:S(2)}, u32[]{:S(2)}) collective-permute-start(bf16[256,2048]{1,0:T(8,128)(2,1)} %get-tuple-element.272), channel_id=1, source_target_pairs={{0,8},{8,0},{16,24},{24,16},{1,9},{9,1},{17,25},{25,17},{2,10},{10... | collective-permute-start | bytes 3145736 | tf_op jit(solution)/shard_map/ppermute | solution.py:405
  192.6 46.6 %collective-permute-start.14 = (bf16[256,2048]{1,0:T(8,128)(2,1)}, bf16[256,2048]{1,0:T(8,128)(2,1)}, u32[]{:S(2)}, u32[]{:S(2)}) collective-permute-start(bf16[256,2048]{1,0:T(8,128)(2,1)} %get-tuple-element.271), channel_id=1, source_target_pairs={{0,8},{8,0},{16,24},{24,16},{1,9},{9,1},{17,25},{25,17},{2,10},{10... | collective-permute-start | bytes 3145736 | tf_op jit(solution)/shard_map/ppermute | solution.py:405
  193.2 54.3 %collective-permute-start.16 = (bf16[256,2048]{1,0:T(8,128)(2,1)}, bf16[256,2048]{1,0:T(8,128)(2,1)}, u32[]{:S(2)}, u32[]{:S(2)}) collective-permute-start(bf16[256,2048]{1,0:T(8,128)(2,1)} %get-tuple-element.271), channel_id=1, source_target_pairs={{0,16},{8,24},{16,0},{24,8},{1,17},{9,25},{17,1},{25,9},{2,18},{10... | collective-permute-start | bytes 3145736 | tf_op jit(solution)/shard_map/ppermute | solution.py:405
  327.5 271.4 %reduce-scatter.7.cloned.1.call-start = ((), (), s32[]{:S(2)}) async-start(), calls=%async_computation.12 | async-start | bytes 9437184 | tf_op jit(solution)/shard_map/reduce_scatter | solution.py:651
  381.8 45.6 %collective-permute-start.22 = (bf16[256,2048]{1,0:T(8,128)(2,1)S(1)}, bf16[256,2048]{1,0:T(8,128)(2,1)}, u32[]{:S(2)}, u32[]{:S(2)}) collective-permute-start(bf16[256,2048]{1,0:T(8,128)(2,1)S(1)} %get-tuple-element.241), channel_id=1, source_target_pairs={{0,8},{8,0},{16,24},{24,16},{1,9},{9,1},{17,25},{25,17},{2,10},{10... | collective-permute-start | bytes 3145736 | tf_op jit(solution)/shard_map/ppermute | solution.py:405
  511.5 65.7 %collective-permute-start.34 = (bf16[512,2048]{1,0:T(8,128)(2,1)}, bf16[512,2048]{1,0:T(8,128)(2,1)}, u32[]{:S(2)}, u32[]{:S(2)}) collective-permute-start(bf16[512,2048]{1,0:T(8,128)(2,1)} %pad_maximum_fusion.4), channel_id=1, source_target_pairs={{0,8},{8,0},{16,24},{24,16},{1,9},{9,1},{17,25},{25,17},{2,10},{10... | collective-permute-start | bytes 6291464 | tf_op jit(solution)/shard_map/ppermute | solution.py:405
  512.3 64.9 %collective-permute-start.35 = (bf16[512,2048]{1,0:T(8,128)(2,1)}, bf16[512,2048]{1,0:T(8,128)(2,1)}, u32[]{:S(2)}, u32[]{:S(2)}) collective-permute-start(bf16[512,2048]{1,0:T(8,128)(2,1)} %pad_maximum_fusion.5), channel_id=1, source_target_pairs={{0,16},{8,24},{16,0},{24,8},{1,17},{9,25},{17,1},{25,9},{2,18},{10... | collective-permute-start | bytes 6291464 | tf_op jit(solution)/shard_map/ppermute | solution.py:405
  542.4 52.4 %collective-permute-start.39 = (bf16[256,2048]{1,0:T(8,128)(2,1)S(1)}, bf16[256,2048]{1,0:T(8,128)(2,1)}, u32[]{:S(2)}, u32[]{:S(2)}) collective-permute-start(bf16[256,2048]{1,0:T(8,128)(2,1)S(1)} %pad_maximum_fusion.8), channel_id=1, source_target_pairs={{0,16},{8,24},{16,0},{24,8},{1,17},{9,25},{17,1},{25,9},{2,18},{10... | collective-permute-start | bytes 3145736 | tf_op jit(solution)/shard_map/ppermute | solution.py:405
  544.1 50.7 %collective-permute-start.38 = (bf16[256,2048]{1,0:T(8,128)(2,1)S(1)}, bf16[256,2048]{1,0:T(8,128)(2,1)}, u32[]{:S(2)}, u32[]{:S(2)}) collective-permute-start(bf16[256,2048]{1,0:T(8,128)(2,1)S(1)} %pad_maximum_fusion.7), channel_id=1, source_target_pairs={{0,8},{8,0},{16,24},{24,16},{1,9},{9,1},{17,25},{25,17},{2,10},{10... | collective-permute-start | bytes 3145736 | tf_op jit(solution)/shard_map/ppermute | solution.py:405
  545.4 49.4 %all-to-all-start = ((bf16[4,64,2048]{2,1,0:T(8,128)(2,1)}), bf16[4,64,2048]{2,1,0:T(8,128)(2,1)S(1)}, u32[]{:S(2)}, u32[]{:S(2)}) async-start(bf16[4,64,2048]{2,1,0:T(8,128)(2,1)} %bitcast.15), calls=%async_computation.1 | async-start | bytes 2097152 | tf_op jit(solution)/shard_map/all_to_all | solution.py:654
  548.9 184.9 %reduce-scatter.9.cloned.1.call-start = ((), (), s32[]{:S(2)}) async-start(), calls=%async_computation.13 | async-start | bytes 7077888 | tf_op jit(solution)/shard_map/reduce_scatter | solution.py:651
  638.6 109.9 %reduce-scatter.11.cloned.1.call-start = ((), (), s32[]{:S(2)}) async-start(), calls=%async_computation.14 | async-start | bytes 2359296 | tf_op jit(solution)/shard_map/reduce_scatter | solution.py:736
  (63 other events, 1345.5 us)
Sparse Core Ops, SparseCore 0:
  10.4 67.4 all-gather.4
  79.5 80.6 all-gather.6
  161.9 80.5 all-gather.8
  243.9 81.0 all-gather.10
  327.6 89.8 reduce-scatter.4
  432.8 88.9 reduce-scatter.6
  638.8 69.3 reduce-scatter.8
  710.4 38.0 reduce-scatter.10

commit v11 on v10

--- a/solution.py
+++ b/solution.py
@@ -313,24 +313,30 @@
     wide = jnp.float32
     step = pl.program_id(0)
 
+    @pl.when(step == 0)
+    def _():
+        sums_ref[...] = jnp.zeros_like(sums_ref)
+
     def make(came):
-        grad = own_ref[...].astype(wide)
-        for part in came:
-            grad = grad + part[...].astype(wide)
-        values = values_ref[...].astype(wide)
-        centred = values - jnp.mean(values, axis=-1, keepdims=True)
-        scale = lax.rsqrt(jnp.mean(centred * centred, axis=-1, keepdims=True) + 1e-05)
-        normal = centred * scale
-        gained = grad * gain_ref[...]
-        along = jnp.mean(gained * normal, axis=-1, keepdims=True)
-        made = gained - jnp.mean(gained, axis=-1, keepdims=True) - normal * along
-        made = base_ref[...].astype(wide) + scale * made
-        low = made.astype(low_ref.dtype)
-        low_ref[...] = low
-        wide_ref[...] = made
-        for row, part in enumerate((grad * normal, grad, low.astype(wide))):
-            line = jnp.sum(part, axis=0, keepdims=True)
-            sums_ref[row : row + 1, :] = jnp.where(step == 0, line, sums_ref[row : row + 1, :] + line)
+        @pl.loop(0, own_ref.shape[0] // 16)
+        def _(group):
+            rows = pl.ds(pl.multiple_of(group * 16, 16), 16)
+            grad = own_ref[rows, :].astype(wide)
+            for part in came:
+                grad = grad + part[rows, :].astype(wide)
+            values = values_ref[rows, :].astype(wide)
+            centred = values - jnp.mean(values, axis=-1, keepdims=True)
+            scale = lax.rsqrt(jnp.mean(centred * centred, axis=-1, keepdims=True) + 1e-05)
+            normal = centred * scale
+            gained = grad * gain_ref[...]
+            along = jnp.mean(gained * normal, axis=-1, keepdims=True)
+            made = gained - jnp.mean(gained, axis=-1, keepdims=True) - normal * along
+            made = base_ref[rows, :].astype(wide) + scale * made
+            low = made.astype(low_ref.dtype)
+            low_ref[rows, :] = low
+            wide_ref[rows, :] = made
+            for at, part in enumerate((grad * normal, grad, low.astype(wide))):
+                sums_ref[8 * at : 8 * at + 8, :] += part[:8] + part[8:]
 
     if not came:
         make(())
@@ -349,20 +355,21 @@
     tile = pl.BlockSpec((count, width), lambda i: (i, 0))
     top = pl.BlockSpec((count, width), lambda i: (jnp.minimum(i, half - 1), 0))
     bottom = pl.BlockSpec((count, width), lambda i: (jnp.maximum(i - half, 0), 0))
-    return pl.pallas_call(
+    low, full, sums = pl.pallas_call(
         partial(norm_back_kernel, parts=len(came)),
         grid=(steps,),
         in_specs=[tile, tile, tile, pl.BlockSpec((1, width), lambda i: (0, 0))] + [top, bottom] * (len(came) // 2),
-        out_specs=[tile, tile, pl.BlockSpec((8, width), lambda i: (0, 0))],
+        out_specs=[tile, tile, pl.BlockSpec((24, width), lambda i: (0, 0))],
         out_shape=[
             jax.ShapeDtypeStruct((rows, width), jnp.bfloat16),
             jax.ShapeDtypeStruct((rows, width), jnp.float32),
-            jax.ShapeDtypeStruct((8, width), jnp.float32),
+            jax.ShapeDtypeStruct((24, width), jnp.float32),
         ],
         compiler_params=pltpu.CompilerParams(vmem_limit_bytes=GRANT),
         cost_estimate=estimate(30 * rows * width, rows),
         name="norm_back",
     )(rest, values, base, gain[None], *came)
+    return low, full, jnp.sum(sums.reshape(3, 8, width), axis=1)
 
 
 def outer_kernel(left_ref, *refs, chunk):
@@ -717,11 +724,9 @@
     begun = order(lambda rows: attend_backward(*attention, rows, seq_count, local_len, 0, pairs // 2), mixed_grad)
     if square:
         out_came = order.add_far(out_sum, out_far, None, at=part)
-    down_slabs = slabs_of_rows(gate(down_sum, begun))
     qkv_grad = order(
         lambda rows: attend_backward(*attention, rows, seq_count, local_len, pairs // 2, pairs, begun), mixed_grad
     )
-    order.after(down_slabs)
     if square:
         order.after(*out_came, *result_came)
         out_sum = order(lambda own, *came: summed(own[:part], came).astype(low), out_sum, *out_came)
@@ -739,21 +744,28 @@
         far = swap_far(order.halves(slots(to_normed, 3, 4), qkv_grad))
         near = order(slots(to_normed, 1, 3), qkv_grad)
         direct = swap_direct(near, half)
-        qkv_sum = slab_sum(gate(slab_product(normed, qkv_grad), *far))
+        down_slabs = slabs_of_rows(gate(down_sum, near))
+        qkv_sum = slab_sum(gate(slab_product(normed, qkv_grad), *far, down_slabs))
         came = order.add_far(near, far, direct)
         normed_own = order(slots(to_normed, 0, 1), qkv_grad)
     else:
+        down_slabs = slabs_of_rows(down_sum)
         qkv_sum = slab_sum(slab_product(normed, qkv_grad))
         normed_own, came = scatter(to_normed, qkv_grad), ()
+    if square:
+        result = order(
+            lambda rest, *came: (middle + (summed(rest[:count], came) + down_bias)).astype(low),
+            result_rest,
+            *result_came,
+        )
+    else:
+        result = (middle + (scatter(to_result, active).astype(wide) + down_bias)).astype(low)
+    result = result.reshape(tokens.shape)
+    qkv_column_sum = order(column_sum, qkv_grad)
     grad_tokens, _, input_sums = order(
         lambda own, *came: norm_back(own, x_low, middle_grad, ln1_gain, came), normed_own, *came
     )
     grad_tokens = grad_tokens.reshape(tokens.shape)
-    if square:
-        outcome = summed(result_rest[:count], result_came)
-    else:
-        outcome = scatter(to_result, active).astype(wide)
-    result = (middle + (outcome + down_bias)).astype(low).reshape(tokens.shape)
     up_slabs = slabs_of_rows(gate(up_sum, *came, normed_own))
     qkv_slabs = slabs_of_rows(qkv_sum)
 
@@ -765,19 +777,18 @@
     grad_w_qkv = rows_of(qkv_slabs).reshape(-1, groups, pairs, 3, PAIR)
     grad_w_qkv = jnp.transpose(grad_w_qkv, (0, 3, 1, 2, 4)).reshape(-1, 3 * model_width)
 
-    head_sum = jnp.transpose(column_sum(qkv_grad).reshape(pairs, 3, PAIR), (1, 0, 2)).reshape(3, slab)
+    head_sum = jnp.transpose(qkv_column_sum.reshape(pairs, 3, PAIR), (1, 0, 2)).reshape(3, slab)
     qv_sum = lax.dynamic_update_slice_in_dim(
         jnp.zeros((2, model_width), wide), head_sum[0::2], me * slab, axis=1
     )
     late = [qv_sum.reshape(-1), input_sums[0], input_sums[1]]
-    order.after(up_slabs)
     sums = order(lambda *parts: jnp.concatenate(parts).reshape(-1, PAIR), *early, *late)
     stages = total_stages()
     for axis, masks in stages:
         others = range(lax.axis_size(axis))
         came = [lax.ppermute(sums, axis, [(i, i ^ mask) for i in others]) for mask in masks]
         if (axis, masks) == stages[-1]:
-            order.after(qkv_slabs)
+            order.after(up_slabs, qkv_slabs)
         sums = order(lambda *parts: sum(parts[1:], parts[0]), sums, *came)
     sums = sums.reshape(-1)
 

time: 777 us -> 770 us (level)
  waiting for transfers between devices: 175 us -> 167 us
    all_to_all x3, waiting for transfers between devices: 17.5 us -> 0.64 us  [slabs_of_rows(): lax.all_to_all(values.reshape(groups, -1, values.shape[1]), 'seq', split_...]
    unnamed x77 -> x79, local copies, waits for them, and re-layouts: 43.3 us -> 42.8 us
  transfers between devices with their start and end apart: 64 -> 64, of which waited for: 22 -> 23; matrix products, arithmetic and copies ran while one was open for 31% -> 31% of each run, Pallas kernels for 33% -> 34%
where the time goes in v11:
time: 770 us; the launch traced here: 764 us
  Pallas kernels  261 us (34%)
  waiting for transfers between devices  167 us (22%)
  matrix products  105 us (14%)
  local copies, waits for them, and re-layouts  99.4 us (13%)
  starting transfers between devices  67.9 us (9%)
  other arithmetic  50 us (6%)
  between operations  15.1 us (2%)
    ppermute x44, waiting for transfers between devices, swap(): return lax.ppermute(values, 'seq', [(i, i ^ bit) for i in range(4)])  144 us
    pallas_call x4, Pallas kernels, outer(): pl.pallas_call(partial(outer_kernel, chunk=512 if width % 512 == 0 else 2...  74.5 us
    pallas_call x2, Pallas kernels, attend_backward(): pl.pallas_call(partial(attend_backward_kernel, blocks=blocks, seqs=seqs,...  57.4 us
    dot_general x4, matrix products, contract(): lax.dot_general(left_side, right_side, (((1,), (0,)), ((), ())), preferre...  54.2 us
    dot_general x5, matrix products, contract_last(): lax.dot_general(left_side, right_side, (((1,), (1,)), ((), ())), preferre...  50.6 us
    ppermute x44, starting transfers between devices, swap(): return lax.ppermute(values, 'seq', [(i, i ^ bit) for i in range(4)])  47.2 us
    unnamed x79, local copies, waits for them, and re-layouts  42.8 us
    pallas_call x1, Pallas kernels, up_and_bend(): pl.pallas_call(partial(up_kernel, chunk=512), grid=(count // TILE,), in_s...  30.5 us
  transfers between devices with their start and end apart: 64, of which 23 were waited for; matrix products, arithmetic and copies ran while one was open for 31% of the time, Pallas kernels for 34%

profile of v11, /device:TPU:0, one launch (start us, length us, event | category | flops | bytes accessed | tf_op | source)
XLA Modules:
  0.0 764.5 jit_solution(7438137738479731200)
XLA Ops:
  26.7 19.0 %collective-permute-done.2 = bf16[256,2048]{1,0:T(8,128)(2,1)} collective-permute-done((bf16[256,2048]{1,0:T(8,128)(2,1)}, bf16[256,2048]{1,0:T(8,128)(2,1)}, u32[]{:S(2)}, u32[]{:S(2)}) %collective-permute-start.2) | collective-permute-done | bytes 1048608 | tf_op jit(solution)/shard_map/ppermute | solution.py:412
  52.5 17.7 %collective-permute-done = bf16[256,2048]{1,0:T(8,128)(2,1)} collective-permute-done((bf16[256,2048]{1,0:T(8,128)(2,1)}, bf16[256,2048]{1,0:T(8,128)(2,1)}, u32[]{:S(2)}, u32[]{:S(2)}) %collective-permute-start) | collective-permute-done | bytes 1048608 | tf_op jit(solution)/shard_map/ppermute | solution.py:412
  78.4 12.9 %collective-permute-done.4 = bf16[256,2048]{1,0:T(8,128)(2,1)} collective-permute-done((bf16[256,2048]{1,0:T(8,128)(2,1)}, bf16[256,2048]{1,0:T(8,128)(2,1)}, u32[]{:S(2)}, u32[]{:S(2)}) %collective-permute-start.4) | collective-permute-done | bytes 1048608 | tf_op jit(solution)/shard_map/ppermute | solution.py:412
  99.8 18.6 %add_convert_fusion.qkv_ref = bf16[2048,1536]{1,0:T(8,128)(2,1)} fusion(bf16[2048,2048]{1,0:T(8,128)(2,1)} %constant_dynamic-update-slice_fusion.left_ref, bf16[2048,1536]{1,0:T(8,128)(2,1)} %all-gather.5.cloned.1.call-done, f32[1536]{0:T(1024)S(1)} %reduce.2), kind=kOutput, calls=%fused_computation.1 | convolution fusion | flops 12891193344 | bytes 20977664 | tf_op jit(solution)/shard_map/dot_general | solution.py:30
  118.4 29.7 %attend_forward.1 = (bf16[2048,512]{1,0:T(8,128)(2,1)}, f32[2048,512]{1,0:T(8,128)}) custom-call(s32[1]{0:T(128)} %bitcast.1.at_ref.mask_ref, f32[8]{0:T(128)} %multiply_power_fusion.slope_ref, bf16[2048,1536]{1,0:T(8,128)(2,1)} %add_convert_fusion.qkv_ref), custom_call_target="tpu_custom_call" | custom-call | flops 2684354560 | bytes 2621440 | tf_op jit(solution)/shard_map/attend_forward/pallas_call | solution.py:165
  155.5 11.2 %collective-permute-done.10 = bf16[512,512]{1,0:T(8,128)(2,1)S(1)} collective-permute-done((bf16[512,512]{1,0:T(8,128)(2,1)}, bf16[512,512]{1,0:T(8,128)(2,1)S(1)}, u32[]{:S(2)}, u32[]{:S(2)}) %collective-permute-start.10) | collective-permute-done | bytes 524320 | tf_op jit(solution)/shard_map/ppermute | solution.py:412
  222.3 16.9 %collective-permute-done.14 = bf16[256,2048]{1,0:T(8,128)(2,1)} collective-permute-done((bf16[256,2048]{1,0:T(8,128)(2,1)}, bf16[256,2048]{1,0:T(8,128)(2,1)}, u32[]{:S(2)}, u32[]{:S(2)}) %collective-permute-start.14) | collective-permute-done | bytes 1048608 | tf_op jit(solution)/shard_map/ppermute | solution.py:412
  249.8 11.0 %collective-permute-done.17 = bf16[256,2048]{1,0:T(8,128)(2,1)S(1)} collective-permute-done((bf16[256,2048]{1,0:T(8,128)(2,1)}, bf16[256,2048]{1,0:T(8,128)(2,1)S(1)}, u32[]{:S(2)}, u32[]{:S(2)}) %collective-permute-start.17) | collective-permute-done | bytes 1048608 | tf_op jit(solution)/shard_map/ppermute | solution.py:412
  271.1 30.5 %up_and_bend.1 = (bf16[2048,2048]{1,0:T(8,128)(2,1)}, f32[2048,2048]{1,0:T(8,128)}) custom-call(bf16[2048,2048]{1,0:T(8,128)(2,1)} %constant_dynamic-update-slice_fusion.7.rows_ref.left_ref, bf16[2048,2048]{1,0:T(8,128)(2,1)} %all-gather.9.cloned.1.call-done.weight_ref, f32[1,2048]{1,0:T(1,128)} %bitcast.134), custom_call_target="tpu_custom_call" | custom-call | flops 8589934592 | bytes 8388608 | tf_op jit(solution)/shard_map/up_and_bend/pallas_call | solution.py:246
  303.7 23.7 %outer.4 = bf16[8,4,64,2048]{3,2,1,0:T(8,128)(2,1)} custom-call(bf16[2048,2048]{1,0:T(8,128)(2,1)} %constant_dynamic-update-slice_fusion.35.left_ref.rows_ref, bf16[2048,2048]{1,0:T(8,128)(2,1)} %get-tuple-element.178.refs_0_), custom_call_target="tpu_custom_call" | custom-call | flops 4294967296 | bytes 4194304 | tf_op jit(solution)/shard_map/outer/pallas_call | solution.py:394
  327.5 25.6 %hidden_gradient.1 = (bf16[2048,2048]{1,0:T(8,128)(2,1)}, f32[1,2048]{1,0:T(1,128)}) custom-call(bf16[2048,2048]{1,0:T(8,128)(2,1)} %constant_dynamic-update-slice_fusion.35.left_ref.rows_ref, bf16[2048,2048]{1,0:T(8,128)(2,1)} %all-gather.11.cloned.1.call-done.weight_ref, f32[2048,2048]{1,0:T(8,128)} %get-tuple-element.153.slope_ref), custom_call_target="tpu_custom_call" | custom-call | flops 6442450944 | bytes 6291456 | tf_op jit(solution)/shard_map/hidden_gradient/pallas_call | solution.py:270
  365.5 16.3 %convolution_convert_fusion.1.own_ref = bf16[1536,2048]{1,0:T(8,128)(2,1)S(1)} fusion(bf16[2048,2048]{1,0:T(8,128)(2,1)} %all-gather.9.cloned.1.call-done.weight_ref, bf16[2048,2048]{1,0:T(8,128)(2,1)S(1)} %copy-done.7), kind=kOutput, calls=%fused_computation.3 | convolution fusion | flops 12888047616 | bytes 20971520 | tf_op jit(solution)/shard_map/dot_general | solution.py:36
  404.1 23.5 %outer.5 = bf16[8,4,64,2048]{3,2,1,0:T(8,128)(2,1)} custom-call(bf16[2048,2048]{1,0:T(8,128)(2,1)} %constant_dynamic-update-slice_fusion.7.rows_ref.left_ref, bf16[2048,2048]{1,0:T(8,128)(2,1)} %get-tuple-element.163.refs_0_), custom_call_target="tpu_custom_call" | custom-call | flops 4294967296 | bytes 4194304 | tf_op jit(solution)/shard_map/outer/pallas_call | solution.py:394
  435.3 14.5 %norm_back.2 = (bf16[512,2048]{1,0:T(8,128)(2,1)}, f32[512,2048]{1,0:T(8,128)}, f32[24,2048]{1,0:T(8,128)}) custom-call(bf16[1536,2048]{1,0:T(8,128)(2,1)} %copy-done.5, f32[512,2048]{1,0:T(8,128)} %copy-done, bf16[512,2048]{1,0:T(8,128)(2,1)} %bitcast.96, f32[1,2048]{1,0:T(1,128)} %bitcast.121, bf16[256,2048]{1,0:T(8,128)(2,1)} %collective-permute-done.22.refs_0_, ...), custom_call_target="tpu_custom_call" | custom-call | flops 7864320 | bytes 7680 | tf_op jit(solution)/shard_map/norm_back/pallas_call | solution.py:358
  450.9 8.9 %mixed_gradient.1 = bf16[512,2048]{1,0:T(8,128)(2,1)} custom-call(bf16[512,2048]{1,0:T(8,128)(2,1)} %get-tuple-element.177.rows_ref, bf16[2048,2048]{1,0:T(8,128)(2,1)} %all-gather.7.cloned.1.call-done.weight_ref), custom_call_target="tpu_custom_call" | custom-call | flops 1073741824 | bytes 1048576 | tf_op jit(solution)/shard_map/mixed_gradient/pallas_call | solution.py:296
  465.8 19.1 %convolution_convert_fusion = bf16[1536,2048]{1,0:T(8,128)(2,1)} fusion(bf16[2048,2048]{1,0:T(8,128)(2,1)} %all-gather.11.cloned.1.call-done.weight_ref, bf16[2048,2048]{1,0:T(8,128)(2,1)} %get-tuple-element.178.refs_0_), kind=kOutput, calls=%fused_computation.2 | convolution fusion | flops 12888047616 | bytes 20971520 | tf_op jit(solution)/shard_map/dot_general | solution.py:30
  516.5 29.2 %attend_backward.2.rest_0_ = bf16[2048,1536]{1,0:T(8,128)(2,1)} custom-call(s32[1]{0:T(128)} %bitcast.1.at_ref.mask_ref, f32[8]{0:T(128)} %multiply_power_fusion.slope_ref, bf16[2048,1536]{1,0:T(8,128)(2,1)} %add_convert_fusion.qkv_ref, f32[2048,512]{1,0:T(8,128)} %get-tuple-element.133.lse_ref, bf16[2048,512]{1,0:T(8,128)(2,1)} %get-tuple-element.132.mixed_ref, ...), custom_call_target="tpu_custom_call" | custom-call | flops 3355443200 | bytes 3276800 | tf_op jit(solution)/shard_map/attend_backward/pallas_call | solution.py:190
  548.8 28.2 %attend_backward.3.refs_0_ = bf16[2048,1536]{1,0:T(8,128)(2,1)} custom-call(s32[1]{0:T(128)} %bitcast.1.at_ref.mask_ref, f32[8]{0:T(128)} %multiply_power_fusion.slope_ref, bf16[2048,1536]{1,0:T(8,128)(2,1)} %add_convert_fusion.qkv_ref, f32[2048,512]{1,0:T(8,128)} %get-tuple-element.133.lse_ref, ...), custom_call_target="tpu_custom_call", output_to_operand_aliasing={{}: (6, {})} | custom-call | flops 3355443200 | bytes 3276800 | tf_op jit(solution)/shard_map/attend_backward/pallas_call | solution.py:190
  577.0 10.2 %collective-permute-done.39 = bf16[256,2048]{1,0:T(8,128)(2,1)S(1)} collective-permute-done((bf16[256,2048]{1,0:T(8,128)(2,1)S(1)}, bf16[256,2048]{1,0:T(8,128)(2,1)S(1)}, u32[]{:S(2)}, u32[]{:S(2)}) %collective-permute-start.39) | collective-permute-done | bytes 1048608 | tf_op jit(solution)/shard_map/ppermute | solution.py:412
  600.6 11.0 %convolution_convert_fusion.2 = bf16[1024,2048]{1,0:T(8,128)(2,1)} fusion(bf16[2048,1536]{1,0:T(8,128)(2,1)} %all-gather.5.cloned.1.call-done, bf16[2048,1536]{1,0:T(8,128)(2,1)S(1)} %bitcast.88), kind=kOutput, calls=%fused_computation.21 | convolution fusion | flops 6444548096 | bytes 13631488 | tf_op jit(solution)/shard_map/dot_general | solution.py:36
  615.2 18.6 %outer.7 = bf16[8,4,64,1536]{3,2,1,0:T(8,128)(2,1)} custom-call(bf16[2048,2048]{1,0:T(8,128)(2,1)} %constant_dynamic-update-slice_fusion.left_ref, bf16[2048,1536]{1,0:T(8,128)(2,1)} %attend_backward.3.refs_0_), custom_call_target="tpu_custom_call" | custom-call | flops 3221225472 | bytes 3145728 | tf_op jit(solution)/shard_map/outer/pallas_call | solution.py:394
  669.6 17.6 %collective-permute-done.43.refs_1_ = bf16[256,2048]{1,0:T(8,128)(2,1)} collective-permute-done((bf16[256,2048]{1,0:T(8,128)(2,1)}, bf16[256,2048]{1,0:T(8,128)(2,1)}, u32[]{:S(2)}, u32[]{:S(2)}) %collective-permute-start.43) | collective-permute-done | bytes 1048608 | tf_op jit(solution)/shard_map/ppermute | solution.py:412
  692.1 14.3 %norm_back.3 = (bf16[512,2048]{1,0:T(8,128)(2,1)}, f32[512,2048]{1,0:T(8,128)}, f32[24,2048]{1,0:T(8,128)}) custom-call(bf16[512,2048]{1,0:T(8,128)(2,1)} %convolution_convert_fusion.3.own_ref, bf16[512,2048]{1,0:T(8,128)(2,1)} %bitcast.93, f32[512,2048]{1,0:T(8,128)} %get-tuple-element.175.base_ref, f32[1,2048]{1,0:T(1,128)} %bitcast.129, ...), custom_call_target="tpu_custom_call" | custom-call | flops 7864320 | bytes 7680 | tf_op jit(solution)/shard_map/norm_back/pallas_call | solution.py:358
  734.3 10.8 %reduce-scatter.11.cloned.1.call-done = bf16[64,2048]{1,0:T(8,128)(2,1)} async-done(((bf16[512,2048]{1,0:T(8,128)(2,1)}), bf16[64,2048]{1,0:T(8,128)(2,1)}) %reduce-scatter.11.cloned.1.call-update) | async-done | bytes 262160 | tf_op jit(solution)/shard_map/reduce_scatter | solution.py:741
  (303 shorter events, 310.3 us)
Async XLA Ops:
  7.2 92.6 %all-gather.5.cloned.1.call-start = ((), (), s32[]{:S(2)}) async-start(), calls=%async_computation.7 | async-start | bytes 7077888 | tf_op jit(solution)/shard_map/all_gather | solution.py:604
  10.3 168.8 %all-gather.7.cloned.1.call-start = ((), (), s32[]{:S(2)}) async-start(), calls=%async_computation.8 | async-start | bytes 9437184 | tf_op jit(solution)/shard_map/all_gather | solution.py:616
  11.1 260.0 %all-gather.9.cloned.1.call-start = ((), (), s32[]{:S(2)}) async-start(), calls=%async_computation.9 | async-start | bytes 9437184 | tf_op jit(solution)/shard_map/all_gather | solution.py:617
  18.3 309.2 %all-gather.11.cloned.1.call-start = ((), (), s32[]{:S(2)}) async-start(), calls=%async_computation.10 | async-start | bytes 9437184 | tf_op jit(solution)/shard_map/all_gather | solution.py:618
  22.9 47.4 %collective-permute-start = (bf16[256,2048]{1,0:T(8,128)(2,1)}, bf16[256,2048]{1,0:T(8,128)(2,1)}, u32[]{:S(2)}, u32[]{:S(2)}) collective-permute-start(bf16[256,2048]{1,0:T(8,128)(2,1)} %get-tuple-element.287), channel_id=1, source_target_pairs={{0,8},{8,0},{16,24},{24,16},{1,9},{9,1},{17,25},{25,17},{2,10},{10... | collective-permute-start | bytes 3145736 | tf_op jit(solution)/shard_map/ppermute | solution.py:412
  23.4 52.7 %collective-permute-start.3 = (bf16[256,2048]{1,0:T(8,128)(2,1)}, bf16[256,2048]{1,0:T(8,128)(2,1)}, u32[]{:S(2)}, u32[]{:S(2)}) collective-permute-start(bf16[256,2048]{1,0:T(8,128)(2,1)} %get-tuple-element.286), channel_id=1, source_target_pairs={{0,16},{8,24},{16,0},{24,8},{1,17},{9,25},{17,1},{25,9},{2,18},{10... | collective-permute-start | bytes 3145736 | tf_op jit(solution)/shard_map/ppermute | solution.py:412
  25.8 490.7 %reduce-scatter.5.cloned.1.call-start = ((), (), s32[]{:S(2)}) async-start(), calls=%async_computation.11 | async-start | bytes 9437184 | tf_op jit(solution)/shard_map/reduce_scatter | solution.py:658
  45.7 45.6 %collective-permute-start.4 = (bf16[256,2048]{1,0:T(8,128)(2,1)}, bf16[256,2048]{1,0:T(8,128)(2,1)}, u32[]{:S(2)}, u32[]{:S(2)}) collective-permute-start(bf16[256,2048]{1,0:T(8,128)(2,1)} %collective-permute-done.2), channel_id=1, source_target_pairs={{0,8},{8,0},{16,24},{24,16},{1,9},{9,1},{17,25},{25,17},{2,10},{10... | collective-permute-start | bytes 3145736 | tf_op jit(solution)/shard_map/ppermute | solution.py:412
  50.9 42.7 %collective-permute-start.5 = (bf16[256,2048]{1,0:T(8,128)(2,1)S(1)}, bf16[256,2048]{1,0:T(8,128)(2,1)S(1)}, u32[]{:S(2)}, u32[]{:S(2)}) collective-permute-start(bf16[256,2048]{1,0:T(8,128)(2,1)S(1)} %collective-permute-done.1), channel_id=1, source_target_pairs={{0,16},{8,24},{16,0},{24,8},{1,17},{9,25},{17,1},{25,9},{2,18},{10... | collective-permute-start | bytes 3145736 | tf_op jit(solution)/shard_map/ppermute | solution.py:412
  95.8 52.3 %collective-permute-start.7 = (bf16[256,2048]{1,0:T(8,128)(2,1)}, bf16[256,2048]{1,0:T(8,128)(2,1)}, u32[]{:S(2)}, u32[]{:S(2)}) collective-permute-start(bf16[256,2048]{1,0:T(8,128)(2,1)} %get-tuple-element.137), channel_id=1, source_target_pairs={{0,16},{8,24},{16,0},{24,8},{1,17},{9,25},{17,1},{25,9},{2,18},{10... | collective-permute-start | bytes 3145736 | tf_op jit(solution)/shard_map/ppermute | solution.py:412
  96.1 52.0 %collective-permute-start.8 = (bf16[256,2048]{1,0:T(8,128)(2,1)}, bf16[256,2048]{1,0:T(8,128)(2,1)}, u32[]{:S(2)}, u32[]{:S(2)}) collective-permute-start(bf16[256,2048]{1,0:T(8,128)(2,1)} %get-tuple-element.137), channel_id=1, source_target_pairs={{0,8},{8,0},{16,24},{24,16},{1,9},{9,1},{17,25},{25,17},{2,10},{10... | collective-permute-start | bytes 3145736 | tf_op jit(solution)/shard_map/ppermute | solution.py:412
  97.8 50.3 %collective-permute-start.6 = (bf16[256,2048]{1,0:T(8,128)(2,1)S(1)}, bf16[256,2048]{1,0:T(8,128)(2,1)}, u32[]{:S(2)}, u32[]{:S(2)}) collective-permute-start(bf16[256,2048]{1,0:T(8,128)(2,1)S(1)} %get-tuple-element.138), channel_id=1, source_target_pairs={{0,8},{8,0},{16,24},{24,16},{1,9},{9,1},{17,25},{25,17},{2,10},{10... | collective-permute-start | bytes 3145736 | tf_op jit(solution)/shard_map/ppermute | solution.py:412
  98.2 50.0 %collective-permute-start.9 = (bf16[256,2048]{1,0:T(8,128)(2,1)S(1)}, bf16[256,2048]{1,0:T(8,128)(2,1)}, u32[]{:S(2)}, u32[]{:S(2)}) collective-permute-start(bf16[256,2048]{1,0:T(8,128)(2,1)S(1)} %get-tuple-element.138), channel_id=1, source_target_pairs={{0,16},{8,24},{16,0},{24,8},{1,17},{9,25},{17,1},{25,9},{2,18},{10... | collective-permute-start | bytes 3145736 | tf_op jit(solution)/shard_map/ppermute | solution.py:412
  190.5 49.5 %collective-permute-start.13 = (bf16[256,2048]{1,0:T(8,128)(2,1)}, bf16[256,2048]{1,0:T(8,128)(2,1)}, u32[]{:S(2)}, u32[]{:S(2)}) collective-permute-start(bf16[256,2048]{1,0:T(8,128)(2,1)} %get-tuple-element.280), channel_id=1, source_target_pairs={{0,8},{8,0},{16,24},{24,16},{1,9},{9,1},{17,25},{25,17},{2,10},{10... | collective-permute-start | bytes 3145736 | tf_op jit(solution)/shard_map/ppermute | solution.py:412
  192.6 46.6 %collective-permute-start.14 = (bf16[256,2048]{1,0:T(8,128)(2,1)}, bf16[256,2048]{1,0:T(8,128)(2,1)}, u32[]{:S(2)}, u32[]{:S(2)}) collective-permute-start(bf16[256,2048]{1,0:T(8,128)(2,1)} %get-tuple-element.279), channel_id=1, source_target_pairs={{0,8},{8,0},{16,24},{24,16},{1,9},{9,1},{17,25},{25,17},{2,10},{10... | collective-permute-start | bytes 3145736 | tf_op jit(solution)/shard_map/ppermute | solution.py:412
  193.2 54.3 %collective-permute-start.16 = (bf16[256,2048]{1,0:T(8,128)(2,1)}, bf16[256,2048]{1,0:T(8,128)(2,1)}, u32[]{:S(2)}, u32[]{:S(2)}) collective-permute-start(bf16[256,2048]{1,0:T(8,128)(2,1)} %get-tuple-element.279), channel_id=1, source_target_pairs={{0,16},{8,24},{16,0},{24,8},{1,17},{9,25},{17,1},{25,9},{2,18},{10... | collective-permute-start | bytes 3145736 | tf_op jit(solution)/shard_map/ppermute | solution.py:412
  327.4 263.5 %reduce-scatter.7.cloned.1.call-start = ((), (), s32[]{:S(2)}) async-start(), calls=%async_computation.12 | async-start | bytes 9437184 | tf_op jit(solution)/shard_map/reduce_scatter | solution.py:658
  382.1 45.5 %collective-permute-start.22 = (bf16[256,2048]{1,0:T(8,128)(2,1)S(1)}, bf16[256,2048]{1,0:T(8,128)(2,1)}, u32[]{:S(2)}, u32[]{:S(2)}) collective-permute-start(bf16[256,2048]{1,0:T(8,128)(2,1)S(1)} %get-tuple-element.249), channel_id=1, source_target_pairs={{0,8},{8,0},{16,24},{24,16},{1,9},{9,1},{17,25},{25,17},{2,10},{10... | collective-permute-start | bytes 3145736 | tf_op jit(solution)/shard_map/ppermute | solution.py:412
  382.3 45.3 %collective-permute-start.27 = (bf16[256,2048]{1,0:T(8,128)(2,1)S(1)}, bf16[256,2048]{1,0:T(8,128)(2,1)}, u32[]{:S(2)}, u32[]{:S(2)}) collective-permute-start(bf16[256,2048]{1,0:T(8,128)(2,1)S(1)} %get-tuple-element.248), channel_id=1, source_target_pairs={{0,16},{8,24},{16,0},{24,8},{1,17},{9,25},{17,1},{25,9},{2,18},{10... | collective-permute-start | bytes 3145736 | tf_op jit(solution)/shard_map/ppermute | solution.py:412
  514.7 62.3 %collective-permute-start.34 = (bf16[512,2048]{1,0:T(8,128)(2,1)}, bf16[512,2048]{1,0:T(8,128)(2,1)}, u32[]{:S(2)}, u32[]{:S(2)}) collective-permute-start(bf16[512,2048]{1,0:T(8,128)(2,1)} %pad_maximum_fusion.4), channel_id=1, source_target_pairs={{0,8},{8,0},{16,24},{24,16},{1,9},{9,1},{17,25},{25,17},{2,10},{10... | collective-permute-start | bytes 6291464 | tf_op jit(solution)/shard_map/ppermute | solution.py:412
  515.2 61.9 %collective-permute-start.35 = (bf16[512,2048]{1,0:T(8,128)(2,1)}, bf16[512,2048]{1,0:T(8,128)(2,1)}, u32[]{:S(2)}, u32[]{:S(2)}) collective-permute-start(bf16[512,2048]{1,0:T(8,128)(2,1)} %pad_maximum_fusion.5), channel_id=1, source_target_pairs={{0,16},{8,24},{16,0},{24,8},{1,17},{9,25},{17,1},{25,9},{2,18},{10... | collective-permute-start | bytes 6291464 | tf_op jit(solution)/shard_map/ppermute | solution.py:412
  546.3 40.9 %collective-permute-start.39 = (bf16[256,2048]{1,0:T(8,128)(2,1)S(1)}, bf16[256,2048]{1,0:T(8,128)(2,1)S(1)}, u32[]{:S(2)}, u32[]{:S(2)}) collective-permute-start(bf16[256,2048]{1,0:T(8,128)(2,1)S(1)} %pad_maximum_fusion.8), channel_id=1, source_target_pairs={{0,16},{8,24},{16,0},{24,8},{1,17},{9,25},{17,1},{25,9},{2,18},{10... | collective-permute-start | bytes 3145736 | tf_op jit(solution)/shard_map/ppermute | solution.py:412
  615.2 108.8 %reduce-scatter.9.cloned.1.call-start = ((), (), s32[]{:S(2)}) async-start(), calls=%async_computation.13 | async-start | bytes 7077888 | tf_op jit(solution)/shard_map/reduce_scatter | solution.py:658
  634.5 110.6 %reduce-scatter.11.cloned.1.call-start = ((), (), s32[]{:S(2)}) async-start(), calls=%async_computation.14 | async-start | bytes 2359296 | tf_op jit(solution)/shard_map/reduce_scatter | solution.py:741
  (64 other events, 1366.6 us)
Sparse Core Ops, SparseCore 0:
  10.4 67.4 all-gather.4
  79.5 80.6 all-gather.6
  161.9 80.5 all-gather.8
  243.9 81.0 all-gather.10
  327.5 89.8 reduce-scatter.4
  433.3 88.7 reduce-scatter.6
  634.6 70.5 reduce-scatter.8
  707.5 37.4 reduce-scatter.10

commit v12 on v11

--- a/solution.py
+++ b/solution.py
@@ -23,7 +23,8 @@
     average = jnp.mean(token_rows, axis=-1, keepdims=True)
     centred = token_rows - average
     spread = jnp.mean(centred * centred, axis=-1, keepdims=True)
-    return centred * lax.rsqrt(spread + 1e-05) * gain_vec + shift_vec
+    scale = lax.rsqrt(spread + 1e-05)
+    return centred * scale * gain_vec + shift_vec, average, scale
 
 
 def contract(left_side, right_side):
@@ -108,9 +109,9 @@
 
 
 def attend_backward_kernel(
-    mask_ref, slope_ref, qkv_ref, lse_ref, mixed_ref, grad_ref, *rest, blocks, seqs, local, start
+    mask_ref, slope_ref, qkv_ref, lse_ref, mixed_ref, *rest, blocks, seqs, local, start, grads
 ):
-    out_ref, dq_ref, dk_ref, dv_ref = rest[-4:]
+    out_ref, dq_ref, dk_ref, dv_ref, grad_ref = rest[-5:]
     pair, sequence = pl.program_id(0) + start, pl.program_id(1)
     mask = mask_ref[0]
     lane = lax.broadcasted_iota(jnp.int32, (BLOCK, PAIR), 1)
@@ -119,6 +120,13 @@
     gap = (query - key).astype(jnp.float32)
     pieces = [row_pieces(mask, sequence, block, seqs, local) for block in range(blocks)]
     everything = slice(0, PAIR)
+
+    @pl.when(sequence == 0)
+    def _():
+        at = 0
+        for part in rest[:grads]:
+            grad_ref[at : at + part.shape[0], :] = part[...]
+            at += part.shape[0]
 
     for i in range(blocks):
         q_pair = load_rows(qkv_ref, pieces[i], Q_COLUMNS)
@@ -180,7 +188,7 @@
     )(mask, slopes, qkv)
 
 
-def attend_backward(mask, slopes, qkv, lse, mixed, grad, seqs, local, start, stop, begun=None):
+def attend_backward(mask, slopes, qkv, lse, mixed, grads, seqs, local, start, stop, begun=None):
     rows, width = qkv.shape
     blocks = rows // seqs // BLOCK
     scored = (stop - start) * seqs * blocks * (blocks + 1) * BLOCK * BLOCK
@@ -188,20 +196,25 @@
     wide = pl.BlockSpec((rows, 3 * PAIR), lambda p, *_: (0, p + start))
     earlier = [] if begun is None else [begun]
     return pl.pallas_call(
-        partial(attend_backward_kernel, blocks=blocks, seqs=seqs, local=local, start=start),
+        partial(
+            attend_backward_kernel, blocks=blocks, seqs=seqs, local=local, start=start, grads=len(grads)
+        ),
         grid_spec=pltpu.PrefetchScalarGridSpec(
             num_scalar_prefetch=2,
             grid=(stop - start, seqs),
-            in_specs=[wide, narrow, narrow, narrow] + [pl.BlockSpec(memory_space=pl.ANY)] * len(earlier),
+            in_specs=[wide, narrow, narrow]
+            + [pl.BlockSpec((grad.shape[0], PAIR), lambda p, *_: (0, p + start)) for grad in grads]
+            + [pl.BlockSpec(memory_space=pl.ANY)] * len(earlier),
             out_specs=wide,
-            scratch_shapes=[pltpu.VMEM((blocks, BLOCK, PAIR), jnp.float32)] * 3,
+            scratch_shapes=[pltpu.VMEM((blocks, BLOCK, PAIR), jnp.float32)] * 3
+            + [pltpu.VMEM((rows, PAIR), jnp.bfloat16)],
         ),
         out_shape=jax.ShapeDtypeStruct((rows, width), jnp.bfloat16),
-        input_output_aliases={6: 0} if earlier else {},
+        input_output_aliases={5 + len(grads): 0} if earlier else {},
         compiler_params=pltpu.CompilerParams(vmem_limit_bytes=GRANT),
         cost_estimate=estimate(scored * 2 * 1280, scored),
         name="attend_backward",
-    )(mask, slopes, qkv, lse, mixed, grad, *earlier)
+    )(mask, slopes, qkv, lse, mixed, *grads, *earlier)
 
 
 def head_columns_kernel(at_ref, in_ref, out_ref):
@@ -308,7 +321,7 @@
     )(rows, weight)
 
 
-def norm_back_kernel(own_ref, values_ref, base_ref, gain_ref, *refs, parts):
+def norm_back_kernel(own_ref, values_ref, average_ref, scale_ref, base_ref, gain_ref, *refs, parts):
     came, (low_ref, wide_ref, sums_ref) = refs[:parts], refs[parts:]
     wide = jnp.float32
     step = pl.program_id(0)
@@ -318,25 +331,20 @@
         sums_ref[...] = jnp.zeros_like(sums_ref)
 
     def make(came):
-        @pl.loop(0, own_ref.shape[0] // 16)
-        def _(group):
-            rows = pl.ds(pl.multiple_of(group * 16, 16), 16)
-            grad = own_ref[rows, :].astype(wide)
-            for part in came:
-                grad = grad + part[rows, :].astype(wide)
-            values = values_ref[rows, :].astype(wide)
-            centred = values - jnp.mean(values, axis=-1, keepdims=True)
-            scale = lax.rsqrt(jnp.mean(centred * centred, axis=-1, keepdims=True) + 1e-05)
-            normal = centred * scale
-            gained = grad * gain_ref[...]
-            along = jnp.mean(gained * normal, axis=-1, keepdims=True)
-            made = gained - jnp.mean(gained, axis=-1, keepdims=True) - normal * along
-            made = base_ref[rows, :].astype(wide) + scale * made
-            low = made.astype(low_ref.dtype)
-            low_ref[rows, :] = low
-            wide_ref[rows, :] = made
-            for at, part in enumerate((grad * normal, grad, low.astype(wide))):
-                sums_ref[8 * at : 8 * at + 8, :] += part[:8] + part[8:]
+        grad = own_ref[...].astype(wide)
+        for part in came:
+            grad = grad + part[...].astype(wide)
+        scale = scale_ref[...]
+        normal = (values_ref[...].astype(wide) - average_ref[...]) * scale
+        gained = grad * gain_ref[...]
+        along = jnp.mean(gained * normal, axis=-1, keepdims=True)
+        across = jnp.mean(gained, axis=-1, keepdims=True)
+        made = base_ref[...].astype(wide) + scale * (gained - across - normal * along)
+        low = made.astype(low_ref.dtype)
+        low_ref[...] = low
+        wide_ref[...] = made
+        for at, part in enumerate((grad * normal, grad, low.astype(wide))):
+            sums_ref[8 * at : 8 * at + 8, :] += jnp.sum(part.reshape(-1, 8, part.shape[1]), axis=0)
 
     if not came:
         make(())
@@ -346,19 +354,21 @@
     pl.when(jnp.logical_not(upper))(lambda: make(came[1::2]))
 
 
-def norm_back(rest, values, base, gain, came):
+def norm_back(rest, values, average, scale, base, gain, came):
     rows, width = values.shape
     steps = 8
     half = steps // 2
     came = list(came or ())
     count = rows // steps
     tile = pl.BlockSpec((count, width), lambda i: (i, 0))
+    thin = pl.BlockSpec((count, 1), lambda i: (i, 0))
     top = pl.BlockSpec((count, width), lambda i: (jnp.minimum(i, half - 1), 0))
     bottom = pl.BlockSpec((count, width), lambda i: (jnp.maximum(i - half, 0), 0))
     low, full, sums = pl.pallas_call(
         partial(norm_back_kernel, parts=len(came)),
         grid=(steps,),
-        in_specs=[tile, tile, tile, pl.BlockSpec((1, width), lambda i: (0, 0))] + [top, bottom] * (len(came) // 2),
+        in_specs=[tile, tile, thin, thin, tile, pl.BlockSpec((1, width), lambda i: (0, 0))]
+        + [top, bottom] * (len(came) // 2),
         out_specs=[tile, tile, pl.BlockSpec((24, width), lambda i: (0, 0))],
         out_shape=[
             jax.ShapeDtypeStruct((rows, width), jnp.bfloat16),
@@ -368,7 +378,7 @@
         compiler_params=pltpu.CompilerParams(vmem_limit_bytes=GRANT),
         cost_estimate=estimate(30 * rows * width, rows),
         name="norm_back",
-    )(rest, values, base, gain[None], *came)
+    )(rest, values, average, scale, base, gain[None], *came)
     return low, full, jnp.sum(sums.reshape(3, 8, width), axis=1)
 
 
@@ -605,7 +615,7 @@
     qkv_bias = head_columns(jnp.concatenate([qv_bias[0], jnp.zeros_like(qv_bias[0]), qv_bias[1]])[None])
     up_bias_slab = own_slab(up_bias, 0)
 
-    first_norm = layer_norm(x, ln1_gain, ln1_shift)
+    first_norm, *first_stats = layer_norm(x, ln1_gain, ln1_shift)
     half = rows_here // 2
 
     def halves_of(values):
@@ -640,7 +650,7 @@
         )
 
     middle = order(lambda rows: x + (contract(rows, full_out) + out_bias), mixed_rows)
-    second_norm = layer_norm(middle, ln2_gain, ln2_shift)
+    second_norm, *second_stats = layer_norm(middle, ln2_gain, ln2_shift)
     second = order.gather(order(halves_of, second_norm))
     mine, theirs = order(pair_halves, mixed_slots)
     upstream_made = order.fill(upstream)
@@ -694,7 +704,7 @@
         second_own, came = scatter(to_second, hidden_grad), ()
         up_sum = slab_sum(slab_product(second, hidden_grad))
     branch_grad, middle_grad, middle_sums = order(
-        lambda own, *came: norm_back(own, middle, dz_low, ln2_gain, came), second_own, *came
+        lambda own, *came: norm_back(own, middle, *second_stats, dz_low, ln2_gain, came), second_own, *came
     )
 
     def column_sum(values):
@@ -713,19 +723,21 @@
     branch_other = pair_swap(branch_grad)
     branch_pair = jnp.concatenate([branch_grad, branch_other], axis=0)
     out_sum = order(lambda columns: outer(columns, branch_pair, groups, 1), mixed_half)
-    mixed_grad = order(lambda *parts: jnp.concatenate(parts, axis=0), *mixed_grad)
     attention = (mask, slopes, qkv, log_totals, attended)
     if square:
         part = out_sum.shape[0] // 4
         out_far = out_sum[3 * part : 3 * part + part // 2], out_sum[3 * part + part // 2 :]
-        out_far = swap_far(gate(out_far, mixed_grad))
-        result_came = order.add_far(result_rest, result_far, None, mixed_grad)
+        out_far = swap_far(gate(out_far, *mixed_grad))
+        result_came = order.add_far(result_rest, result_far, None, *mixed_grad)
     order.after(down_sum)
-    begun = order(lambda rows: attend_backward(*attention, rows, seq_count, local_len, 0, pairs // 2), mixed_grad)
+    begun = order(
+        lambda *grads: attend_backward(*attention, grads, seq_count, local_len, 0, pairs // 2), *mixed_grad
+    )
     if square:
         out_came = order.add_far(out_sum, out_far, None, at=part)
     qkv_grad = order(
-        lambda rows: attend_backward(*attention, rows, seq_count, local_len, pairs // 2, pairs, begun), mixed_grad
+        lambda *grads: attend_backward(*attention, grads, seq_count, local_len, pairs // 2, pairs, begun),
+        *mixed_grad,
     )
     if square:
         order.after(*out_came, *result_came)
@@ -742,10 +754,11 @@
     order.after(up_sum)
     if square:
         far = swap_far(order.halves(slots(to_normed, 3, 4), qkv_grad))
+        qkv_sum = slab_sum(gate(slab_product(normed, qkv_grad), *far, grad_w_out))
         near = order(slots(to_normed, 1, 3), qkv_grad)
         direct = swap_direct(near, half)
-        down_slabs = slabs_of_rows(gate(down_sum, near))
-        qkv_sum = slab_sum(gate(slab_product(normed, qkv_grad), *far, down_slabs))
+        down_slabs = slabs_of_rows(gate(down_sum, *far))
+        order.after(down_slabs)
         came = order.add_far(near, far, direct)
         normed_own = order(slots(to_normed, 0, 1), qkv_grad)
     else:
@@ -763,7 +776,7 @@
     result = result.reshape(tokens.shape)
     qkv_column_sum = order(column_sum, qkv_grad)
     grad_tokens, _, input_sums = order(
-        lambda own, *came: norm_back(own, x_low, middle_grad, ln1_gain, came), normed_own, *came
+        lambda own, *came: norm_back(own, x_low, *first_stats, middle_grad, ln1_gain, came), normed_own, *came
     )
     grad_tokens = grad_tokens.reshape(tokens.shape)
     up_slabs = slabs_of_rows(gate(up_sum, *came, normed_own))

time: 770 us -> 765 us (level)
    unnamed x79 -> x92, local copies, waits for them, and re-layouts: 42.8 us -> 42.8 us
  transfers between devices with their start and end apart: 64 -> 64, of which waited for: 23 -> 23; matrix products, arithmetic and copies ran while one was open for 31% -> 31% of each run, Pallas kernels for 34% -> 33%
where the time goes in v12:
time: 765 us; the launch traced here: 760 us
  Pallas kernels  254 us (33%)
  waiting for transfers between devices  174 us (23%)
  matrix products  104 us (14%)
  local copies, waits for them, and re-layouts  97.1 us (13%)
  starting transfers between devices  68 us (9%)
  other arithmetic  48.1 us (6%)
  between operations  15.1 us (2%)
    ppermute x44, waiting for transfers between devices, swap(): return lax.ppermute(values, 'seq', [(i, i ^ bit) for i in range(4)])  149 us
    pallas_call x4, Pallas kernels, outer(): pl.pallas_call(partial(outer_kernel, chunk=512 if width % 512 == 0 else 2...  74.3 us
    pallas_call x2, Pallas kernels, attend_backward(): pl.pallas_call(partial(attend_backward_kernel, blocks=blocks, seqs=seqs,...  57.6 us
    dot_general x4, matrix products, contract(): lax.dot_general(left_side, right_side, (((1,), (0,)), ((), ())), preferre...  54.2 us
    dot_general x5, matrix products, contract_last(): lax.dot_general(left_side, right_side, (((1,), (1,)), ((), ())), preferre...  49.8 us
    ppermute x44, starting transfers between devices, swap(): return lax.ppermute(values, 'seq', [(i, i ^ bit) for i in range(4)])  48.1 us
    unnamed x92, local copies, waits for them, and re-layouts  42.8 us
    pallas_call x1, Pallas kernels, up_and_bend(): pl.pallas_call(partial(up_kernel, chunk=512), grid=(count // TILE,), in_s...  30.6 us
  transfers between devices with their start and end apart: 64, of which 23 were waited for; matrix products, arithmetic and copies ran while one was open for 31% of the time, Pallas kernels for 33%

profile of v12, /device:TPU:0, one launch (start us, length us, event | category | flops | bytes accessed | tf_op | source)
XLA Modules:
  0.0 759.5 jit_solution(6924960521455726194)
XLA Ops:
  27.8 19.0 %collective-permute-done.2 = bf16[256,2048]{1,0:T(8,128)(2,1)} collective-permute-done((bf16[256,2048]{1,0:T(8,128)(2,1)}, bf16[256,2048]{1,0:T(8,128)(2,1)}, u32[]{:S(2)}, u32[]{:S(2)}) %collective-permute-start.2) | collective-permute-done | bytes 1048608 | tf_op jit(solution)/shard_map/ppermute | solution.py:422
  53.7 17.7 %collective-permute-done = bf16[256,2048]{1,0:T(8,128)(2,1)} collective-permute-done((bf16[256,2048]{1,0:T(8,128)(2,1)}, bf16[256,2048]{1,0:T(8,128)(2,1)}, u32[]{:S(2)}, u32[]{:S(2)}) %collective-permute-start) | collective-permute-done | bytes 1048608 | tf_op jit(solution)/shard_map/ppermute | solution.py:422
  79.6 12.8 %collective-permute-done.4 = bf16[256,2048]{1,0:T(8,128)(2,1)} collective-permute-done((bf16[256,2048]{1,0:T(8,128)(2,1)}, bf16[256,2048]{1,0:T(8,128)(2,1)}, u32[]{:S(2)}, u32[]{:S(2)}) %collective-permute-start.4) | collective-permute-done | bytes 1048608 | tf_op jit(solution)/shard_map/ppermute | solution.py:422
  101.0 18.6 %add_convert_fusion.qkv_ref = bf16[2048,1536]{1,0:T(8,128)(2,1)} fusion(bf16[2048,2048]{1,0:T(8,128)(2,1)} %constant_dynamic-update-slice_fusion.left_ref, bf16[2048,1536]{1,0:T(8,128)(2,1)} %all-gather.5.cloned.1.call-done, f32[1536]{0:T(1024)S(1)} %reduce.2), kind=kOutput, calls=%fused_computation.1 | convolution fusion | flops 12891193344 | bytes 20977664 | tf_op jit(solution)/shard_map/dot_general | solution.py:31
  119.6 29.7 %attend_forward.1 = (bf16[2048,512]{1,0:T(8,128)(2,1)}, f32[2048,512]{1,0:T(8,128)}) custom-call(s32[1]{0:T(128)} %bitcast.1.at_ref.mask_ref, f32[8]{0:T(128)} %multiply_power_fusion.slope_ref, bf16[2048,1536]{1,0:T(8,128)(2,1)} %add_convert_fusion.qkv_ref), custom_call_target="tpu_custom_call" | custom-call | flops 2684354560 | bytes 2621440 | tf_op jit(solution)/shard_map/attend_forward/pallas_call | solution.py:173
  156.7 11.2 %collective-permute-done.10 = bf16[512,512]{1,0:T(8,128)(2,1)S(1)} collective-permute-done((bf16[512,512]{1,0:T(8,128)(2,1)}, bf16[512,512]{1,0:T(8,128)(2,1)S(1)}, u32[]{:S(2)}, u32[]{:S(2)}) %collective-permute-start.10) | collective-permute-done | bytes 524320 | tf_op jit(solution)/shard_map/ppermute | solution.py:422
  223.5 16.8 %collective-permute-done.14 = bf16[256,2048]{1,0:T(8,128)(2,1)} collective-permute-done((bf16[256,2048]{1,0:T(8,128)(2,1)}, bf16[256,2048]{1,0:T(8,128)(2,1)}, u32[]{:S(2)}, u32[]{:S(2)}) %collective-permute-start.14) | collective-permute-done | bytes 1048608 | tf_op jit(solution)/shard_map/ppermute | solution.py:422
  251.0 10.8 %collective-permute-done.17 = bf16[256,2048]{1,0:T(8,128)(2,1)S(1)} collective-permute-done((bf16[256,2048]{1,0:T(8,128)(2,1)}, bf16[256,2048]{1,0:T(8,128)(2,1)S(1)}, u32[]{:S(2)}, u32[]{:S(2)}) %collective-permute-start.17) | collective-permute-done | bytes 1048608 | tf_op jit(solution)/shard_map/ppermute | solution.py:422
  272.2 30.6 %up_and_bend.1 = (bf16[2048,2048]{1,0:T(8,128)(2,1)}, f32[2048,2048]{1,0:T(8,128)}) custom-call(bf16[2048,2048]{1,0:T(8,128)(2,1)} %constant_dynamic-update-slice_fusion.7.rows_ref.left_ref, bf16[2048,2048]{1,0:T(8,128)(2,1)} %all-gather.9.cloned.1.call-done.weight_ref, f32[1,2048]{1,0:T(1,128)} %bitcast.148), custom_call_target="tpu_custom_call" | custom-call | flops 8589934592 | bytes 8388608 | tf_op jit(solution)/shard_map/up_and_bend/pallas_call | solution.py:259
  304.9 23.6 %outer.4 = bf16[8,4,64,2048]{3,2,1,0:T(8,128)(2,1)} custom-call(bf16[2048,2048]{1,0:T(8,128)(2,1)} %constant_dynamic-update-slice_fusion.31.left_ref.rows_ref, bf16[2048,2048]{1,0:T(8,128)(2,1)} %get-tuple-element.180.refs_0_), custom_call_target="tpu_custom_call" | custom-call | flops 4294967296 | bytes 4194304 | tf_op jit(solution)/shard_map/outer/pallas_call | solution.py:404
  328.6 25.6 %hidden_gradient.1 = (bf16[2048,2048]{1,0:T(8,128)(2,1)}, f32[1,2048]{1,0:T(1,128)}) custom-call(bf16[2048,2048]{1,0:T(8,128)(2,1)} %constant_dynamic-update-slice_fusion.31.left_ref.rows_ref, bf16[2048,2048]{1,0:T(8,128)(2,1)} %all-gather.11.cloned.1.call-done.weight_ref, f32[2048,2048]{1,0:T(8,128)} %get-tuple-element.155.slope_ref), custom_call_target="tpu_custom_call" | custom-call | flops 6442450944 | bytes 6291456 | tf_op jit(solution)/shard_map/hidden_gradient/pallas_call | solution.py:283
  354.2 8.8 %convolution_convert_fusion.6 = bf16[512,2048]{1,0:T(8,128)(2,1)S(1)} fusion(bf16[2048,2048]{1,0:T(8,128)(2,1)} %all-gather.9.cloned.1.call-done.weight_ref, bf16[2048,2048]{1,0:T(8,128)(2,1)} %get-tuple-element.165.refs_0_), kind=kOutput, calls=%fused_computation.26 | convolution fusion | flops 4296015872 | bytes 12582912 | tf_op jit(solution)/shard_map/dot_general | solution.py:37
  366.5 16.3 %convolution_convert_fusion.1.own_ref = bf16[1536,2048]{1,0:T(8,128)(2,1)S(1)} fusion(bf16[2048,2048]{1,0:T(8,128)(2,1)} %all-gather.9.cloned.1.call-done.weight_ref, bf16[2048,2048]{1,0:T(8,128)(2,1)S(1)} %copy-done.7), kind=kOutput, calls=%fused_computation.3 | convolution fusion | flops 12888047616 | bytes 20971520 | tf_op jit(solution)/shard_map/dot_general | solution.py:37
  405.1 23.5 %outer.5 = bf16[8,4,64,2048]{3,2,1,0:T(8,128)(2,1)} custom-call(bf16[2048,2048]{1,0:T(8,128)(2,1)} %constant_dynamic-update-slice_fusion.7.rows_ref.left_ref, bf16[2048,2048]{1,0:T(8,128)(2,1)} %get-tuple-element.165.refs_0_), custom_call_target="tpu_custom_call" | custom-call | flops 4294967296 | bytes 4194304 | tf_op jit(solution)/shard_map/outer/pallas_call | solution.py:404
  436.9 11.1 %norm_back.2 = (bf16[512,2048]{1,0:T(8,128)(2,1)}, f32[512,2048]{1,0:T(8,128)}, f32[24,2048]{1,0:T(8,128)}) custom-call(bf16[1536,2048]{1,0:T(8,128)(2,1)} %copy-done.5, f32[512,2048]{1,0:T(8,128)} %copy-done, f32[512,1]{1,0:T(8,128)} %copy.65.average_ref, f32[512,1]{1,0:T(8,128)} %copy.66.scale_ref, bf16[512,2048]{1,0:T(8,128)(2,1)} %bitcast.106, ...), custom_call_target="tpu_custom_call" | custom-call | flops 7864320 | bytes 7680 | tf_op jit(solution)/shard_map/norm_back/pallas_call | solution.py:367
  449.0 8.9 %mixed_gradient.1 = bf16[512,2048]{1,0:T(8,128)(2,1)} custom-call(bf16[512,2048]{1,0:T(8,128)(2,1)} %get-tuple-element.179.rows_ref, bf16[2048,2048]{1,0:T(8,128)(2,1)} %all-gather.7.cloned.1.call-done.weight_ref), custom_call_target="tpu_custom_call" | custom-call | flops 1073741824 | bytes 1048576 | tf_op jit(solution)/shard_map/mixed_gradient/pallas_call | solution.py:309
  457.9 19.1 %convolution_convert_fusion = bf16[1536,2048]{1,0:T(8,128)(2,1)} fusion(bf16[2048,2048]{1,0:T(8,128)(2,1)} %all-gather.11.cloned.1.call-done.weight_ref, bf16[2048,2048]{1,0:T(8,128)(2,1)} %get-tuple-element.180.refs_0_), kind=kOutput, calls=%fused_computation.2 | convolution fusion | flops 12888047616 | bytes 20971520 | tf_op jit(solution)/shard_map/dot_general | solution.py:31
  484.7 8.8 %outer.6 = bf16[1,4,256,2048]{3,2,1,0:T(8,128)(2,1)} custom-call(bf16[1024,1024]{1,0:T(8,128)(2,1)} %pad_maximum_fusion.3.left_ref, bf16[1024,2048]{1,0:T(8,128)(2,1)} %pad_maximum_fusion.refs_0_), custom_call_target="tpu_custom_call" | custom-call | flops 1073741824 | bytes 1048576 | tf_op jit(solution)/shard_map/outer/pallas_call | solution.py:404
  517.1 29.0 %attend_backward.2.rest_4_ = bf16[2048,1536]{1,0:T(8,128)(2,1)} custom-call(s32[1]{0:T(128)} %bitcast.1.at_ref.mask_ref, f32[8]{0:T(128)} %multiply_power_fusion.slope_ref, bf16[2048,1536]{1,0:T(8,128)(2,1)} %add_convert_fusion.qkv_ref, f32[2048,512]{1,0:T(8,128)} %get-tuple-element.135.lse_ref, bf16[2048,512]{1,0:T(8,128)(2,1)} %get-tuple-element.134.mixed_ref, ...), custom_call_target="tpu_custom_call" | custom-call | flops 3355443200 | bytes 3276800 | tf_op jit(solution)/shard_map/attend_backward/pallas_call | solution.py:198
  550.5 28.5 %attend_backward.3.refs_0_ = bf16[2048,1536]{1,0:T(8,128)(2,1)} custom-call(s32[1]{0:T(128)} %bitcast.1.at_ref.mask_ref, f32[8]{0:T(128)} %multiply_power_fusion.slope_ref, bf16[2048,1536]{1,0:T(8,128)(2,1)} %add_convert_fusion.qkv_ref, f32[2048,512]{1,0:T(8,128)} %get-tuple-element.135.lse_ref, ...), custom_call_target="tpu_custom_call", output_to_operand_aliasing={{}: (9, {})} | custom-call | flops 3355443200 | bytes 3276800 | tf_op jit(solution)/shard_map/attend_backward/pallas_call | solution.py:198
  600.8 18.5 %outer.7 = bf16[8,4,64,1536]{3,2,1,0:T(8,128)(2,1)} custom-call(bf16[2048,2048]{1,0:T(8,128)(2,1)} %constant_dynamic-update-slice_fusion.left_ref, bf16[2048,1536]{1,0:T(8,128)(2,1)} %attend_backward.3.refs_0_), custom_call_target="tpu_custom_call" | custom-call | flops 3221225472 | bytes 3145728 | tf_op jit(solution)/shard_map/outer/pallas_call | solution.py:404
  634.0 9.8 %convolution_convert_fusion.2 = bf16[1024,2048]{1,0:T(8,128)(2,1)S(1)} fusion(bf16[2048,1536]{1,0:T(8,128)(2,1)} %all-gather.5.cloned.1.call-done, bf16[2048,1536]{1,0:T(8,128)(2,1)} %attend_backward.3.refs_0_), kind=kOutput, calls=%fused_computation.21 | convolution fusion | flops 6444548096 | bytes 13631488 | tf_op jit(solution)/shard_map/dot_general | solution.py:37
  675.6 16.4 %collective-permute-done.43.refs_1_ = bf16[256,2048]{1,0:T(8,128)(2,1)S(1)} collective-permute-done((bf16[256,2048]{1,0:T(8,128)(2,1)}, bf16[256,2048]{1,0:T(8,128)(2,1)S(1)}, u32[]{:S(2)}, u32[]{:S(2)}) %collective-permute-start.43) | collective-permute-done | bytes 1048608 | tf_op jit(solution)/shard_map/ppermute | solution.py:422
  697.9 10.7 %norm_back.3 = (bf16[512,2048]{1,0:T(8,128)(2,1)}, f32[512,2048]{1,0:T(8,128)}, f32[24,2048]{1,0:T(8,128)}) custom-call(bf16[512,2048]{1,0:T(8,128)(2,1)} %convolution_convert_fusion.3.own_ref, bf16[512,2048]{1,0:T(8,128)(2,1)} %bitcast.103, f32[512,1]{1,0:T(8,128)} %bitcast.124, f32[512,1]{1,0:T(8,128)} %bitcast.123, ...), custom_call_target="tpu_custom_call" | custom-call | flops 7864320 | bytes 7680 | tf_op jit(solution)/shard_map/norm_back/pallas_call | solution.py:367
  (316 shorter events, 318.5 us)
Async XLA Ops:
  7.2 93.8 %all-gather.5.cloned.1.call-start = ((), (), s32[]{:S(2)}) async-start(), calls=%async_computation.7 | async-start | bytes 7077888 | tf_op jit(solution)/shard_map/all_gather | solution.py:614
  10.3 169.9 %all-gather.7.cloned.1.call-start = ((), (), s32[]{:S(2)}) async-start(), calls=%async_computation.8 | async-start | bytes 9437184 | tf_op jit(solution)/shard_map/all_gather | solution.py:626
  11.1 261.1 %all-gather.9.cloned.1.call-start = ((), (), s32[]{:S(2)}) async-start(), calls=%async_computation.9 | async-start | bytes 9437184 | tf_op jit(solution)/shard_map/all_gather | solution.py:627
  19.5 309.2 %all-gather.11.cloned.1.call-start = ((), (), s32[]{:S(2)}) async-start(), calls=%async_computation.10 | async-start | bytes 9437184 | tf_op jit(solution)/shard_map/all_gather | solution.py:628
  24.0 47.4 %collective-permute-start = (bf16[256,2048]{1,0:T(8,128)(2,1)}, bf16[256,2048]{1,0:T(8,128)(2,1)}, u32[]{:S(2)}, u32[]{:S(2)}) collective-permute-start(bf16[256,2048]{1,0:T(8,128)(2,1)} %get-tuple-element.291), channel_id=1, source_target_pairs={{0,8},{8,0},{16,24},{24,16},{1,9},{9,1},{17,25},{25,17},{2,10},{10... | collective-permute-start | bytes 3145736 | tf_op jit(solution)/shard_map/ppermute | solution.py:422
  24.6 52.7 %collective-permute-start.3 = (bf16[256,2048]{1,0:T(8,128)(2,1)}, bf16[256,2048]{1,0:T(8,128)(2,1)}, u32[]{:S(2)}, u32[]{:S(2)}) collective-permute-start(bf16[256,2048]{1,0:T(8,128)(2,1)} %get-tuple-element.290), channel_id=1, source_target_pairs={{0,16},{8,24},{16,0},{24,8},{1,17},{9,25},{17,1},{25,9},{2,18},{10... | collective-permute-start | bytes 3145736 | tf_op jit(solution)/shard_map/ppermute | solution.py:422
  26.9 490.1 %reduce-scatter.5.cloned.1.call-start = ((), (), s32[]{:S(2)}) async-start(), calls=%async_computation.11 | async-start | bytes 9437184 | tf_op jit(solution)/shard_map/reduce_scatter | solution.py:668
  46.8 45.6 %collective-permute-start.4 = (bf16[256,2048]{1,0:T(8,128)(2,1)}, bf16[256,2048]{1,0:T(8,128)(2,1)}, u32[]{:S(2)}, u32[]{:S(2)}) collective-permute-start(bf16[256,2048]{1,0:T(8,128)(2,1)} %collective-permute-done.2), channel_id=1, source_target_pairs={{0,8},{8,0},{16,24},{24,16},{1,9},{9,1},{17,25},{25,17},{2,10},{10... | collective-permute-start | bytes 3145736 | tf_op jit(solution)/shard_map/ppermute | solution.py:422
  52.1 42.7 %collective-permute-start.5 = (bf16[256,2048]{1,0:T(8,128)(2,1)S(1)}, bf16[256,2048]{1,0:T(8,128)(2,1)S(1)}, u32[]{:S(2)}, u32[]{:S(2)}) collective-permute-start(bf16[256,2048]{1,0:T(8,128)(2,1)S(1)} %collective-permute-done.1), channel_id=1, source_target_pairs={{0,16},{8,24},{16,0},{24,8},{1,17},{9,25},{17,1},{25,9},{2,18},{10... | collective-permute-start | bytes 3145736 | tf_op jit(solution)/shard_map/ppermute | solution.py:422
  96.9 52.4 %collective-permute-start.7 = (bf16[256,2048]{1,0:T(8,128)(2,1)}, bf16[256,2048]{1,0:T(8,128)(2,1)}, u32[]{:S(2)}, u32[]{:S(2)}) collective-permute-start(bf16[256,2048]{1,0:T(8,128)(2,1)} %get-tuple-element.139), channel_id=1, source_target_pairs={{0,16},{8,24},{16,0},{24,8},{1,17},{9,25},{17,1},{25,9},{2,18},{10... | collective-permute-start | bytes 3145736 | tf_op jit(solution)/shard_map/ppermute | solution.py:422
  97.3 52.1 %collective-permute-start.8 = (bf16[256,2048]{1,0:T(8,128)(2,1)}, bf16[256,2048]{1,0:T(8,128)(2,1)}, u32[]{:S(2)}, u32[]{:S(2)}) collective-permute-start(bf16[256,2048]{1,0:T(8,128)(2,1)} %get-tuple-element.139), channel_id=1, source_target_pairs={{0,8},{8,0},{16,24},{24,16},{1,9},{9,1},{17,25},{25,17},{2,10},{10... | collective-permute-start | bytes 3145736 | tf_op jit(solution)/shard_map/ppermute | solution.py:422
  98.9 50.4 %collective-permute-start.6 = (bf16[256,2048]{1,0:T(8,128)(2,1)S(1)}, bf16[256,2048]{1,0:T(8,128)(2,1)}, u32[]{:S(2)}, u32[]{:S(2)}) collective-permute-start(bf16[256,2048]{1,0:T(8,128)(2,1)S(1)} %get-tuple-element.140), channel_id=1, source_target_pairs={{0,8},{8,0},{16,24},{24,16},{1,9},{9,1},{17,25},{25,17},{2,10},{10... | collective-permute-start | bytes 3145736 | tf_op jit(solution)/shard_map/ppermute | solution.py:422
  99.3 50.0 %collective-permute-start.9 = (bf16[256,2048]{1,0:T(8,128)(2,1)S(1)}, bf16[256,2048]{1,0:T(8,128)(2,1)}, u32[]{:S(2)}, u32[]{:S(2)}) collective-permute-start(bf16[256,2048]{1,0:T(8,128)(2,1)S(1)} %get-tuple-element.140), channel_id=1, source_target_pairs={{0,16},{8,24},{16,0},{24,8},{1,17},{9,25},{17,1},{25,9},{2,18},{10... | collective-permute-start | bytes 3145736 | tf_op jit(solution)/shard_map/ppermute | solution.py:422
  191.5 49.6 %collective-permute-start.13 = (bf16[256,2048]{1,0:T(8,128)(2,1)}, bf16[256,2048]{1,0:T(8,128)(2,1)}, u32[]{:S(2)}, u32[]{:S(2)}) collective-permute-start(bf16[256,2048]{1,0:T(8,128)(2,1)} %get-tuple-element.284), channel_id=1, source_target_pairs={{0,8},{8,0},{16,24},{24,16},{1,9},{9,1},{17,25},{25,17},{2,10},{10... | collective-permute-start | bytes 3145736 | tf_op jit(solution)/shard_map/ppermute | solution.py:422
  193.7 46.6 %collective-permute-start.14 = (bf16[256,2048]{1,0:T(8,128)(2,1)}, bf16[256,2048]{1,0:T(8,128)(2,1)}, u32[]{:S(2)}, u32[]{:S(2)}) collective-permute-start(bf16[256,2048]{1,0:T(8,128)(2,1)} %get-tuple-element.283), channel_id=1, source_target_pairs={{0,8},{8,0},{16,24},{24,16},{1,9},{9,1},{17,25},{25,17},{2,10},{10... | collective-permute-start | bytes 3145736 | tf_op jit(solution)/shard_map/ppermute | solution.py:422
  194.3 54.3 %collective-permute-start.16 = (bf16[256,2048]{1,0:T(8,128)(2,1)}, bf16[256,2048]{1,0:T(8,128)(2,1)}, u32[]{:S(2)}, u32[]{:S(2)}) collective-permute-start(bf16[256,2048]{1,0:T(8,128)(2,1)} %get-tuple-element.283), channel_id=1, source_target_pairs={{0,16},{8,24},{16,0},{24,8},{1,17},{9,25},{17,1},{25,9},{2,18},{10... | collective-permute-start | bytes 3145736 | tf_op jit(solution)/shard_map/ppermute | solution.py:422
  328.6 262.5 %reduce-scatter.7.cloned.1.call-start = ((), (), s32[]{:S(2)}) async-start(), calls=%async_computation.12 | async-start | bytes 9437184 | tf_op jit(solution)/shard_map/reduce_scatter | solution.py:668
  383.0 45.6 %collective-permute-start.22 = (bf16[256,2048]{1,0:T(8,128)(2,1)S(1)}, bf16[256,2048]{1,0:T(8,128)(2,1)}, u32[]{:S(2)}, u32[]{:S(2)}) collective-permute-start(bf16[256,2048]{1,0:T(8,128)(2,1)S(1)} %get-tuple-element.253), channel_id=1, source_target_pairs={{0,8},{8,0},{16,24},{24,16},{1,9},{9,1},{17,25},{25,17},{2,10},{10... | collective-permute-start | bytes 3145736 | tf_op jit(solution)/shard_map/ppermute | solution.py:422
  383.4 45.3 %collective-permute-start.27 = (bf16[256,2048]{1,0:T(8,128)(2,1)S(1)}, bf16[256,2048]{1,0:T(8,128)(2,1)}, u32[]{:S(2)}, u32[]{:S(2)}) collective-permute-start(bf16[256,2048]{1,0:T(8,128)(2,1)S(1)} %get-tuple-element.252), channel_id=1, source_target_pairs={{0,16},{8,24},{16,0},{24,8},{1,17},{9,25},{17,1},{25,9},{2,18},{10... | collective-permute-start | bytes 3145736 | tf_op jit(solution)/shard_map/ppermute | solution.py:422
  433.1 193.5 %reduce-scatter.9.cloned.1.call-start = ((), (), s32[]{:S(2)}) async-start(), calls=%async_computation.13 | async-start | bytes 2359296 | tf_op jit(solution)/shard_map/reduce_scatter | solution.py:753
  434.9 42.1 %collective-permute-start.28 = (bf16[256,2048]{1,0:T(8,128)(2,1)}, bf16[256,2048]{1,0:T(8,128)(2,1)S(1)}, u32[]{:S(2)}, u32[]{:S(2)}) collective-permute-start(bf16[256,2048]{1,0:T(8,128)(2,1)} %get-tuple-element.181), channel_id=1, source_target_pairs={{0,8},{8,0},{16,24},{24,16},{1,9},{9,1},{17,25},{25,17},{2,10},{10... | collective-permute-start | bytes 3145736 | tf_op jit(solution)/shard_map/ppermute | solution.py:422
  515.4 63.6 %collective-permute-start.34 = (bf16[512,2048]{1,0:T(8,128)(2,1)}, bf16[512,2048]{1,0:T(8,128)(2,1)}, u32[]{:S(2)}, u32[]{:S(2)}) collective-permute-start(bf16[512,2048]{1,0:T(8,128)(2,1)} %pad_maximum_fusion.4), channel_id=1, source_target_pairs={{0,8},{8,0},{16,24},{24,16},{1,9},{9,1},{17,25},{25,17},{2,10},{10... | collective-permute-start | bytes 6291464 | tf_op jit(solution)/shard_map/ppermute | solution.py:422
  515.8 63.2 %collective-permute-start.35 = (bf16[512,2048]{1,0:T(8,128)(2,1)}, bf16[512,2048]{1,0:T(8,128)(2,1)}, u32[]{:S(2)}, u32[]{:S(2)}) collective-permute-start(bf16[512,2048]{1,0:T(8,128)(2,1)} %pad_maximum_fusion.5), channel_id=1, source_target_pairs={{0,16},{8,24},{16,0},{24,8},{1,17},{9,25},{17,1},{25,9},{2,18},{10... | collective-permute-start | bytes 6291464 | tf_op jit(solution)/shard_map/ppermute | solution.py:422
  591.0 132.1 %reduce-scatter.11.cloned.1.call-start = ((), (), s32[]{:S(2)}) async-start(), calls=%async_computation.14 | async-start | bytes 7077888 | tf_op jit(solution)/shard_map/reduce_scatter | solution.py:668
  (70 other events, 1369.0 us)
Sparse Core Ops, SparseCore 0:
  10.4 67.4 all-gather.4
  79.5 80.6 all-gather.6
  161.9 80.5 all-gather.8
  243.9 81.0 all-gather.10
  328.7 89.8 reduce-scatter.4
  433.2 89.5 reduce-scatter.6
  591.1 35.4 reduce-scatter.8
  628.9 68.3 reduce-scatter.10

commit v13 on v12

--- a/solution.py
+++ b/solution.py
@@ -299,6 +299,27 @@
     )(rows, weight, slope)
 
 
+def product_kernel(rows_ref, weight_ref, out_ref):
+    out_ref[...] = contract(rows_ref[...], weight_ref[...]).astype(out_ref.dtype)
+
+
+def product_of(rows, weight, count):
+    depth, width = weight.shape
+    return pl.pallas_call(
+        product_kernel,
+        grid=(count // TILE,),
+        in_specs=[
+            pl.BlockSpec((TILE, depth), lambda i: (i, 0)),
+            pl.BlockSpec((depth, width), lambda i: (0, 0), pipeline_mode=pl.Buffered(1)),
+        ],
+        out_specs=pl.BlockSpec((TILE, width), lambda i: (i, 0)),
+        out_shape=jax.ShapeDtypeStruct((count, width), jnp.bfloat16),
+        compiler_params=pltpu.CompilerParams(vmem_limit_bytes=GRANT),
+        cost_estimate=estimate(2 * count * depth * width, 0),
+        name="product",
+    )(rows, weight)
+
+
 def mixed_grad_kernel(rows_ref, weight_ref, out_ref):
     out_ref[...] = contract_last(rows_ref[...], weight_ref[...]).astype(out_ref.dtype)
 
@@ -654,11 +675,12 @@
     second = order.gather(order(halves_of, second_norm))
     mine, theirs = order(pair_halves, mixed_slots)
     upstream_made = order.fill(upstream)
-    mixed_half = order(lambda *parts: jnp.concatenate(parts, axis=0), mine, pair_swap(theirs))
+    theirs = pair_swap(theirs)
     dz_sum = order(lambda values: jnp.sum(values.astype(wide), axis=0), dz_low)
     second = whole(order.pass_on(second))
     upstream = order.pass_on(upstream, second)
     active, slope = order(lambda rows: up_and_bend(rows, up_slab, up_bias_slab[None]), second)
+    mixed_half = order(lambda *parts: jnp.concatenate(parts, axis=0), mine, theirs)
     upstream = order.complete(upstream_made, upstream)
 
     def slab_product(left, right):
@@ -715,11 +737,10 @@
     )
     early = [middle_sums[2], middle_sums[0], middle_sums[1], hidden_sum, dz_sum]
     mixed_grad = order(lambda rows: mixed_gradient(rows, full_out, slab), branch_grad)
-    if square:
-        mixed_grad = gate(mixed_grad, *result_far)
     mixed_grad = exchange(by_index([mixed_grad[:, j * slab : (j + 1) * slab] for j in range(groups)], me))
     if square:
-        result_rest = order(slots(to_result, 0, 3), active)
+        result_rest = order(lambda rows: product_of(rows, down_slab, 3 * count), active)
+        result_came = order.add_far(result_rest, result_far, None)
     branch_other = pair_swap(branch_grad)
     branch_pair = jnp.concatenate([branch_grad, branch_other], axis=0)
     out_sum = order(lambda columns: outer(columns, branch_pair, groups, 1), mixed_half)
@@ -728,7 +749,6 @@
         part = out_sum.shape[0] // 4
         out_far = out_sum[3 * part : 3 * part + part // 2], out_sum[3 * part + part // 2 :]
         out_far = swap_far(gate(out_far, *mixed_grad))
-        result_came = order.add_far(result_rest, result_far, None, *mixed_grad)
     order.after(down_sum)
     begun = order(
         lambda *grads: attend_backward(*attention, grads, seq_count, local_len, 0, pairs // 2), *mixed_grad
@@ -754,12 +774,11 @@
     order.after(up_sum)
     if square:
         far = swap_far(order.halves(slots(to_normed, 3, 4), qkv_grad))
-        qkv_sum = slab_sum(gate(slab_product(normed, qkv_grad), *far, grad_w_out))
         near = order(slots(to_normed, 1, 3), qkv_grad)
         direct = swap_direct(near, half)
-        down_slabs = slabs_of_rows(gate(down_sum, *far))
-        order.after(down_slabs)
+        qkv_sum = slab_sum(gate(slab_product(normed, qkv_grad), *far, *direct, grad_w_out))
         came = order.add_far(near, far, direct)
+        down_slabs = slabs_of_rows(gate(down_sum, *came))
         normed_own = order(slots(to_normed, 0, 1), qkv_grad)
     else:
         down_slabs = slabs_of_rows(down_sum)
@@ -801,7 +820,7 @@
         others = range(lax.axis_size(axis))
         came = [lax.ppermute(sums, axis, [(i, i ^ mask) for i in others]) for mask in masks]
         if (axis, masks) == stages[-1]:
-            order.after(up_slabs, qkv_slabs)
+            order.after(down_slabs, up_slabs, qkv_slabs)
         sums = order(lambda *parts: sum(parts[1:], parts[0]), sums, *came)
     sums = sums.reshape(-1)
 

time: 765 us -> 762 us (level)
  matrix products: 104 us -> 84.4 us
  Pallas kernels: 254 us -> 272 us
  waiting for transfers between devices: 174 us -> 165 us
    dot_general x4 -> x3, matrix products: 54.2 us -> 33 us  [contract(): lax.dot_general(left_side, right_side, (((1,), (0,)), ((), ())), preferre...]
    pallas_call x0 -> x1, Pallas kernels: none -> 18.9 us  [product_of(): pl.pallas_call(product_kernel, grid=(count // TILE,), in_specs=[pl.BlockS...]
    ppermute x44, waiting for transfers between devices: 149 us -> 140 us  [swap(): return lax.ppermute(values, 'seq', [(i, i ^ bit) for i in range(4)])]
    unnamed x92 -> x98, local copies, waits for them, and re-layouts: 42.8 us -> 44 us
  transfers between devices with their start and end apart: 64 -> 64, of which waited for: 23 -> 23; matrix products, arithmetic and copies ran while one was open for 31% -> 29% of each run, Pallas kernels for 33% -> 36%
where the time goes in v13:
time: 762 us; the launch traced here: 757 us
  Pallas kernels  272 us (36%)
  waiting for transfers between devices  165 us (22%)
  local copies, waits for them, and re-layouts  99.3 us (13%)
  matrix products  84.4 us (11%)
  starting transfers between devices  68.8 us (9%)
  other arithmetic  51.4 us (7%)
  between operations  15.1 us (2%)
    ppermute x44, waiting for transfers between devices, swap(): return lax.ppermute(values, 'seq', [(i, i ^ bit) for i in range(4)])  140 us
    pallas_call x4, Pallas kernels, outer(): pl.pallas_call(partial(outer_kernel, chunk=512 if width % 512 == 0 else 2...  74.3 us
    pallas_call x2, Pallas kernels, attend_backward(): pl.pallas_call(partial(attend_backward_kernel, blocks=blocks, seqs=seqs,...  57.6 us
    dot_general x5, matrix products, contract_last(): lax.dot_general(left_side, right_side, (((1,), (1,)), ((), ())), preferre...  51.4 us
    ppermute x44, starting transfers between devices, swap(): return lax.ppermute(values, 'seq', [(i, i ^ bit) for i in range(4)])  48.5 us
    unnamed x98, local copies, waits for them, and re-layouts  44 us
    dot_general x3, matrix products, contract(): lax.dot_general(left_side, right_side, (((1,), (0,)), ((), ())), preferre...  33 us
    pallas_call x1, Pallas kernels, up_and_bend(): pl.pallas_call(partial(up_kernel, chunk=512), grid=(count // TILE,), in_s...  30.6 us
  transfers between devices with their start and end apart: 64, of which 23 were waited for; matrix products, arithmetic and copies ran while one was open for 29% of the time, Pallas kernels for 36%

profile of v13, /device:TPU:0, one launch (start us, length us, event | category | flops | bytes accessed | tf_op | source)
XLA Modules:
  0.0 756.7 jit_solution(10524180992927593987)
XLA Ops:
  27.8 19.0 %collective-permute-done.2 = bf16[256,2048]{1,0:T(8,128)(2,1)} collective-permute-done((bf16[256,2048]{1,0:T(8,128)(2,1)}, bf16[256,2048]{1,0:T(8,128)(2,1)}, u32[]{:S(2)}, u32[]{:S(2)}) %collective-permute-start.2) | collective-permute-done | bytes 1048608 | tf_op jit(solution)/shard_map/ppermute | solution.py:443
  53.7 17.7 %collective-permute-done = bf16[256,2048]{1,0:T(8,128)(2,1)} collective-permute-done((bf16[256,2048]{1,0:T(8,128)(2,1)}, bf16[256,2048]{1,0:T(8,128)(2,1)}, u32[]{:S(2)}, u32[]{:S(2)}) %collective-permute-start) | collective-permute-done | bytes 1048608 | tf_op jit(solution)/shard_map/ppermute | solution.py:443
  79.6 12.9 %collective-permute-done.4 = bf16[256,2048]{1,0:T(8,128)(2,1)} collective-permute-done((bf16[256,2048]{1,0:T(8,128)(2,1)}, bf16[256,2048]{1,0:T(8,128)(2,1)}, u32[]{:S(2)}, u32[]{:S(2)}) %collective-permute-start.4) | collective-permute-done | bytes 1048608 | tf_op jit(solution)/shard_map/ppermute | solution.py:443
  101.1 18.6 %add_convert_fusion.qkv_ref = bf16[2048,1536]{1,0:T(8,128)(2,1)} fusion(bf16[2048,2048]{1,0:T(8,128)(2,1)} %constant_dynamic-update-slice_fusion.left_ref, bf16[2048,1536]{1,0:T(8,128)(2,1)} %all-gather.5.cloned.1.call-done, f32[1536]{0:T(1024)S(1)} %reduce.2), kind=kOutput, calls=%fused_computation.1 | convolution fusion | flops 12891193344 | bytes 20977664 | tf_op jit(solution)/shard_map/dot_general | solution.py:31
  119.7 29.7 %attend_forward.1 = (bf16[2048,512]{1,0:T(8,128)(2,1)}, f32[2048,512]{1,0:T(8,128)}) custom-call(s32[1]{0:T(128)} %bitcast.1.at_ref.mask_ref, f32[8]{0:T(128)} %multiply_power_fusion.slope_ref, bf16[2048,1536]{1,0:T(8,128)(2,1)} %add_convert_fusion.qkv_ref), custom_call_target="tpu_custom_call" | custom-call | flops 2684354560 | bytes 2621440 | tf_op jit(solution)/shard_map/attend_forward/pallas_call | solution.py:173
  156.8 11.2 %collective-permute-done.10 = bf16[512,512]{1,0:T(8,128)(2,1)S(1)} collective-permute-done((bf16[512,512]{1,0:T(8,128)(2,1)}, bf16[512,512]{1,0:T(8,128)(2,1)S(1)}, u32[]{:S(2)}, u32[]{:S(2)}) %collective-permute-start.10) | collective-permute-done | bytes 524320 | tf_op jit(solution)/shard_map/ppermute | solution.py:443
  221.7 18.7 %collective-permute-done.14 = bf16[256,2048]{1,0:T(8,128)(2,1)} collective-permute-done((bf16[256,2048]{1,0:T(8,128)(2,1)}, bf16[256,2048]{1,0:T(8,128)(2,1)}, u32[]{:S(2)}, u32[]{:S(2)}) %collective-permute-start.14) | collective-permute-done | bytes 1048608 | tf_op jit(solution)/shard_map/ppermute | solution.py:443
  250.7 11.3 %collective-permute-done.17 = bf16[256,2048]{1,0:T(8,128)(2,1)} collective-permute-done((bf16[256,2048]{1,0:T(8,128)(2,1)}, bf16[256,2048]{1,0:T(8,128)(2,1)}, u32[]{:S(2)}, u32[]{:S(2)}) %collective-permute-start.17) | collective-permute-done | bytes 1048608 | tf_op jit(solution)/shard_map/ppermute | solution.py:443
  268.6 30.6 %up_and_bend.1 = (bf16[2048,2048]{1,0:T(8,128)(2,1)}, f32[2048,2048]{1,0:T(8,128)}) custom-call(bf16[2048,2048]{1,0:T(8,128)(2,1)} %constant_dynamic-update-slice_fusion.7.rows_ref.left_ref, bf16[2048,2048]{1,0:T(8,128)(2,1)} %all-gather.9.cloned.1.call-done.weight_ref, f32[1,2048]{1,0:T(1,128)} %bitcast.149), custom_call_target="tpu_custom_call" | custom-call | flops 8589934592 | bytes 8388608 | tf_op jit(solution)/shard_map/up_and_bend/pallas_call | solution.py:259
  308.2 23.5 %outer.4 = bf16[8,4,64,2048]{3,2,1,0:T(8,128)(2,1)} custom-call(bf16[2048,2048]{1,0:T(8,128)(2,1)} %constant_dynamic-update-slice_fusion.31.left_ref.rows_ref, bf16[2048,2048]{1,0:T(8,128)(2,1)} %get-tuple-element.177.refs_0_.rows_ref), custom_call_target="tpu_custom_call" | custom-call | flops 4294967296 | bytes 4194304 | tf_op jit(solution)/shard_map/outer/pallas_call | solution.py:425
  331.9 25.6 %hidden_gradient.1 = (bf16[2048,2048]{1,0:T(8,128)(2,1)}, f32[1,2048]{1,0:T(1,128)}) custom-call(bf16[2048,2048]{1,0:T(8,128)(2,1)} %constant_dynamic-update-slice_fusion.31.left_ref.rows_ref, bf16[2048,2048]{1,0:T(8,128)(2,1)} %all-gather.11.cloned.1.call-done.weight_ref, f32[2048,2048]{1,0:T(8,128)} %get-tuple-element.150.slope_ref), custom_call_target="tpu_custom_call" | custom-call | flops 6442450944 | bytes 6291456 | tf_op jit(solution)/shard_map/hidden_gradient/pallas_call | solution.py:283
  357.4 8.6 %convolution_convert_fusion.5 = bf16[512,2048]{1,0:T(8,128)(2,1)S(1)} fusion(bf16[2048,2048]{1,0:T(8,128)(2,1)} %all-gather.9.cloned.1.call-done.weight_ref, bf16[2048,2048]{1,0:T(8,128)(2,1)} %get-tuple-element.162.refs_0_), kind=kOutput, calls=%fused_computation.24 | convolution fusion | flops 4296015872 | bytes 12582912 | tf_op jit(solution)/shard_map/dot_general | solution.py:37
  369.4 18.1 %convolution_convert_fusion.own_ref = bf16[1536,2048]{1,0:T(8,128)(2,1)S(1)} fusion(bf16[2048,2048]{1,0:T(8,128)(2,1)} %all-gather.9.cloned.1.call-done.weight_ref, bf16[2048,2048]{1,0:T(8,128)(2,1)} %get-tuple-element.162.refs_0_), kind=kOutput, calls=%fused_computation.2 | convolution fusion | flops 12888047616 | bytes 20971520 | tf_op jit(solution)/shard_map/dot_general | solution.py:37
  407.2 23.5 %outer.5 = bf16[8,4,64,2048]{3,2,1,0:T(8,128)(2,1)} custom-call(bf16[2048,2048]{1,0:T(8,128)(2,1)} %constant_dynamic-update-slice_fusion.7.rows_ref.left_ref, bf16[2048,2048]{1,0:T(8,128)(2,1)} %get-tuple-element.162.refs_0_), custom_call_target="tpu_custom_call" | custom-call | flops 4294967296 | bytes 4194304 | tf_op jit(solution)/shard_map/outer/pallas_call | solution.py:425
  440.9 10.9 %norm_back.2 = (bf16[512,2048]{1,0:T(8,128)(2,1)}, f32[512,2048]{1,0:T(8,128)}, f32[24,2048]{1,0:T(8,128)}) custom-call(bf16[1536,2048]{1,0:T(8,128)(2,1)} %copy-done.5, f32[512,2048]{1,0:T(8,128)} %copy-done, f32[512,1]{1,0:T(8,128)} %copy.65.average_ref, f32[512,1]{1,0:T(8,128)} %copy.66.scale_ref, bf16[512,2048]{1,0:T(8,128)(2,1)} %bitcast.107, ...), custom_call_target="tpu_custom_call" | custom-call | flops 7864320 | bytes 7680 | tf_op jit(solution)/shard_map/norm_back/pallas_call | solution.py:388
  452.8 8.9 %mixed_gradient.1 = bf16[512,2048]{1,0:T(8,128)(2,1)} custom-call(bf16[512,2048]{1,0:T(8,128)(2,1)} %get-tuple-element.176.rows_ref, bf16[2048,2048]{1,0:T(8,128)(2,1)} %all-gather.7.cloned.1.call-done.weight_ref), custom_call_target="tpu_custom_call" | custom-call | flops 1073741824 | bytes 1048576 | tf_op jit(solution)/shard_map/mixed_gradient/pallas_call | solution.py:330
  467.5 18.9 %product.1 = bf16[1536,2048]{1,0:T(8,128)(2,1)} custom-call(bf16[2048,2048]{1,0:T(8,128)(2,1)} %get-tuple-element.177.refs_0_.rows_ref, bf16[2048,2048]{1,0:T(8,128)(2,1)} %all-gather.11.cloned.1.call-done.weight_ref), custom_call_target="tpu_custom_call" | custom-call | flops 3221225472 | bytes 3145728 | tf_op jit(solution)/shard_map/product/pallas_call | solution.py:308
  497.8 8.8 %outer.6 = bf16[1,4,256,2048]{3,2,1,0:T(8,128)(2,1)} custom-call(bf16[1024,1024]{1,0:T(8,128)(2,1)} %pad_maximum_fusion.3.left_ref, bf16[1024,2048]{1,0:T(8,128)(2,1)} %pad_maximum_fusion.refs_0_), custom_call_target="tpu_custom_call" | custom-call | flops 1073741824 | bytes 1048576 | tf_op jit(solution)/shard_map/outer/pallas_call | solution.py:425
  513.1 29.0 %attend_backward.2.rest_4_ = bf16[2048,1536]{1,0:T(8,128)(2,1)} custom-call(s32[1]{0:T(128)} %bitcast.1.at_ref.mask_ref, f32[8]{0:T(128)} %multiply_power_fusion.slope_ref, bf16[2048,1536]{1,0:T(8,128)(2,1)} %add_convert_fusion.qkv_ref, f32[2048,512]{1,0:T(8,128)} %get-tuple-element.132.lse_ref, bf16[2048,512]{1,0:T(8,128)(2,1)} %get-tuple-element.131.mixed_ref, ...), custom_call_target="tpu_custom_call" | custom-call | flops 3355443200 | bytes 3276800 | tf_op jit(solution)/shard_map/attend_backward/pallas_call | solution.py:198
  546.8 28.6 %attend_backward.3.refs_0_ = bf16[2048,1536]{1,0:T(8,128)(2,1)} custom-call(s32[1]{0:T(128)} %bitcast.1.at_ref.mask_ref, f32[8]{0:T(128)} %multiply_power_fusion.slope_ref, bf16[2048,1536]{1,0:T(8,128)(2,1)} %add_convert_fusion.qkv_ref, f32[2048,512]{1,0:T(8,128)} %get-tuple-element.132.lse_ref, ...), custom_call_target="tpu_custom_call", output_to_operand_aliasing={{}: (9, {})} | custom-call | flops 3355443200 | bytes 3276800 | tf_op jit(solution)/shard_map/attend_backward/pallas_call | solution.py:198
  575.4 16.0 %collective-permute-done.39 = bf16[256,2048]{1,0:T(8,128)(2,1)S(1)} collective-permute-done((bf16[256,2048]{1,0:T(8,128)(2,1)S(1)}, bf16[256,2048]{1,0:T(8,128)(2,1)S(1)}, u32[]{:S(2)}, u32[]{:S(2)}) %collective-permute-start.39) | collective-permute-done | bytes 1048608 | tf_op jit(solution)/shard_map/ppermute | solution.py:443
  605.1 9.8 %convolution_convert_fusion.1 = bf16[1024,2048]{1,0:T(8,128)(2,1)S(1)} fusion(bf16[2048,1536]{1,0:T(8,128)(2,1)} %all-gather.5.cloned.1.call-done, bf16[2048,1536]{1,0:T(8,128)(2,1)} %attend_backward.3.refs_0_), kind=kOutput, calls=%fused_computation.19 | convolution fusion | flops 6444548096 | bytes 13631488 | tf_op jit(solution)/shard_map/dot_general | solution.py:37
  620.6 18.5 %outer.7 = bf16[8,4,64,1536]{3,2,1,0:T(8,128)(2,1)} custom-call(bf16[2048,2048]{1,0:T(8,128)(2,1)} %constant_dynamic-update-slice_fusion.left_ref, bf16[2048,1536]{1,0:T(8,128)(2,1)} %attend_backward.3.refs_0_), custom_call_target="tpu_custom_call" | custom-call | flops 3221225472 | bytes 3145728 | tf_op jit(solution)/shard_map/outer/pallas_call | solution.py:425
  683.3 10.9 %norm_back.3 = (bf16[512,2048]{1,0:T(8,128)(2,1)}, f32[512,2048]{1,0:T(8,128)}, f32[24,2048]{1,0:T(8,128)}) custom-call(bf16[512,2048]{1,0:T(8,128)(2,1)} %convolution_convert_fusion.2.own_ref, bf16[512,2048]{1,0:T(8,128)(2,1)} %bitcast.102, f32[512,1]{1,0:T(8,128)} %bitcast.125, f32[512,1]{1,0:T(8,128)} %bitcast.124, ...), custom_call_target="tpu_custom_call" | custom-call | flops 7864320 | bytes 7680 | tf_op jit(solution)/shard_map/norm_back/pallas_call | solution.py:388
  (323 shorter events, 312.2 us)
Async XLA Ops:
  7.2 93.9 %all-gather.5.cloned.1.call-start = ((), (), s32[]{:S(2)}) async-start(), calls=%async_computation.7 | async-start | bytes 7077888 | tf_op jit(solution)/shard_map/all_gather | solution.py:635
  10.3 170.0 %all-gather.7.cloned.1.call-start = ((), (), s32[]{:S(2)}) async-start(), calls=%async_computation.8 | async-start | bytes 9437184 | tf_op jit(solution)/shard_map/all_gather | solution.py:647
  11.1 257.5 %all-gather.9.cloned.1.call-start = ((), (), s32[]{:S(2)}) async-start(), calls=%async_computation.9 | async-start | bytes 9437184 | tf_op jit(solution)/shard_map/all_gather | solution.py:648
  19.5 312.4 %all-gather.11.cloned.1.call-start = ((), (), s32[]{:S(2)}) async-start(), calls=%async_computation.10 | async-start | bytes 9437184 | tf_op jit(solution)/shard_map/all_gather | solution.py:649
  24.0 47.4 %collective-permute-start = (bf16[256,2048]{1,0:T(8,128)(2,1)}, bf16[256,2048]{1,0:T(8,128)(2,1)}, u32[]{:S(2)}, u32[]{:S(2)}) collective-permute-start(bf16[256,2048]{1,0:T(8,128)(2,1)} %get-tuple-element.285), channel_id=1, source_target_pairs={{0,8},{8,0},{16,24},{24,16},{1,9},{9,1},{17,25},{25,17},{2,10},{10... | collective-permute-start | bytes 3145736 | tf_op jit(solution)/shard_map/ppermute | solution.py:443
  24.6 52.7 %collective-permute-start.3 = (bf16[256,2048]{1,0:T(8,128)(2,1)}, bf16[256,2048]{1,0:T(8,128)(2,1)}, u32[]{:S(2)}, u32[]{:S(2)}) collective-permute-start(bf16[256,2048]{1,0:T(8,128)(2,1)} %get-tuple-element.284), channel_id=1, source_target_pairs={{0,16},{8,24},{16,0},{24,8},{1,17},{9,25},{17,1},{25,9},{2,18},{10... | collective-permute-start | bytes 3145736 | tf_op jit(solution)/shard_map/ppermute | solution.py:443
  27.0 486.1 %reduce-scatter.5.cloned.1.call-start = ((), (), s32[]{:S(2)}) async-start(), calls=%async_computation.11 | async-start | bytes 9437184 | tf_op jit(solution)/shard_map/reduce_scatter | solution.py:690
  97.0 52.4 %collective-permute-start.7 = (bf16[256,2048]{1,0:T(8,128)(2,1)}, bf16[256,2048]{1,0:T(8,128)(2,1)}, u32[]{:S(2)}, u32[]{:S(2)}) collective-permute-start(bf16[256,2048]{1,0:T(8,128)(2,1)} %get-tuple-element.136), channel_id=1, source_target_pairs={{0,16},{8,24},{16,0},{24,8},{1,17},{9,25},{17,1},{25,9},{2,18},{10... | collective-permute-start | bytes 3145736 | tf_op jit(solution)/shard_map/ppermute | solution.py:443
  97.4 52.1 %collective-permute-start.8 = (bf16[256,2048]{1,0:T(8,128)(2,1)}, bf16[256,2048]{1,0:T(8,128)(2,1)}, u32[]{:S(2)}, u32[]{:S(2)}) collective-permute-start(bf16[256,2048]{1,0:T(8,128)(2,1)} %get-tuple-element.136), channel_id=1, source_target_pairs={{0,8},{8,0},{16,24},{24,16},{1,9},{9,1},{17,25},{25,17},{2,10},{10... | collective-permute-start | bytes 3145736 | tf_op jit(solution)/shard_map/ppermute | solution.py:443
  99.0 50.4 %collective-permute-start.6 = (bf16[256,2048]{1,0:T(8,128)(2,1)S(1)}, bf16[256,2048]{1,0:T(8,128)(2,1)}, u32[]{:S(2)}, u32[]{:S(2)}) collective-permute-start(bf16[256,2048]{1,0:T(8,128)(2,1)S(1)} %get-tuple-element.137), channel_id=1, source_target_pairs={{0,8},{8,0},{16,24},{24,16},{1,9},{9,1},{17,25},{25,17},{2,10},{10... | collective-permute-start | bytes 3145736 | tf_op jit(solution)/shard_map/ppermute | solution.py:443
  99.4 50.1 %collective-permute-start.9 = (bf16[256,2048]{1,0:T(8,128)(2,1)S(1)}, bf16[256,2048]{1,0:T(8,128)(2,1)}, u32[]{:S(2)}, u32[]{:S(2)}) collective-permute-start(bf16[256,2048]{1,0:T(8,128)(2,1)S(1)} %get-tuple-element.137), channel_id=1, source_target_pairs={{0,16},{8,24},{16,0},{24,8},{1,17},{9,25},{17,1},{25,9},{2,18},{10... | collective-permute-start | bytes 3145736 | tf_op jit(solution)/shard_map/ppermute | solution.py:443
  191.7 49.5 %collective-permute-start.13 = (bf16[256,2048]{1,0:T(8,128)(2,1)}, bf16[256,2048]{1,0:T(8,128)(2,1)}, u32[]{:S(2)}, u32[]{:S(2)}) collective-permute-start(bf16[256,2048]{1,0:T(8,128)(2,1)} %get-tuple-element.278), channel_id=1, source_target_pairs={{0,8},{8,0},{16,24},{24,16},{1,9},{9,1},{17,25},{25,17},{2,10},{10... | collective-permute-start | bytes 3145736 | tf_op jit(solution)/shard_map/ppermute | solution.py:443
  193.8 46.6 %collective-permute-start.14 = (bf16[256,2048]{1,0:T(8,128)(2,1)}, bf16[256,2048]{1,0:T(8,128)(2,1)}, u32[]{:S(2)}, u32[]{:S(2)}) collective-permute-start(bf16[256,2048]{1,0:T(8,128)(2,1)} %get-tuple-element.277), channel_id=1, source_target_pairs={{0,8},{8,0},{16,24},{24,16},{1,9},{9,1},{17,25},{25,17},{2,10},{10... | collective-permute-start | bytes 3145736 | tf_op jit(solution)/shard_map/ppermute | solution.py:443
  194.4 53.9 %collective-permute-start.16 = (bf16[256,2048]{1,0:T(8,128)(2,1)}, bf16[256,2048]{1,0:T(8,128)(2,1)}, u32[]{:S(2)}, u32[]{:S(2)}) collective-permute-start(bf16[256,2048]{1,0:T(8,128)(2,1)} %get-tuple-element.277), channel_id=1, source_target_pairs={{0,16},{8,24},{16,0},{24,8},{1,17},{9,25},{17,1},{25,9},{2,18},{10... | collective-permute-start | bytes 3145736 | tf_op jit(solution)/shard_map/ppermute | solution.py:443
  221.6 77.6 %collective-permute-start.21 = (bf16[512,1024]{1,0:T(8,128)(2,1)S(1)}, bf16[512,1024]{1,0:T(8,128)(2,1)S(1)}, u32[]{:S(2)}, u32[]{:S(2)}) collective-permute-start(bf16[512,1024]{1,0:T(8,128)(2,1)S(1)} %copy.63), channel_id=1, source_target_pairs={{0,1},{1,0},{2,3},{3,2},{4,5},{5,4},{6,7},{7,6},{8,9},{9,8},{10,11... | collective-permute-start | bytes 3145736 | tf_op jit(solution)/shard_map/ppermute | solution.py:661
  331.8 263.6 %reduce-scatter.7.cloned.1.call-start = ((), (), s32[]{:S(2)}) async-start(), calls=%async_computation.12 | async-start | bytes 9437184 | tf_op jit(solution)/shard_map/reduce_scatter | solution.py:690
  437.5 201.6 %reduce-scatter.9.cloned.1.call-start = ((), (), s32[]{:S(2)}) async-start(), calls=%async_computation.13 | async-start | bytes 2359296 | tf_op jit(solution)/shard_map/reduce_scatter | solution.py:773
  437.6 48.8 %collective-permute-start.28 = (bf16[256,2048]{1,0:T(8,128)(2,1)}, bf16[256,2048]{1,0:T(8,128)(2,1)}, u32[]{:S(2)}, u32[]{:S(2)}) collective-permute-start(bf16[256,2048]{1,0:T(8,128)(2,1)} %get-tuple-element.178), channel_id=1, source_target_pairs={{0,8},{8,0},{16,24},{24,16},{1,9},{9,1},{17,25},{25,17},{2,10},{10... | collective-permute-start | bytes 3145736 | tf_op jit(solution)/shard_map/ppermute | solution.py:443
  438.4 48.8 %collective-permute-start.29 = (bf16[256,2048]{1,0:T(8,128)(2,1)S(1)}, bf16[256,2048]{1,0:T(8,128)(2,1)}, u32[]{:S(2)}, u32[]{:S(2)}) collective-permute-start(bf16[256,2048]{1,0:T(8,128)(2,1)S(1)} %get-tuple-element.179), channel_id=1, source_target_pairs={{0,16},{8,24},{16,0},{24,8},{1,17},{9,25},{17,1},{25,9},{2,18},{10... | collective-permute-start | bytes 3145736 | tf_op jit(solution)/shard_map/ppermute | solution.py:443
  511.7 63.7 %collective-permute-start.31 = (bf16[512,2048]{1,0:T(8,128)(2,1)}, bf16[512,2048]{1,0:T(8,128)(2,1)}, u32[]{:S(2)}, u32[]{:S(2)}) collective-permute-start(bf16[512,2048]{1,0:T(8,128)(2,1)} %pad_maximum_fusion.5), channel_id=1, source_target_pairs={{0,16},{8,24},{16,0},{24,8},{1,17},{9,25},{17,1},{25,9},{2,18},{10... | collective-permute-start | bytes 6291464 | tf_op jit(solution)/shard_map/ppermute | solution.py:443
  512.8 62.6 %collective-permute-start.30 = (bf16[512,2048]{1,0:T(8,128)(2,1)}, bf16[512,2048]{1,0:T(8,128)(2,1)}, u32[]{:S(2)}, u32[]{:S(2)}) collective-permute-start(bf16[512,2048]{1,0:T(8,128)(2,1)} %pad_maximum_fusion.4), channel_id=1, source_target_pairs={{0,8},{8,0},{16,24},{24,16},{1,9},{9,1},{17,25},{25,17},{2,10},{10... | collective-permute-start | bytes 6291464 | tf_op jit(solution)/shard_map/ppermute | solution.py:443
  543.8 47.6 %collective-permute-start.39 = (bf16[256,2048]{1,0:T(8,128)(2,1)S(1)}, bf16[256,2048]{1,0:T(8,128)(2,1)S(1)}, u32[]{:S(2)}, u32[]{:S(2)}) collective-permute-start(bf16[256,2048]{1,0:T(8,128)(2,1)S(1)} %pad_maximum_fusion.8), channel_id=1, source_target_pairs={{0,16},{8,24},{16,0},{24,8},{1,17},{9,25},{17,1},{25,9},{2,18},{10... | collective-permute-start | bytes 3145736 | tf_op jit(solution)/shard_map/ppermute | solution.py:443
  545.4 46.0 %collective-permute-start.38 = (bf16[256,2048]{1,0:T(8,128)(2,1)S(1)}, bf16[256,2048]{1,0:T(8,128)(2,1)}, u32[]{:S(2)}, u32[]{:S(2)}) collective-permute-start(bf16[256,2048]{1,0:T(8,128)(2,1)S(1)} %pad_maximum_fusion.7), channel_id=1, source_target_pairs={{0,8},{8,0},{16,24},{24,16},{1,9},{9,1},{17,25},{25,17},{2,10},{10... | collective-permute-start | bytes 3145736 | tf_op jit(solution)/shard_map/ppermute | solution.py:443
  595.3 131.4 %reduce-scatter.11.cloned.1.call-start = ((), (), s32[]{:S(2)}) async-start(), calls=%async_computation.14 | async-start | bytes 7077888 | tf_op jit(solution)/shard_map/reduce_scatter | solution.py:690
  (73 other events, 1453.3 us)
Sparse Core Ops, SparseCore 0:
  10.4 67.4 all-gather.4
  79.5 80.6 all-gather.6
  161.9 80.5 all-gather.8
  243.9 81.0 all-gather.10
  331.9 89.8 reduce-scatter.4
  437.6 89.6 reduce-scatter.6
  595.5 35.5 reduce-scatter.8
  649.7 76.9 reduce-scatter.10

commit v14 on v13

--- a/solution.py
+++ b/solution.py
@@ -403,39 +403,33 @@
     return low, full, jnp.sum(sums.reshape(3, 8, width), axis=1)
 
 
-def outer_kernel(left_ref, *refs, chunk):
-    right_refs, out_ref = refs[:-1], refs[-1]
+def outer_kernel(left_ref, right_ref, out_ref, *, chunk):
+    left = left_ref[...]
     shards = out_ref.shape[0]
     for at in range(0, out_ref.shape[3], chunk):
         columns = slice(at, at + chunk)
-        made, row = None, 0
-        for right_ref in right_refs:
-            count = right_ref.shape[0]
-            part = contract_first(left_ref[row : row + count, :], right_ref[:, columns])
-            made = part if made is None else made + part
-            row += count
-        out_ref[:, 0, :, columns] = made.astype(out_ref.dtype).reshape(shards, -1, made.shape[1])
-
-
-def outer(left, rights, groups, shards):
-    rights = rights if isinstance(rights, (list, tuple)) else [rights]
+        made = contract_first(left, right_ref[:, columns]).astype(out_ref.dtype)
+        out_ref[:, 0, :, columns] = made.reshape(shards, -1, made.shape[1])
+
+
+def outer(left, right, groups, shards, part_of=(0, 1)):
+    at, parts = part_of
     tokens, rows = left.shape
-    width = rights[0].shape[1]
+    width = right.shape[1] // parts
     part = rows // groups
     made = pl.pallas_call(
-        partial(outer_kernel, chunk=512 if width % 512 == 0 else 256),
+        partial(outer_kernel, chunk=next(c for c in (512, 384, 256, 128) if width % c == 0)),
         grid=(groups,),
-        in_specs=[pl.BlockSpec((tokens, part), lambda i: (0, i))]
-        + [
-            pl.BlockSpec((right.shape[0], width), lambda i: (0, 0), pipeline_mode=pl.Buffered(1))
-            for right in rights
+        in_specs=[
+            pl.BlockSpec((tokens, part), lambda i: (0, i)),
+            pl.BlockSpec((tokens, width), lambda i: (0, at), pipeline_mode=pl.Buffered(1)),
         ],
         out_specs=pl.BlockSpec((shards, 1, part // shards, width), lambda i: (0, i, 0, 0)),
         out_shape=jax.ShapeDtypeStruct((shards, groups, part // shards, width), jnp.bfloat16),
         compiler_params=pltpu.CompilerParams(vmem_limit_bytes=GRANT),
         cost_estimate=estimate(2 * tokens * rows * width, 0),
         name="outer",
-    )(left, *rights)
+    )(left, right)
     return made.reshape(rows, width)
 
 
@@ -683,8 +677,8 @@
     mixed_half = order(lambda *parts: jnp.concatenate(parts, axis=0), mine, theirs)
     upstream = order.complete(upstream_made, upstream)
 
-    def slab_product(left, right):
-        return order(lambda rows: outer(rows, right, groups, shards), left)
+    def slab_product(left, right, part_of=(0, 1)):
+        return order(lambda rows, others: outer(rows, others, groups, shards, part_of), left, right)
 
     def slab_sum(made):
         return lax.psum_scatter(made, "fsdp", scatter_dimension=0, tiled=True)
@@ -740,49 +734,60 @@
     mixed_grad = exchange(by_index([mixed_grad[:, j * slab : (j + 1) * slab] for j in range(groups)], me))
     if square:
         result_rest = order(lambda rows: product_of(rows, down_slab, 3 * count), active)
+        order.after(*mixed_grad)
         result_came = order.add_far(result_rest, result_far, None)
+    attention = (mask, slopes, qkv, log_totals, attended)
+    order.after(down_sum)
+    begun = order(
+        lambda *grads: attend_backward(*attention, grads, seq_count, local_len, 0, pairs // 2), *mixed_grad
+    )
     branch_other = pair_swap(branch_grad)
     branch_pair = jnp.concatenate([branch_grad, branch_other], axis=0)
     out_sum = order(lambda columns: outer(columns, branch_pair, groups, 1), mixed_half)
-    attention = (mask, slopes, qkv, log_totals, attended)
     if square:
         part = out_sum.shape[0] // 4
         out_far = out_sum[3 * part : 3 * part + part // 2], out_sum[3 * part + part // 2 :]
-        out_far = swap_far(gate(out_far, *mixed_grad))
-    order.after(down_sum)
-    begun = order(
-        lambda *grads: attend_backward(*attention, grads, seq_count, local_len, 0, pairs // 2), *mixed_grad
+        out_far = swap_far(out_far)
+    first_sum = slab_product(normed, begun, (0, 2))
+    if square:
+        first_sum = gate(first_sum, *result_came)
+        order.after(*result_came)
+    first_sum = slab_sum(first_sum)
+    qkv_grad = order(
+        lambda begun, *grads: attend_backward(
+            *attention, grads, seq_count, local_len, pairs // 2, pairs, begun
+        ),
+        begun,
+        *mixed_grad,
     )
     if square:
         out_came = order.add_far(out_sum, out_far, None, at=part)
-    qkv_grad = order(
-        lambda *grads: attend_backward(*attention, grads, seq_count, local_len, pairs // 2, pairs, begun),
-        *mixed_grad,
-    )
-    if square:
-        order.after(*out_came, *result_came)
-        out_sum = order(lambda own, *came: summed(own[:part], came).astype(low), out_sum, *out_came)
-        order.after(*out_came)
     else:
         out_sum = lax.psum_scatter(out_sum, "seq", scatter_dimension=0, tiled=True)
+    order.after(up_sum)
+    if square:
+        far = swap_far(order.halves(slots(to_normed, 3, 4), qkv_grad))
+        order.after(first_sum)
+        near = order(slots(to_normed, 1, 3), qkv_grad)
+        direct = swap_direct(near, half)
+        order.after(*out_came)
+        out_sum = order(lambda own, *came: summed(own[:part], came).astype(low), out_sum, *out_came)
     out_sum = out_sum.reshape(-1, 1, out_rows, model_width)
     zero = jnp.zeros_like(out_sum)
     out_sum = jnp.concatenate(
         [jnp.where(parity == 0, out_sum, zero), jnp.where(parity == 1, out_sum, zero)], axis=1
     ).reshape(-1, model_width)
+    if square:
+        out_sum = gate(out_sum, *far)
     grad_w_out = lax.psum_scatter(out_sum, "fsdp", scatter_dimension=0, tiled=True).astype(wide)
-    order.after(up_sum)
-    if square:
-        far = swap_far(order.halves(slots(to_normed, 3, 4), qkv_grad))
-        near = order(slots(to_normed, 1, 3), qkv_grad)
-        direct = swap_direct(near, half)
-        qkv_sum = slab_sum(gate(slab_product(normed, qkv_grad), *far, *direct, grad_w_out))
+    second_sum = slab_product(normed, qkv_grad, (1, 2))
+    if square:
+        second_sum = slab_sum(gate(second_sum, *far, *direct, grad_w_out))
         came = order.add_far(near, far, direct)
         down_slabs = slabs_of_rows(gate(down_sum, *came))
         normed_own = order(slots(to_normed, 0, 1), qkv_grad)
     else:
-        down_slabs = slabs_of_rows(down_sum)
-        qkv_sum = slab_sum(slab_product(normed, qkv_grad))
+        second_sum, down_slabs = slab_sum(second_sum), slabs_of_rows(down_sum)
         normed_own, came = scatter(to_normed, qkv_grad), ()
     if square:
         result = order(
@@ -799,14 +804,18 @@
     )
     grad_tokens = grad_tokens.reshape(tokens.shape)
     up_slabs = slabs_of_rows(gate(up_sum, *came, normed_own))
-    qkv_slabs = slabs_of_rows(qkv_sum)
+    first_slabs = slabs_of_rows(gate(first_sum, *came, normed_own))
+    second_slabs = slabs_of_rows(second_sum)
 
     def rows_of(slabs):
         return jnp.swapaxes(slabs, 0, 1).astype(wide)
 
     grad_w_down = rows_of(down_slabs).reshape(-1, hidden_width).T
     grad_w_up = rows_of(up_slabs).reshape(-1, hidden_width)
-    grad_w_qkv = rows_of(qkv_slabs).reshape(-1, groups, pairs, 3, PAIR)
+    grad_w_qkv = [
+        rows_of(part).reshape(-1, groups, pairs // 2, 3, PAIR) for part in (first_slabs, second_slabs)
+    ]
+    grad_w_qkv = jnp.concatenate(grad_w_qkv, axis=2)
     grad_w_qkv = jnp.transpose(grad_w_qkv, (0, 3, 1, 2, 4)).reshape(-1, 3 * model_width)
 
     head_sum = jnp.transpose(qkv_column_sum.reshape(pairs, 3, PAIR), (1, 0, 2)).reshape(3, slab)
@@ -820,7 +829,7 @@
         others = range(lax.axis_size(axis))
         came = [lax.ppermute(sums, axis, [(i, i ^ mask) for i in others]) for mask in masks]
         if (axis, masks) == stages[-1]:
-            order.after(down_slabs, up_slabs, qkv_slabs)
+            order.after(down_slabs, up_slabs, first_slabs, second_slabs)
         sums = order(lambda *parts: sum(parts[1:], parts[0]), sums, *came)
     sums = sums.reshape(-1)
 

time: 762 us -> 775 us (1.017)
  Pallas kernels: 272 us -> 280 us
  local copies, waits for them, and re-layouts: 99.3 us -> 91.5 us
    reduce_scatter x1, waiting for transfers between devices: 0.02 us -> 18.9 us  [local(): lax.psum_scatter(out_sum, 'fsdp', scatter_dimension=0, tiled=True)]
    ppermute x7, waiting for transfers between devices: 15.2 us -> 1.3 us  [local(): lax.ppermute(sums, axis, [(i, i ^ mask) for i in others])]
    pallas_call x4 -> x5, Pallas kernels: 74.3 us -> 81.7 us  [outer(): pl.pallas_call(partial(outer_kernel, chunk=next((c for c in (512, 384, 25...]
    unnamed x98 -> x96, local copies, waits for them, and re-layouts: 44 us -> 41.1 us
  transfers between devices with their start and end apart: 64 -> 66, of which waited for: 23 -> 23; matrix products, arithmetic and copies ran while one was open for 29% -> 29% of each run, Pallas kernels for 36% -> 36%
where the time goes in v14:
time: 775 us; the launch traced here: 765 us
  Pallas kernels  280 us (36%)
  waiting for transfers between devices  170 us (22%)
  local copies, waits for them, and re-layouts  91.5 us (12%)
  matrix products  85.6 us (11%)
  starting transfers between devices  73.1 us (9%)
  other arithmetic  49.6 us (6%)
  between operations  14.9 us (2%)
    ppermute x44, waiting for transfers between devices, swap(): return lax.ppermute(values, 'seq', [(i, i ^ bit) for i in range(4)])  136 us
    pallas_call x5, Pallas kernels, outer(): pl.pallas_call(partial(outer_kernel, chunk=next((c for c in (512, 384, 25...  81.7 us
    pallas_call x2, Pallas kernels, attend_backward(): pl.pallas_call(partial(attend_backward_kernel, blocks=blocks, seqs=seqs,...  57.6 us
    dot_general x5, matrix products, contract_last(): lax.dot_general(left_side, right_side, (((1,), (1,)), ((), ())), preferre...  52.7 us
    ppermute x44, starting transfers between devices, swap(): return lax.ppermute(values, 'seq', [(i, i ^ bit) for i in range(4)])  48.4 us
    unnamed x96, local copies, waits for them, and re-layouts  41.1 us
    dot_general x3, matrix products, contract(): lax.dot_general(left_side, right_side, (((1,), (0,)), ((), ())), preferre...  32.9 us
    pallas_call x1, Pallas kernels, up_and_bend(): pl.pallas_call(partial(up_kernel, chunk=512), grid=(count // TILE,), in_s...  30.6 us
  transfers between devices with their start and end apart: 66, of which 23 were waited for; matrix products, arithmetic and copies ran while one was open for 29% of the time, Pallas kernels for 36%

profile of v14, /device:TPU:0, one launch (start us, length us, event | category | flops | bytes accessed | tf_op | source)
XLA Modules:
  0.0 765.2 jit_solution(11308878004881669278)
XLA Ops:
  28.2 18.7 %collective-permute-done.2 = bf16[256,2048]{1,0:T(8,128)(2,1)} collective-permute-done((bf16[256,2048]{1,0:T(8,128)(2,1)}, bf16[256,2048]{1,0:T(8,128)(2,1)}, u32[]{:S(2)}, u32[]{:S(2)}) %collective-permute-start.2) | collective-permute-done | bytes 1048608 | tf_op jit(solution)/shard_map/ppermute | solution.py:437
  53.7 17.7 %collective-permute-done = bf16[256,2048]{1,0:T(8,128)(2,1)} collective-permute-done((bf16[256,2048]{1,0:T(8,128)(2,1)}, bf16[256,2048]{1,0:T(8,128)(2,1)}, u32[]{:S(2)}, u32[]{:S(2)}) %collective-permute-start) | collective-permute-done | bytes 1048608 | tf_op jit(solution)/shard_map/ppermute | solution.py:437
  79.6 12.8 %collective-permute-done.4 = bf16[256,2048]{1,0:T(8,128)(2,1)} collective-permute-done((bf16[256,2048]{1,0:T(8,128)(2,1)}, bf16[256,2048]{1,0:T(8,128)(2,1)}, u32[]{:S(2)}, u32[]{:S(2)}) %collective-permute-start.4) | collective-permute-done | bytes 1048608 | tf_op jit(solution)/shard_map/ppermute | solution.py:437
  101.1 18.6 %add_convert_fusion.qkv_ref = bf16[2048,1536]{1,0:T(8,128)(2,1)} fusion(bf16[2048,2048]{1,0:T(8,128)(2,1)} %constant_dynamic-update-slice_fusion.left_ref, bf16[2048,1536]{1,0:T(8,128)(2,1)} %all-gather.5.cloned.1.call-done, f32[1536]{0:T(1024)S(1)} %reduce.2), kind=kOutput, calls=%fused_computation.1 | convolution fusion | flops 12891193344 | bytes 20977664 | tf_op jit(solution)/shard_map/dot_general | solution.py:31
  119.7 29.7 %attend_forward.1 = (bf16[2048,512]{1,0:T(8,128)(2,1)}, f32[2048,512]{1,0:T(8,128)}) custom-call(s32[1]{0:T(128)} %bitcast.1.at_ref.mask_ref, f32[8]{0:T(128)} %multiply_power_fusion.slope_ref, bf16[2048,1536]{1,0:T(8,128)(2,1)} %add_convert_fusion.qkv_ref), custom_call_target="tpu_custom_call" | custom-call | flops 2684354560 | bytes 2621440 | tf_op jit(solution)/shard_map/attend_forward/pallas_call | solution.py:173
  156.8 11.2 %collective-permute-done.10 = bf16[512,512]{1,0:T(8,128)(2,1)S(1)} collective-permute-done((bf16[512,512]{1,0:T(8,128)(2,1)}, bf16[512,512]{1,0:T(8,128)(2,1)S(1)}, u32[]{:S(2)}, u32[]{:S(2)}) %collective-permute-start.10) | collective-permute-done | bytes 524320 | tf_op jit(solution)/shard_map/ppermute | solution.py:437
  221.7 18.7 %collective-permute-done.14 = bf16[256,2048]{1,0:T(8,128)(2,1)} collective-permute-done((bf16[256,2048]{1,0:T(8,128)(2,1)}, bf16[256,2048]{1,0:T(8,128)(2,1)}, u32[]{:S(2)}, u32[]{:S(2)}) %collective-permute-start.14) | collective-permute-done | bytes 1048608 | tf_op jit(solution)/shard_map/ppermute | solution.py:437
  250.8 11.3 %collective-permute-done.17 = bf16[256,2048]{1,0:T(8,128)(2,1)} collective-permute-done((bf16[256,2048]{1,0:T(8,128)(2,1)}, bf16[256,2048]{1,0:T(8,128)(2,1)}, u32[]{:S(2)}, u32[]{:S(2)}) %collective-permute-start.17) | collective-permute-done | bytes 1048608 | tf_op jit(solution)/shard_map/ppermute | solution.py:437
  268.6 30.6 %up_and_bend.1 = (bf16[2048,2048]{1,0:T(8,128)(2,1)}, f32[2048,2048]{1,0:T(8,128)}) custom-call(bf16[2048,2048]{1,0:T(8,128)(2,1)} %constant_dynamic-update-slice_fusion.7.rows_ref.left_ref, bf16[2048,2048]{1,0:T(8,128)(2,1)} %all-gather.9.cloned.1.call-done.weight_ref, f32[1,2048]{1,0:T(1,128)} %bitcast.156), custom_call_target="tpu_custom_call" | custom-call | flops 8589934592 | bytes 8388608 | tf_op jit(solution)/shard_map/up_and_bend/pallas_call | solution.py:259
  308.2 23.5 %outer.5 = bf16[8,4,64,2048]{3,2,1,0:T(8,128)(2,1)} custom-call(bf16[2048,2048]{1,0:T(8,128)(2,1)} %constant_dynamic-update-slice_fusion.31.left_ref.rows_ref, bf16[2048,2048]{1,0:T(8,128)(2,1)} %get-tuple-element.186.right_ref.rows_ref), custom_call_target="tpu_custom_call" | custom-call | flops 4294967296 | bytes 4194304 | tf_op jit(solution)/shard_map/outer/pallas_call | solution.py:420
  331.8 25.6 %hidden_gradient.1 = (bf16[2048,2048]{1,0:T(8,128)(2,1)}, f32[1,2048]{1,0:T(1,128)}) custom-call(bf16[2048,2048]{1,0:T(8,128)(2,1)} %constant_dynamic-update-slice_fusion.31.left_ref.rows_ref, bf16[2048,2048]{1,0:T(8,128)(2,1)} %all-gather.11.cloned.1.call-done.weight_ref, f32[2048,2048]{1,0:T(8,128)} %get-tuple-element.157.slope_ref), custom_call_target="tpu_custom_call" | custom-call | flops 6442450944 | bytes 6291456 | tf_op jit(solution)/shard_map/hidden_gradient/pallas_call | solution.py:283
  369.3 18.1 %convolution_convert_fusion.own_ref = bf16[1536,2048]{1,0:T(8,128)(2,1)S(1)} fusion(bf16[2048,2048]{1,0:T(8,128)(2,1)} %all-gather.9.cloned.1.call-done.weight_ref, bf16[2048,2048]{1,0:T(8,128)(2,1)} %get-tuple-element.176.right_ref), kind=kOutput, calls=%fused_computation.2 | convolution fusion | flops 12888047616 | bytes 20971520 | tf_op jit(solution)/shard_map/dot_general | solution.py:37
  406.0 23.6 %outer.6 = bf16[8,4,64,2048]{3,2,1,0:T(8,128)(2,1)} custom-call(bf16[2048,2048]{1,0:T(8,128)(2,1)} %constant_dynamic-update-slice_fusion.7.rows_ref.left_ref, bf16[2048,2048]{1,0:T(8,128)(2,1)} %get-tuple-element.176.right_ref), custom_call_target="tpu_custom_call" | custom-call | flops 4294967296 | bytes 4194304 | tf_op jit(solution)/shard_map/outer/pallas_call | solution.py:420
  440.8 11.0 %norm_back.2 = (bf16[512,2048]{1,0:T(8,128)(2,1)}, f32[512,2048]{1,0:T(8,128)}, f32[24,2048]{1,0:T(8,128)}) custom-call(bf16[1536,2048]{1,0:T(8,128)(2,1)} %copy-done.5, f32[512,2048]{1,0:T(8,128)} %copy-done, f32[512,1]{1,0:T(8,128)} %copy.65.average_ref, f32[512,1]{1,0:T(8,128)} %copy.66.scale_ref, bf16[512,2048]{1,0:T(8,128)(2,1)} %bitcast.111, ...), custom_call_target="tpu_custom_call" | custom-call | flops 7864320 | bytes 7680 | tf_op jit(solution)/shard_map/norm_back/pallas_call | solution.py:388
  452.9 8.9 %mixed_gradient.1 = bf16[512,2048]{1,0:T(8,128)(2,1)} custom-call(bf16[512,2048]{1,0:T(8,128)(2,1)} %get-tuple-element.185.rows_ref, bf16[2048,2048]{1,0:T(8,128)(2,1)} %all-gather.7.cloned.1.call-done.weight_ref), custom_call_target="tpu_custom_call" | custom-call | flops 1073741824 | bytes 1048576 | tf_op jit(solution)/shard_map/mixed_gradient/pallas_call | solution.py:330
  468.5 18.9 %product.1 = bf16[1536,2048]{1,0:T(8,128)(2,1)} custom-call(bf16[2048,2048]{1,0:T(8,128)(2,1)} %get-tuple-element.186.right_ref.rows_ref, bf16[2048,2048]{1,0:T(8,128)(2,1)} %all-gather.11.cloned.1.call-done.weight_ref), custom_call_target="tpu_custom_call" | custom-call | flops 3221225472 | bytes 3145728 | tf_op jit(solution)/shard_map/product/pallas_call | solution.py:308
  501.2 28.4 %attend_backward.2.right_ref.rest_4_ = bf16[2048,1536]{1,0:T(8,128)(2,1)} custom-call(s32[1]{0:T(128)} %bitcast.1.at_ref.mask_ref, f32[8]{0:T(128)} %multiply_power_fusion.slope_ref, bf16[2048,1536]{1,0:T(8,128)(2,1)} %add_convert_fusion.qkv_ref, f32[2048,512]{1,0:T(8,128)} %get-tuple-element.139.lse_ref, bf16[2048,512]{1,0:T(8,128)(2,1)} %get-tuple-element.138.mixed_ref, ...), custom_call_target="tpu_custom_call" | custom-call | flops 3355443200 | bytes 3276800 | tf_op jit(solution)/shard_map/attend_backward/pallas_call | solution.py:198
  538.2 12.9 %outer.8 = bf16[8,4,64,768]{3,2,1,0:T(8,128)(2,1)} custom-call(bf16[2048,2048]{1,0:T(8,128)(2,1)} %constant_dynamic-update-slice_fusion.left_ref, bf16[2048,1536]{1,0:T(8,128)(2,1)} %attend_backward.2.right_ref.rest_4_), custom_call_target="tpu_custom_call" | custom-call | flops 1610612736 | bytes 1572864 | tf_op jit(solution)/shard_map/outer/pallas_call | solution.py:420
  555.5 29.3 %attend_backward.3.right_ref = bf16[2048,1536]{1,0:T(8,128)(2,1)} custom-call(s32[1]{0:T(128)} %bitcast.1.at_ref.mask_ref, f32[8]{0:T(128)} %multiply_power_fusion.slope_ref, bf16[2048,1536]{1,0:T(8,128)(2,1)} %add_convert_fusion.qkv_ref, f32[2048,512]{1,0:T(8,128)} %get-tuple-element.139.lse_ref, ...), custom_call_target="tpu_custom_call", output_to_operand_aliasing={{}: (9, {})} | custom-call | flops 3355443200 | bytes 3276800 | tf_op jit(solution)/shard_map/attend_backward/pallas_call | solution.py:198
  597.9 11.1 %convolution_convert_fusion.1 = bf16[1024,2048]{1,0:T(8,128)(2,1)} fusion(bf16[2048,1536]{1,0:T(8,128)(2,1)} %all-gather.5.cloned.1.call-done, bf16[2048,1536]{1,0:T(8,128)(2,1)} %attend_backward.3.right_ref), kind=kOutput, calls=%fused_computation.19 | convolution fusion | flops 6444548096 | bytes 13631488 | tf_op jit(solution)/shard_map/dot_general | solution.py:37
  616.9 14.5 %collective-permute-done.38 = bf16[256,2048]{1,0:T(8,128)(2,1)S(1)} collective-permute-done((bf16[256,2048]{1,0:T(8,128)(2,1)}, bf16[256,2048]{1,0:T(8,128)(2,1)S(1)}, u32[]{:S(2)}, u32[]{:S(2)}) %collective-permute-start.38) | collective-permute-done | bytes 1048608 | tf_op jit(solution)/shard_map/ppermute | solution.py:437
  635.7 13.1 %outer.9 = bf16[8,4,64,768]{3,2,1,0:T(8,128)(2,1)} custom-call(bf16[2048,2048]{1,0:T(8,128)(2,1)} %constant_dynamic-update-slice_fusion.left_ref, bf16[2048,1536]{1,0:T(8,128)(2,1)} %attend_backward.3.right_ref), custom_call_target="tpu_custom_call" | custom-call | flops 1610612736 | bytes 1572864 | tf_op jit(solution)/shard_map/outer/pallas_call | solution.py:420
  648.8 18.9 %reduce-scatter.12.cloned.1.call-done = bf16[64,2048]{1,0:T(8,128)(2,1)} async-done(((bf16[512,2048]{1,0:T(8,128)(2,1)}), bf16[64,2048]{1,0:T(8,128)(2,1)}) %reduce-scatter.12.cloned.1.call-update) | async-done | bytes 262160 | tf_op jit(solution)/shard_map/reduce_scatter | solution.py:782
  701.4 10.9 %norm_back.3 = (bf16[512,2048]{1,0:T(8,128)(2,1)}, f32[512,2048]{1,0:T(8,128)}, f32[24,2048]{1,0:T(8,128)}) custom-call(bf16[512,2048]{1,0:T(8,128)(2,1)} %convolution_convert_fusion.2.own_ref, bf16[512,2048]{1,0:T(8,128)(2,1)} %bitcast.107, f32[512,1]{1,0:T(8,128)} %bitcast.132, f32[512,1]{1,0:T(8,128)} %bitcast.131, ...), custom_call_target="tpu_custom_call" | custom-call | flops 7864320 | bytes 7680 | tf_op jit(solution)/shard_map/norm_back/pallas_call | solution.py:388
  (328 shorter events, 312.3 us)
Async XLA Ops:
  7.2 93.9 %all-gather.5.cloned.1.call-start = ((), (), s32[]{:S(2)}) async-start(), calls=%async_computation.9 | async-start | bytes 7077888 | tf_op jit(solution)/shard_map/all_gather | solution.py:629
  10.3 170.0 %all-gather.7.cloned.1.call-start = ((), (), s32[]{:S(2)}) async-start(), calls=%async_computation.10 | async-start | bytes 9437184 | tf_op jit(solution)/shard_map/all_gather | solution.py:641
  11.1 257.5 %all-gather.9.cloned.1.call-start = ((), (), s32[]{:S(2)}) async-start(), calls=%async_computation.11 | async-start | bytes 9437184 | tf_op jit(solution)/shard_map/all_gather | solution.py:642
  19.5 312.3 %all-gather.11.cloned.1.call-start = ((), (), s32[]{:S(2)}) async-start(), calls=%async_computation.12 | async-start | bytes 9437184 | tf_op jit(solution)/shard_map/all_gather | solution.py:643
  24.0 47.4 %collective-permute-start = (bf16[256,2048]{1,0:T(8,128)(2,1)}, bf16[256,2048]{1,0:T(8,128)(2,1)}, u32[]{:S(2)}, u32[]{:S(2)}) collective-permute-start(bf16[256,2048]{1,0:T(8,128)(2,1)} %get-tuple-element.299), channel_id=1, source_target_pairs={{0,8},{8,0},{16,24},{24,16},{1,9},{9,1},{17,25},{25,17},{2,10},{10... | collective-permute-start | bytes 3145736 | tf_op jit(solution)/shard_map/ppermute | solution.py:437
  24.6 52.7 %collective-permute-start.3 = (bf16[256,2048]{1,0:T(8,128)(2,1)}, bf16[256,2048]{1,0:T(8,128)(2,1)}, u32[]{:S(2)}, u32[]{:S(2)}) collective-permute-start(bf16[256,2048]{1,0:T(8,128)(2,1)} %get-tuple-element.298), channel_id=1, source_target_pairs={{0,16},{8,24},{16,0},{24,8},{1,17},{9,25},{17,1},{25,9},{2,18},{10... | collective-permute-start | bytes 3145736 | tf_op jit(solution)/shard_map/ppermute | solution.py:437
  26.9 474.2 %reduce-scatter.6.cloned.1.call-start = ((), (), s32[]{:S(2)}) async-start(), calls=%async_computation.13 | async-start | bytes 9437184 | tf_op jit(solution)/shard_map/reduce_scatter | solution.py:684
  46.8 45.6 %collective-permute-start.4 = (bf16[256,2048]{1,0:T(8,128)(2,1)}, bf16[256,2048]{1,0:T(8,128)(2,1)}, u32[]{:S(2)}, u32[]{:S(2)}) collective-permute-start(bf16[256,2048]{1,0:T(8,128)(2,1)} %collective-permute-done.2), channel_id=1, source_target_pairs={{0,8},{8,0},{16,24},{24,16},{1,9},{9,1},{17,25},{25,17},{2,10},{10... | collective-permute-start | bytes 3145736 | tf_op jit(solution)/shard_map/ppermute | solution.py:437
  97.0 52.4 %collective-permute-start.7 = (bf16[256,2048]{1,0:T(8,128)(2,1)}, bf16[256,2048]{1,0:T(8,128)(2,1)}, u32[]{:S(2)}, u32[]{:S(2)}) collective-permute-start(bf16[256,2048]{1,0:T(8,128)(2,1)} %get-tuple-element.143), channel_id=1, source_target_pairs={{0,16},{8,24},{16,0},{24,8},{1,17},{9,25},{17,1},{25,9},{2,18},{10... | collective-permute-start | bytes 3145736 | tf_op jit(solution)/shard_map/ppermute | solution.py:437
  97.4 52.1 %collective-permute-start.8 = (bf16[256,2048]{1,0:T(8,128)(2,1)}, bf16[256,2048]{1,0:T(8,128)(2,1)}, u32[]{:S(2)}, u32[]{:S(2)}) collective-permute-start(bf16[256,2048]{1,0:T(8,128)(2,1)} %get-tuple-element.143), channel_id=1, source_target_pairs={{0,8},{8,0},{16,24},{24,16},{1,9},{9,1},{17,25},{25,17},{2,10},{10... | collective-permute-start | bytes 3145736 | tf_op jit(solution)/shard_map/ppermute | solution.py:437
  99.0 50.4 %collective-permute-start.6 = (bf16[256,2048]{1,0:T(8,128)(2,1)S(1)}, bf16[256,2048]{1,0:T(8,128)(2,1)}, u32[]{:S(2)}, u32[]{:S(2)}) collective-permute-start(bf16[256,2048]{1,0:T(8,128)(2,1)S(1)} %get-tuple-element.144), channel_id=1, source_target_pairs={{0,8},{8,0},{16,24},{24,16},{1,9},{9,1},{17,25},{25,17},{2,10},{10... | collective-permute-start | bytes 3145736 | tf_op jit(solution)/shard_map/ppermute | solution.py:437
  99.4 50.1 %collective-permute-start.9 = (bf16[256,2048]{1,0:T(8,128)(2,1)S(1)}, bf16[256,2048]{1,0:T(8,128)(2,1)}, u32[]{:S(2)}, u32[]{:S(2)}) collective-permute-start(bf16[256,2048]{1,0:T(8,128)(2,1)S(1)} %get-tuple-element.144), channel_id=1, source_target_pairs={{0,16},{8,24},{16,0},{24,8},{1,17},{9,25},{17,1},{25,9},{2,18},{10... | collective-permute-start | bytes 3145736 | tf_op jit(solution)/shard_map/ppermute | solution.py:437
  191.7 49.5 %collective-permute-start.13 = (bf16[256,2048]{1,0:T(8,128)(2,1)}, bf16[256,2048]{1,0:T(8,128)(2,1)}, u32[]{:S(2)}, u32[]{:S(2)}) collective-permute-start(bf16[256,2048]{1,0:T(8,128)(2,1)} %get-tuple-element.292), channel_id=1, source_target_pairs={{0,8},{8,0},{16,24},{24,16},{1,9},{9,1},{17,25},{25,17},{2,10},{10... | collective-permute-start | bytes 3145736 | tf_op jit(solution)/shard_map/ppermute | solution.py:437
  193.8 46.6 %collective-permute-start.14 = (bf16[256,2048]{1,0:T(8,128)(2,1)}, bf16[256,2048]{1,0:T(8,128)(2,1)}, u32[]{:S(2)}, u32[]{:S(2)}) collective-permute-start(bf16[256,2048]{1,0:T(8,128)(2,1)} %get-tuple-element.291), channel_id=1, source_target_pairs={{0,8},{8,0},{16,24},{24,16},{1,9},{9,1},{17,25},{25,17},{2,10},{10... | collective-permute-start | bytes 3145736 | tf_op jit(solution)/shard_map/ppermute | solution.py:437
  194.4 53.9 %collective-permute-start.16 = (bf16[256,2048]{1,0:T(8,128)(2,1)}, bf16[256,2048]{1,0:T(8,128)(2,1)}, u32[]{:S(2)}, u32[]{:S(2)}) collective-permute-start(bf16[256,2048]{1,0:T(8,128)(2,1)} %get-tuple-element.291), channel_id=1, source_target_pairs={{0,16},{8,24},{16,0},{24,8},{1,17},{9,25},{17,1},{25,9},{2,18},{10... | collective-permute-start | bytes 3145736 | tf_op jit(solution)/shard_map/ppermute | solution.py:437
  221.6 77.5 %collective-permute-start.21 = (bf16[512,1024]{1,0:T(8,128)(2,1)S(1)}, bf16[512,1024]{1,0:T(8,128)(2,1)S(1)}, u32[]{:S(2)}, u32[]{:S(2)}) collective-permute-start(bf16[512,1024]{1,0:T(8,128)(2,1)S(1)} %copy.63), channel_id=1, source_target_pairs={{0,1},{1,0},{2,3},{3,2},{4,5},{5,4},{6,7},{7,6},{8,9},{9,8},{10,11... | collective-permute-start | bytes 3145736 | tf_op jit(solution)/shard_map/ppermute | solution.py:655
  331.7 255.6 %reduce-scatter.8.cloned.1.call-start = ((), (), s32[]{:S(2)}) async-start(), calls=%async_computation.14 | async-start | bytes 9437184 | tf_op jit(solution)/shard_map/reduce_scatter | solution.py:684
  437.4 160.4 %reduce-scatter.10.cloned.1.call-start = ((), (), s32[]{:S(2)}) async-start(), calls=%async_computation.15 | async-start | bytes 3538944 | tf_op jit(solution)/shard_map/reduce_scatter | solution.py:684
  437.5 51.8 %collective-permute-start.28 = (bf16[256,2048]{1,0:T(8,128)(2,1)S(1)}, bf16[256,2048]{1,0:T(8,128)(2,1)}, u32[]{:S(2)}, u32[]{:S(2)}) collective-permute-start(bf16[256,2048]{1,0:T(8,128)(2,1)S(1)} %get-tuple-element.187), channel_id=1, source_target_pairs={{0,8},{8,0},{16,24},{24,16},{1,9},{9,1},{17,25},{25,17},{2,10},{10... | collective-permute-start | bytes 3145736 | tf_op jit(solution)/shard_map/ppermute | solution.py:437
  438.3 51.0 %collective-permute-start.29 = (bf16[256,2048]{1,0:T(8,128)(2,1)S(1)}, bf16[256,2048]{1,0:T(8,128)(2,1)}, u32[]{:S(2)}, u32[]{:S(2)}) collective-permute-start(bf16[256,2048]{1,0:T(8,128)(2,1)S(1)} %get-tuple-element.188), channel_id=1, source_target_pairs={{0,16},{8,24},{16,0},{24,8},{1,17},{9,25},{17,1},{25,9},{2,18},{10... | collective-permute-start | bytes 3145736 | tf_op jit(solution)/shard_map/ppermute | solution.py:437
  494.9 56.2 %collective-permute-start.34 = (bf16[512,2048]{1,0:T(8,128)(2,1)S(1)}, bf16[512,2048]{1,0:T(8,128)(2,1)}, u32[]{:S(2)}, u32[]{:S(2)}) collective-permute-start(bf16[512,2048]{1,0:T(8,128)(2,1)S(1)} %pad_maximum_fusion.5), channel_id=1, source_target_pairs={{0,16},{8,24},{16,0},{24,8},{1,17},{9,25},{17,1},{25,9},{2,18},{10... | collective-permute-start | bytes 6291464 | tf_op jit(solution)/shard_map/ppermute | solution.py:437
  497.5 53.6 %collective-permute-start.33 = (bf16[512,2048]{1,0:T(8,128)(2,1)}, bf16[512,2048]{1,0:T(8,128)(2,1)}, u32[]{:S(2)}, u32[]{:S(2)}) collective-permute-start(bf16[512,2048]{1,0:T(8,128)(2,1)} %pad_maximum_fusion.4), channel_id=1, source_target_pairs={{0,8},{8,0},{16,24},{24,16},{1,9},{9,1},{17,25},{25,17},{2,10},{10... | collective-permute-start | bytes 6291464 | tf_op jit(solution)/shard_map/ppermute | solution.py:437
  551.2 116.5 %reduce-scatter.12.cloned.1.call-start = ((), (), s32[]{:S(2)}) async-start(), calls=%async_computation.16 | async-start | bytes 2359296 | tf_op jit(solution)/shard_map/reduce_scatter | solution.py:782
  631.4 112.6 %reduce-scatter.14.cloned.1.call-start = ((), (), s32[]{:S(2)}) async-start(), calls=%async_computation.17 | async-start | bytes 3538944 | tf_op jit(solution)/shard_map/reduce_scatter | solution.py:684
  (74 other events, 1473.9 us)
Sparse Core Ops, SparseCore 0:
  10.4 67.4 all-gather.4
  79.5 80.6 all-gather.6
  161.9 80.5 all-gather.8
  243.9 81.0 all-gather.10
  331.8 89.9 reduce-scatter.5
  437.6 89.6 reduce-scatter.7
  551.3 40.2 reduce-scatter.9
  631.5 36.1 reduce-scatter.11
  670.0 39.0 reduce-scatter.13

commit v15 on v14

--- a/solution.py
+++ b/solution.py
@@ -782,12 +782,12 @@
     grad_w_out = lax.psum_scatter(out_sum, "fsdp", scatter_dimension=0, tiled=True).astype(wide)
     second_sum = slab_product(normed, qkv_grad, (1, 2))
     if square:
-        second_sum = slab_sum(gate(second_sum, *far, *direct, grad_w_out))
+        second_sum = slab_sum(gate(second_sum, *far, *direct))
         came = order.add_far(near, far, direct)
-        down_slabs = slabs_of_rows(gate(down_sum, *came))
+        order.after(grad_w_out)
         normed_own = order(slots(to_normed, 0, 1), qkv_grad)
     else:
-        second_sum, down_slabs = slab_sum(second_sum), slabs_of_rows(down_sum)
+        second_sum = slab_sum(second_sum)
         normed_own, came = scatter(to_normed, qkv_grad), ()
     if square:
         result = order(
@@ -803,8 +803,9 @@
         lambda own, *came: norm_back(own, x_low, *first_stats, middle_grad, ln1_gain, came), normed_own, *came
     )
     grad_tokens = grad_tokens.reshape(tokens.shape)
-    up_slabs = slabs_of_rows(gate(up_sum, *came, normed_own))
-    first_slabs = slabs_of_rows(gate(first_sum, *came, normed_own))
+    three = jnp.concatenate([down_sum, up_sum, first_sum], axis=1)
+    three = slabs_of_rows(gate(three, *came, normed_own))
+    down_slabs, up_slabs, first_slabs = jnp.split(three, [hidden_slab, 2 * hidden_slab], axis=2)
     second_slabs = slabs_of_rows(second_sum)
 
     def rows_of(slabs):
@@ -829,7 +830,7 @@
         others = range(lax.axis_size(axis))
         came = [lax.ppermute(sums, axis, [(i, i ^ mask) for i in others]) for mask in masks]
         if (axis, masks) == stages[-1]:
-            order.after(down_slabs, up_slabs, first_slabs, second_slabs)
+            order.after(three, second_slabs)
         sums = order(lambda *parts: sum(parts[1:], parts[0]), sums, *came)
     sums = sums.reshape(-1)
 

time: 775 us -> 748 us (0.965)
  waiting for transfers between devices: 170 us -> 151 us
  starting transfers between devices: 73.1 us -> 65.1 us
    reduce_scatter x1, waiting for transfers between devices: 18.9 us -> 0.01 us  [local(): lax.psum_scatter(out_sum, 'fsdp', scatter_dimension=0, tiled=True)]
    all_to_all x4 -> x2, waiting for transfers between devices: 13.1 us -> 2.17 us  [slabs_of_rows(): lax.all_to_all(values.reshape(groups, -1, values.shape[1]), 'seq', split_...]
    ppermute x7, waiting for transfers between devices: 1.3 us -> 9.17 us  [local(): lax.ppermute(sums, axis, [(i, i ^ mask) for i in others])]
    unnamed x96 -> x108, local copies, waits for them, and re-layouts: 41.1 us -> 41.1 us
  transfers between devices with their start and end apart: 66 -> 64, of which waited for: 23 -> 22; matrix products, arithmetic and copies ran while one was open for 29% -> 30% of each run, Pallas kernels for 36% -> 37%
where the time goes in v15:
time: 748 us; the launch traced here: 743 us
  Pallas kernels  280 us (37%)
  waiting for transfers between devices  151 us (20%)
  local copies, waits for them, and re-layouts  92.4 us (12%)
  matrix products  85.7 us (11%)
  starting transfers between devices  65.1 us (9%)
  other arithmetic  54.2 us (7%)
  between operations  14.9 us (2%)
    ppermute x44, waiting for transfers between devices, swap(): return lax.ppermute(values, 'seq', [(i, i ^ bit) for i in range(4)])  138 us
    pallas_call x5, Pallas kernels, outer(): pl.pallas_call(partial(outer_kernel, chunk=next((c for c in (512, 384, 25...  81.8 us
    pallas_call x2, Pallas kernels, attend_backward(): pl.pallas_call(partial(attend_backward_kernel, blocks=blocks, seqs=seqs,...  57.6 us
    dot_general x5, matrix products, contract_last(): lax.dot_general(left_side, right_side, (((1,), (1,)), ((), ())), preferre...  52.9 us
    ppermute x44, starting transfers between devices, swap(): return lax.ppermute(values, 'seq', [(i, i ^ bit) for i in range(4)])  47.8 us
    unnamed x108, local copies, waits for them, and re-layouts  41.1 us
    dot_general x3, matrix products, contract(): lax.dot_general(left_side, right_side, (((1,), (0,)), ((), ())), preferre...  32.8 us
    pallas_call x1, Pallas kernels, up_and_bend(): pl.pallas_call(partial(up_kernel, chunk=512), grid=(count // TILE,), in_s...  30.6 us
  transfers between devices with their start and end apart: 64, of which 22 were waited for; matrix products, arithmetic and copies ran while one was open for 30% of the time, Pallas kernels for 37%

profile of v15, /device:TPU:0, one launch (start us, length us, event | category | flops | bytes accessed | tf_op | source)
XLA Modules:
  0.0 743.0 jit_solution(10210174321611102665)
XLA Ops:
  28.2 18.7 %collective-permute-done.2 = bf16[256,2048]{1,0:T(8,128)(2,1)} collective-permute-done((bf16[256,2048]{1,0:T(8,128)(2,1)}, bf16[256,2048]{1,0:T(8,128)(2,1)}, u32[]{:S(2)}, u32[]{:S(2)}) %collective-permute-start.2) | collective-permute-done | bytes 1048608 | tf_op jit(solution)/shard_map/ppermute | solution.py:437
  53.7 17.7 %collective-permute-done = bf16[256,2048]{1,0:T(8,128)(2,1)} collective-permute-done((bf16[256,2048]{1,0:T(8,128)(2,1)}, bf16[256,2048]{1,0:T(8,128)(2,1)}, u32[]{:S(2)}, u32[]{:S(2)}) %collective-permute-start) | collective-permute-done | bytes 1048608 | tf_op jit(solution)/shard_map/ppermute | solution.py:437
  79.6 12.9 %collective-permute-done.4 = bf16[256,2048]{1,0:T(8,128)(2,1)} collective-permute-done((bf16[256,2048]{1,0:T(8,128)(2,1)}, bf16[256,2048]{1,0:T(8,128)(2,1)}, u32[]{:S(2)}, u32[]{:S(2)}) %collective-permute-start.4) | collective-permute-done | bytes 1048608 | tf_op jit(solution)/shard_map/ppermute | solution.py:437
  101.1 18.6 %add_convert_fusion.qkv_ref = bf16[2048,1536]{1,0:T(8,128)(2,1)} fusion(bf16[2048,2048]{1,0:T(8,128)(2,1)} %constant_dynamic-update-slice_fusion.left_ref, bf16[2048,1536]{1,0:T(8,128)(2,1)} %all-gather.5.cloned.1.call-done, f32[1536]{0:T(1024)S(1)} %reduce.2), kind=kOutput, calls=%fused_computation.1 | convolution fusion | flops 12891193344 | bytes 20977664 | tf_op jit(solution)/shard_map/dot_general | solution.py:31
  119.7 29.7 %attend_forward.1 = (bf16[2048,512]{1,0:T(8,128)(2,1)}, f32[2048,512]{1,0:T(8,128)}) custom-call(s32[1]{0:T(128)} %bitcast.1.at_ref.mask_ref, f32[8]{0:T(128)} %multiply_power_fusion.slope_ref, bf16[2048,1536]{1,0:T(8,128)(2,1)} %add_convert_fusion.qkv_ref), custom_call_target="tpu_custom_call" | custom-call | flops 2684354560 | bytes 2621440 | tf_op jit(solution)/shard_map/attend_forward/pallas_call | solution.py:173
  156.8 11.2 %collective-permute-done.10 = bf16[512,512]{1,0:T(8,128)(2,1)S(1)} collective-permute-done((bf16[512,512]{1,0:T(8,128)(2,1)}, bf16[512,512]{1,0:T(8,128)(2,1)S(1)}, u32[]{:S(2)}, u32[]{:S(2)}) %collective-permute-start.10) | collective-permute-done | bytes 524320 | tf_op jit(solution)/shard_map/ppermute | solution.py:437
  221.7 18.7 %collective-permute-done.14 = bf16[256,2048]{1,0:T(8,128)(2,1)} collective-permute-done((bf16[256,2048]{1,0:T(8,128)(2,1)}, bf16[256,2048]{1,0:T(8,128)(2,1)}, u32[]{:S(2)}, u32[]{:S(2)}) %collective-permute-start.14) | collective-permute-done | bytes 1048608 | tf_op jit(solution)/shard_map/ppermute | solution.py:437
  250.8 11.3 %collective-permute-done.17 = bf16[256,2048]{1,0:T(8,128)(2,1)} collective-permute-done((bf16[256,2048]{1,0:T(8,128)(2,1)}, bf16[256,2048]{1,0:T(8,128)(2,1)}, u32[]{:S(2)}, u32[]{:S(2)}) %collective-permute-start.17) | collective-permute-done | bytes 1048608 | tf_op jit(solution)/shard_map/ppermute | solution.py:437
  268.6 30.6 %up_and_bend.1 = (bf16[2048,2048]{1,0:T(8,128)(2,1)}, f32[2048,2048]{1,0:T(8,128)}) custom-call(bf16[2048,2048]{1,0:T(8,128)(2,1)} %constant_dynamic-update-slice_fusion.7.rows_ref.left_ref, bf16[2048,2048]{1,0:T(8,128)(2,1)} %all-gather.9.cloned.1.call-done.weight_ref, f32[1,2048]{1,0:T(1,128)} %bitcast.155), custom_call_target="tpu_custom_call" | custom-call | flops 8589934592 | bytes 8388608 | tf_op jit(solution)/shard_map/up_and_bend/pallas_call | solution.py:259
  308.2 23.5 %outer.5 = bf16[8,4,64,2048]{3,2,1,0:T(8,128)(2,1)} custom-call(bf16[2048,2048]{1,0:T(8,128)(2,1)} %constant_dynamic-update-slice_fusion.31.left_ref.rows_ref, bf16[2048,2048]{1,0:T(8,128)(2,1)} %get-tuple-element.184.right_ref.rows_ref), custom_call_target="tpu_custom_call" | custom-call | flops 4294967296 | bytes 4194304 | tf_op jit(solution)/shard_map/outer/pallas_call | solution.py:420
  331.8 25.6 %hidden_gradient.1 = (bf16[2048,2048]{1,0:T(8,128)(2,1)}, f32[1,2048]{1,0:T(1,128)}) custom-call(bf16[2048,2048]{1,0:T(8,128)(2,1)} %constant_dynamic-update-slice_fusion.31.left_ref.rows_ref, bf16[2048,2048]{1,0:T(8,128)(2,1)} %all-gather.11.cloned.1.call-done.weight_ref, f32[2048,2048]{1,0:T(8,128)} %get-tuple-element.155.slope_ref), custom_call_target="tpu_custom_call" | custom-call | flops 6442450944 | bytes 6291456 | tf_op jit(solution)/shard_map/hidden_gradient/pallas_call | solution.py:283
  369.3 18.1 %convolution_convert_fusion.own_ref = bf16[1536,2048]{1,0:T(8,128)(2,1)S(1)} fusion(bf16[2048,2048]{1,0:T(8,128)(2,1)} %all-gather.9.cloned.1.call-done.weight_ref, bf16[2048,2048]{1,0:T(8,128)(2,1)} %get-tuple-element.174.right_ref), kind=kOutput, calls=%fused_computation.2 | convolution fusion | flops 12888047616 | bytes 20971520 | tf_op jit(solution)/shard_map/dot_general | solution.py:37
  406.0 23.6 %outer.6 = bf16[8,4,64,2048]{3,2,1,0:T(8,128)(2,1)} custom-call(bf16[2048,2048]{1,0:T(8,128)(2,1)} %constant_dynamic-update-slice_fusion.7.rows_ref.left_ref, bf16[2048,2048]{1,0:T(8,128)(2,1)} %get-tuple-element.174.right_ref), custom_call_target="tpu_custom_call" | custom-call | flops 4294967296 | bytes 4194304 | tf_op jit(solution)/shard_map/outer/pallas_call | solution.py:420
  440.9 11.0 %norm_back.2 = (bf16[512,2048]{1,0:T(8,128)(2,1)}, f32[512,2048]{1,0:T(8,128)}, f32[24,2048]{1,0:T(8,128)}) custom-call(bf16[1536,2048]{1,0:T(8,128)(2,1)} %copy-done.5, f32[512,2048]{1,0:T(8,128)} %copy-done, f32[512,1]{1,0:T(8,128)} %copy.45.average_ref, f32[512,1]{1,0:T(8,128)} %copy.46.scale_ref, bf16[512,2048]{1,0:T(8,128)(2,1)} %bitcast.110, ...), custom_call_target="tpu_custom_call" | custom-call | flops 7864320 | bytes 7680 | tf_op jit(solution)/shard_map/norm_back/pallas_call | solution.py:388
  453.5 8.9 %mixed_gradient.1 = bf16[512,2048]{1,0:T(8,128)(2,1)} custom-call(bf16[512,2048]{1,0:T(8,128)(2,1)} %get-tuple-element.183.rows_ref, bf16[2048,2048]{1,0:T(8,128)(2,1)} %all-gather.7.cloned.1.call-done.weight_ref), custom_call_target="tpu_custom_call" | custom-call | flops 1073741824 | bytes 1048576 | tf_op jit(solution)/shard_map/mixed_gradient/pallas_call | solution.py:330
  469.1 18.9 %product.1 = bf16[1536,2048]{1,0:T(8,128)(2,1)} custom-call(bf16[2048,2048]{1,0:T(8,128)(2,1)} %get-tuple-element.184.right_ref.rows_ref, bf16[2048,2048]{1,0:T(8,128)(2,1)} %all-gather.11.cloned.1.call-done.weight_ref), custom_call_target="tpu_custom_call" | custom-call | flops 3221225472 | bytes 3145728 | tf_op jit(solution)/shard_map/product/pallas_call | solution.py:308
  501.9 28.4 %attend_backward.2.right_ref.rest_4_ = bf16[2048,1536]{1,0:T(8,128)(2,1)} custom-call(s32[1]{0:T(128)} %bitcast.1.at_ref.mask_ref, f32[8]{0:T(128)} %multiply_power_fusion.slope_ref, bf16[2048,1536]{1,0:T(8,128)(2,1)} %add_convert_fusion.qkv_ref, f32[2048,512]{1,0:T(8,128)} %get-tuple-element.137.lse_ref, bf16[2048,512]{1,0:T(8,128)(2,1)} %get-tuple-element.136.mixed_ref, ...), custom_call_target="tpu_custom_call" | custom-call | flops 3355443200 | bytes 3276800 | tf_op jit(solution)/shard_map/attend_backward/pallas_call | solution.py:198
  530.2 8.7 %outer.7 = bf16[1,4,256,2048]{3,2,1,0:T(8,128)(2,1)} custom-call(bf16[1024,1024]{1,0:T(8,128)(2,1)} %pad_maximum_fusion.4.left_ref, bf16[1024,2048]{1,0:T(8,128)(2,1)} %pad_maximum_fusion.right_ref), custom_call_target="tpu_custom_call" | custom-call | flops 1073741824 | bytes 1048576 | tf_op jit(solution)/shard_map/outer/pallas_call | solution.py:420
  538.9 12.9 %outer.8 = bf16[8,4,64,768]{3,2,1,0:T(8,128)(2,1)} custom-call(bf16[2048,2048]{1,0:T(8,128)(2,1)} %constant_dynamic-update-slice_fusion.left_ref, bf16[2048,1536]{1,0:T(8,128)(2,1)} %attend_backward.2.right_ref.rest_4_), custom_call_target="tpu_custom_call" | custom-call | flops 1610612736 | bytes 1572864 | tf_op jit(solution)/shard_map/outer/pallas_call | solution.py:420
  556.0 29.3 %attend_backward.3.right_ref = bf16[2048,1536]{1,0:T(8,128)(2,1)} custom-call(s32[1]{0:T(128)} %bitcast.1.at_ref.mask_ref, f32[8]{0:T(128)} %multiply_power_fusion.slope_ref, bf16[2048,1536]{1,0:T(8,128)(2,1)} %add_convert_fusion.qkv_ref, f32[2048,512]{1,0:T(8,128)} %get-tuple-element.137.lse_ref, ...), custom_call_target="tpu_custom_call", output_to_operand_aliasing={{}: (9, {})} | custom-call | flops 3355443200 | bytes 3276800 | tf_op jit(solution)/shard_map/attend_backward/pallas_call | solution.py:198
  598.3 11.1 %convolution_convert_fusion.1 = bf16[1024,2048]{1,0:T(8,128)(2,1)} fusion(bf16[2048,1536]{1,0:T(8,128)(2,1)} %all-gather.5.cloned.1.call-done, bf16[2048,1536]{1,0:T(8,128)(2,1)} %attend_backward.3.right_ref), kind=kOutput, calls=%fused_computation.19 | convolution fusion | flops 6444548096 | bytes 13631488 | tf_op jit(solution)/shard_map/dot_general | solution.py:37
  617.5 14.3 %collective-permute-done.38 = bf16[256,2048]{1,0:T(8,128)(2,1)S(1)} collective-permute-done((bf16[256,2048]{1,0:T(8,128)(2,1)}, bf16[256,2048]{1,0:T(8,128)(2,1)S(1)}, u32[]{:S(2)}, u32[]{:S(2)}) %collective-permute-start.38) | collective-permute-done | bytes 1048608 | tf_op jit(solution)/shard_map/ppermute | solution.py:437
  636.3 13.1 %outer.9 = bf16[8,4,64,768]{3,2,1,0:T(8,128)(2,1)} custom-call(bf16[2048,2048]{1,0:T(8,128)(2,1)} %constant_dynamic-update-slice_fusion.left_ref, bf16[2048,1536]{1,0:T(8,128)(2,1)} %attend_backward.3.right_ref), custom_call_target="tpu_custom_call" | custom-call | flops 1610612736 | bytes 1572864 | tf_op jit(solution)/shard_map/outer/pallas_call | solution.py:420
  690.8 10.9 %norm_back.3 = (bf16[512,2048]{1,0:T(8,128)(2,1)}, f32[512,2048]{1,0:T(8,128)}, f32[24,2048]{1,0:T(8,128)}) custom-call(bf16[512,2048]{1,0:T(8,128)(2,1)} %convolution_convert_fusion.2.own_ref, bf16[512,2048]{1,0:T(8,128)(2,1)} %bitcast.106, f32[512,1]{1,0:T(8,128)} %bitcast.131, f32[512,1]{1,0:T(8,128)} %bitcast.130, ...), custom_call_target="tpu_custom_call" | custom-call | flops 7864320 | bytes 7680 | tf_op jit(solution)/shard_map/norm_back/pallas_call | solution.py:388
  (337 shorter events, 300.4 us)
Async XLA Ops:
  7.2 93.9 %all-gather.5.cloned.1.call-start = ((), (), s32[]{:S(2)}) async-start(), calls=%async_computation.7 | async-start | bytes 7077888 | tf_op jit(solution)/shard_map/all_gather | solution.py:629
  10.3 170.0 %all-gather.7.cloned.1.call-start = ((), (), s32[]{:S(2)}) async-start(), calls=%async_computation.8 | async-start | bytes 9437184 | tf_op jit(solution)/shard_map/all_gather | solution.py:641
  11.1 257.5 %all-gather.9.cloned.1.call-start = ((), (), s32[]{:S(2)}) async-start(), calls=%async_computation.9 | async-start | bytes 9437184 | tf_op jit(solution)/shard_map/all_gather | solution.py:642
  19.5 312.4 %all-gather.11.cloned.1.call-start = ((), (), s32[]{:S(2)}) async-start(), calls=%async_computation.10 | async-start | bytes 9437184 | tf_op jit(solution)/shard_map/all_gather | solution.py:643
  24.1 47.4 %collective-permute-start = (bf16[256,2048]{1,0:T(8,128)(2,1)}, bf16[256,2048]{1,0:T(8,128)(2,1)}, u32[]{:S(2)}, u32[]{:S(2)}) collective-permute-start(bf16[256,2048]{1,0:T(8,128)(2,1)} %get-tuple-element.297), channel_id=1, source_target_pairs={{0,8},{8,0},{16,24},{24,16},{1,9},{9,1},{17,25},{25,17},{2,10},{10... | collective-permute-start | bytes 3145736 | tf_op jit(solution)/shard_map/ppermute | solution.py:437
  24.6 52.7 %collective-permute-start.3 = (bf16[256,2048]{1,0:T(8,128)(2,1)}, bf16[256,2048]{1,0:T(8,128)(2,1)}, u32[]{:S(2)}, u32[]{:S(2)}) collective-permute-start(bf16[256,2048]{1,0:T(8,128)(2,1)} %get-tuple-element.296), channel_id=1, source_target_pairs={{0,16},{8,24},{16,0},{24,8},{1,17},{9,25},{17,1},{25,9},{2,18},{10... | collective-permute-start | bytes 3145736 | tf_op jit(solution)/shard_map/ppermute | solution.py:437
  26.9 474.9 %reduce-scatter.6.cloned.1.call-start = ((), (), s32[]{:S(2)}) async-start(), calls=%async_computation.11 | async-start | bytes 9437184 | tf_op jit(solution)/shard_map/reduce_scatter | solution.py:684
  46.9 45.6 %collective-permute-start.4 = (bf16[256,2048]{1,0:T(8,128)(2,1)}, bf16[256,2048]{1,0:T(8,128)(2,1)}, u32[]{:S(2)}, u32[]{:S(2)}) collective-permute-start(bf16[256,2048]{1,0:T(8,128)(2,1)} %collective-permute-done.2), channel_id=1, source_target_pairs={{0,8},{8,0},{16,24},{24,16},{1,9},{9,1},{17,25},{25,17},{2,10},{10... | collective-permute-start | bytes 3145736 | tf_op jit(solution)/shard_map/ppermute | solution.py:437
  97.1 52.4 %collective-permute-start.7 = (bf16[256,2048]{1,0:T(8,128)(2,1)}, bf16[256,2048]{1,0:T(8,128)(2,1)}, u32[]{:S(2)}, u32[]{:S(2)}) collective-permute-start(bf16[256,2048]{1,0:T(8,128)(2,1)} %get-tuple-element.141), channel_id=1, source_target_pairs={{0,16},{8,24},{16,0},{24,8},{1,17},{9,25},{17,1},{25,9},{2,18},{10... | collective-permute-start | bytes 3145736 | tf_op jit(solution)/shard_map/ppermute | solution.py:437
  97.4 52.1 %collective-permute-start.8 = (bf16[256,2048]{1,0:T(8,128)(2,1)}, bf16[256,2048]{1,0:T(8,128)(2,1)}, u32[]{:S(2)}, u32[]{:S(2)}) collective-permute-start(bf16[256,2048]{1,0:T(8,128)(2,1)} %get-tuple-element.141), channel_id=1, source_target_pairs={{0,8},{8,0},{16,24},{24,16},{1,9},{9,1},{17,25},{25,17},{2,10},{10... | collective-permute-start | bytes 3145736 | tf_op jit(solution)/shard_map/ppermute | solution.py:437
  99.1 50.4 %collective-permute-start.6 = (bf16[256,2048]{1,0:T(8,128)(2,1)S(1)}, bf16[256,2048]{1,0:T(8,128)(2,1)}, u32[]{:S(2)}, u32[]{:S(2)}) collective-permute-start(bf16[256,2048]{1,0:T(8,128)(2,1)S(1)} %get-tuple-element.142), channel_id=1, source_target_pairs={{0,8},{8,0},{16,24},{24,16},{1,9},{9,1},{17,25},{25,17},{2,10},{10... | collective-permute-start | bytes 3145736 | tf_op jit(solution)/shard_map/ppermute | solution.py:437
  99.5 50.1 %collective-permute-start.9 = (bf16[256,2048]{1,0:T(8,128)(2,1)S(1)}, bf16[256,2048]{1,0:T(8,128)(2,1)}, u32[]{:S(2)}, u32[]{:S(2)}) collective-permute-start(bf16[256,2048]{1,0:T(8,128)(2,1)S(1)} %get-tuple-element.142), channel_id=1, source_target_pairs={{0,16},{8,24},{16,0},{24,8},{1,17},{9,25},{17,1},{25,9},{2,18},{10... | collective-permute-start | bytes 3145736 | tf_op jit(solution)/shard_map/ppermute | solution.py:437
  191.7 49.5 %collective-permute-start.13 = (bf16[256,2048]{1,0:T(8,128)(2,1)}, bf16[256,2048]{1,0:T(8,128)(2,1)}, u32[]{:S(2)}, u32[]{:S(2)}) collective-permute-start(bf16[256,2048]{1,0:T(8,128)(2,1)} %get-tuple-element.290), channel_id=1, source_target_pairs={{0,8},{8,0},{16,24},{24,16},{1,9},{9,1},{17,25},{25,17},{2,10},{10... | collective-permute-start | bytes 3145736 | tf_op jit(solution)/shard_map/ppermute | solution.py:437
  193.9 46.6 %collective-permute-start.14 = (bf16[256,2048]{1,0:T(8,128)(2,1)}, bf16[256,2048]{1,0:T(8,128)(2,1)}, u32[]{:S(2)}, u32[]{:S(2)}) collective-permute-start(bf16[256,2048]{1,0:T(8,128)(2,1)} %get-tuple-element.289), channel_id=1, source_target_pairs={{0,8},{8,0},{16,24},{24,16},{1,9},{9,1},{17,25},{25,17},{2,10},{10... | collective-permute-start | bytes 3145736 | tf_op jit(solution)/shard_map/ppermute | solution.py:437
  194.4 53.9 %collective-permute-start.16 = (bf16[256,2048]{1,0:T(8,128)(2,1)}, bf16[256,2048]{1,0:T(8,128)(2,1)}, u32[]{:S(2)}, u32[]{:S(2)}) collective-permute-start(bf16[256,2048]{1,0:T(8,128)(2,1)} %get-tuple-element.289), channel_id=1, source_target_pairs={{0,16},{8,24},{16,0},{24,8},{1,17},{9,25},{17,1},{25,9},{2,18},{10... | collective-permute-start | bytes 3145736 | tf_op jit(solution)/shard_map/ppermute | solution.py:437
  221.6 77.5 %collective-permute-start.21 = (bf16[512,1024]{1,0:T(8,128)(2,1)S(1)}, bf16[512,1024]{1,0:T(8,128)(2,1)S(1)}, u32[]{:S(2)}, u32[]{:S(2)}) collective-permute-start(bf16[512,1024]{1,0:T(8,128)(2,1)S(1)} %copy.43), channel_id=1, source_target_pairs={{0,1},{1,0},{2,3},{3,2},{4,5},{5,4},{6,7},{7,6},{8,9},{9,8},{10,11... | collective-permute-start | bytes 3145736 | tf_op jit(solution)/shard_map/ppermute | solution.py:655
  331.8 256.3 %reduce-scatter.8.cloned.1.call-start = ((), (), s32[]{:S(2)}) async-start(), calls=%async_computation.12 | async-start | bytes 9437184 | tf_op jit(solution)/shard_map/reduce_scatter | solution.py:684
  437.5 160.8 %reduce-scatter.10.cloned.1.call-start = ((), (), s32[]{:S(2)}) async-start(), calls=%async_computation.13 | async-start | bytes 3538944 | tf_op jit(solution)/shard_map/reduce_scatter | solution.py:684
  437.5 52.4 %collective-permute-start.28 = (bf16[256,2048]{1,0:T(8,128)(2,1)S(1)}, bf16[256,2048]{1,0:T(8,128)(2,1)}, u32[]{:S(2)}, u32[]{:S(2)}) collective-permute-start(bf16[256,2048]{1,0:T(8,128)(2,1)S(1)} %get-tuple-element.185), channel_id=1, source_target_pairs={{0,8},{8,0},{16,24},{24,16},{1,9},{9,1},{17,25},{25,17},{2,10},{10... | collective-permute-start | bytes 3145736 | tf_op jit(solution)/shard_map/ppermute | solution.py:437
  438.3 51.6 %collective-permute-start.29 = (bf16[256,2048]{1,0:T(8,128)(2,1)S(1)}, bf16[256,2048]{1,0:T(8,128)(2,1)}, u32[]{:S(2)}, u32[]{:S(2)}) collective-permute-start(bf16[256,2048]{1,0:T(8,128)(2,1)S(1)} %get-tuple-element.186), channel_id=1, source_target_pairs={{0,16},{8,24},{16,0},{24,8},{1,17},{9,25},{17,1},{25,9},{2,18},{10... | collective-permute-start | bytes 3145736 | tf_op jit(solution)/shard_map/ppermute | solution.py:437
  495.4 56.4 %collective-permute-start.34 = (bf16[512,2048]{1,0:T(8,128)(2,1)S(1)}, bf16[512,2048]{1,0:T(8,128)(2,1)}, u32[]{:S(2)}, u32[]{:S(2)}) collective-permute-start(bf16[512,2048]{1,0:T(8,128)(2,1)S(1)} %pad_maximum_fusion.6), channel_id=1, source_target_pairs={{0,16},{8,24},{16,0},{24,8},{1,17},{9,25},{17,1},{25,9},{2,18},{10... | collective-permute-start | bytes 6291464 | tf_op jit(solution)/shard_map/ppermute | solution.py:437
  498.2 53.7 %collective-permute-start.33 = (bf16[512,2048]{1,0:T(8,128)(2,1)}, bf16[512,2048]{1,0:T(8,128)(2,1)}, u32[]{:S(2)}, u32[]{:S(2)}) collective-permute-start(bf16[512,2048]{1,0:T(8,128)(2,1)} %pad_maximum_fusion.5), channel_id=1, source_target_pairs={{0,8},{8,0},{16,24},{24,16},{1,9},{9,1},{17,25},{25,17},{2,10},{10... | collective-permute-start | bytes 6291464 | tf_op jit(solution)/shard_map/ppermute | solution.py:437
  551.9 118.2 %reduce-scatter.12.cloned.1.call-start = ((), (), s32[]{:S(2)}) async-start(), calls=%async_computation.14 | async-start | bytes 2359296 | tf_op jit(solution)/shard_map/reduce_scatter | solution.py:782
  631.9 88.4 %reduce-scatter.14.cloned.1.call-start = ((), (), s32[]{:S(2)}) async-start(), calls=%async_computation.15 | async-start | bytes 3538944 | tf_op jit(solution)/shard_map/reduce_scatter | solution.py:684
  (78 other events, 1440.0 us)
Sparse Core Ops, SparseCore 0:
  10.4 67.4 all-gather.4
  79.5 80.6 all-gather.6
  161.9 80.5 all-gather.8
  243.9 81.0 all-gather.10
  331.9 89.8 reduce-scatter.5
  437.6 89.6 reduce-scatter.7
  552.0 40.2 reduce-scatter.9
  632.0 36.1 reduce-scatter.11
  670.5 39.0 reduce-scatter.13

commit v16 on v15

--- a/solution.py
+++ b/solution.py
@@ -750,8 +750,9 @@
         out_far = swap_far(out_far)
     first_sum = slab_product(normed, begun, (0, 2))
     if square:
-        first_sum = gate(first_sum, *result_came)
+        first_sum = gate(first_sum, *result_came, *out_far)
         order.after(*result_came)
+        out_came = order.add_far(out_sum, out_far, None, at=part)
     first_sum = slab_sum(first_sum)
     qkv_grad = order(
         lambda begun, *grads: attend_backward(
@@ -760,9 +761,7 @@
         begun,
         *mixed_grad,
     )
-    if square:
-        out_came = order.add_far(out_sum, out_far, None, at=part)
-    else:
+    if not square:
         out_sum = lax.psum_scatter(out_sum, "seq", scatter_dimension=0, tiled=True)
     order.after(up_sum)
     if square:
@@ -789,15 +788,6 @@
     else:
         second_sum = slab_sum(second_sum)
         normed_own, came = scatter(to_normed, qkv_grad), ()
-    if square:
-        result = order(
-            lambda rest, *came: (middle + (summed(rest[:count], came) + down_bias)).astype(low),
-            result_rest,
-            *result_came,
-        )
-    else:
-        result = (middle + (scatter(to_result, active).astype(wide) + down_bias)).astype(low)
-    result = result.reshape(tokens.shape)
     qkv_column_sum = order(column_sum, qkv_grad)
     grad_tokens, _, input_sums = order(
         lambda own, *came: norm_back(own, x_low, *first_stats, middle_grad, ln1_gain, came), normed_own, *came
@@ -829,9 +819,22 @@
     for axis, masks in stages:
         others = range(lax.axis_size(axis))
         came = [lax.ppermute(sums, axis, [(i, i ^ mask) for i in others]) for mask in masks]
+        if (axis, masks) == stages[1]:
+            order.after(three)
         if (axis, masks) == stages[-1]:
-            order.after(three, second_slabs)
+            order.after(second_slabs)
         sums = order(lambda *parts: sum(parts[1:], parts[0]), sums, *came)
+        if (axis, masks) != stages[0]:
+            continue
+        if square:
+            result = order(
+                lambda rest, *came: (middle + (summed(rest[:count], came) + down_bias)).astype(low),
+                result_rest,
+                *result_came,
+            )
+        else:
+            result = (middle + (scatter(to_result, active).astype(wide) + down_bias)).astype(low)
+        result = result.reshape(tokens.shape)
     sums = sums.reshape(-1)
 
     def cut(at, count):

time: 748 us -> 759 us (1.015)
    ppermute x44, waiting for transfers between devices: 138 us -> 147 us  [swap(): return lax.ppermute(values, 'seq', [(i, i ^ bit) for i in range(4)])]
    unnamed x108 -> x98, local copies, waits for them, and re-layouts: 41.1 us -> 43.5 us
  transfers between devices with their start and end apart: 64 -> 64, of which waited for: 22 -> 22; matrix products, arithmetic and copies ran while one was open for 30% -> 31% of each run, Pallas kernels for 37% -> 37%
where the time goes in v16:
time: 759 us; the launch traced here: 754 us
  Pallas kernels  280 us (37%)
  waiting for transfers between devices  151 us (20%)
  local copies, waits for them, and re-layouts  98.1 us (13%)
  matrix products  85.8 us (11%)
  starting transfers between devices  65 us (9%)
  other arithmetic  58.7 us (8%)
  between operations  14.9 us (2%)
    ppermute x44, waiting for transfers between devices, swap(): return lax.ppermute(values, 'seq', [(i, i ^ bit) for i in range(4)])  147 us
    pallas_call x5, Pallas kernels, outer(): pl.pallas_call(partial(outer_kernel, chunk=next((c for c in (512, 384, 25...  82.2 us
    pallas_call x2, Pallas kernels, attend_backward(): pl.pallas_call(partial(attend_backward_kernel, blocks=blocks, seqs=seqs,...  56.8 us
    dot_general x5, matrix products, contract_last(): lax.dot_general(left_side, right_side, (((1,), (1,)), ((), ())), preferre...  52.9 us
    ppermute x44, starting transfers between devices, swap(): return lax.ppermute(values, 'seq', [(i, i ^ bit) for i in range(4)])  47.1 us
    unnamed x98, local copies, waits for them, and re-layouts  43.5 us
    dot_general x3, matrix products, contract(): lax.dot_general(left_side, right_side, (((1,), (0,)), ((), ())), preferre...  32.9 us
    pallas_call x1, Pallas kernels, up_and_bend(): pl.pallas_call(partial(up_kernel, chunk=512), grid=(count // TILE,), in_s...  30.6 us
  transfers between devices with their start and end apart: 64, of which 22 were waited for; matrix products, arithmetic and copies ran while one was open for 31% of the time, Pallas kernels for 37%

profile of v16, /device:TPU:0, one launch (start us, length us, event | category | flops | bytes accessed | tf_op | source)
XLA Modules:
  0.0 754.0 jit_solution(14643059780998541947)
XLA Ops:
  28.1 18.7 %collective-permute-done.2 = bf16[256,2048]{1,0:T(8,128)(2,1)} collective-permute-done((bf16[256,2048]{1,0:T(8,128)(2,1)}, bf16[256,2048]{1,0:T(8,128)(2,1)}, u32[]{:S(2)}, u32[]{:S(2)}) %collective-permute-start.2) | collective-permute-done | bytes 1048608 | tf_op jit(solution)/shard_map/ppermute | solution.py:437
  53.7 17.7 %collective-permute-done = bf16[256,2048]{1,0:T(8,128)(2,1)} collective-permute-done((bf16[256,2048]{1,0:T(8,128)(2,1)}, bf16[256,2048]{1,0:T(8,128)(2,1)}, u32[]{:S(2)}, u32[]{:S(2)}) %collective-permute-start) | collective-permute-done | bytes 1048608 | tf_op jit(solution)/shard_map/ppermute | solution.py:437
  79.6 12.8 %collective-permute-done.4 = bf16[256,2048]{1,0:T(8,128)(2,1)} collective-permute-done((bf16[256,2048]{1,0:T(8,128)(2,1)}, bf16[256,2048]{1,0:T(8,128)(2,1)}, u32[]{:S(2)}, u32[]{:S(2)}) %collective-permute-start.4) | collective-permute-done | bytes 1048608 | tf_op jit(solution)/shard_map/ppermute | solution.py:437
  101.0 18.6 %add_convert_fusion.qkv_ref = bf16[2048,1536]{1,0:T(8,128)(2,1)} fusion(bf16[2048,2048]{1,0:T(8,128)(2,1)} %constant_dynamic-update-slice_fusion.left_ref, bf16[2048,1536]{1,0:T(8,128)(2,1)} %all-gather.5.cloned.1.call-done, f32[1536]{0:T(1024)S(1)} %reduce.2), kind=kOutput, calls=%fused_computation.1 | convolution fusion | flops 12891193344 | bytes 20977664 | tf_op jit(solution)/shard_map/dot_general | solution.py:31
  119.6 29.7 %attend_forward.1 = (bf16[2048,512]{1,0:T(8,128)(2,1)}, f32[2048,512]{1,0:T(8,128)}) custom-call(s32[1]{0:T(128)} %bitcast.1.at_ref.mask_ref, f32[8]{0:T(128)} %multiply_power_fusion.slope_ref, bf16[2048,1536]{1,0:T(8,128)(2,1)} %add_convert_fusion.qkv_ref), custom_call_target="tpu_custom_call" | custom-call | flops 2684354560 | bytes 2621440 | tf_op jit(solution)/shard_map/attend_forward/pallas_call | solution.py:173
  156.7 11.2 %collective-permute-done.10 = bf16[512,512]{1,0:T(8,128)(2,1)S(1)} collective-permute-done((bf16[512,512]{1,0:T(8,128)(2,1)}, bf16[512,512]{1,0:T(8,128)(2,1)S(1)}, u32[]{:S(2)}, u32[]{:S(2)}) %collective-permute-start.10) | collective-permute-done | bytes 524320 | tf_op jit(solution)/shard_map/ppermute | solution.py:437
  221.6 18.8 %collective-permute-done.14 = bf16[256,2048]{1,0:T(8,128)(2,1)} collective-permute-done((bf16[256,2048]{1,0:T(8,128)(2,1)}, bf16[256,2048]{1,0:T(8,128)(2,1)}, u32[]{:S(2)}, u32[]{:S(2)}) %collective-permute-start.14) | collective-permute-done | bytes 1048608 | tf_op jit(solution)/shard_map/ppermute | solution.py:437
  250.7 11.3 %collective-permute-done.17 = bf16[256,2048]{1,0:T(8,128)(2,1)} collective-permute-done((bf16[256,2048]{1,0:T(8,128)(2,1)}, bf16[256,2048]{1,0:T(8,128)(2,1)}, u32[]{:S(2)}, u32[]{:S(2)}) %collective-permute-start.17) | collective-permute-done | bytes 1048608 | tf_op jit(solution)/shard_map/ppermute | solution.py:437
  268.5 30.6 %up_and_bend.1 = (bf16[2048,2048]{1,0:T(8,128)(2,1)}, f32[2048,2048]{1,0:T(8,128)}) custom-call(bf16[2048,2048]{1,0:T(8,128)(2,1)} %constant_dynamic-update-slice_fusion.7.rows_ref.left_ref, bf16[2048,2048]{1,0:T(8,128)(2,1)} %all-gather.9.cloned.1.call-done.weight_ref, f32[1,2048]{1,0:T(1,128)} %bitcast.152), custom_call_target="tpu_custom_call" | custom-call | flops 8589934592 | bytes 8388608 | tf_op jit(solution)/shard_map/up_and_bend/pallas_call | solution.py:259
  308.2 23.5 %outer.5 = bf16[8,4,64,2048]{3,2,1,0:T(8,128)(2,1)} custom-call(bf16[2048,2048]{1,0:T(8,128)(2,1)} %constant_dynamic-update-slice_fusion.31.left_ref.rows_ref, bf16[2048,2048]{1,0:T(8,128)(2,1)} %get-tuple-element.184.right_ref.rows_ref), custom_call_target="tpu_custom_call" | custom-call | flops 4294967296 | bytes 4194304 | tf_op jit(solution)/shard_map/outer/pallas_call | solution.py:420
  331.8 25.4 %hidden_gradient.1 = (bf16[2048,2048]{1,0:T(8,128)(2,1)}, f32[1,2048]{1,0:T(1,128)}) custom-call(bf16[2048,2048]{1,0:T(8,128)(2,1)} %constant_dynamic-update-slice_fusion.31.left_ref.rows_ref, bf16[2048,2048]{1,0:T(8,128)(2,1)} %all-gather.11.cloned.1.call-done.weight_ref, f32[2048,2048]{1,0:T(8,128)} %get-tuple-element.155.slope_ref), custom_call_target="tpu_custom_call" | custom-call | flops 6442450944 | bytes 6291456 | tf_op jit(solution)/shard_map/hidden_gradient/pallas_call | solution.py:283
  369.1 18.1 %convolution_convert_fusion.own_ref = bf16[1536,2048]{1,0:T(8,128)(2,1)S(1)} fusion(bf16[2048,2048]{1,0:T(8,128)(2,1)} %all-gather.9.cloned.1.call-done.weight_ref, bf16[2048,2048]{1,0:T(8,128)(2,1)} %get-tuple-element.174.right_ref), kind=kOutput, calls=%fused_computation.2 | convolution fusion | flops 12888047616 | bytes 20971520 | tf_op jit(solution)/shard_map/dot_general | solution.py:37
  405.6 23.6 %outer.6 = bf16[8,4,64,2048]{3,2,1,0:T(8,128)(2,1)} custom-call(bf16[2048,2048]{1,0:T(8,128)(2,1)} %constant_dynamic-update-slice_fusion.7.rows_ref.left_ref, bf16[2048,2048]{1,0:T(8,128)(2,1)} %get-tuple-element.174.right_ref), custom_call_target="tpu_custom_call" | custom-call | flops 4294967296 | bytes 4194304 | tf_op jit(solution)/shard_map/outer/pallas_call | solution.py:420
  440.4 11.3 %norm_back.2 = (bf16[512,2048]{1,0:T(8,128)(2,1)}, f32[512,2048]{1,0:T(8,128)}, f32[24,2048]{1,0:T(8,128)}) custom-call(bf16[1536,2048]{1,0:T(8,128)(2,1)} %copy-done.5, f32[512,2048]{1,0:T(8,128)} %copy-done, f32[512,1]{1,0:T(8,128)} %copy.45.average_ref, f32[512,1]{1,0:T(8,128)} %copy.46.scale_ref, bf16[512,2048]{1,0:T(8,128)(2,1)} %bitcast.108, ...), custom_call_target="tpu_custom_call" | custom-call | flops 7864320 | bytes 7680 | tf_op jit(solution)/shard_map/norm_back/pallas_call | solution.py:388
  453.4 8.9 %mixed_gradient.1 = bf16[512,2048]{1,0:T(8,128)(2,1)} custom-call(bf16[512,2048]{1,0:T(8,128)(2,1)} %get-tuple-element.183.rows_ref, bf16[2048,2048]{1,0:T(8,128)(2,1)} %all-gather.7.cloned.1.call-done.weight_ref), custom_call_target="tpu_custom_call" | custom-call | flops 1073741824 | bytes 1048576 | tf_op jit(solution)/shard_map/mixed_gradient/pallas_call | solution.py:330
  468.9 11.4 %collective-permute-done.30.rest_1_ = bf16[512,512]{1,0:T(8,128)(2,1)S(1)} collective-permute-done((bf16[512,512]{1,0:T(8,128)(2,1)S(1)}, bf16[512,512]{1,0:T(8,128)(2,1)S(1)}, u32[]{:S(2)}, u32[]{:S(2)}) %collective-permute-start.30) | collective-permute-done | bytes 524320 | tf_op jit(solution)/shard_map/ppermute | solution.py:437
  480.2 19.1 %product.1 = bf16[1536,2048]{1,0:T(8,128)(2,1)} custom-call(bf16[2048,2048]{1,0:T(8,128)(2,1)} %get-tuple-element.184.right_ref.rows_ref, bf16[2048,2048]{1,0:T(8,128)(2,1)} %all-gather.11.cloned.1.call-done.weight_ref), custom_call_target="tpu_custom_call" | custom-call | flops 3221225472 | bytes 3145728 | tf_op jit(solution)/shard_map/product/pallas_call | solution.py:308
  513.5 28.3 %attend_backward.2.right_ref.rest_4_ = bf16[2048,1536]{1,0:T(8,128)(2,1)} custom-call(s32[1]{0:T(128)} %bitcast.1.at_ref.mask_ref, f32[8]{0:T(128)} %multiply_power_fusion.slope_ref, bf16[2048,1536]{1,0:T(8,128)(2,1)} %add_convert_fusion.qkv_ref, f32[2048,512]{1,0:T(8,128)} %get-tuple-element.137.lse_ref, bf16[2048,512]{1,0:T(8,128)(2,1)} %get-tuple-element.136.mixed_ref, ...), custom_call_target="tpu_custom_call" | custom-call | flops 3355443200 | bytes 3276800 | tf_op jit(solution)/shard_map/attend_backward/pallas_call | solution.py:198
  541.9 8.8 %outer.7 = bf16[1,4,256,2048]{3,2,1,0:T(8,128)(2,1)} custom-call(bf16[1024,1024]{1,0:T(8,128)(2,1)} %pad_maximum_fusion.4.left_ref, bf16[1024,2048]{1,0:T(8,128)(2,1)} %pad_maximum_fusion.right_ref), custom_call_target="tpu_custom_call" | custom-call | flops 1073741824 | bytes 1048576 | tf_op jit(solution)/shard_map/outer/pallas_call | solution.py:420
  553.3 12.9 %outer.8 = bf16[8,4,64,768]{3,2,1,0:T(8,128)(2,1)} custom-call(bf16[2048,2048]{1,0:T(8,128)(2,1)} %constant_dynamic-update-slice_fusion.left_ref, bf16[2048,1536]{1,0:T(8,128)(2,1)} %attend_backward.2.right_ref.rest_4_), custom_call_target="tpu_custom_call" | custom-call | flops 1610612736 | bytes 1572864 | tf_op jit(solution)/shard_map/outer/pallas_call | solution.py:420
  572.5 28.5 %attend_backward.3.right_ref = bf16[2048,1536]{1,0:T(8,128)(2,1)} custom-call(s32[1]{0:T(128)} %bitcast.1.at_ref.mask_ref, f32[8]{0:T(128)} %multiply_power_fusion.slope_ref, bf16[2048,1536]{1,0:T(8,128)(2,1)} %add_convert_fusion.qkv_ref, f32[2048,512]{1,0:T(8,128)} %get-tuple-element.137.lse_ref, ...), custom_call_target="tpu_custom_call", output_to_operand_aliasing={{}: (9, {})} | custom-call | flops 3355443200 | bytes 3276800 | tf_op jit(solution)/shard_map/attend_backward/pallas_call | solution.py:198
  611.0 11.1 %convolution_convert_fusion.1 = bf16[1024,2048]{1,0:T(8,128)(2,1)} fusion(bf16[2048,1536]{1,0:T(8,128)(2,1)} %all-gather.5.cloned.1.call-done, bf16[2048,1536]{1,0:T(8,128)(2,1)} %attend_backward.3.right_ref), kind=kOutput, calls=%fused_computation.19 | convolution fusion | flops 6444548096 | bytes 13631488 | tf_op jit(solution)/shard_map/dot_general | solution.py:37
  637.9 13.3 %outer.9 = bf16[8,4,64,768]{3,2,1,0:T(8,128)(2,1)} custom-call(bf16[2048,2048]{1,0:T(8,128)(2,1)} %constant_dynamic-update-slice_fusion.left_ref, bf16[2048,1536]{1,0:T(8,128)(2,1)} %attend_backward.3.right_ref), custom_call_target="tpu_custom_call" | custom-call | flops 1610612736 | bytes 1572864 | tf_op jit(solution)/shard_map/outer/pallas_call | solution.py:420
  701.5 11.1 %norm_back.3 = (bf16[512,2048]{1,0:T(8,128)(2,1)}, f32[512,2048]{1,0:T(8,128)}, f32[24,2048]{1,0:T(8,128)}) custom-call(bf16[512,2048]{1,0:T(8,128)(2,1)} %convolution_convert_fusion.2.own_ref, bf16[512,2048]{1,0:T(8,128)(2,1)} %bitcast.104, f32[512,1]{1,0:T(8,128)} %bitcast.128, f32[512,1]{1,0:T(8,128)} %bitcast.127, ...), custom_call_target="tpu_custom_call" | custom-call | flops 7864320 | bytes 7680 | tf_op jit(solution)/shard_map/norm_back/pallas_call | solution.py:388
  (326 shorter events, 314.2 us)
Async XLA Ops:
  7.2 93.8 %all-gather.5.cloned.1.call-start = ((), (), s32[]{:S(2)}) async-start(), calls=%async_computation.7 | async-start | bytes 7077888 | tf_op jit(solution)/shard_map/all_gather | solution.py:629
  10.3 169.9 %all-gather.7.cloned.1.call-start = ((), (), s32[]{:S(2)}) async-start(), calls=%async_computation.8 | async-start | bytes 9437184 | tf_op jit(solution)/shard_map/all_gather | solution.py:641
  11.1 257.4 %all-gather.9.cloned.1.call-start = ((), (), s32[]{:S(2)}) async-start(), calls=%async_computation.9 | async-start | bytes 9437184 | tf_op jit(solution)/shard_map/all_gather | solution.py:642
  19.4 312.3 %all-gather.11.cloned.1.call-start = ((), (), s32[]{:S(2)}) async-start(), calls=%async_computation.10 | async-start | bytes 9437184 | tf_op jit(solution)/shard_map/all_gather | solution.py:643
  24.0 47.4 %collective-permute-start = (bf16[256,2048]{1,0:T(8,128)(2,1)}, bf16[256,2048]{1,0:T(8,128)(2,1)}, u32[]{:S(2)}, u32[]{:S(2)}) collective-permute-start(bf16[256,2048]{1,0:T(8,128)(2,1)} %get-tuple-element.297), channel_id=1, source_target_pairs={{0,8},{8,0},{16,24},{24,16},{1,9},{9,1},{17,25},{25,17},{2,10},{10... | collective-permute-start | bytes 3145736 | tf_op jit(solution)/shard_map/ppermute | solution.py:437
  24.6 52.7 %collective-permute-start.3 = (bf16[256,2048]{1,0:T(8,128)(2,1)}, bf16[256,2048]{1,0:T(8,128)(2,1)}, u32[]{:S(2)}, u32[]{:S(2)}) collective-permute-start(bf16[256,2048]{1,0:T(8,128)(2,1)} %get-tuple-element.296), channel_id=1, source_target_pairs={{0,16},{8,24},{16,0},{24,8},{1,17},{9,25},{17,1},{25,9},{2,18},{10... | collective-permute-start | bytes 3145736 | tf_op jit(solution)/shard_map/ppermute | solution.py:437
  26.9 486.6 %reduce-scatter.6.cloned.1.call-start = ((), (), s32[]{:S(2)}) async-start(), calls=%async_computation.11 | async-start | bytes 9437184 | tf_op jit(solution)/shard_map/reduce_scatter | solution.py:684
  97.0 52.4 %collective-permute-start.7 = (bf16[256,2048]{1,0:T(8,128)(2,1)}, bf16[256,2048]{1,0:T(8,128)(2,1)}, u32[]{:S(2)}, u32[]{:S(2)}) collective-permute-start(bf16[256,2048]{1,0:T(8,128)(2,1)} %get-tuple-element.141), channel_id=1, source_target_pairs={{0,16},{8,24},{16,0},{24,8},{1,17},{9,25},{17,1},{25,9},{2,18},{10... | collective-permute-start | bytes 3145736 | tf_op jit(solution)/shard_map/ppermute | solution.py:437
  97.3 52.1 %collective-permute-start.8 = (bf16[256,2048]{1,0:T(8,128)(2,1)}, bf16[256,2048]{1,0:T(8,128)(2,1)}, u32[]{:S(2)}, u32[]{:S(2)}) collective-permute-start(bf16[256,2048]{1,0:T(8,128)(2,1)} %get-tuple-element.141), channel_id=1, source_target_pairs={{0,8},{8,0},{16,24},{24,16},{1,9},{9,1},{17,25},{25,17},{2,10},{10... | collective-permute-start | bytes 3145736 | tf_op jit(solution)/shard_map/ppermute | solution.py:437
  99.0 50.4 %collective-permute-start.6 = (bf16[256,2048]{1,0:T(8,128)(2,1)S(1)}, bf16[256,2048]{1,0:T(8,128)(2,1)}, u32[]{:S(2)}, u32[]{:S(2)}) collective-permute-start(bf16[256,2048]{1,0:T(8,128)(2,1)S(1)} %get-tuple-element.142), channel_id=1, source_target_pairs={{0,8},{8,0},{16,24},{24,16},{1,9},{9,1},{17,25},{25,17},{2,10},{10... | collective-permute-start | bytes 3145736 | tf_op jit(solution)/shard_map/ppermute | solution.py:437
  99.4 50.0 %collective-permute-start.9 = (bf16[256,2048]{1,0:T(8,128)(2,1)S(1)}, bf16[256,2048]{1,0:T(8,128)(2,1)}, u32[]{:S(2)}, u32[]{:S(2)}) collective-permute-start(bf16[256,2048]{1,0:T(8,128)(2,1)S(1)} %get-tuple-element.142), channel_id=1, source_target_pairs={{0,16},{8,24},{16,0},{24,8},{1,17},{9,25},{17,1},{25,9},{2,18},{10... | collective-permute-start | bytes 3145736 | tf_op jit(solution)/shard_map/ppermute | solution.py:437
  191.6 49.5 %collective-permute-start.13 = (bf16[256,2048]{1,0:T(8,128)(2,1)}, bf16[256,2048]{1,0:T(8,128)(2,1)}, u32[]{:S(2)}, u32[]{:S(2)}) collective-permute-start(bf16[256,2048]{1,0:T(8,128)(2,1)} %get-tuple-element.290), channel_id=1, source_target_pairs={{0,8},{8,0},{16,24},{24,16},{1,9},{9,1},{17,25},{25,17},{2,10},{10... | collective-permute-start | bytes 3145736 | tf_op jit(solution)/shard_map/ppermute | solution.py:437
  194.4 53.9 %collective-permute-start.16 = (bf16[256,2048]{1,0:T(8,128)(2,1)}, bf16[256,2048]{1,0:T(8,128)(2,1)}, u32[]{:S(2)}, u32[]{:S(2)}) collective-permute-start(bf16[256,2048]{1,0:T(8,128)(2,1)} %get-tuple-element.289), channel_id=1, source_target_pairs={{0,16},{8,24},{16,0},{24,8},{1,17},{9,25},{17,1},{25,9},{2,18},{10... | collective-permute-start | bytes 3145736 | tf_op jit(solution)/shard_map/ppermute | solution.py:437
  221.5 77.6 %collective-permute-start.21 = (bf16[512,1024]{1,0:T(8,128)(2,1)S(1)}, bf16[512,1024]{1,0:T(8,128)(2,1)S(1)}, u32[]{:S(2)}, u32[]{:S(2)}) collective-permute-start(bf16[512,1024]{1,0:T(8,128)(2,1)S(1)} %copy.43), channel_id=1, source_target_pairs={{0,1},{1,0},{2,3},{3,2},{4,5},{5,4},{6,7},{7,6},{8,9},{9,8},{10,11... | collective-permute-start | bytes 3145736 | tf_op jit(solution)/shard_map/ppermute | solution.py:655
  331.7 269.2 %reduce-scatter.8.cloned.1.call-start = ((), (), s32[]{:S(2)}) async-start(), calls=%async_computation.12 | async-start | bytes 9437184 | tf_op jit(solution)/shard_map/reduce_scatter | solution.py:684
  437.3 173.7 %reduce-scatter.10.cloned.1.call-start = ((), (), s32[]{:S(2)}) async-start(), calls=%async_computation.13 | async-start | bytes 3538944 | tf_op jit(solution)/shard_map/reduce_scatter | solution.py:684
  439.0 60.3 %collective-permute-start.28 = (bf16[256,2048]{1,0:T(8,128)(2,1)S(1)}, bf16[256,2048]{1,0:T(8,128)(2,1)}, u32[]{:S(2)}, u32[]{:S(2)}) collective-permute-start(bf16[256,2048]{1,0:T(8,128)(2,1)S(1)} %get-tuple-element.185), channel_id=1, source_target_pairs={{0,8},{8,0},{16,24},{24,16},{1,9},{9,1},{17,25},{25,17},{2,10},{10... | collective-permute-start | bytes 3145736 | tf_op jit(solution)/shard_map/ppermute | solution.py:437
  439.8 59.5 %collective-permute-start.29 = (bf16[256,2048]{1,0:T(8,128)(2,1)S(1)}, bf16[256,2048]{1,0:T(8,128)(2,1)}, u32[]{:S(2)}, u32[]{:S(2)}) collective-permute-start(bf16[256,2048]{1,0:T(8,128)(2,1)S(1)} %get-tuple-element.186), channel_id=1, source_target_pairs={{0,16},{8,24},{16,0},{24,8},{1,17},{9,25},{17,1},{25,9},{2,18},{10... | collective-permute-start | bytes 3145736 | tf_op jit(solution)/shard_map/ppermute | solution.py:437
  504.8 61.4 %collective-permute-start.34 = (bf16[512,2048]{1,0:T(8,128)(2,1)S(1)}, bf16[512,2048]{1,0:T(8,128)(2,1)}, u32[]{:S(2)}, u32[]{:S(2)}) collective-permute-start(bf16[512,2048]{1,0:T(8,128)(2,1)S(1)} %pad_maximum_fusion.6), channel_id=1, source_target_pairs={{0,16},{8,24},{16,0},{24,8},{1,17},{9,25},{17,1},{25,9},{2,18},{10... | collective-permute-start | bytes 6291464 | tf_op jit(solution)/shard_map/ppermute | solution.py:437
  507.9 58.3 %collective-permute-start.33 = (bf16[512,2048]{1,0:T(8,128)(2,1)}, bf16[512,2048]{1,0:T(8,128)(2,1)}, u32[]{:S(2)}, u32[]{:S(2)}) collective-permute-start(bf16[512,2048]{1,0:T(8,128)(2,1)} %pad_maximum_fusion.5), channel_id=1, source_target_pairs={{0,8},{8,0},{16,24},{24,16},{1,9},{9,1},{17,25},{25,17},{2,10},{10... | collective-permute-start | bytes 6291464 | tf_op jit(solution)/shard_map/ppermute | solution.py:437
  567.1 106.6 %reduce-scatter.12.cloned.1.call-start = ((), (), s32[]{:S(2)}) async-start(), calls=%async_computation.14 | async-start | bytes 2359296 | tf_op jit(solution)/shard_map/reduce_scatter | solution.py:781
  570.1 52.0 %collective-permute-start.41 = (bf16[256,2048]{1,0:T(8,128)(2,1)S(1)}, bf16[256,2048]{1,0:T(8,128)(2,1)}, u32[]{:S(2)}, u32[]{:S(2)}) collective-permute-start(bf16[256,2048]{1,0:T(8,128)(2,1)S(1)} %pad_maximum_fusion.9), channel_id=1, source_target_pairs={{0,16},{8,24},{16,0},{24,8},{1,17},{9,25},{17,1},{25,9},{2,18},{10... | collective-permute-start | bytes 3145736 | tf_op jit(solution)/shard_map/ppermute | solution.py:437
  570.8 51.3 %collective-permute-start.40 = (bf16[256,2048]{1,0:T(8,128)(2,1)S(1)}, bf16[256,2048]{1,0:T(8,128)(2,1)}, u32[]{:S(2)}, u32[]{:S(2)}) collective-permute-start(bf16[256,2048]{1,0:T(8,128)(2,1)S(1)} %pad_maximum_fusion.8), channel_id=1, source_target_pairs={{0,8},{8,0},{16,24},{24,16},{1,9},{9,1},{17,25},{25,17},{2,10},{10... | collective-permute-start | bytes 3145736 | tf_op jit(solution)/shard_map/ppermute | solution.py:437
  633.4 98.2 %reduce-scatter.14.cloned.1.call-start = ((), (), s32[]{:S(2)}) async-start(), calls=%async_computation.15 | async-start | bytes 3538944 | tf_op jit(solution)/shard_map/reduce_scatter | solution.py:684
  (73 other events, 1405.6 us)
Sparse Core Ops, SparseCore 0:
  10.4 67.4 all-gather.4
  79.5 80.6 all-gather.6
  161.9 80.5 all-gather.8
  243.9 81.0 all-gather.10
  331.8 89.8 reduce-scatter.5
  437.4 89.6 reduce-scatter.7
  567.2 40.9 reduce-scatter.9
  633.6 36.2 reduce-scatter.11
  672.1 38.9 reduce-scatter.13

commit v17 on v16

--- a/solution.py
+++ b/solution.py
@@ -741,7 +741,7 @@
     begun = order(
         lambda *grads: attend_backward(*attention, grads, seq_count, local_len, 0, pairs // 2), *mixed_grad
     )
-    branch_other = pair_swap(branch_grad)
+    branch_other = pair_swap(gate(branch_grad, result_rest) if square else branch_grad)
     branch_pair = jnp.concatenate([branch_grad, branch_other], axis=0)
     out_sum = order(lambda columns: outer(columns, branch_pair, groups, 1), mixed_half)
     if square:
@@ -780,6 +780,7 @@
         out_sum = gate(out_sum, *far)
     grad_w_out = lax.psum_scatter(out_sum, "fsdp", scatter_dimension=0, tiled=True).astype(wide)
     second_sum = slab_product(normed, qkv_grad, (1, 2))
+    qkv_column_sum = order(column_sum, qkv_grad)
     if square:
         second_sum = slab_sum(gate(second_sum, *far, *direct))
         came = order.add_far(near, far, direct)
@@ -788,7 +789,6 @@
     else:
         second_sum = slab_sum(second_sum)
         normed_own, came = scatter(to_normed, qkv_grad), ()
-    qkv_column_sum = order(column_sum, qkv_grad)
     grad_tokens, _, input_sums = order(
         lambda own, *came: norm_back(own, x_low, *first_stats, middle_grad, ln1_gain, came), normed_own, *came
     )

time: 759 us -> 739 us (0.974)
  waiting for transfers between devices: 151 us -> 138 us
    ppermute x44, waiting for transfers between devices: 147 us -> 133 us  [swap(): return lax.ppermute(values, 'seq', [(i, i ^ bit) for i in range(4)])]
    unnamed x98 -> x100, local copies, waits for them, and re-layouts: 43.5 us -> 41.2 us
  transfers between devices with their start and end apart: 64 -> 64, of which waited for: 22 -> 22; matrix products, arithmetic and copies ran while one was open for 31% -> 31% of each run, Pallas kernels for 37% -> 38%
where the time goes in v17:
time: 739 us; the launch traced here: 734 us
  Pallas kernels  280 us (38%)
  waiting for transfers between devices  138 us (19%)
  local copies, waits for them, and re-layouts  92.8 us (13%)
  matrix products  85.6 us (12%)
  starting transfers between devices  67.8 us (9%)
  other arithmetic  54.8 us (7%)
  between operations  15 us (2%)
    ppermute x44, waiting for transfers between devices, swap(): return lax.ppermute(values, 'seq', [(i, i ^ bit) for i in range(4)])  133 us
    pallas_call x5, Pallas kernels, outer(): pl.pallas_call(partial(outer_kernel, chunk=next((c for c in (512, 384, 25...  82 us
    pallas_call x2, Pallas kernels, attend_backward(): pl.pallas_call(partial(attend_backward_kernel, blocks=blocks, seqs=seqs,...  56.9 us
    dot_general x5, matrix products, contract_last(): lax.dot_general(left_side, right_side, (((1,), (1,)), ((), ())), preferre...  52.7 us
    ppermute x44, starting transfers between devices, swap(): return lax.ppermute(values, 'seq', [(i, i ^ bit) for i in range(4)])  47.7 us
    unnamed x100, local copies, waits for them, and re-layouts  41.2 us
    dot_general x3, matrix products, contract(): lax.dot_general(left_side, right_side, (((1,), (0,)), ((), ())), preferre...  32.9 us
    pallas_call x1, Pallas kernels, up_and_bend(): pl.pallas_call(partial(up_kernel, chunk=512), grid=(count // TILE,), in_s...  30.6 us
  transfers between devices with their start and end apart: 64, of which 22 were waited for; matrix products, arithmetic and copies ran while one was open for 31% of the time, Pallas kernels for 38%

profile of v17, /device:TPU:0, one launch (start us, length us, event | category | flops | bytes accessed | tf_op | source)
XLA Modules:
  0.0 733.6 jit_solution(5375719639667772304)
XLA Ops:
  28.2 18.7 %collective-permute-done.2 = bf16[256,2048]{1,0:T(8,128)(2,1)} collective-permute-done((bf16[256,2048]{1,0:T(8,128)(2,1)}, bf16[256,2048]{1,0:T(8,128)(2,1)}, u32[]{:S(2)}, u32[]{:S(2)}) %collective-permute-start.2) | collective-permute-done | bytes 1048608 | tf_op jit(solution)/shard_map/ppermute | solution.py:437
  53.7 17.7 %collective-permute-done = bf16[256,2048]{1,0:T(8,128)(2,1)} collective-permute-done((bf16[256,2048]{1,0:T(8,128)(2,1)}, bf16[256,2048]{1,0:T(8,128)(2,1)}, u32[]{:S(2)}, u32[]{:S(2)}) %collective-permute-start) | collective-permute-done | bytes 1048608 | tf_op jit(solution)/shard_map/ppermute | solution.py:437
  79.6 12.8 %collective-permute-done.4 = bf16[256,2048]{1,0:T(8,128)(2,1)} collective-permute-done((bf16[256,2048]{1,0:T(8,128)(2,1)}, bf16[256,2048]{1,0:T(8,128)(2,1)}, u32[]{:S(2)}, u32[]{:S(2)}) %collective-permute-start.4) | collective-permute-done | bytes 1048608 | tf_op jit(solution)/shard_map/ppermute | solution.py:437
  101.1 18.6 %add_convert_fusion.qkv_ref = bf16[2048,1536]{1,0:T(8,128)(2,1)} fusion(bf16[2048,2048]{1,0:T(8,128)(2,1)} %constant_dynamic-update-slice_fusion.left_ref, bf16[2048,1536]{1,0:T(8,128)(2,1)} %all-gather.5.cloned.1.call-done, f32[1536]{0:T(1024)S(1)} %reduce.2), kind=kOutput, calls=%fused_computation.1 | convolution fusion | flops 12891193344 | bytes 20977664 | tf_op jit(solution)/shard_map/dot_general | solution.py:31
  119.7 29.7 %attend_forward.1 = (bf16[2048,512]{1,0:T(8,128)(2,1)}, f32[2048,512]{1,0:T(8,128)}) custom-call(s32[1]{0:T(128)} %bitcast.1.at_ref.mask_ref, f32[8]{0:T(128)} %multiply_power_fusion.slope_ref, bf16[2048,1536]{1,0:T(8,128)(2,1)} %add_convert_fusion.qkv_ref), custom_call_target="tpu_custom_call" | custom-call | flops 2684354560 | bytes 2621440 | tf_op jit(solution)/shard_map/attend_forward/pallas_call | solution.py:173
  156.8 11.2 %collective-permute-done.10 = bf16[512,512]{1,0:T(8,128)(2,1)S(1)} collective-permute-done((bf16[512,512]{1,0:T(8,128)(2,1)}, bf16[512,512]{1,0:T(8,128)(2,1)S(1)}, u32[]{:S(2)}, u32[]{:S(2)}) %collective-permute-start.10) | collective-permute-done | bytes 524320 | tf_op jit(solution)/shard_map/ppermute | solution.py:437
  221.7 18.7 %collective-permute-done.14 = bf16[256,2048]{1,0:T(8,128)(2,1)} collective-permute-done((bf16[256,2048]{1,0:T(8,128)(2,1)}, bf16[256,2048]{1,0:T(8,128)(2,1)}, u32[]{:S(2)}, u32[]{:S(2)}) %collective-permute-start.14) | collective-permute-done | bytes 1048608 | tf_op jit(solution)/shard_map/ppermute | solution.py:437
  250.7 11.3 %collective-permute-done.17 = bf16[256,2048]{1,0:T(8,128)(2,1)} collective-permute-done((bf16[256,2048]{1,0:T(8,128)(2,1)}, bf16[256,2048]{1,0:T(8,128)(2,1)}, u32[]{:S(2)}, u32[]{:S(2)}) %collective-permute-start.17) | collective-permute-done | bytes 1048608 | tf_op jit(solution)/shard_map/ppermute | solution.py:437
  268.5 30.6 %up_and_bend.1 = (bf16[2048,2048]{1,0:T(8,128)(2,1)}, f32[2048,2048]{1,0:T(8,128)}) custom-call(bf16[2048,2048]{1,0:T(8,128)(2,1)} %constant_dynamic-update-slice_fusion.7.rows_ref.left_ref, bf16[2048,2048]{1,0:T(8,128)(2,1)} %all-gather.9.cloned.1.call-done.weight_ref, f32[1,2048]{1,0:T(1,128)} %bitcast.152), custom_call_target="tpu_custom_call" | custom-call | flops 8589934592 | bytes 8388608 | tf_op jit(solution)/shard_map/up_and_bend/pallas_call | solution.py:259
  308.2 23.5 %outer.5 = bf16[8,4,64,2048]{3,2,1,0:T(8,128)(2,1)} custom-call(bf16[2048,2048]{1,0:T(8,128)(2,1)} %constant_dynamic-update-slice_fusion.31.left_ref.rows_ref, bf16[2048,2048]{1,0:T(8,128)(2,1)} %get-tuple-element.185.right_ref.rows_ref), custom_call_target="tpu_custom_call" | custom-call | flops 4294967296 | bytes 4194304 | tf_op jit(solution)/shard_map/outer/pallas_call | solution.py:420
  331.8 25.4 %hidden_gradient.1 = (bf16[2048,2048]{1,0:T(8,128)(2,1)}, f32[1,2048]{1,0:T(1,128)}) custom-call(bf16[2048,2048]{1,0:T(8,128)(2,1)} %constant_dynamic-update-slice_fusion.31.left_ref.rows_ref, bf16[2048,2048]{1,0:T(8,128)(2,1)} %all-gather.11.cloned.1.call-done.weight_ref, f32[2048,2048]{1,0:T(8,128)} %get-tuple-element.156.slope_ref), custom_call_target="tpu_custom_call" | custom-call | flops 6442450944 | bytes 6291456 | tf_op jit(solution)/shard_map/hidden_gradient/pallas_call | solution.py:283
  357.2 8.6 %convolution_convert_fusion.5 = bf16[512,2048]{1,0:T(8,128)(2,1)S(1)} fusion(bf16[2048,2048]{1,0:T(8,128)(2,1)} %all-gather.9.cloned.1.call-done.weight_ref, bf16[2048,2048]{1,0:T(8,128)(2,1)} %get-tuple-element.175.right_ref), kind=kOutput, calls=%fused_computation.24 | convolution fusion | flops 4296015872 | bytes 12582912 | tf_op jit(solution)/shard_map/dot_general | solution.py:37
  369.1 18.1 %convolution_convert_fusion.own_ref = bf16[1536,2048]{1,0:T(8,128)(2,1)S(1)} fusion(bf16[2048,2048]{1,0:T(8,128)(2,1)} %all-gather.9.cloned.1.call-done.weight_ref, bf16[2048,2048]{1,0:T(8,128)(2,1)} %get-tuple-element.175.right_ref), kind=kOutput, calls=%fused_computation.2 | convolution fusion | flops 12888047616 | bytes 20971520 | tf_op jit(solution)/shard_map/dot_general | solution.py:37
  405.5 23.6 %outer.6 = bf16[8,4,64,2048]{3,2,1,0:T(8,128)(2,1)} custom-call(bf16[2048,2048]{1,0:T(8,128)(2,1)} %constant_dynamic-update-slice_fusion.7.rows_ref.left_ref, bf16[2048,2048]{1,0:T(8,128)(2,1)} %get-tuple-element.175.right_ref), custom_call_target="tpu_custom_call" | custom-call | flops 4294967296 | bytes 4194304 | tf_op jit(solution)/shard_map/outer/pallas_call | solution.py:420
  440.4 11.4 %norm_back.2 = (bf16[512,2048]{1,0:T(8,128)(2,1)}, f32[512,2048]{1,0:T(8,128)}, f32[24,2048]{1,0:T(8,128)}) custom-call(bf16[1536,2048]{1,0:T(8,128)(2,1)} %copy-done.5, f32[512,2048]{1,0:T(8,128)} %copy-done, f32[512,1]{1,0:T(8,128)} %copy.45.average_ref, f32[512,1]{1,0:T(8,128)} %copy.46.scale_ref, bf16[512,2048]{1,0:T(8,128)(2,1)} %bitcast.108, ...), custom_call_target="tpu_custom_call" | custom-call | flops 7864320 | bytes 7680 | tf_op jit(solution)/shard_map/norm_back/pallas_call | solution.py:388
  452.8 8.9 %mixed_gradient.1 = bf16[512,2048]{1,0:T(8,128)(2,1)} custom-call(bf16[512,2048]{1,0:T(8,128)(2,1)} %get-tuple-element.196.rows_ref, bf16[2048,2048]{1,0:T(8,128)(2,1)} %all-gather.7.cloned.1.call-done.weight_ref), custom_call_target="tpu_custom_call" | custom-call | flops 1073741824 | bytes 1048576 | tf_op jit(solution)/shard_map/mixed_gradient/pallas_call | solution.py:330
  468.4 18.9 %product.1 = bf16[1536,2048]{1,0:T(8,128)(2,1)} custom-call(bf16[2048,2048]{1,0:T(8,128)(2,1)} %get-tuple-element.185.right_ref.rows_ref, bf16[2048,2048]{1,0:T(8,128)(2,1)} %all-gather.11.cloned.1.call-done.weight_ref), custom_call_target="tpu_custom_call" | custom-call | flops 3221225472 | bytes 3145728 | tf_op jit(solution)/shard_map/product/pallas_call | solution.py:308
  501.0 28.4 %attend_backward.2.right_ref.rest_4_ = bf16[2048,1536]{1,0:T(8,128)(2,1)} custom-call(s32[1]{0:T(128)} %bitcast.1.at_ref.mask_ref, f32[8]{0:T(128)} %multiply_power_fusion.slope_ref, bf16[2048,1536]{1,0:T(8,128)(2,1)} %add_convert_fusion.qkv_ref, f32[2048,512]{1,0:T(8,128)} %get-tuple-element.138.lse_ref, bf16[2048,512]{1,0:T(8,128)(2,1)} %get-tuple-element.137.mixed_ref, ...), custom_call_target="tpu_custom_call" | custom-call | flops 3355443200 | bytes 3276800 | tf_op jit(solution)/shard_map/attend_backward/pallas_call | solution.py:198
  529.4 8.8 %outer.7 = bf16[1,4,256,2048]{3,2,1,0:T(8,128)(2,1)} custom-call(bf16[1024,1024]{1,0:T(8,128)(2,1)} %pad_maximum_fusion.4.left_ref, bf16[1024,2048]{1,0:T(8,128)(2,1)} %pad_maximum_fusion.right_ref), custom_call_target="tpu_custom_call" | custom-call | flops 1073741824 | bytes 1048576 | tf_op jit(solution)/shard_map/outer/pallas_call | solution.py:420
  541.8 12.9 %outer.8 = bf16[8,4,64,768]{3,2,1,0:T(8,128)(2,1)} custom-call(bf16[2048,2048]{1,0:T(8,128)(2,1)} %constant_dynamic-update-slice_fusion.left_ref, bf16[2048,1536]{1,0:T(8,128)(2,1)} %attend_backward.2.right_ref.rest_4_), custom_call_target="tpu_custom_call" | custom-call | flops 1610612736 | bytes 1572864 | tf_op jit(solution)/shard_map/outer/pallas_call | solution.py:420
  560.7 28.6 %attend_backward.3.right_ref = bf16[2048,1536]{1,0:T(8,128)(2,1)} custom-call(s32[1]{0:T(128)} %bitcast.1.at_ref.mask_ref, f32[8]{0:T(128)} %multiply_power_fusion.slope_ref, bf16[2048,1536]{1,0:T(8,128)(2,1)} %add_convert_fusion.qkv_ref, f32[2048,512]{1,0:T(8,128)} %get-tuple-element.138.lse_ref, ...), custom_call_target="tpu_custom_call", output_to_operand_aliasing={{}: (9, {})} | custom-call | flops 3355443200 | bytes 3276800 | tf_op jit(solution)/shard_map/attend_backward/pallas_call | solution.py:198
  599.2 11.1 %convolution_convert_fusion.1 = bf16[1024,2048]{1,0:T(8,128)(2,1)} fusion(bf16[2048,1536]{1,0:T(8,128)(2,1)} %all-gather.5.cloned.1.call-done, bf16[2048,1536]{1,0:T(8,128)(2,1)} %attend_backward.3.right_ref), kind=kOutput, calls=%fused_computation.19 | convolution fusion | flops 6444548096 | bytes 13631488 | tf_op jit(solution)/shard_map/dot_general | solution.py:37
  625.2 13.1 %outer.9 = bf16[8,4,64,768]{3,2,1,0:T(8,128)(2,1)} custom-call(bf16[2048,2048]{1,0:T(8,128)(2,1)} %constant_dynamic-update-slice_fusion.left_ref, bf16[2048,1536]{1,0:T(8,128)(2,1)} %attend_backward.3.right_ref), custom_call_target="tpu_custom_call" | custom-call | flops 1610612736 | bytes 1572864 | tf_op jit(solution)/shard_map/outer/pallas_call | solution.py:420
  679.7 11.2 %norm_back.3 = (bf16[512,2048]{1,0:T(8,128)(2,1)}, f32[512,2048]{1,0:T(8,128)}, f32[24,2048]{1,0:T(8,128)}) custom-call(bf16[512,2048]{1,0:T(8,128)(2,1)} %convolution_convert_fusion.2.own_ref, bf16[512,2048]{1,0:T(8,128)(2,1)} %bitcast.104, f32[512,1]{1,0:T(8,128)} %bitcast.128, f32[512,1]{1,0:T(8,128)} %bitcast.127, ...), custom_call_target="tpu_custom_call" | custom-call | flops 7864320 | bytes 7680 | tf_op jit(solution)/shard_map/norm_back/pallas_call | solution.py:388
  (328 shorter events, 296.6 us)
Async XLA Ops:
  7.2 93.9 %all-gather.5.cloned.1.call-start = ((), (), s32[]{:S(2)}) async-start(), calls=%async_computation.7 | async-start | bytes 7077888 | tf_op jit(solution)/shard_map/all_gather | solution.py:629
  10.3 170.0 %all-gather.7.cloned.1.call-start = ((), (), s32[]{:S(2)}) async-start(), calls=%async_computation.8 | async-start | bytes 9437184 | tf_op jit(solution)/shard_map/all_gather | solution.py:641
  11.1 257.5 %all-gather.9.cloned.1.call-start = ((), (), s32[]{:S(2)}) async-start(), calls=%async_computation.9 | async-start | bytes 9437184 | tf_op jit(solution)/shard_map/all_gather | solution.py:642
  19.5 312.3 %all-gather.11.cloned.1.call-start = ((), (), s32[]{:S(2)}) async-start(), calls=%async_computation.10 | async-start | bytes 9437184 | tf_op jit(solution)/shard_map/all_gather | solution.py:643
  24.0 47.4 %collective-permute-start = (bf16[256,2048]{1,0:T(8,128)(2,1)}, bf16[256,2048]{1,0:T(8,128)(2,1)}, u32[]{:S(2)}, u32[]{:S(2)}) collective-permute-start(bf16[256,2048]{1,0:T(8,128)(2,1)} %get-tuple-element.299), channel_id=1, source_target_pairs={{0,8},{8,0},{16,24},{24,16},{1,9},{9,1},{17,25},{25,17},{2,10},{10... | collective-permute-start | bytes 3145736 | tf_op jit(solution)/shard_map/ppermute | solution.py:437
  24.6 52.7 %collective-permute-start.3 = (bf16[256,2048]{1,0:T(8,128)(2,1)}, bf16[256,2048]{1,0:T(8,128)(2,1)}, u32[]{:S(2)}, u32[]{:S(2)}) collective-permute-start(bf16[256,2048]{1,0:T(8,128)(2,1)} %get-tuple-element.298), channel_id=1, source_target_pairs={{0,16},{8,24},{16,0},{24,8},{1,17},{9,25},{17,1},{25,9},{2,18},{10... | collective-permute-start | bytes 3145736 | tf_op jit(solution)/shard_map/ppermute | solution.py:437
  26.9 474.1 %reduce-scatter.6.cloned.1.call-start = ((), (), s32[]{:S(2)}) async-start(), calls=%async_computation.11 | async-start | bytes 9437184 | tf_op jit(solution)/shard_map/reduce_scatter | solution.py:684
  97.0 52.4 %collective-permute-start.7 = (bf16[256,2048]{1,0:T(8,128)(2,1)}, bf16[256,2048]{1,0:T(8,128)(2,1)}, u32[]{:S(2)}, u32[]{:S(2)}) collective-permute-start(bf16[256,2048]{1,0:T(8,128)(2,1)} %get-tuple-element.142), channel_id=1, source_target_pairs={{0,16},{8,24},{16,0},{24,8},{1,17},{9,25},{17,1},{25,9},{2,18},{10... | collective-permute-start | bytes 3145736 | tf_op jit(solution)/shard_map/ppermute | solution.py:437
  97.4 52.1 %collective-permute-start.8 = (bf16[256,2048]{1,0:T(8,128)(2,1)}, bf16[256,2048]{1,0:T(8,128)(2,1)}, u32[]{:S(2)}, u32[]{:S(2)}) collective-permute-start(bf16[256,2048]{1,0:T(8,128)(2,1)} %get-tuple-element.142), channel_id=1, source_target_pairs={{0,8},{8,0},{16,24},{24,16},{1,9},{9,1},{17,25},{25,17},{2,10},{10... | collective-permute-start | bytes 3145736 | tf_op jit(solution)/shard_map/ppermute | solution.py:437
  99.0 50.4 %collective-permute-start.6 = (bf16[256,2048]{1,0:T(8,128)(2,1)S(1)}, bf16[256,2048]{1,0:T(8,128)(2,1)}, u32[]{:S(2)}, u32[]{:S(2)}) collective-permute-start(bf16[256,2048]{1,0:T(8,128)(2,1)S(1)} %get-tuple-element.143), channel_id=1, source_target_pairs={{0,8},{8,0},{16,24},{24,16},{1,9},{9,1},{17,25},{25,17},{2,10},{10... | collective-permute-start | bytes 3145736 | tf_op jit(solution)/shard_map/ppermute | solution.py:437
  99.4 50.1 %collective-permute-start.9 = (bf16[256,2048]{1,0:T(8,128)(2,1)S(1)}, bf16[256,2048]{1,0:T(8,128)(2,1)}, u32[]{:S(2)}, u32[]{:S(2)}) collective-permute-start(bf16[256,2048]{1,0:T(8,128)(2,1)S(1)} %get-tuple-element.143), channel_id=1, source_target_pairs={{0,16},{8,24},{16,0},{24,8},{1,17},{9,25},{17,1},{25,9},{2,18},{10... | collective-permute-start | bytes 3145736 | tf_op jit(solution)/shard_map/ppermute | solution.py:437
  191.6 49.5 %collective-permute-start.13 = (bf16[256,2048]{1,0:T(8,128)(2,1)}, bf16[256,2048]{1,0:T(8,128)(2,1)}, u32[]{:S(2)}, u32[]{:S(2)}) collective-permute-start(bf16[256,2048]{1,0:T(8,128)(2,1)} %get-tuple-element.292), channel_id=1, source_target_pairs={{0,8},{8,0},{16,24},{24,16},{1,9},{9,1},{17,25},{25,17},{2,10},{10... | collective-permute-start | bytes 3145736 | tf_op jit(solution)/shard_map/ppermute | solution.py:437
  194.4 53.9 %collective-permute-start.16 = (bf16[256,2048]{1,0:T(8,128)(2,1)}, bf16[256,2048]{1,0:T(8,128)(2,1)}, u32[]{:S(2)}, u32[]{:S(2)}) collective-permute-start(bf16[256,2048]{1,0:T(8,128)(2,1)} %get-tuple-element.291), channel_id=1, source_target_pairs={{0,16},{8,24},{16,0},{24,8},{1,17},{9,25},{17,1},{25,9},{2,18},{10... | collective-permute-start | bytes 3145736 | tf_op jit(solution)/shard_map/ppermute | solution.py:437
  221.6 77.6 %collective-permute-start.21 = (bf16[512,1024]{1,0:T(8,128)(2,1)S(1)}, bf16[512,1024]{1,0:T(8,128)(2,1)S(1)}, u32[]{:S(2)}, u32[]{:S(2)}) collective-permute-start(bf16[512,1024]{1,0:T(8,128)(2,1)S(1)} %copy.43), channel_id=1, source_target_pairs={{0,1},{1,0},{2,3},{3,2},{4,5},{5,4},{6,7},{7,6},{8,9},{9,8},{10,11... | collective-permute-start | bytes 3145736 | tf_op jit(solution)/shard_map/ppermute | solution.py:655
  331.7 257.6 %reduce-scatter.8.cloned.1.call-start = ((), (), s32[]{:S(2)}) async-start(), calls=%async_computation.12 | async-start | bytes 9437184 | tf_op jit(solution)/shard_map/reduce_scatter | solution.py:684
  437.3 162.0 %reduce-scatter.10.cloned.1.call-start = ((), (), s32[]{:S(2)}) async-start(), calls=%async_computation.13 | async-start | bytes 3538944 | tf_op jit(solution)/shard_map/reduce_scatter | solution.py:684
  439.1 50.3 %collective-permute-start.28 = (bf16[256,2048]{1,0:T(8,128)(2,1)S(1)}, bf16[256,2048]{1,0:T(8,128)(2,1)}, u32[]{:S(2)}, u32[]{:S(2)}) collective-permute-start(bf16[256,2048]{1,0:T(8,128)(2,1)S(1)} %get-tuple-element.186), channel_id=1, source_target_pairs={{0,8},{8,0},{16,24},{24,16},{1,9},{9,1},{17,25},{25,17},{2,10},{10... | collective-permute-start | bytes 3145736 | tf_op jit(solution)/shard_map/ppermute | solution.py:437
  439.9 49.5 %collective-permute-start.29 = (bf16[256,2048]{1,0:T(8,128)(2,1)S(1)}, bf16[256,2048]{1,0:T(8,128)(2,1)}, u32[]{:S(2)}, u32[]{:S(2)}) collective-permute-start(bf16[256,2048]{1,0:T(8,128)(2,1)S(1)} %get-tuple-element.187), channel_id=1, source_target_pairs={{0,16},{8,24},{16,0},{24,8},{1,17},{9,25},{17,1},{25,9},{2,18},{10... | collective-permute-start | bytes 3145736 | tf_op jit(solution)/shard_map/ppermute | solution.py:437
  494.9 59.9 %collective-permute-start.34 = (bf16[512,2048]{1,0:T(8,128)(2,1)S(1)}, bf16[512,2048]{1,0:T(8,128)(2,1)}, u32[]{:S(2)}, u32[]{:S(2)}) collective-permute-start(bf16[512,2048]{1,0:T(8,128)(2,1)S(1)} %pad_maximum_fusion.6), channel_id=1, source_target_pairs={{0,16},{8,24},{16,0},{24,8},{1,17},{9,25},{17,1},{25,9},{2,18},{10... | collective-permute-start | bytes 6291464 | tf_op jit(solution)/shard_map/ppermute | solution.py:437
  497.5 57.3 %collective-permute-start.33 = (bf16[512,2048]{1,0:T(8,128)(2,1)}, bf16[512,2048]{1,0:T(8,128)(2,1)}, u32[]{:S(2)}, u32[]{:S(2)}) collective-permute-start(bf16[512,2048]{1,0:T(8,128)(2,1)} %pad_maximum_fusion.5), channel_id=1, source_target_pairs={{0,8},{8,0},{16,24},{24,16},{1,9},{9,1},{17,25},{25,17},{2,10},{10... | collective-permute-start | bytes 6291464 | tf_op jit(solution)/shard_map/ppermute | solution.py:437
  555.3 102.4 %reduce-scatter.12.cloned.1.call-start = ((), (), s32[]{:S(2)}) async-start(), calls=%async_computation.14 | async-start | bytes 2359296 | tf_op jit(solution)/shard_map/reduce_scatter | solution.py:781
  558.3 52.1 %collective-permute-start.39 = (bf16[256,2048]{1,0:T(8,128)(2,1)S(1)}, bf16[256,2048]{1,0:T(8,128)(2,1)}, u32[]{:S(2)}, u32[]{:S(2)}) collective-permute-start(bf16[256,2048]{1,0:T(8,128)(2,1)S(1)} %pad_maximum_fusion.9), channel_id=1, source_target_pairs={{0,16},{8,24},{16,0},{24,8},{1,17},{9,25},{17,1},{25,9},{2,18},{10... | collective-permute-start | bytes 3145736 | tf_op jit(solution)/shard_map/ppermute | solution.py:437
  559.0 51.4 %collective-permute-start.38 = (bf16[256,2048]{1,0:T(8,128)(2,1)S(1)}, bf16[256,2048]{1,0:T(8,128)(2,1)}, u32[]{:S(2)}, u32[]{:S(2)}) collective-permute-start(bf16[256,2048]{1,0:T(8,128)(2,1)S(1)} %pad_maximum_fusion.8), channel_id=1, source_target_pairs={{0,8},{8,0},{16,24},{24,16},{1,9},{9,1},{17,25},{25,17},{2,10},{10... | collective-permute-start | bytes 3145736 | tf_op jit(solution)/shard_map/ppermute | solution.py:437
  620.4 90.9 %reduce-scatter.14.cloned.1.call-start = ((), (), s32[]{:S(2)}) async-start(), calls=%async_computation.15 | async-start | bytes 3538944 | tf_op jit(solution)/shard_map/reduce_scatter | solution.py:684
  (74 other events, 1344.0 us)
Sparse Core Ops, SparseCore 0:
  10.4 67.4 all-gather.4
  79.5 80.6 all-gather.6
  161.9 80.5 all-gather.8
  243.9 81.0 all-gather.10
  331.8 89.8 reduce-scatter.5
  437.4 89.6 reduce-scatter.7
  555.4 40.9 reduce-scatter.9
  620.5 37.0 reduce-scatter.11
  659.9 39.1 reduce-scatter.13

commit v18 on v17

--- a/solution.py
+++ b/solution.py
@@ -671,10 +671,10 @@
     upstream_made = order.fill(upstream)
     theirs = pair_swap(theirs)
     dz_sum = order(lambda values: jnp.sum(values.astype(wide), axis=0), dz_low)
-    second = whole(order.pass_on(second))
+    mixed_half = order(lambda *parts: jnp.concatenate(parts, axis=0), mine, theirs)
+    second = whole(order.pass_on(second, mixed_half))
     upstream = order.pass_on(upstream, second)
     active, slope = order(lambda rows: up_and_bend(rows, up_slab, up_bias_slab[None]), second)
-    mixed_half = order(lambda *parts: jnp.concatenate(parts, axis=0), mine, theirs)
     upstream = order.complete(upstream_made, upstream)
 
     def slab_product(left, right, part_of=(0, 1)):
@@ -769,6 +769,7 @@
         order.after(first_sum)
         near = order(slots(to_normed, 1, 3), qkv_grad)
         direct = swap_direct(near, half)
+        qkv_column_sum = order(column_sum, qkv_grad)
         order.after(*out_came)
         out_sum = order(lambda own, *came: summed(own[:part], came).astype(low), out_sum, *out_came)
     out_sum = out_sum.reshape(-1, 1, out_rows, model_width)
@@ -780,7 +781,6 @@
         out_sum = gate(out_sum, *far)
     grad_w_out = lax.psum_scatter(out_sum, "fsdp", scatter_dimension=0, tiled=True).astype(wide)
     second_sum = slab_product(normed, qkv_grad, (1, 2))
-    qkv_column_sum = order(column_sum, qkv_grad)
     if square:
         second_sum = slab_sum(gate(second_sum, *far, *direct))
         came = order.add_far(near, far, direct)
@@ -788,6 +788,7 @@
         normed_own = order(slots(to_normed, 0, 1), qkv_grad)
     else:
         second_sum = slab_sum(second_sum)
+        qkv_column_sum = order(column_sum, qkv_grad)
         normed_own, came = scatter(to_normed, qkv_grad), ()
     grad_tokens, _, input_sums = order(
         lambda own, *came: norm_back(own, x_low, *first_stats, middle_grad, ln1_gain, came), normed_own, *came

time: 739 us -> 739 us (level)
    unnamed x100 -> x92, local copies, waits for them, and re-layouts: 41.2 us -> 42.6 us
  transfers between devices with their start and end apart: 64 -> 64, of which waited for: 22 -> 22; matrix products, arithmetic and copies ran while one was open for 31% -> 32% of each run, Pallas kernels for 38% -> 38%
where the time goes in v18:
time: 739 us; the launch traced here: 734 us
  Pallas kernels  280 us (38%)
  waiting for transfers between devices  132 us (18%)
  local copies, waits for them, and re-layouts  97.4 us (13%)
  matrix products  85.6 us (12%)
  starting transfers between devices  66.4 us (9%)
  other arithmetic  57.2 us (8%)
  between operations  14.9 us (2%)
    ppermute x44, waiting for transfers between devices, swap(): return lax.ppermute(values, 'seq', [(i, i ^ bit) for i in range(4)])  129 us
    pallas_call x5, Pallas kernels, outer(): pl.pallas_call(partial(outer_kernel, chunk=next((c for c in (512, 384, 25...  81.9 us
    pallas_call x2, Pallas kernels, attend_backward(): pl.pallas_call(partial(attend_backward_kernel, blocks=blocks, seqs=seqs,...  56.7 us
    dot_general x5, matrix products, contract_last(): lax.dot_general(left_side, right_side, (((1,), (1,)), ((), ())), preferre...  52.8 us
    ppermute x44, starting transfers between devices, swap(): return lax.ppermute(values, 'seq', [(i, i ^ bit) for i in range(4)])  48.5 us
    unnamed x92, local copies, waits for them, and re-layouts  42.6 us
    dot_general x3, matrix products, contract(): lax.dot_general(left_side, right_side, (((1,), (0,)), ((), ())), preferre...  32.8 us
    pallas_call x1, Pallas kernels, up_and_bend(): pl.pallas_call(partial(up_kernel, chunk=512), grid=(count // TILE,), in_s...  30.6 us
  transfers between devices with their start and end apart: 64, of which 22 were waited for; matrix products, arithmetic and copies ran while one was open for 32% of the time, Pallas kernels for 38%

profile of v18, /device:TPU:0, one launch (start us, length us, event | category | flops | bytes accessed | tf_op | source)
XLA Modules:
  0.0 734.1 jit_solution(2218010782112024740)
XLA Ops:
  28.0 18.9 %collective-permute-done.2 = bf16[256,2048]{1,0:T(8,128)(2,1)} collective-permute-done((bf16[256,2048]{1,0:T(8,128)(2,1)}, bf16[256,2048]{1,0:T(8,128)(2,1)}, u32[]{:S(2)}, u32[]{:S(2)}) %collective-permute-start.2) | collective-permute-done | bytes 1048608 | tf_op jit(solution)/shard_map/ppermute | solution.py:437
  53.7 17.7 %collective-permute-done = bf16[256,2048]{1,0:T(8,128)(2,1)} collective-permute-done((bf16[256,2048]{1,0:T(8,128)(2,1)}, bf16[256,2048]{1,0:T(8,128)(2,1)}, u32[]{:S(2)}, u32[]{:S(2)}) %collective-permute-start) | collective-permute-done | bytes 1048608 | tf_op jit(solution)/shard_map/ppermute | solution.py:437
  79.6 12.8 %collective-permute-done.4 = bf16[256,2048]{1,0:T(8,128)(2,1)} collective-permute-done((bf16[256,2048]{1,0:T(8,128)(2,1)}, bf16[256,2048]{1,0:T(8,128)(2,1)}, u32[]{:S(2)}, u32[]{:S(2)}) %collective-permute-start.4) | collective-permute-done | bytes 1048608 | tf_op jit(solution)/shard_map/ppermute | solution.py:437
  101.0 18.6 %add_convert_fusion.qkv_ref = bf16[2048,1536]{1,0:T(8,128)(2,1)} fusion(bf16[2048,2048]{1,0:T(8,128)(2,1)} %constant_dynamic-update-slice_fusion.left_ref, bf16[2048,1536]{1,0:T(8,128)(2,1)} %all-gather.5.cloned.1.call-done, f32[1536]{0:T(1024)S(1)} %reduce.2), kind=kOutput, calls=%fused_computation.1 | convolution fusion | flops 12891193344 | bytes 20977664 | tf_op jit(solution)/shard_map/dot_general | solution.py:31
  119.6 29.7 %attend_forward.1 = (bf16[2048,512]{1,0:T(8,128)(2,1)}, f32[2048,512]{1,0:T(8,128)}) custom-call(s32[1]{0:T(128)} %bitcast.1.at_ref.mask_ref, f32[8]{0:T(128)} %multiply_power_fusion.slope_ref, bf16[2048,1536]{1,0:T(8,128)(2,1)} %add_convert_fusion.qkv_ref), custom_call_target="tpu_custom_call" | custom-call | flops 2684354560 | bytes 2621440 | tf_op jit(solution)/shard_map/attend_forward/pallas_call | solution.py:173
  155.4 12.5 %collective-permute-done.10 = bf16[512,512]{1,0:T(8,128)(2,1)S(1)} collective-permute-done((bf16[512,512]{1,0:T(8,128)(2,1)}, bf16[512,512]{1,0:T(8,128)(2,1)S(1)}, u32[]{:S(2)}, u32[]{:S(2)}) %collective-permute-start.10) | collective-permute-done | bytes 524320 | tf_op jit(solution)/shard_map/ppermute | solution.py:437
  226.8 13.2 %collective-permute-done.15 = bf16[256,2048]{1,0:T(8,128)(2,1)} collective-permute-done((bf16[256,2048]{1,0:T(8,128)(2,1)}, bf16[256,2048]{1,0:T(8,128)(2,1)}, u32[]{:S(2)}, u32[]{:S(2)}) %collective-permute-start.15) | collective-permute-done | bytes 1048608 | tf_op jit(solution)/shard_map/ppermute | solution.py:437
  252.7 11.5 %collective-permute-done.18 = bf16[256,2048]{1,0:T(8,128)(2,1)S(1)} collective-permute-done((bf16[256,2048]{1,0:T(8,128)(2,1)}, bf16[256,2048]{1,0:T(8,128)(2,1)S(1)}, u32[]{:S(2)}, u32[]{:S(2)}) %collective-permute-start.18) | collective-permute-done | bytes 1048608 | tf_op jit(solution)/shard_map/ppermute | solution.py:437
  271.0 30.6 %up_and_bend.1 = (bf16[2048,2048]{1,0:T(8,128)(2,1)}, f32[2048,2048]{1,0:T(8,128)}) custom-call(bf16[2048,2048]{1,0:T(8,128)(2,1)} %constant_dynamic-update-slice_fusion.15.rows_ref.left_ref, bf16[2048,2048]{1,0:T(8,128)(2,1)} %all-gather.9.cloned.1.call-done.weight_ref, f32[1,2048]{1,0:T(1,128)} %bitcast.152), custom_call_target="tpu_custom_call" | custom-call | flops 8589934592 | bytes 8388608 | tf_op jit(solution)/shard_map/up_and_bend/pallas_call | solution.py:259
  303.8 23.6 %outer.5 = bf16[8,4,64,2048]{3,2,1,0:T(8,128)(2,1)} custom-call(bf16[2048,2048]{1,0:T(8,128)(2,1)} %constant_dynamic-update-slice_fusion.31.left_ref.rows_ref, bf16[2048,2048]{1,0:T(8,128)(2,1)} %get-tuple-element.189.right_ref.rows_ref), custom_call_target="tpu_custom_call" | custom-call | flops 4294967296 | bytes 4194304 | tf_op jit(solution)/shard_map/outer/pallas_call | solution.py:420
  327.5 25.3 %hidden_gradient.1 = (bf16[2048,2048]{1,0:T(8,128)(2,1)}, f32[1,2048]{1,0:T(1,128)}) custom-call(bf16[2048,2048]{1,0:T(8,128)(2,1)} %constant_dynamic-update-slice_fusion.31.left_ref.rows_ref, bf16[2048,2048]{1,0:T(8,128)(2,1)} %all-gather.11.cloned.1.call-done.weight_ref, f32[2048,2048]{1,0:T(8,128)} %get-tuple-element.162.slope_ref), custom_call_target="tpu_custom_call" | custom-call | flops 6442450944 | bytes 6291456 | tf_op jit(solution)/shard_map/hidden_gradient/pallas_call | solution.py:283
  352.8 8.6 %convolution_convert_fusion.5 = bf16[512,2048]{1,0:T(8,128)(2,1)S(1)} fusion(bf16[2048,2048]{1,0:T(8,128)(2,1)} %all-gather.9.cloned.1.call-done.weight_ref, bf16[2048,2048]{1,0:T(8,128)(2,1)} %get-tuple-element.179.right_ref), kind=kOutput, calls=%fused_computation.24 | convolution fusion | flops 4296015872 | bytes 12582912 | tf_op jit(solution)/shard_map/dot_general | solution.py:37
  365.0 18.2 %convolution_convert_fusion.own_ref = bf16[1536,2048]{1,0:T(8,128)(2,1)S(1)} fusion(bf16[2048,2048]{1,0:T(8,128)(2,1)} %all-gather.9.cloned.1.call-done.weight_ref, bf16[2048,2048]{1,0:T(8,128)(2,1)} %get-tuple-element.179.right_ref), kind=kOutput, calls=%fused_computation.2 | convolution fusion | flops 12888047616 | bytes 20971520 | tf_op jit(solution)/shard_map/dot_general | solution.py:37
  402.1 23.6 %outer.6 = bf16[8,4,64,2048]{3,2,1,0:T(8,128)(2,1)} custom-call(bf16[2048,2048]{1,0:T(8,128)(2,1)} %constant_dynamic-update-slice_fusion.15.rows_ref.left_ref, bf16[2048,2048]{1,0:T(8,128)(2,1)} %get-tuple-element.179.right_ref), custom_call_target="tpu_custom_call" | custom-call | flops 4294967296 | bytes 4194304 | tf_op jit(solution)/shard_map/outer/pallas_call | solution.py:420
  436.5 11.9 %norm_back.2 = (bf16[512,2048]{1,0:T(8,128)(2,1)}, f32[512,2048]{1,0:T(8,128)}, f32[24,2048]{1,0:T(8,128)}) custom-call(bf16[1536,2048]{1,0:T(8,128)(2,1)} %copy-done.5, f32[512,2048]{1,0:T(8,128)} %copy-done, f32[512,1]{1,0:T(8,128)} %copy.45.average_ref, f32[512,1]{1,0:T(8,128)} %copy.46.scale_ref, bf16[512,2048]{1,0:T(8,128)(2,1)} %bitcast.108, ...), custom_call_target="tpu_custom_call" | custom-call | flops 7864320 | bytes 7680 | tf_op jit(solution)/shard_map/norm_back/pallas_call | solution.py:388
  450.1 8.9 %mixed_gradient.1 = bf16[512,2048]{1,0:T(8,128)(2,1)} custom-call(bf16[512,2048]{1,0:T(8,128)(2,1)} %get-tuple-element.200.rows_ref, bf16[2048,2048]{1,0:T(8,128)(2,1)} %all-gather.7.cloned.1.call-done.weight_ref), custom_call_target="tpu_custom_call" | custom-call | flops 1073741824 | bytes 1048576 | tf_op jit(solution)/shard_map/mixed_gradient/pallas_call | solution.py:330
  465.7 18.9 %product.1 = bf16[1536,2048]{1,0:T(8,128)(2,1)} custom-call(bf16[2048,2048]{1,0:T(8,128)(2,1)} %get-tuple-element.189.right_ref.rows_ref, bf16[2048,2048]{1,0:T(8,128)(2,1)} %all-gather.11.cloned.1.call-done.weight_ref), custom_call_target="tpu_custom_call" | custom-call | flops 3221225472 | bytes 3145728 | tf_op jit(solution)/shard_map/product/pallas_call | solution.py:308
  497.1 28.4 %attend_backward.2.right_ref.rest_4_ = bf16[2048,1536]{1,0:T(8,128)(2,1)} custom-call(s32[1]{0:T(128)} %bitcast.1.at_ref.mask_ref, f32[8]{0:T(128)} %multiply_power_fusion.slope_ref, bf16[2048,1536]{1,0:T(8,128)(2,1)} %add_convert_fusion.qkv_ref, f32[2048,512]{1,0:T(8,128)} %get-tuple-element.140.lse_ref, bf16[2048,512]{1,0:T(8,128)(2,1)} %get-tuple-element.139.mixed_ref, ...), custom_call_target="tpu_custom_call" | custom-call | flops 3355443200 | bytes 3276800 | tf_op jit(solution)/shard_map/attend_backward/pallas_call | solution.py:198
  525.5 8.8 %outer.7 = bf16[1,4,256,2048]{3,2,1,0:T(8,128)(2,1)} custom-call(bf16[1024,1024]{1,0:T(8,128)(2,1)} %pad_maximum_fusion.4.left_ref, bf16[1024,2048]{1,0:T(8,128)(2,1)} %pad_maximum_fusion.right_ref), custom_call_target="tpu_custom_call" | custom-call | flops 1073741824 | bytes 1048576 | tf_op jit(solution)/shard_map/outer/pallas_call | solution.py:420
  538.1 12.9 %outer.8 = bf16[8,4,64,768]{3,2,1,0:T(8,128)(2,1)} custom-call(bf16[2048,2048]{1,0:T(8,128)(2,1)} %constant_dynamic-update-slice_fusion.left_ref, bf16[2048,1536]{1,0:T(8,128)(2,1)} %attend_backward.2.right_ref.rest_4_), custom_call_target="tpu_custom_call" | custom-call | flops 1610612736 | bytes 1572864 | tf_op jit(solution)/shard_map/outer/pallas_call | solution.py:420
  557.8 28.3 %attend_backward.3.right_ref = bf16[2048,1536]{1,0:T(8,128)(2,1)} custom-call(s32[1]{0:T(128)} %bitcast.1.at_ref.mask_ref, f32[8]{0:T(128)} %multiply_power_fusion.slope_ref, bf16[2048,1536]{1,0:T(8,128)(2,1)} %add_convert_fusion.qkv_ref, f32[2048,512]{1,0:T(8,128)} %get-tuple-element.140.lse_ref, ...), custom_call_target="tpu_custom_call", output_to_operand_aliasing={{}: (9, {})} | custom-call | flops 3355443200 | bytes 3276800 | tf_op jit(solution)/shard_map/attend_backward/pallas_call | solution.py:198
  595.2 11.1 %convolution_convert_fusion.1 = bf16[1024,2048]{1,0:T(8,128)(2,1)} fusion(bf16[2048,1536]{1,0:T(8,128)(2,1)} %all-gather.5.cloned.1.call-done, bf16[2048,1536]{1,0:T(8,128)(2,1)} %attend_backward.3.right_ref), kind=kOutput, calls=%fused_computation.19 | convolution fusion | flops 6444548096 | bytes 13631488 | tf_op jit(solution)/shard_map/dot_general | solution.py:37
  622.7 12.9 %outer.9 = bf16[8,4,64,768]{3,2,1,0:T(8,128)(2,1)} custom-call(bf16[2048,2048]{1,0:T(8,128)(2,1)} %constant_dynamic-update-slice_fusion.left_ref, bf16[2048,1536]{1,0:T(8,128)(2,1)} %attend_backward.3.right_ref), custom_call_target="tpu_custom_call" | custom-call | flops 1610612736 | bytes 1572864 | tf_op jit(solution)/shard_map/outer/pallas_call | solution.py:420
  682.8 11.2 %norm_back.3 = (bf16[512,2048]{1,0:T(8,128)(2,1)}, f32[512,2048]{1,0:T(8,128)}, f32[24,2048]{1,0:T(8,128)}) custom-call(bf16[512,2048]{1,0:T(8,128)(2,1)} %convolution_convert_fusion.2.own_ref, bf16[512,2048]{1,0:T(8,128)(2,1)} %bitcast.104, f32[512,1]{1,0:T(8,128)} %bitcast.128, f32[512,1]{1,0:T(8,128)} %bitcast.127, ...), custom_call_target="tpu_custom_call" | custom-call | flops 7864320 | bytes 7680 | tf_op jit(solution)/shard_map/norm_back/pallas_call | solution.py:388
  (320 shorter events, 300.6 us)
Async XLA Ops:
  7.2 93.8 %all-gather.5.cloned.1.call-start = ((), (), s32[]{:S(2)}) async-start(), calls=%async_computation.7 | async-start | bytes 7077888 | tf_op jit(solution)/shard_map/all_gather | solution.py:629
  10.3 169.9 %all-gather.7.cloned.1.call-start = ((), (), s32[]{:S(2)}) async-start(), calls=%async_computation.8 | async-start | bytes 9437184 | tf_op jit(solution)/shard_map/all_gather | solution.py:641
  11.1 260.0 %all-gather.9.cloned.1.call-start = ((), (), s32[]{:S(2)}) async-start(), calls=%async_computation.9 | async-start | bytes 9437184 | tf_op jit(solution)/shard_map/all_gather | solution.py:642
  19.4 308.0 %all-gather.11.cloned.1.call-start = ((), (), s32[]{:S(2)}) async-start(), calls=%async_computation.10 | async-start | bytes 9437184 | tf_op jit(solution)/shard_map/all_gather | solution.py:643
  24.0 47.4 %collective-permute-start = (bf16[256,2048]{1,0:T(8,128)(2,1)}, bf16[256,2048]{1,0:T(8,128)(2,1)}, u32[]{:S(2)}, u32[]{:S(2)}) collective-permute-start(bf16[256,2048]{1,0:T(8,128)(2,1)} %get-tuple-element.303), channel_id=1, source_target_pairs={{0,8},{8,0},{16,24},{24,16},{1,9},{9,1},{17,25},{25,17},{2,10},{10... | collective-permute-start | bytes 3145736 | tf_op jit(solution)/shard_map/ppermute | solution.py:437
  24.6 52.7 %collective-permute-start.3 = (bf16[256,2048]{1,0:T(8,128)(2,1)}, bf16[256,2048]{1,0:T(8,128)(2,1)}, u32[]{:S(2)}, u32[]{:S(2)}) collective-permute-start(bf16[256,2048]{1,0:T(8,128)(2,1)} %get-tuple-element.302), channel_id=1, source_target_pairs={{0,16},{8,24},{16,0},{24,8},{1,17},{9,25},{17,1},{25,9},{2,18},{10... | collective-permute-start | bytes 3145736 | tf_op jit(solution)/shard_map/ppermute | solution.py:437
  26.9 470.2 %reduce-scatter.6.cloned.1.call-start = ((), (), s32[]{:S(2)}) async-start(), calls=%async_computation.11 | async-start | bytes 9437184 | tf_op jit(solution)/shard_map/reduce_scatter | solution.py:684
  96.9 52.4 %collective-permute-start.7 = (bf16[256,2048]{1,0:T(8,128)(2,1)}, bf16[256,2048]{1,0:T(8,128)(2,1)}, u32[]{:S(2)}, u32[]{:S(2)}) collective-permute-start(bf16[256,2048]{1,0:T(8,128)(2,1)} %get-tuple-element.144), channel_id=1, source_target_pairs={{0,16},{8,24},{16,0},{24,8},{1,17},{9,25},{17,1},{25,9},{2,18},{10... | collective-permute-start | bytes 3145736 | tf_op jit(solution)/shard_map/ppermute | solution.py:437
  97.3 52.1 %collective-permute-start.8 = (bf16[256,2048]{1,0:T(8,128)(2,1)}, bf16[256,2048]{1,0:T(8,128)(2,1)}, u32[]{:S(2)}, u32[]{:S(2)}) collective-permute-start(bf16[256,2048]{1,0:T(8,128)(2,1)} %get-tuple-element.144), channel_id=1, source_target_pairs={{0,8},{8,0},{16,24},{24,16},{1,9},{9,1},{17,25},{25,17},{2,10},{10... | collective-permute-start | bytes 3145736 | tf_op jit(solution)/shard_map/ppermute | solution.py:437
  98.9 50.4 %collective-permute-start.6 = (bf16[256,2048]{1,0:T(8,128)(2,1)S(1)}, bf16[256,2048]{1,0:T(8,128)(2,1)}, u32[]{:S(2)}, u32[]{:S(2)}) collective-permute-start(bf16[256,2048]{1,0:T(8,128)(2,1)S(1)} %get-tuple-element.145), channel_id=1, source_target_pairs={{0,8},{8,0},{16,24},{24,16},{1,9},{9,1},{17,25},{25,17},{2,10},{10... | collective-permute-start | bytes 3145736 | tf_op jit(solution)/shard_map/ppermute | solution.py:437
  99.3 50.1 %collective-permute-start.9 = (bf16[256,2048]{1,0:T(8,128)(2,1)S(1)}, bf16[256,2048]{1,0:T(8,128)(2,1)}, u32[]{:S(2)}, u32[]{:S(2)}) collective-permute-start(bf16[256,2048]{1,0:T(8,128)(2,1)S(1)} %get-tuple-element.145), channel_id=1, source_target_pairs={{0,16},{8,24},{16,0},{24,8},{1,17},{9,25},{17,1},{25,9},{2,18},{10... | collective-permute-start | bytes 3145736 | tf_op jit(solution)/shard_map/ppermute | solution.py:437
  192.3 51.0 %collective-permute-start.13 = (bf16[256,2048]{1,0:T(8,128)(2,1)}, bf16[256,2048]{1,0:T(8,128)(2,1)}, u32[]{:S(2)}, u32[]{:S(2)}) collective-permute-start(bf16[256,2048]{1,0:T(8,128)(2,1)} %get-tuple-element.296), channel_id=1, source_target_pairs={{0,8},{8,0},{16,24},{24,16},{1,9},{9,1},{17,25},{25,17},{2,10},{10... | collective-permute-start | bytes 3145736 | tf_op jit(solution)/shard_map/ppermute | solution.py:437
  193.8 46.3 %collective-permute-start.15 = (bf16[256,2048]{1,0:T(8,128)(2,1)}, bf16[256,2048]{1,0:T(8,128)(2,1)}, u32[]{:S(2)}, u32[]{:S(2)}) collective-permute-start(bf16[256,2048]{1,0:T(8,128)(2,1)} %get-tuple-element.295), channel_id=1, source_target_pairs={{0,8},{8,0},{16,24},{24,16},{1,9},{9,1},{17,25},{25,17},{2,10},{10... | collective-permute-start | bytes 3145736 | tf_op jit(solution)/shard_map/ppermute | solution.py:437
  194.3 56.0 %collective-permute-start.17 = (bf16[256,2048]{1,0:T(8,128)(2,1)}, bf16[256,2048]{1,0:T(8,128)(2,1)}, u32[]{:S(2)}, u32[]{:S(2)}) collective-permute-start(bf16[256,2048]{1,0:T(8,128)(2,1)} %get-tuple-element.295), channel_id=1, source_target_pairs={{0,16},{8,24},{16,0},{24,8},{1,17},{9,25},{17,1},{25,9},{2,18},{10... | collective-permute-start | bytes 3145736 | tf_op jit(solution)/shard_map/ppermute | solution.py:437
  327.4 258.7 %reduce-scatter.8.cloned.1.call-start = ((), (), s32[]{:S(2)}) async-start(), calls=%async_computation.12 | async-start | bytes 9437184 | tf_op jit(solution)/shard_map/reduce_scatter | solution.py:684
  432.7 162.5 %reduce-scatter.10.cloned.1.call-start = ((), (), s32[]{:S(2)}) async-start(), calls=%async_computation.13 | async-start | bytes 3538944 | tf_op jit(solution)/shard_map/reduce_scatter | solution.py:684
  434.5 51.3 %collective-permute-start.28 = (bf16[256,2048]{1,0:T(8,128)(2,1)S(1)}, bf16[256,2048]{1,0:T(8,128)(2,1)}, u32[]{:S(2)}, u32[]{:S(2)}) collective-permute-start(bf16[256,2048]{1,0:T(8,128)(2,1)S(1)} %get-tuple-element.190), channel_id=1, source_target_pairs={{0,8},{8,0},{16,24},{24,16},{1,9},{9,1},{17,25},{25,17},{2,10},{10... | collective-permute-start | bytes 3145736 | tf_op jit(solution)/shard_map/ppermute | solution.py:437
  435.0 50.9 %collective-permute-start.29 = (bf16[256,2048]{1,0:T(8,128)(2,1)S(1)}, bf16[256,2048]{1,0:T(8,128)(2,1)}, u32[]{:S(2)}, u32[]{:S(2)}) collective-permute-start(bf16[256,2048]{1,0:T(8,128)(2,1)S(1)} %get-tuple-element.191), channel_id=1, source_target_pairs={{0,16},{8,24},{16,0},{24,8},{1,17},{9,25},{17,1},{25,9},{2,18},{10... | collective-permute-start | bytes 3145736 | tf_op jit(solution)/shard_map/ppermute | solution.py:437
  491.3 59.7 %collective-permute-start.34 = (bf16[512,2048]{1,0:T(8,128)(2,1)S(1)}, bf16[512,2048]{1,0:T(8,128)(2,1)}, u32[]{:S(2)}, u32[]{:S(2)}) collective-permute-start(bf16[512,2048]{1,0:T(8,128)(2,1)S(1)} %pad_maximum_fusion.6), channel_id=1, source_target_pairs={{0,16},{8,24},{16,0},{24,8},{1,17},{9,25},{17,1},{25,9},{2,18},{10... | collective-permute-start | bytes 6291464 | tf_op jit(solution)/shard_map/ppermute | solution.py:437
  493.6 57.4 %collective-permute-start.33 = (bf16[512,2048]{1,0:T(8,128)(2,1)}, bf16[512,2048]{1,0:T(8,128)(2,1)}, u32[]{:S(2)}, u32[]{:S(2)}) collective-permute-start(bf16[512,2048]{1,0:T(8,128)(2,1)} %pad_maximum_fusion.5), channel_id=1, source_target_pairs={{0,8},{8,0},{16,24},{24,16},{1,9},{9,1},{17,25},{25,17},{2,10},{10... | collective-permute-start | bytes 6291464 | tf_op jit(solution)/shard_map/ppermute | solution.py:437
  551.3 107.8 %reduce-scatter.12.cloned.1.call-start = ((), (), s32[]{:S(2)}) async-start(), calls=%async_computation.14 | async-start | bytes 2359296 | tf_op jit(solution)/shard_map/reduce_scatter | solution.py:782
  554.4 55.7 %collective-permute-start.41 = (bf16[256,2048]{1,0:T(8,128)(2,1)S(1)}, bf16[256,2048]{1,0:T(8,128)(2,1)}, u32[]{:S(2)}, u32[]{:S(2)}) collective-permute-start(bf16[256,2048]{1,0:T(8,128)(2,1)S(1)} %pad_maximum_fusion.9), channel_id=1, source_target_pairs={{0,16},{8,24},{16,0},{24,8},{1,17},{9,25},{17,1},{25,9},{2,18},{10... | collective-permute-start | bytes 3145736 | tf_op jit(solution)/shard_map/ppermute | solution.py:437
  556.2 53.8 %collective-permute-start.40 = (bf16[256,2048]{1,0:T(8,128)(2,1)S(1)}, bf16[256,2048]{1,0:T(8,128)(2,1)}, u32[]{:S(2)}, u32[]{:S(2)}) collective-permute-start(bf16[256,2048]{1,0:T(8,128)(2,1)S(1)} %pad_maximum_fusion.8), channel_id=1, source_target_pairs={{0,8},{8,0},{16,24},{24,16},{1,9},{9,1},{17,25},{25,17},{2,10},{10... | collective-permute-start | bytes 3145736 | tf_op jit(solution)/shard_map/ppermute | solution.py:437
  618.6 93.2 %reduce-scatter.14.cloned.1.call-start = ((), (), s32[]{:S(2)}) async-start(), calls=%async_computation.15 | async-start | bytes 3538944 | tf_op jit(solution)/shard_map/reduce_scatter | solution.py:684
  (70 other events, 1271.6 us)
Sparse Core Ops, SparseCore 0:
  10.4 67.4 all-gather.4
  79.5 80.6 all-gather.6
  161.9 80.5 all-gather.8
  243.9 81.0 all-gather.10
  327.5 89.4 reduce-scatter.5
  432.9 88.6 reduce-scatter.7
  551.5 39.0 reduce-scatter.9
  618.7 33.6 reduce-scatter.11
  654.7 39.0 reduce-scatter.13

commit v19 on v18

--- a/solution.py
+++ b/solution.py
@@ -780,10 +780,11 @@
     if square:
         out_sum = gate(out_sum, *far)
     grad_w_out = lax.psum_scatter(out_sum, "fsdp", scatter_dimension=0, tiled=True).astype(wide)
+    if square:
+        came = order.add_far(near, far, direct)
     second_sum = slab_product(normed, qkv_grad, (1, 2))
     if square:
         second_sum = slab_sum(gate(second_sum, *far, *direct))
-        came = order.add_far(near, far, direct)
         order.after(grad_w_out)
         normed_own = order(slots(to_normed, 0, 1), qkv_grad)
     else:

time: 739 us -> 731 us (0.989)
    unnamed x92 -> x94, local copies, waits for them, and re-layouts: 42.6 us -> 40.8 us
where the time goes in v19:
time: 731 us; the launch traced here: 726 us
  Pallas kernels  280 us (38%)
  waiting for transfers between devices  129 us (18%)
  local copies, waits for them, and re-layouts  94.6 us (13%)
  matrix products  85.6 us (12%)
  starting transfers between devices  65.6 us (9%)
  other arithmetic  56.5 us (8%)
  between operations  14.9 us (2%)
    ppermute x44, waiting for transfers between devices, swap(): return lax.ppermute(values, 'seq', [(i, i ^ bit) for i in range(4)])  125 us
    pallas_call x5, Pallas kernels, outer(): pl.pallas_call(partial(outer_kernel, chunk=next((c for c in (512, 384, 25...  82.1 us
    pallas_call x2, Pallas kernels, attend_backward(): pl.pallas_call(partial(attend_backward_kernel, blocks=blocks, seqs=seqs,...  56.9 us
    dot_general x5, matrix products, contract_last(): lax.dot_general(left_side, right_side, (((1,), (1,)), ((), ())), preferre...  52.8 us
    ppermute x44, starting transfers between devices, swap(): return lax.ppermute(values, 'seq', [(i, i ^ bit) for i in range(4)])  47.9 us
    unnamed x94, local copies, waits for them, and re-layouts  40.8 us
    dot_general x3, matrix products, contract(): lax.dot_general(left_side, right_side, (((1,), (0,)), ((), ())), preferre...  32.8 us
    pallas_call x1, Pallas kernels, up_and_bend(): pl.pallas_call(partial(up_kernel, chunk=512), grid=(count // TILE,), in_s...  30.6 us
  transfers between devices with their start and end apart: 64, of which 22 were waited for; matrix products, arithmetic and copies ran while one was open for 32% of the time, Pallas kernels for 38%

profile of v19, /device:TPU:0, one launch (start us, length us, event | category | flops | bytes accessed | tf_op | source)
XLA Modules:
  0.0 726.3 jit_solution(2066229958259381685)
XLA Ops:
  28.0 18.9 %collective-permute-done.2 = bf16[256,2048]{1,0:T(8,128)(2,1)} collective-permute-done((bf16[256,2048]{1,0:T(8,128)(2,1)}, bf16[256,2048]{1,0:T(8,128)(2,1)}, u32[]{:S(2)}, u32[]{:S(2)}) %collective-permute-start.2) | collective-permute-done | bytes 1048608 | tf_op jit(solution)/shard_map/ppermute | solution.py:437
  53.7 17.7 %collective-permute-done = bf16[256,2048]{1,0:T(8,128)(2,1)} collective-permute-done((bf16[256,2048]{1,0:T(8,128)(2,1)}, bf16[256,2048]{1,0:T(8,128)(2,1)}, u32[]{:S(2)}, u32[]{:S(2)}) %collective-permute-start) | collective-permute-done | bytes 1048608 | tf_op jit(solution)/shard_map/ppermute | solution.py:437
  79.6 12.8 %collective-permute-done.4 = bf16[256,2048]{1,0:T(8,128)(2,1)} collective-permute-done((bf16[256,2048]{1,0:T(8,128)(2,1)}, bf16[256,2048]{1,0:T(8,128)(2,1)}, u32[]{:S(2)}, u32[]{:S(2)}) %collective-permute-start.4) | collective-permute-done | bytes 1048608 | tf_op jit(solution)/shard_map/ppermute | solution.py:437
  101.0 18.6 %add_convert_fusion.qkv_ref = bf16[2048,1536]{1,0:T(8,128)(2,1)} fusion(bf16[2048,2048]{1,0:T(8,128)(2,1)} %constant_dynamic-update-slice_fusion.left_ref, bf16[2048,1536]{1,0:T(8,128)(2,1)} %all-gather.5.cloned.1.call-done, f32[1536]{0:T(1024)S(1)} %reduce.2), kind=kOutput, calls=%fused_computation.1 | convolution fusion | flops 12891193344 | bytes 20977664 | tf_op jit(solution)/shard_map/dot_general | solution.py:31
  119.6 29.7 %attend_forward.1 = (bf16[2048,512]{1,0:T(8,128)(2,1)}, f32[2048,512]{1,0:T(8,128)}) custom-call(s32[1]{0:T(128)} %bitcast.1.at_ref.mask_ref, f32[8]{0:T(128)} %multiply_power_fusion.slope_ref, bf16[2048,1536]{1,0:T(8,128)(2,1)} %add_convert_fusion.qkv_ref), custom_call_target="tpu_custom_call" | custom-call | flops 2684354560 | bytes 2621440 | tf_op jit(solution)/shard_map/attend_forward/pallas_call | solution.py:173
  155.4 12.5 %collective-permute-done.10 = bf16[512,512]{1,0:T(8,128)(2,1)S(1)} collective-permute-done((bf16[512,512]{1,0:T(8,128)(2,1)}, bf16[512,512]{1,0:T(8,128)(2,1)S(1)}, u32[]{:S(2)}, u32[]{:S(2)}) %collective-permute-start.10) | collective-permute-done | bytes 524320 | tf_op jit(solution)/shard_map/ppermute | solution.py:437
  226.8 13.3 %collective-permute-done.15 = bf16[256,2048]{1,0:T(8,128)(2,1)} collective-permute-done((bf16[256,2048]{1,0:T(8,128)(2,1)}, bf16[256,2048]{1,0:T(8,128)(2,1)}, u32[]{:S(2)}, u32[]{:S(2)}) %collective-permute-start.15) | collective-permute-done | bytes 1048608 | tf_op jit(solution)/shard_map/ppermute | solution.py:437
  252.7 11.6 %collective-permute-done.18 = bf16[256,2048]{1,0:T(8,128)(2,1)S(1)} collective-permute-done((bf16[256,2048]{1,0:T(8,128)(2,1)}, bf16[256,2048]{1,0:T(8,128)(2,1)S(1)}, u32[]{:S(2)}, u32[]{:S(2)}) %collective-permute-start.18) | collective-permute-done | bytes 1048608 | tf_op jit(solution)/shard_map/ppermute | solution.py:437
  271.1 30.6 %up_and_bend.1 = (bf16[2048,2048]{1,0:T(8,128)(2,1)}, f32[2048,2048]{1,0:T(8,128)}) custom-call(bf16[2048,2048]{1,0:T(8,128)(2,1)} %constant_dynamic-update-slice_fusion.15.rows_ref.left_ref, bf16[2048,2048]{1,0:T(8,128)(2,1)} %all-gather.9.cloned.1.call-done.weight_ref, f32[1,2048]{1,0:T(1,128)} %bitcast.152), custom_call_target="tpu_custom_call" | custom-call | flops 8589934592 | bytes 8388608 | tf_op jit(solution)/shard_map/up_and_bend/pallas_call | solution.py:259
  303.8 23.6 %outer.5 = bf16[8,4,64,2048]{3,2,1,0:T(8,128)(2,1)} custom-call(bf16[2048,2048]{1,0:T(8,128)(2,1)} %constant_dynamic-update-slice_fusion.31.left_ref.rows_ref, bf16[2048,2048]{1,0:T(8,128)(2,1)} %get-tuple-element.189.right_ref.rows_ref), custom_call_target="tpu_custom_call" | custom-call | flops 4294967296 | bytes 4194304 | tf_op jit(solution)/shard_map/outer/pallas_call | solution.py:420
  327.5 25.3 %hidden_gradient.1 = (bf16[2048,2048]{1,0:T(8,128)(2,1)}, f32[1,2048]{1,0:T(1,128)}) custom-call(bf16[2048,2048]{1,0:T(8,128)(2,1)} %constant_dynamic-update-slice_fusion.31.left_ref.rows_ref, bf16[2048,2048]{1,0:T(8,128)(2,1)} %all-gather.11.cloned.1.call-done.weight_ref, f32[2048,2048]{1,0:T(8,128)} %get-tuple-element.162.slope_ref), custom_call_target="tpu_custom_call" | custom-call | flops 6442450944 | bytes 6291456 | tf_op jit(solution)/shard_map/hidden_gradient/pallas_call | solution.py:283
  352.9 8.6 %convolution_convert_fusion.5 = bf16[512,2048]{1,0:T(8,128)(2,1)S(1)} fusion(bf16[2048,2048]{1,0:T(8,128)(2,1)} %all-gather.9.cloned.1.call-done.weight_ref, bf16[2048,2048]{1,0:T(8,128)(2,1)} %get-tuple-element.179.right_ref), kind=kOutput, calls=%fused_computation.24 | convolution fusion | flops 4296015872 | bytes 12582912 | tf_op jit(solution)/shard_map/dot_general | solution.py:37
  365.0 18.2 %convolution_convert_fusion.own_ref = bf16[1536,2048]{1,0:T(8,128)(2,1)S(1)} fusion(bf16[2048,2048]{1,0:T(8,128)(2,1)} %all-gather.9.cloned.1.call-done.weight_ref, bf16[2048,2048]{1,0:T(8,128)(2,1)} %get-tuple-element.179.right_ref), kind=kOutput, calls=%fused_computation.2 | convolution fusion | flops 12888047616 | bytes 20971520 | tf_op jit(solution)/shard_map/dot_general | solution.py:37
  402.1 23.6 %outer.6 = bf16[8,4,64,2048]{3,2,1,0:T(8,128)(2,1)} custom-call(bf16[2048,2048]{1,0:T(8,128)(2,1)} %constant_dynamic-update-slice_fusion.15.rows_ref.left_ref, bf16[2048,2048]{1,0:T(8,128)(2,1)} %get-tuple-element.179.right_ref), custom_call_target="tpu_custom_call" | custom-call | flops 4294967296 | bytes 4194304 | tf_op jit(solution)/shard_map/outer/pallas_call | solution.py:420
  436.5 11.9 %norm_back.2 = (bf16[512,2048]{1,0:T(8,128)(2,1)}, f32[512,2048]{1,0:T(8,128)}, f32[24,2048]{1,0:T(8,128)}) custom-call(bf16[1536,2048]{1,0:T(8,128)(2,1)} %copy-done.5, f32[512,2048]{1,0:T(8,128)} %copy-done, f32[512,1]{1,0:T(8,128)} %copy.45.average_ref, f32[512,1]{1,0:T(8,128)} %copy.46.scale_ref, bf16[512,2048]{1,0:T(8,128)(2,1)} %bitcast.108, ...), custom_call_target="tpu_custom_call" | custom-call | flops 7864320 | bytes 7680 | tf_op jit(solution)/shard_map/norm_back/pallas_call | solution.py:388
  450.1 8.9 %mixed_gradient.1 = bf16[512,2048]{1,0:T(8,128)(2,1)} custom-call(bf16[512,2048]{1,0:T(8,128)(2,1)} %get-tuple-element.200.rows_ref, bf16[2048,2048]{1,0:T(8,128)(2,1)} %all-gather.7.cloned.1.call-done.weight_ref), custom_call_target="tpu_custom_call" | custom-call | flops 1073741824 | bytes 1048576 | tf_op jit(solution)/shard_map/mixed_gradient/pallas_call | solution.py:330
  465.7 18.9 %product.1 = bf16[1536,2048]{1,0:T(8,128)(2,1)} custom-call(bf16[2048,2048]{1,0:T(8,128)(2,1)} %get-tuple-element.189.right_ref.rows_ref, bf16[2048,2048]{1,0:T(8,128)(2,1)} %all-gather.11.cloned.1.call-done.weight_ref), custom_call_target="tpu_custom_call" | custom-call | flops 3221225472 | bytes 3145728 | tf_op jit(solution)/shard_map/product/pallas_call | solution.py:308
  497.1 28.4 %attend_backward.2.right_ref.rest_4_ = bf16[2048,1536]{1,0:T(8,128)(2,1)} custom-call(s32[1]{0:T(128)} %bitcast.1.at_ref.mask_ref, f32[8]{0:T(128)} %multiply_power_fusion.slope_ref, bf16[2048,1536]{1,0:T(8,128)(2,1)} %add_convert_fusion.qkv_ref, f32[2048,512]{1,0:T(8,128)} %get-tuple-element.140.lse_ref, bf16[2048,512]{1,0:T(8,128)(2,1)} %get-tuple-element.139.mixed_ref, ...), custom_call_target="tpu_custom_call" | custom-call | flops 3355443200 | bytes 3276800 | tf_op jit(solution)/shard_map/attend_backward/pallas_call | solution.py:198
  525.6 8.8 %outer.7 = bf16[1,4,256,2048]{3,2,1,0:T(8,128)(2,1)} custom-call(bf16[1024,1024]{1,0:T(8,128)(2,1)} %pad_maximum_fusion.4.left_ref, bf16[1024,2048]{1,0:T(8,128)(2,1)} %pad_maximum_fusion.right_ref), custom_call_target="tpu_custom_call" | custom-call | flops 1073741824 | bytes 1048576 | tf_op jit(solution)/shard_map/outer/pallas_call | solution.py:420
  538.1 12.9 %outer.8 = bf16[8,4,64,768]{3,2,1,0:T(8,128)(2,1)} custom-call(bf16[2048,2048]{1,0:T(8,128)(2,1)} %constant_dynamic-update-slice_fusion.left_ref, bf16[2048,1536]{1,0:T(8,128)(2,1)} %attend_backward.2.right_ref.rest_4_), custom_call_target="tpu_custom_call" | custom-call | flops 1610612736 | bytes 1572864 | tf_op jit(solution)/shard_map/outer/pallas_call | solution.py:420
  557.8 28.4 %attend_backward.3.right_ref = bf16[2048,1536]{1,0:T(8,128)(2,1)} custom-call(s32[1]{0:T(128)} %bitcast.1.at_ref.mask_ref, f32[8]{0:T(128)} %multiply_power_fusion.slope_ref, bf16[2048,1536]{1,0:T(8,128)(2,1)} %add_convert_fusion.qkv_ref, f32[2048,512]{1,0:T(8,128)} %get-tuple-element.140.lse_ref, ...), custom_call_target="tpu_custom_call", output_to_operand_aliasing={{}: (9, {})} | custom-call | flops 3355443200 | bytes 3276800 | tf_op jit(solution)/shard_map/attend_backward/pallas_call | solution.py:198
  595.3 11.1 %convolution_convert_fusion.1 = bf16[1024,2048]{1,0:T(8,128)(2,1)} fusion(bf16[2048,1536]{1,0:T(8,128)(2,1)} %all-gather.5.cloned.1.call-done, bf16[2048,1536]{1,0:T(8,128)(2,1)} %attend_backward.3.right_ref), kind=kOutput, calls=%fused_computation.19 | convolution fusion | flops 6444548096 | bytes 13631488 | tf_op jit(solution)/shard_map/dot_general | solution.py:37
  626.3 13.0 %outer.9 = bf16[8,4,64,768]{3,2,1,0:T(8,128)(2,1)} custom-call(bf16[2048,2048]{1,0:T(8,128)(2,1)} %constant_dynamic-update-slice_fusion.left_ref, bf16[2048,1536]{1,0:T(8,128)(2,1)} %attend_backward.3.right_ref), custom_call_target="tpu_custom_call" | custom-call | flops 1610612736 | bytes 1572864 | tf_op jit(solution)/shard_map/outer/pallas_call | solution.py:420
  675.6 11.2 %norm_back.3 = (bf16[512,2048]{1,0:T(8,128)(2,1)}, f32[512,2048]{1,0:T(8,128)}, f32[24,2048]{1,0:T(8,128)}) custom-call(bf16[512,2048]{1,0:T(8,128)(2,1)} %convolution_convert_fusion.2.own_ref, bf16[512,2048]{1,0:T(8,128)(2,1)} %bitcast.104, f32[512,1]{1,0:T(8,128)} %bitcast.128, f32[512,1]{1,0:T(8,128)} %bitcast.127, ...), custom_call_target="tpu_custom_call" | custom-call | flops 7864320 | bytes 7680 | tf_op jit(solution)/shard_map/norm_back/pallas_call | solution.py:388
  (322 shorter events, 292.5 us)
Async XLA Ops:
  7.2 93.8 %all-gather.5.cloned.1.call-start = ((), (), s32[]{:S(2)}) async-start(), calls=%async_computation.7 | async-start | bytes 7077888 | tf_op jit(solution)/shard_map/all_gather | solution.py:629
  10.3 169.9 %all-gather.7.cloned.1.call-start = ((), (), s32[]{:S(2)}) async-start(), calls=%async_computation.8 | async-start | bytes 9437184 | tf_op jit(solution)/shard_map/all_gather | solution.py:641
  11.1 260.0 %all-gather.9.cloned.1.call-start = ((), (), s32[]{:S(2)}) async-start(), calls=%async_computation.9 | async-start | bytes 9437184 | tf_op jit(solution)/shard_map/all_gather | solution.py:642
  19.5 308.1 %all-gather.11.cloned.1.call-start = ((), (), s32[]{:S(2)}) async-start(), calls=%async_computation.10 | async-start | bytes 9437184 | tf_op jit(solution)/shard_map/all_gather | solution.py:643
  24.0 47.4 %collective-permute-start = (bf16[256,2048]{1,0:T(8,128)(2,1)}, bf16[256,2048]{1,0:T(8,128)(2,1)}, u32[]{:S(2)}, u32[]{:S(2)}) collective-permute-start(bf16[256,2048]{1,0:T(8,128)(2,1)} %get-tuple-element.303), channel_id=1, source_target_pairs={{0,8},{8,0},{16,24},{24,16},{1,9},{9,1},{17,25},{25,17},{2,10},{10... | collective-permute-start | bytes 3145736 | tf_op jit(solution)/shard_map/ppermute | solution.py:437
  24.6 52.7 %collective-permute-start.3 = (bf16[256,2048]{1,0:T(8,128)(2,1)}, bf16[256,2048]{1,0:T(8,128)(2,1)}, u32[]{:S(2)}, u32[]{:S(2)}) collective-permute-start(bf16[256,2048]{1,0:T(8,128)(2,1)} %get-tuple-element.302), channel_id=1, source_target_pairs={{0,16},{8,24},{16,0},{24,8},{1,17},{9,25},{17,1},{25,9},{2,18},{10... | collective-permute-start | bytes 3145736 | tf_op jit(solution)/shard_map/ppermute | solution.py:437
  26.9 470.2 %reduce-scatter.6.cloned.1.call-start = ((), (), s32[]{:S(2)}) async-start(), calls=%async_computation.11 | async-start | bytes 9437184 | tf_op jit(solution)/shard_map/reduce_scatter | solution.py:684
  96.9 52.4 %collective-permute-start.7 = (bf16[256,2048]{1,0:T(8,128)(2,1)}, bf16[256,2048]{1,0:T(8,128)(2,1)}, u32[]{:S(2)}, u32[]{:S(2)}) collective-permute-start(bf16[256,2048]{1,0:T(8,128)(2,1)} %get-tuple-element.144), channel_id=1, source_target_pairs={{0,16},{8,24},{16,0},{24,8},{1,17},{9,25},{17,1},{25,9},{2,18},{10... | collective-permute-start | bytes 3145736 | tf_op jit(solution)/shard_map/ppermute | solution.py:437
  97.3 52.1 %collective-permute-start.8 = (bf16[256,2048]{1,0:T(8,128)(2,1)}, bf16[256,2048]{1,0:T(8,128)(2,1)}, u32[]{:S(2)}, u32[]{:S(2)}) collective-permute-start(bf16[256,2048]{1,0:T(8,128)(2,1)} %get-tuple-element.144), channel_id=1, source_target_pairs={{0,8},{8,0},{16,24},{24,16},{1,9},{9,1},{17,25},{25,17},{2,10},{10... | collective-permute-start | bytes 3145736 | tf_op jit(solution)/shard_map/ppermute | solution.py:437
  98.9 50.4 %collective-permute-start.6 = (bf16[256,2048]{1,0:T(8,128)(2,1)S(1)}, bf16[256,2048]{1,0:T(8,128)(2,1)}, u32[]{:S(2)}, u32[]{:S(2)}) collective-permute-start(bf16[256,2048]{1,0:T(8,128)(2,1)S(1)} %get-tuple-element.145), channel_id=1, source_target_pairs={{0,8},{8,0},{16,24},{24,16},{1,9},{9,1},{17,25},{25,17},{2,10},{10... | collective-permute-start | bytes 3145736 | tf_op jit(solution)/shard_map/ppermute | solution.py:437
  99.3 50.0 %collective-permute-start.9 = (bf16[256,2048]{1,0:T(8,128)(2,1)S(1)}, bf16[256,2048]{1,0:T(8,128)(2,1)}, u32[]{:S(2)}, u32[]{:S(2)}) collective-permute-start(bf16[256,2048]{1,0:T(8,128)(2,1)S(1)} %get-tuple-element.145), channel_id=1, source_target_pairs={{0,16},{8,24},{16,0},{24,8},{1,17},{9,25},{17,1},{25,9},{2,18},{10... | collective-permute-start | bytes 3145736 | tf_op jit(solution)/shard_map/ppermute | solution.py:437
  192.3 51.0 %collective-permute-start.13 = (bf16[256,2048]{1,0:T(8,128)(2,1)}, bf16[256,2048]{1,0:T(8,128)(2,1)}, u32[]{:S(2)}, u32[]{:S(2)}) collective-permute-start(bf16[256,2048]{1,0:T(8,128)(2,1)} %get-tuple-element.296), channel_id=1, source_target_pairs={{0,8},{8,0},{16,24},{24,16},{1,9},{9,1},{17,25},{25,17},{2,10},{10... | collective-permute-start | bytes 3145736 | tf_op jit(solution)/shard_map/ppermute | solution.py:437
  193.8 46.2 %collective-permute-start.15 = (bf16[256,2048]{1,0:T(8,128)(2,1)}, bf16[256,2048]{1,0:T(8,128)(2,1)}, u32[]{:S(2)}, u32[]{:S(2)}) collective-permute-start(bf16[256,2048]{1,0:T(8,128)(2,1)} %get-tuple-element.295), channel_id=1, source_target_pairs={{0,8},{8,0},{16,24},{24,16},{1,9},{9,1},{17,25},{25,17},{2,10},{10... | collective-permute-start | bytes 3145736 | tf_op jit(solution)/shard_map/ppermute | solution.py:437
  194.3 56.0 %collective-permute-start.17 = (bf16[256,2048]{1,0:T(8,128)(2,1)}, bf16[256,2048]{1,0:T(8,128)(2,1)}, u32[]{:S(2)}, u32[]{:S(2)}) collective-permute-start(bf16[256,2048]{1,0:T(8,128)(2,1)} %get-tuple-element.295), channel_id=1, source_target_pairs={{0,16},{8,24},{16,0},{24,8},{1,17},{9,25},{17,1},{25,9},{2,18},{10... | collective-permute-start | bytes 3145736 | tf_op jit(solution)/shard_map/ppermute | solution.py:437
  327.4 258.8 %reduce-scatter.8.cloned.1.call-start = ((), (), s32[]{:S(2)}) async-start(), calls=%async_computation.12 | async-start | bytes 9437184 | tf_op jit(solution)/shard_map/reduce_scatter | solution.py:684
  432.7 162.6 %reduce-scatter.10.cloned.1.call-start = ((), (), s32[]{:S(2)}) async-start(), calls=%async_computation.13 | async-start | bytes 3538944 | tf_op jit(solution)/shard_map/reduce_scatter | solution.py:684
  434.5 51.3 %collective-permute-start.28 = (bf16[256,2048]{1,0:T(8,128)(2,1)S(1)}, bf16[256,2048]{1,0:T(8,128)(2,1)}, u32[]{:S(2)}, u32[]{:S(2)}) collective-permute-start(bf16[256,2048]{1,0:T(8,128)(2,1)S(1)} %get-tuple-element.190), channel_id=1, source_target_pairs={{0,8},{8,0},{16,24},{24,16},{1,9},{9,1},{17,25},{25,17},{2,10},{10... | collective-permute-start | bytes 3145736 | tf_op jit(solution)/shard_map/ppermute | solution.py:437
  435.0 50.9 %collective-permute-start.29 = (bf16[256,2048]{1,0:T(8,128)(2,1)S(1)}, bf16[256,2048]{1,0:T(8,128)(2,1)}, u32[]{:S(2)}, u32[]{:S(2)}) collective-permute-start(bf16[256,2048]{1,0:T(8,128)(2,1)S(1)} %get-tuple-element.191), channel_id=1, source_target_pairs={{0,16},{8,24},{16,0},{24,8},{1,17},{9,25},{17,1},{25,9},{2,18},{10... | collective-permute-start | bytes 3145736 | tf_op jit(solution)/shard_map/ppermute | solution.py:437
  491.3 59.8 %collective-permute-start.34 = (bf16[512,2048]{1,0:T(8,128)(2,1)S(1)}, bf16[512,2048]{1,0:T(8,128)(2,1)}, u32[]{:S(2)}, u32[]{:S(2)}) collective-permute-start(bf16[512,2048]{1,0:T(8,128)(2,1)S(1)} %pad_maximum_fusion.6), channel_id=1, source_target_pairs={{0,16},{8,24},{16,0},{24,8},{1,17},{9,25},{17,1},{25,9},{2,18},{10... | collective-permute-start | bytes 6291464 | tf_op jit(solution)/shard_map/ppermute | solution.py:437
  493.7 57.4 %collective-permute-start.33 = (bf16[512,2048]{1,0:T(8,128)(2,1)}, bf16[512,2048]{1,0:T(8,128)(2,1)}, u32[]{:S(2)}, u32[]{:S(2)}) collective-permute-start(bf16[512,2048]{1,0:T(8,128)(2,1)} %pad_maximum_fusion.5), channel_id=1, source_target_pairs={{0,8},{8,0},{16,24},{24,16},{1,9},{9,1},{17,25},{25,17},{2,10},{10... | collective-permute-start | bytes 6291464 | tf_op jit(solution)/shard_map/ppermute | solution.py:437
  551.4 101.2 %reduce-scatter.12.cloned.1.call-start = ((), (), s32[]{:S(2)}) async-start(), calls=%async_computation.14 | async-start | bytes 2359296 | tf_op jit(solution)/shard_map/reduce_scatter | solution.py:782
  554.4 55.7 %collective-permute-start.41 = (bf16[256,2048]{1,0:T(8,128)(2,1)S(1)}, bf16[256,2048]{1,0:T(8,128)(2,1)}, u32[]{:S(2)}, u32[]{:S(2)}) collective-permute-start(bf16[256,2048]{1,0:T(8,128)(2,1)S(1)} %pad_maximum_fusion.9), channel_id=1, source_target_pairs={{0,16},{8,24},{16,0},{24,8},{1,17},{9,25},{17,1},{25,9},{2,18},{10... | collective-permute-start | bytes 3145736 | tf_op jit(solution)/shard_map/ppermute | solution.py:437
  556.3 53.9 %collective-permute-start.40 = (bf16[256,2048]{1,0:T(8,128)(2,1)S(1)}, bf16[256,2048]{1,0:T(8,128)(2,1)}, u32[]{:S(2)}, u32[]{:S(2)}) collective-permute-start(bf16[256,2048]{1,0:T(8,128)(2,1)S(1)} %pad_maximum_fusion.8), channel_id=1, source_target_pairs={{0,8},{8,0},{16,24},{24,16},{1,9},{9,1},{17,25},{25,17},{2,10},{10... | collective-permute-start | bytes 3145736 | tf_op jit(solution)/shard_map/ppermute | solution.py:437
  618.7 85.6 %reduce-scatter.14.cloned.1.call-start = ((), (), s32[]{:S(2)}) async-start(), calls=%async_computation.15 | async-start | bytes 3538944 | tf_op jit(solution)/shard_map/reduce_scatter | solution.py:684
  (71 other events, 1289.4 us)
Sparse Core Ops, SparseCore 0:
  10.4 67.4 all-gather.4
  79.5 80.6 all-gather.6
  161.9 80.5 all-gather.8
  243.9 81.0 all-gather.10
  327.6 89.4 reduce-scatter.5
  432.9 88.6 reduce-scatter.7
  551.5 39.0 reduce-scatter.9
  618.8 33.6 reduce-scatter.11
  654.8 41.6 reduce-scatter.13
